TPU v7x, 32 devices: a whole 2x2x4 slice. The times are simulated.
32 devices in a mesh: seq: 4 (over z), batch: 4 (over x, core), mp: 2 (over y).
Axes of the slice: x: 2, y: 2, z: 4, core: 2. Of those that a mesh axis runs over, the one named last changes fastest.
Arguments:
- layer_input: float32 [8, 4096, 1024], P('batch', 'seq'), may hold values from -6 to 6
- lengths: int32 [8, 4], P('batch'), may hold values from 0 to 4096, as said below
- random_blocks: int32 [8, 64, 3], P('batch', 'seq'), may hold values from 0 to 63, as said below
- first_gain: float32 [1024], replicated, may hold values from 0.25 to 1.75
- first_bias: float32 [1024], replicated, may hold values from -1.5 to 1.5
- qkv_weight: bfloat16 [1024, 3, 1024], P(None, None, 'mp'), may hold values from -0.25 to 0.25
- out_weight: bfloat16 [1024, 1024], P('mp'), may hold values from -1.5 to 1.5
- second_gain: float32 [1024], replicated, may hold values from 0.25 to 1.75
- second_bias: float32 [1024], replicated, may hold values from -1.5 to 1.5
- up_weight: bfloat16 [1024, 4096], P(None, 'mp'), may hold values from -0.1875 to 0.1875
- up_bias: float32 [4096], P('mp'), may hold values from -3 to 3
- down_weight: bfloat16 [4096, 1024], P('mp'), may hold values from -0.09375 to 0.09375
- down_bias: float32 [1024], replicated, may hold values from -3 to 3
- cotangent: float32 [8, 4096, 1024], P('batch', 'seq'), may hold values from -6 to 6
Outputs:
- layer_output: float32 [8, 4096, 1024], P('batch', 'seq')
- input_grad: float32 [8, 4096, 1024], P('batch', 'seq')
- first_gain_grad: float32 [1024], replicated
- first_bias_grad: float32 [1024], replicated
- qkv_grad: float32 [1024, 3, 1024], P('seq', None, 'mp')
- out_grad: float32 [1024, 1024], P('mp', 'seq')
- second_gain_grad: float32 [1024], replicated
- second_bias_grad: float32 [1024], replicated
- up_grad: float32 [1024, 4096], P('seq', 'mp')
- up_bias_grad: float32 [4096], P('mp')
- down_grad: float32 [4096, 1024], P('mp', 'seq')
- down_bias_grad: float32 [1024], replicated
Inputs may be any that keep to these rules, and one draw needn't show every extreme that they name: Row s holds the lengths of the 4 documents packed in order from the first token of sequence s, some possibly empty; the tokens after them are padding. `random_blocks`: entry [s, i, j] is a block of sequence s that holds some token of the document, or of the padding, that holds the first token of block i.
All inputs are finite; a program needn't handle non-finite values.
Results may differ from a plain program's by a relative error of at most 0.019.
The roundings to bfloat16 on the way count: a program that leaves them out, or rounds other values in their place, can miss the bound.
Values may be sent and summed in bfloat16 or wider, within the bound.
A program may use at most 384 MiB of HBM per device.

v0:
```python
import jax
import jax.numpy as jnp
from jax import lax
from jax.sharding import PartitionSpec as P

BLOCK = 64
GLOB = 2
WIN = 3
NBLK = 64
MB = 2
HD = 64
LIST = 8
LEN = 4096


NEG = -1e30
EPS = 1e-05
HIGH = lax.Precision.HIGHEST


def norm_stats(rows):
    centre = rows - jnp.mean(rows, axis=-1, keepdims=True)
    spread = jnp.mean(centre * centre, axis=-1, keepdims=True)
    inverse = lax.rsqrt(spread + EPS)
    return (centre * inverse, inverse)


def norm_back(grad_out, normed, inverse, gain):
    scaled = grad_out * gain
    return inverse * (
        scaled
        - jnp.mean(scaled, axis=-1, keepdims=True)
        - normed * jnp.mean(scaled * normed, axis=-1, keepdims=True)
    )


def segment_of(places, doc_ends):
    return jnp.sum((places[..., None] >= doc_ends).astype(jnp.int32), axis=-1)


def block_lists(blocks, randoms):
    leading = randoms.shape[:-1]
    globals_part = jnp.broadcast_to(jnp.arange(GLOB, dtype=jnp.int32), leading + (GLOB,))
    window_part = jnp.broadcast_to(
        blocks[:, None] + jnp.arange(WIN, dtype=jnp.int32) - WIN // 2, leading + (WIN,)
    )
    block_list = jnp.concatenate([globals_part, window_part, randoms], axis=-1)
    inside = (block_list >= 0) & (block_list < NBLK)
    same_entry = block_list[..., :, None] == block_list[..., None, :]
    order_ids = jnp.arange(LIST)
    earlier = order_ids[None, :] < order_ids[:, None]
    repeated = jnp.any(same_entry & earlier, axis=-1)
    return (block_list, inside & jnp.logical_not(repeated))


def fetch_rows(key_rows, values, wanted):
    batch_seqs, local_rows, head_cols = key_rows.shape
    total_rows = local_rows * lax.axis_size("seq")
    empty_rows = jnp.zeros((batch_seqs, wanted.shape[1], head_cols), jnp.bfloat16)
    initial = (empty_rows, empty_rows)
    empty_whole = jnp.zeros((batch_seqs, total_rows, head_cols), jnp.bfloat16)
    initial = initial + (empty_whole, empty_whole)
    shards_in = (
        lax.all_gather(key_rows, "seq", axis=1, tiled=True),
        lax.all_gather(values, "seq", axis=1, tiled=True),
    )
    piece_rows = shards_in[0].shape[1]
    inside = ((wanted >= 0) & (wanted < piece_rows))[..., None]
    take_index = jnp.clip(wanted, 0, piece_rows - 1)[..., None]
    picked = tuple(
        (
            jnp.where(inside, jnp.take_along_axis(source, take_index, axis=1), previous)
            for source, previous in zip(shards_in, initial[:2])
        )
    )
    placed = tuple((source for source in shards_in))
    return picked + placed


def scatter_rows(kv_source):
    return lax.psum_scatter(
        kv_source.astype(jnp.bfloat16), "seq", scatter_dimension=0, tiled=True
    ).astype(jnp.float32)


def global_partial(seq_item):
    query_rows, key_rows, value_rows, keep_mask = seq_item
    head_count = query_rows.shape[1] // HD
    query_heads = query_rows.reshape(query_rows.shape[0], head_count, HD)
    key_heads = key_rows.reshape(key_rows.shape[0], head_count, HD)
    value_heads = value_rows.astype(jnp.float32).reshape(value_rows.shape[0], head_count, HD)
    raw_scores = jnp.einsum(
        "qhd,khd->hqk", query_heads, key_heads, preferred_element_type=jnp.float32
    ) * HD ** (-0.5)
    masked = jnp.where(keep_mask[None], raw_scores, NEG)
    row_top = jnp.max(masked, axis=-1)
    weights = jnp.exp(masked - row_top[..., None]) * keep_mask[None].astype(jnp.float32)
    numer = jnp.einsum("hqk,khd->hqd", weights, value_heads, precision=HIGH)
    return (row_top, jnp.sum(weights, axis=-1), numer)


def global_back(seq_item):
    query_rows, key_rows, value_rows, keep_mask, row_top, row_total, glob_out, glob_grad = seq_item
    row_count, head_cols = query_rows.shape
    head_count = head_cols // HD
    query_heads = query_rows.reshape(row_count, head_count, HD)
    key_heads = key_rows.reshape(key_rows.shape[0], head_count, HD)
    value_heads = value_rows.astype(jnp.float32).reshape(value_rows.shape[0], head_count, HD)
    raw_scores = jnp.einsum(
        "qhd,khd->hqk", query_heads, key_heads, preferred_element_type=jnp.float32
    ) * HD ** (-0.5)
    masked = jnp.where(keep_mask[None], raw_scores, NEG)
    probs_glob = (
        jnp.exp(masked - row_top[..., None])
        * keep_mask[None].astype(jnp.float32)
        / row_total[..., None]
    )
    grad_heads = glob_grad.astype(jnp.float32).reshape(row_count, head_count, HD)
    prob_grad = jnp.einsum("qhd,khd->hqk", grad_heads, value_heads, precision=HIGH)
    delta = jnp.einsum("qhd,hqd->hq", grad_heads, glob_out, precision=HIGH)
    score_grad = (probs_glob * (prob_grad - delta[..., None])).astype(jnp.bfloat16)
    query_grad = jnp.einsum(
        "hqk,khd->qhd", score_grad, key_heads, preferred_element_type=jnp.float32
    ) * HD ** (-0.5)
    key_grad = jnp.einsum(
        "hqk,qhd->khd", score_grad, query_heads, preferred_element_type=jnp.float32
    ) * HD ** (-0.5)
    value_grad = jnp.einsum("hqk,qhd->khd", probs_glob, grad_heads, precision=HIGH)
    return (
        query_grad.reshape(row_count, head_cols),
        key_grad.reshape(-1, head_cols),
        value_grad.reshape(-1, head_cols),
    )


def local(
    layer_input,
    lengths,
    random_blocks,
    first_gain,
    first_bias,
    qkv_weight,
    out_weight,
    second_gain,
    second_bias,
    up_weight,
    up_bias,
    down_weight,
    down_bias,
    cotangent,
):
    seq_index = lax.axis_index("seq")
    local_seqs, local_rows, model_width = layer_input.shape
    blocks_dev = local_rows // BLOCK
    head_cols = qkv_weight.shape[2]
    head_count = head_cols // HD
    unit_cols = up_weight.shape[1]
    score_scale = HD ** (-0.5)
    glob_rows = GLOB * BLOCK
    batch_seqs = local_seqs // MB
    picked_rows = blocks_dev * LIST * BLOCK
    qkv_flat = qkv_weight.reshape(model_width, 3 * head_cols)
    doc_ends = jnp.cumsum(lengths, axis=1)
    places = seq_index * local_rows + jnp.arange(local_rows, dtype=jnp.int32)
    seg_local = segment_of(places[None, :], doc_ends[:, None, :])
    valid_rows = (places[None, :] < doc_ends[:, -1:]).astype(jnp.float32)
    glob_flag = (places < glob_rows)[None, :, None]
    query_blocks = seq_index * blocks_dev + jnp.arange(blocks_dev, dtype=jnp.int32)
    block_list, admitted = block_lists(query_blocks, random_blocks)
    key_places = block_list[..., None] * BLOCK + jnp.arange(BLOCK, dtype=jnp.int32)
    key_segs = segment_of(key_places, doc_ends[:, None, None, None, :]).reshape(
        local_seqs, blocks_dev, LIST * BLOCK
    )
    admit_keys = jnp.broadcast_to(admitted[..., None], key_places.shape).reshape(
        local_seqs, blocks_dev, LIST * BLOCK
    )
    query_segs = seg_local.reshape(local_seqs, blocks_dev, BLOCK)
    list_mask = admit_keys[:, :, None, :] & (query_segs[..., None] == key_segs[:, :, None, :])
    wanted_all = jnp.clip(key_places, 0, LEN - 1).reshape(local_seqs, picked_rows)
    glob_segs = segment_of(jnp.arange(glob_rows, dtype=jnp.int32)[None, :], doc_ends[:, None, :])
    qkv_total = jnp.zeros((model_width, 3 * head_cols), jnp.float32)
    out_total = jnp.zeros(out_weight.shape, jnp.float32)
    up_total = jnp.zeros(up_weight.shape, jnp.float32)
    down_total = jnp.zeros(down_weight.shape, jnp.float32)
    gain_one_total = jnp.zeros((model_width,), jnp.float32)
    bias_one_total = jnp.zeros((model_width,), jnp.float32)
    gain_two_total = jnp.zeros((model_width,), jnp.float32)
    bias_two_total = jnp.zeros((model_width,), jnp.float32)
    up_bias_total = jnp.zeros((unit_cols,), jnp.float32)
    down_bias_total = jnp.zeros((model_width,), jnp.float32)
    outputs_all = []
    input_grads = []
    for micro_index in range(MB):
        first_seq = micro_index * batch_seqs
        last_seq = first_seq + batch_seqs
        rows_in = layer_input[first_seq:last_seq]
        ends_now = doc_ends[first_seq:last_seq]
        valid_now = valid_rows[first_seq:last_seq]
        mask_now = list_mask[first_seq:last_seq]
        wanted = wanted_all[first_seq:last_seq]
        glob_segs_now = glob_segs[first_seq:last_seq]
        normed_one, inverse_one = norm_stats(rows_in)
        first_low = (
            (normed_one * first_gain + first_bias).astype(jnp.bfloat16).reshape(-1, model_width)
        )
        qkv_rows = (
            jnp.dot(first_low, qkv_flat, preferred_element_type=jnp.float32)
            .astype(jnp.bfloat16)
            .reshape(batch_seqs, local_rows, 3, head_cols)
        )
        queries = qkv_rows[:, :, 0]
        key_rows = qkv_rows[:, :, 1]
        values = qkv_rows[:, :, 2]
        glob_queries_own = queries[:, :glob_rows]
        picked_keys, picked_values, whole_keys, whole_values = fetch_rows(key_rows, values, wanted)
        glob_queries = glob_queries_own
        seg_whole = segment_of(jnp.arange(LEN, dtype=jnp.int32)[None, :], ends_now[:, None, :])
        glob_mask = glob_segs_now[:, :, None] == seg_whole[:, None, :]

        def global_here():
            return lax.map(global_partial, (glob_queries, whole_keys, whole_values, glob_mask))

        def global_skip():
            return (
                jnp.zeros((batch_seqs, head_count, glob_rows), jnp.float32),
                jnp.ones((batch_seqs, head_count, glob_rows), jnp.float32),
                jnp.zeros((batch_seqs, head_count, glob_rows, HD), jnp.float32),
            )

        glob_top, glob_total, glob_numer = lax.cond(seq_index == 0, global_here, global_skip)
        glob_out = glob_numer / glob_total[..., None]
        query_split = queries.reshape(batch_seqs, blocks_dev, BLOCK, head_count, HD)
        key_split = picked_keys.reshape(batch_seqs, blocks_dev, LIST * BLOCK, head_count, HD)
        value_split = picked_values.reshape(batch_seqs, blocks_dev, LIST * BLOCK, head_count, HD)
        raw_scores = (
            jnp.einsum(
                "sbqhd,sbkhd->sbhqk", query_split, key_split, preferred_element_type=jnp.float32
            )
            * score_scale
        )
        keep_now = mask_now[:, :, None]
        masked = jnp.where(keep_now, raw_scores, NEG)
        row_top = jnp.max(masked, axis=-1, keepdims=True)
        weights = jnp.exp(masked - row_top) * keep_now.astype(jnp.float32)
        row_total = jnp.sum(weights, axis=-1, keepdims=True)
        probs_list = weights / row_total
        probs_low = probs_list.astype(jnp.bfloat16)
        listed = jnp.einsum(
            "sbhqk,sbkhd->sbqhd", probs_low, value_split, preferred_element_type=jnp.float32
        ).reshape(batch_seqs, local_rows, head_cols)
        glob_rows_out = jnp.transpose(glob_out, (0, 2, 1, 3)).reshape(
            batch_seqs, glob_rows, head_cols
        )
        glob_full = jnp.pad(glob_rows_out, ((0, 0), (0, local_rows - glob_rows), (0, 0)))
        attended = jnp.where(glob_flag, glob_full, listed) * valid_now[..., None]
        attended_low = attended.astype(jnp.bfloat16).reshape(-1, head_cols)
        branch = lax.psum(
            jnp.dot(attended_low, out_weight, preferred_element_type=jnp.float32).astype(
                jnp.bfloat16
            ),
            "mp",
        ).astype(jnp.float32)
        hidden = rows_in + branch.reshape(rows_in.shape)
        normed_two, inverse_two = norm_stats(hidden)
        second_low = (
            (normed_two * second_gain + second_bias).astype(jnp.bfloat16).reshape(-1, model_width)
        )
        pre_act = jnp.dot(second_low, up_weight, preferred_element_type=jnp.float32) + up_bias
        activated = jax.nn.gelu(pre_act, approximate=True).astype(jnp.bfloat16)
        ffn_branch = lax.psum(
            jnp.dot(activated, down_weight, preferred_element_type=jnp.float32).astype(
                jnp.bfloat16
            ),
            "mp",
        ).astype(jnp.float32)
        outputs_all.append(hidden + ffn_branch.reshape(rows_in.shape) + down_bias)
        grad_rows = cotangent[first_seq:last_seq].reshape(-1, model_width)
        down_bias_total = down_bias_total + jnp.sum(grad_rows, axis=0)
        grad_low = grad_rows.astype(jnp.bfloat16)
        down_total = down_total + jnp.einsum(
            "rf,rd->fd", activated, grad_low, preferred_element_type=jnp.float32
        )
        act_grad = jnp.einsum(
            "rd,fd->rf", grad_low, down_weight, preferred_element_type=jnp.float32
        )
        _, gelu_pull = jax.vjp(lambda inner: jax.nn.gelu(inner, approximate=True), pre_act)
        pre_grad = gelu_pull(act_grad)[0].astype(jnp.bfloat16)
        up_bias_total = up_bias_total + jnp.sum(pre_grad.astype(jnp.float32), axis=0)
        up_total = up_total + jnp.einsum(
            "rd,rf->df", second_low, pre_grad, preferred_element_type=jnp.float32
        )
        second_grad = (
            lax.psum(
                jnp.einsum(
                    "rf,df->rd", pre_grad, up_weight, preferred_element_type=jnp.float32
                ).astype(jnp.bfloat16),
                "mp",
            )
            .astype(jnp.float32)
            .reshape(rows_in.shape)
        )
        gain_two_total = gain_two_total + jnp.sum(second_grad * normed_two, axis=(0, 1))
        bias_two_total = bias_two_total + jnp.sum(second_grad, axis=(0, 1))
        hidden_grad = grad_rows.reshape(rows_in.shape) + norm_back(
            second_grad, normed_two, inverse_two, second_gain
        )
        hidden_low = hidden_grad.astype(jnp.bfloat16).reshape(-1, model_width)
        out_total = out_total + jnp.einsum(
            "rc,rd->cd", attended_low, hidden_low, preferred_element_type=jnp.float32
        )
        attended_grad = jnp.einsum(
            "rd,cd->rc", hidden_low, out_weight, preferred_element_type=jnp.float32
        ).astype(jnp.bfloat16).reshape(batch_seqs, local_rows, head_cols) * valid_now[
            ..., None
        ].astype(
            jnp.bfloat16
        )
        list_grad = jnp.where(glob_flag, jnp.zeros_like(attended_grad), attended_grad).reshape(
            batch_seqs, blocks_dev, BLOCK, head_count, HD
        )
        prob_grad = jnp.einsum(
            "sbqhd,sbkhd->sbhqk", list_grad, value_split, preferred_element_type=jnp.float32
        )
        delta = jnp.sum(probs_list * prob_grad, axis=-1, keepdims=True)
        score_grad = (probs_list * (prob_grad - delta)).astype(jnp.bfloat16)
        query_grad = (
            jnp.einsum(
                "sbhqk,sbkhd->sbqhd", score_grad, key_split, preferred_element_type=jnp.float32
            )
            * score_scale
        ).reshape(batch_seqs, local_rows, head_cols)
        key_picked_grad = (
            jnp.einsum(
                "sbhqk,sbqhd->sbkhd", score_grad, query_split, preferred_element_type=jnp.float32
            )
            * score_scale
        )
        value_picked_grad = jnp.einsum(
            "sbhqk,sbqhd->sbkhd", probs_low, list_grad, preferred_element_type=jnp.float32
        )
        picked_grads = jnp.concatenate(
            [
                key_picked_grad.reshape(batch_seqs, picked_rows, head_cols),
                value_picked_grad.reshape(batch_seqs, picked_rows, head_cols),
            ],
            axis=-1,
        )
        seg_ids = wanted * batch_seqs + jnp.arange(batch_seqs, dtype=jnp.int32)[:, None]
        kv_term = jax.ops.segment_sum(
            picked_grads.reshape(batch_seqs * picked_rows, 2 * head_cols),
            seg_ids.reshape(-1),
            num_segments=LEN * batch_seqs,
        ).reshape(LEN, batch_seqs, 2 * head_cols)
        glob_grad_own = attended_grad[:, :glob_rows]

        def back_here():
            return lax.map(
                global_back,
                (
                    glob_queries,
                    whole_keys,
                    whole_values,
                    glob_mask,
                    glob_top,
                    glob_total,
                    glob_out,
                    glob_grad_own,
                ),
            )

        def back_skip():
            return (
                jnp.zeros((batch_seqs, glob_rows, head_cols), jnp.float32),
                jnp.zeros((batch_seqs, LEN, head_cols), jnp.float32),
                jnp.zeros((batch_seqs, LEN, head_cols), jnp.float32),
            )

        glob_query_grad, whole_key_grad, whole_value_grad = lax.cond(
            seq_index == 0, back_here, back_skip
        )
        glob_dense = jnp.transpose(
            jnp.concatenate([whole_key_grad, whole_value_grad], axis=-1), (1, 0, 2)
        )
        kv_source = kv_term + glob_dense
        kv_grad = jnp.transpose(scatter_rows(kv_source), (1, 0, 2))
        glob_query_full = jnp.pad(glob_query_grad, ((0, 0), (0, local_rows - glob_rows), (0, 0)))
        query_total = query_grad + jnp.where(glob_flag, glob_query_full, 0.0)
        qkv_low_grad = (
            jnp.stack([query_total, kv_grad[..., :head_cols], kv_grad[..., head_cols:]], axis=2)
            .astype(jnp.bfloat16)
            .reshape(-1, 3 * head_cols)
        )
        qkv_total = qkv_total + jnp.einsum(
            "rd,rc->dc", first_low, qkv_low_grad, preferred_element_type=jnp.float32
        )
        first_grad = (
            lax.psum(
                jnp.einsum(
                    "rc,dc->rd", qkv_low_grad, qkv_flat, preferred_element_type=jnp.float32
                ).astype(jnp.bfloat16),
                "mp",
            )
            .astype(jnp.float32)
            .reshape(rows_in.shape)
        )
        gain_one_total = gain_one_total + jnp.sum(first_grad * normed_one, axis=(0, 1))
        bias_one_total = bias_one_total + jnp.sum(first_grad, axis=(0, 1))
        input_grads.append(hidden_grad + norm_back(first_grad, normed_one, inverse_one, first_gain))
    matrix_grads = (
        lax.psum_scatter(
            qkv_total.reshape(model_width, 3, head_cols).astype(jnp.bfloat16),
            "seq",
            scatter_dimension=0,
            tiled=True,
        ).astype(jnp.float32),
        lax.psum_scatter(
            out_total.astype(jnp.bfloat16), "seq", scatter_dimension=1, tiled=True
        ).astype(jnp.float32),
        lax.psum_scatter(
            up_total.astype(jnp.bfloat16), "seq", scatter_dimension=0, tiled=True
        ).astype(jnp.float32),
        lax.psum_scatter(
            down_total.astype(jnp.bfloat16), "seq", scatter_dimension=1, tiled=True
        ).astype(jnp.float32),
    )
    matrix_grads = (
        lax.psum(matrix_grads[0].astype(jnp.bfloat16), "batch").astype(jnp.float32),
        lax.psum(matrix_grads[1].astype(jnp.bfloat16), "batch").astype(jnp.float32),
        lax.psum(matrix_grads[2].astype(jnp.bfloat16), "batch").astype(jnp.float32),
        lax.psum(matrix_grads[3].astype(jnp.bfloat16), "batch").astype(jnp.float32),
    )
    vector_grads = lax.psum(
        (
            gain_one_total,
            bias_one_total,
            gain_two_total,
            bias_two_total,
            up_bias_total,
            down_bias_total,
        ),
        ("seq", "batch"),
    )
    return (
        jnp.concatenate(outputs_all, axis=0),
        jnp.concatenate(input_grads, axis=0),
        vector_grads[0],
        vector_grads[1],
        matrix_grads[0],
        matrix_grads[1],
        vector_grads[2],
        vector_grads[3],
        matrix_grads[2],
        vector_grads[4],
        matrix_grads[3],
        vector_grads[5],
    )


def solution(mesh):
    placed = (
        P("batch", "seq", None),
        P("batch", None),
        P("batch", "seq", None),
        P(),
        P(),
        P(None, None, "mp"),
        P("mp", None),
        P(),
        P(),
        P(None, "mp"),
        P("mp"),
        P("mp", None),
        P(),
        P("batch", "seq", None),
    )
    return jax.shard_map(
        local,
        mesh=mesh,
        in_specs=placed,
        out_specs=(
            P("batch", "seq", None),
            P("batch", "seq", None),
            P(),
            P(),
            P("seq", None, "mp"),
            P("mp", "seq"),
            P(),
            P(),
            P("seq", "mp"),
            P("mp"),
            P("mp", "seq"),
            P(),
        ),
        check_vma=False,
    )
```

profile of v0, /device:TPU:0, one launch (start us, length us, event | category | flops | bytes accessed | tf_op | source)
XLA Modules:
  0.0 2626.9 jit_solution(2381194683994051421)
XLA Ops:
  79.8 42.3 %all-gather.13.cloned.1.call-done = bf16[1,4096,1,512]{3,1,2,0:T(8,128)(2,1)} async-done(((bf16[1,1024,1,512]{3,1,2,0:T(8,128)(2,1)}), bf16[1,4096,1,512]{3,1,2,0:T(8,128)(2,1)}) %all-gather.13.cloned.1.call-update) | async-done | bytes 4194320 | tf_op jit(solution)/shard_map/all_gather | solution.py:64
  122.1 80.9 %all-gather.15.cloned.1.call-done = bf16[1,4096,1,512]{3,1,2,0:T(8,128)(2,1)} async-done(((bf16[1,1024,1,512]{3,1,2,0:T(8,128)(2,1)}), bf16[1,4096,1,512]{3,1,2,0:T(8,128)(2,1)}) %all-gather.15.cloned.1.call-update) | async-done | bytes 4194320 | tf_op jit(solution)/shard_map/all_gather | solution.py:65
  203.0 43.6 %conditional.5 = (f32[1,8,128]{2,1,0:T(8,128)}, f32[1,8,128]{2,1,0:T(8,128)S(1)}, f32[1,8,128,64]{2,3,1,0:T(8,128)S(1)}) conditional(s32[]{:T(128)} %convert_element_type.322, () %tuple.55, (pred[1,128,4096]{2,1,0:T(8,128)(4,1)}, bf16[1,128,512]{1,2,0:T(8,128)(2,1)S(1)}, bf16[1,4096,512]{2,1,0:T(8,128)(2,1)}, ...), branch_computations={%region_21.23_spmd, %region_22.26_spmd} | conditional | flops 3808950272 | bytes 84295704 | solution.py:230
  247.5 36.4 %all-gather.9.cloned.1.call-done = bf16[1,4096,1,512]{3,1,2,0:T(8,128)(2,1)} async-done(((bf16[1,1024,1,512]{3,1,2,0:T(8,128)(2,1)}), bf16[1,4096,1,512]{3,1,2,0:T(8,128)(2,1)}) %all-gather.9.cloned.1.call-update) | async-done | bytes 4194320 | tf_op jit(solution)/shard_map/all_gather | solution.py:64
  283.9 80.7 %all-gather.11.cloned.1.call-done = bf16[1,4096,1,512]{3,1,2,0:T(8,128)(2,1)} async-done(((bf16[1,1024,1,512]{3,1,2,0:T(8,128)(2,1)}), bf16[1,4096,1,512]{3,1,2,0:T(8,128)(2,1)}) %all-gather.11.cloned.1.call-update) | async-done | bytes 4194320 | tf_op jit(solution)/shard_map/all_gather | solution.py:65
  364.7 42.6 %conditional.4 = (f32[1,8,128]{2,1,0:T(8,128)}, f32[1,8,128]{2,1,0:T(8,128)S(1)}, f32[1,8,128,64]{2,3,1,0:T(8,128)S(1)}) conditional(s32[]{:T(128)} %convert_element_type.322, () %tuple.53, (pred[1,128,4096]{2,1,0:T(8,128)(4,1)S(1)}, bf16[1,128,512]{1,2,0:T(8,128)(2,1)S(1)}, bf16[1,4096,512]{2,1,0:T(8,128)(2,1)}, ...), branch_computations={%region_5.6_spmd, %region_6.9_spmd} | conditional | flops 3808950272 | bytes 84295704 | solution.py:230
  408.2 36.6 %gather_fusion = bf16[8192,512]{1,0:T(8,128)(2,1)} fusion(bf16[4096,512]{1,0:T(8,128)(2,1)} %bitcast.462, s32[8192]{0:T(1024)S(1)} %broadcast_clamp_fusion.4), kind=kCustom, calls=%fused_computation.clone | custom fusion | bytes 16809984 | tf_op jit(solution)/shard_map/jit(take_along_axis)/gather | solution.py:72
  444.8 36.7 %gather_fusion.1 = bf16[8192,512]{1,0:T(8,128)(2,1)} fusion(bf16[4096,512]{1,0:T(8,128)(2,1)} %bitcast.459, s32[8192]{0:T(1024)S(1)} %broadcast_clamp_fusion.4), kind=kCustom, calls=%fused_computation.1.clone | custom fusion | bytes 16809984 | tf_op jit(solution)/shard_map/jit(take_along_axis)/gather | solution.py:72
  537.6 36.7 %gather_fusion.2 = bf16[8192,512]{1,0:T(8,128)(2,1)} fusion(bf16[4096,512]{1,0:T(8,128)(2,1)} %bitcast.468, s32[8192]{0:T(1024)S(1)} %broadcast_clamp_fusion.3), kind=kCustom, calls=%fused_computation.2.clone | custom fusion | bytes 16809984 | tf_op jit(solution)/shard_map/jit(take_along_axis)/gather | solution.py:72
  574.3 36.7 %gather_fusion.3 = bf16[8192,512]{1,0:T(8,128)(2,1)} fusion(bf16[4096,512]{1,0:T(8,128)(2,1)} %bitcast.465, s32[8192]{0:T(1024)S(1)} %broadcast_clamp_fusion.3), kind=kCustom, calls=%fused_computation.3.clone | custom fusion | bytes 16809984 | tf_op jit(solution)/shard_map/jit(take_along_axis)/gather | solution.py:72
  824.6 106.5 %all-reduce.22.cloned.1.call-done = (bf16[1,1024,1024]{2,1,0:T(8,128)(2,1)}, bf16[1,1024,1024]{2,1,0:T(8,128)(2,1)}) async-done(((bf16[1,1024,1024]{2,1,0:T(8,128)(2,1)}, bf16[1,1024,1024]{2,1,0:T(8,128)(2,1)}), (bf16[1,1024,1024]{2,1,0:T(8,128)(2,1)}, bf16[1,1024,1024]{2,1,0:T(8,128)(2,1)})) %all-reduce.22.cloned.1.call-update) | async-done | bytes 4194320 | tf_op jit(solution)/shard_map/psum | solution.py:257
  999.7 106.9 %all-reduce.20.cloned.1.call-done = (bf16[1024,1024]{1,0:T(8,128)(2,1)}, bf16[1024,1024]{1,0:T(8,128)(2,1)}) async-done(((bf16[1024,1024]{1,0:T(8,128)(2,1)}, bf16[1024,1024]{1,0:T(8,128)(2,1)}), (bf16[1024,1024]{1,0:T(8,128)(2,1)}, bf16[1024,1024]{1,0:T(8,128)(2,1)})) %all-reduce.20.cloned.1.call-update) | async-done | bytes 4194320 | tf_op jit(solution)/shard_map/psum | solution.py:293
  1308.8 75.3 %conditional.7 = (f32[1,1024,512]{2,1,0:T(8,128)S(1)}, f32[1,4096,512]{2,1,0:T(8,128)}, f32[1,4096,512]{2,1,0:T(8,128)}) conditional(s32[]{:T(128)} %convert_element_type.322, () %tuple.59, (pred[1,128,4096]{2,1,0:T(8,128)(4,1)}, bf16[1,128,512]{1,2,0:T(8,128)(2,1)S(1)}, bf16[1,4096,512]{2,1,0:T(8,128)(2,1)}, f32[1,8,128]{2,1,0:T(8,128)}, ...), branch_computations={%region_46.48_spmd, %region_47.49_spmd} | conditional | flops 5405080576 | bytes 235028608 | solution.py:378
  1396.6 82.4 %scatter_fusion.1 = f32[4096,1024]{1,0:T(8,128)} fusion(f32[4096,1024]{1,0:T(8,128)} %maximum_bitcast_fusion.3, s32[8192]{0:T(1024)S(1)} %copy-done.64, f32[8192,1024]{1,0:T(8,128)} %copy.259), kind=kCustom, calls=%fused_computation.5 | custom fusion | flops 8388608 | bytes 100696064 | tf_op jit(solution)/shard_map/scatter-add | solution.py:349
  1637.9 33.5 %copy.242 = f32[8192,1024]{1,0:T(8,128)} copy(f32[8192,1024]{0,1:T(8,128)} %maximum_bitcast_fusion) | data formatting | bytes 67108864 | tf_op jit(solution)/shard_map/reshape | solution.py:350
  1671.5 75.1 %conditional.6 = (f32[1,1024,512]{2,1,0:T(8,128)S(1)}, f32[1,4096,512]{2,1,0:T(8,128)}, f32[1,4096,512]{2,1,0:T(8,128)}) conditional(s32[]{:T(128)} %convert_element_type.322, () %tuple.57, (pred[1,128,4096]{2,1,0:T(8,128)(4,1)S(1)}, bf16[1,128,512]{1,2,0:T(8,128)(2,1)S(1)}, bf16[1,4096,512]{2,1,0:T(8,128)(2,1)}, f32[1,8,128]{2,1,0:T(8,128)}, ...), branch_computations={%region_35.37_spmd, %region_36.38_spmd} | conditional | flops 5405080576 | bytes 235028608 | solution.py:378
  1759.1 82.4 %scatter_fusion = f32[4096,1024]{1,0:T(8,128)} fusion(f32[4096,1024]{1,0:T(8,128)} %maximum_bitcast_fusion.2, s32[8192]{0:T(1024)S(1)} %copy-done.65, f32[8192,1024]{1,0:T(8,128)} %copy.242), kind=kCustom, calls=%fused_computation.4 | custom fusion | flops 8388608 | bytes 100696064 | tf_op jit(solution)/shard_map/scatter-add | solution.py:349
  1952.0 40.9 %reduce-scatter.7.cloned.1.call-done = bf16[1024,1,1024]{2,0,1:T(8,128)(2,1)} async-done(((bf16[4096,1,1024]{2,0,1:T(8,128)(2,1)}), bf16[1024,1,1024]{2,0,1:T(8,128)(2,1)}) %reduce-scatter.7.cloned.1.call-update) | async-done | bytes 2097168 | tf_op jit(solution)/shard_map/reduce_scatter | solution.py:81
  2043.0 57.8 %reduce-scatter.17.cloned.1.call-done = bf16[2048,256]{1,0:T(8,128)(2,1)} async-done(((bf16[2048,1024]{1,0:T(8,128)(2,1)}), bf16[2048,256]{1,0:T(8,128)(2,1)}) %reduce-scatter.17.cloned.1.call-update) | async-done | bytes 1048592 | tf_op jit(solution)/shard_map/reduce_scatter | solution.py:422
  2100.8 79.6 %reduce-scatter.15.cloned.1.call-done = bf16[256,2048]{1,0:T(8,128)(2,1)} async-done(((bf16[1024,2048]{1,0:T(8,128)(2,1)}), bf16[256,2048]{1,0:T(8,128)(2,1)}) %reduce-scatter.15.cloned.1.call-update) | async-done | bytes 1048592 | tf_op jit(solution)/shard_map/reduce_scatter | solution.py:419
  2180.5 63.0 %reduce-scatter.11.cloned.1.call-done = bf16[256,3,512]{0,2,1:T(8,128)(2,1)} async-done(((bf16[1024,3,512]{0,2,1:T(8,128)(2,1)}), bf16[256,3,512]{0,2,1:T(8,128)(2,1)}) %reduce-scatter.11.cloned.1.call-update) | async-done | bytes 786448 | tf_op jit(solution)/shard_map/reduce_scatter | solution.py:410
  2257.1 58.3 %all-reduce.16.cloned.1.call-done = (bf16[256,3,512]{0,2,1:T(8,128)(2,1)}, bf16[512,256]{1,0:T(8,128)(2,1)}, bf16[256,2048]{1,0:T(8,128)(2,1)}, bf16[2048,256]{1,0:T(8,128)(2,1)}) async-done(((bf16[256,3,512]{0,2,1:T(8,128)(2,1)}, bf16[512,256]{1,0:T(8,128)(2,1)}, bf16[256,2048]{1,0:T(8,128)(2,1)}, bf16[2048,256]{1,0:T(8,128)(2,1)}), (bf16[256,3,512]{0,2,1:T(8,128)(2,1)}, bf16[512,256]{1,0:T(8,128)(2,1)}, ...) | async-done | bytes 3145744 | tf_op jit(solution)/shard_map/psum | solution.py:427
  2324.0 194.3 %all-reduce.18.cloned.1.call-done = (bf16[1,1024,1024]{2,1,0:T(8,128)(2,1)}, bf16[1,1024,1024]{2,1,0:T(8,128)(2,1)}, bf16[1024,1024]{1,0:T(8,128)(2,1)}, bf16[1024,1024]{1,0:T(8,128)(2,1)}) async-done(((bf16[1,1024,1024]{2,1,0:T(8,128)(2,1)}, bf16[1,1024,1024]{2,1,0:T(8,128)(2,1)}, bf16[1024,1024]{1,0:T(8,128)(2,1)}, bf16[1024,1024]{1,0:T(8,128)(2,1)}), (bf16[1,1024,1024]{2,1,0:T(8,128)(2,1)}, ...) | async-done | bytes 8388624 | tf_op jit(solution)/shard_map/psum | solution.py:270
  2558.9 61.2 %all-reduce.6 = (f32[1024]{0:T(1024)}, f32[1024]{0:T(1024)}, f32[1024]{0:T(1024)}, f32[1024]{0:T(1024)}, f32[2048]{0:T(1024)}, /*index=5*/f32[1024]{0:T(1024)}) all-reduce(f32[1024]{0:T(1024)S(1)} %add.348, f32[1024]{0:T(1024)S(1)} %add.349, f32[1024]{0:T(1024)S(1)} %add.352, ...), channel_id=1, replica_groups=mesh['seq'=4,'batch'=4,'mp'=2] {'seq','batch'}, use_global_device_ids=true, to_apply=%region_55.57 | all-reduce | flops 7168 | bytes 57344 | tf_op jit(solution)/shard_map/psum | solution.py:432
  (522 shorter events, 1256.0 us)
Async XLA Ops:
  7.2 812.1 %copy-start = (bf16[512,1024]{1,0:T(8,128)(2,1)S(1)}, bf16[512,1024]{1,0:T(8,128)(2,1)}, u32[]{:S(2)}) copy-start(bf16[512,1024]{1,0:T(8,128)(2,1)} %param.30) | copy-start | bytes 3145732
  7.2 115.0 %all-gather.13.cloned.1.call-start = ((), (), s32[]{:S(2)}) async-start(), calls=%async_computation.14 | async-start | bytes 5242880 | tf_op jit(solution)/shard_map/all_gather | solution.py:64
  38.5 164.5 %all-gather.15.cloned.1.call-start = ((), (), s32[]{:S(2)}) async-start(), calls=%async_computation.15 | async-start | bytes 5242880 | tf_op jit(solution)/shard_map/all_gather | solution.py:65
  39.9 244.0 %all-gather.9.cloned.1.call-start = ((), (), s32[]{:S(2)}) async-start(), calls=%async_computation.12 | async-start | bytes 5242880 | tf_op jit(solution)/shard_map/all_gather | solution.py:64
  59.3 305.4 %all-gather.11.cloned.1.call-start = ((), (), s32[]{:S(2)}) async-start(), calls=%async_computation.13 | async-start | bytes 5242880 | tf_op jit(solution)/shard_map/all_gather | solution.py:65
  61.6 869.5 %all-reduce.22.cloned.1.call-start = ((), (), s32[]{:S(2)}) async-start(), calls=%async_computation.19 | async-start | bytes 8388608 | tf_op jit(solution)/shard_map/psum | solution.py:257
  66.1 137.0 %copy-start.55 = (bf16[1,128,512]{1,2,0:T(8,128)(2,1)}, bf16[1,128,512]{1,2,0:T(8,128)(2,1)S(1)}, u32[]{:S(2)}) copy-start(bf16[1,128,512]{1,2,0:T(8,128)(2,1)S(1)} %slice.146) | copy-start | bytes 393220
  69.3 295.4 %copy-start.53 = (bf16[1,128,512]{1,2,0:T(8,128)(2,1)}, bf16[1,128,512]{1,2,0:T(8,128)(2,1)S(1)}, u32[]{:S(2)}) copy-start(bf16[1,128,512]{1,2,0:T(8,128)(2,1)S(1)} %slice.139) | copy-start | bytes 393220
  78.7 286.0 %copy-start.21 = (pred[1,128,4096]{2,1,0:T(8,128)(4,1)}, pred[1,128,4096]{2,1,0:T(8,128)(4,1)S(1)}, u32[]{:S(2)}) copy-start(pred[1,128,4096]{2,1,0:T(8,128)(4,1)S(1)} %broadcast_compare_fusion.1) | copy-start | bytes 1572868
  246.6 118.1 %copy-start.102 = (f32[1,8,128]{2,1,0:T(8,128)}, f32[1,8,128]{2,1,0:T(8,128)S(1)}, u32[]{:S(2)}) copy-start(f32[1,8,128]{2,1,0:T(8,128)S(1)} %get-tuple-element.226) | copy-start | bytes 12292
  246.7 118.0 %copy-start.49 = (f32[1,8,128,64]{2,3,1,0:T(8,128)}, f32[1,8,128,64]{2,3,1,0:T(8,128)S(1)}, u32[]{:S(2)}) copy-start(f32[1,8,128,64]{2,3,1,0:T(8,128)S(1)} %broadcast_divide_fusion.2) | copy-start | bytes 786436
  824.6 282.0 %all-reduce.20.cloned.1.call-start = ((), (), s32[]{:S(2)}) async-start(), calls=%async_computation.18 | async-start | bytes 8388608 | tf_op jit(solution)/shard_map/psum | solution.py:293
  936.7 178.7 %copy-start.76 = (f32[1024]{0:T(1024)}, f32[1024]{0:T(1024)S(1)}, u32[]{:S(2)}) copy-start(f32[1024]{0:T(1024)S(1)} %broadcast_multiply_fusion.11) | copy-start | bytes 12292
  936.8 178.7 %copy-start.74 = (f32[1024]{0:T(1024)}, f32[1024]{0:T(1024)S(1)}, u32[]{:S(2)}) copy-start(f32[1024]{0:T(1024)S(1)} %broadcast_multiply_fusion.9) | copy-start | bytes 12292
  937.4 178.1 %copy-start.86 = (f32[1024]{0:T(1024)}, f32[1024]{0:T(1024)S(1)}, u32[]{:S(2)}) copy-start(f32[1024]{0:T(1024)S(1)} %add_rsqrt_fusion) | copy-start | bytes 12292
  941.8 173.6 %copy-start.88 = (f32[1024]{0:T(1024)}, f32[1024]{0:T(1024)S(1)}, u32[]{:S(2)}) copy-start(f32[1024]{0:T(1024)S(1)} %add_rsqrt_fusion.2) | copy-start | bytes 12292
  998.2 945.2 %reduce-scatter.9.cloned.1.call-start = ((), (), s32[]{:S(2)}) async-start(), calls=%async_computation.7 | async-start | bytes 10485760 | tf_op jit(solution)/shard_map/reduce_scatter | solution.py:81
  1488.2 504.8 %reduce-scatter.7.cloned.1.call-start = ((), (), s32[]{:S(2)}) async-start(), calls=%async_computation.6 | async-start | bytes 10485760 | tf_op jit(solution)/shard_map/reduce_scatter | solution.py:81
  1850.7 192.3 %reduce-scatter.13.cloned.1.call-start = ((), (), s32[]{:S(2)}) async-start(), calls=%async_computation.9 | async-start | bytes 1310720 | tf_op jit(solution)/shard_map/reduce_scatter | solution.py:416
  1859.6 241.2 %reduce-scatter.17.cloned.1.call-start = ((), (), s32[]{:S(2)}) async-start(), calls=%async_computation.11 | async-start | bytes 5242880 | tf_op jit(solution)/shard_map/reduce_scatter | solution.py:422
  1883.1 297.3 %reduce-scatter.15.cloned.1.call-start = ((), (), s32[]{:S(2)}) async-start(), calls=%async_computation.10 | async-start | bytes 5242880 | tf_op jit(solution)/shard_map/reduce_scatter | solution.py:419
  1899.2 344.3 %reduce-scatter.11.cloned.1.call-start = ((), (), s32[]{:S(2)}) async-start(), calls=%async_computation.8 | async-start | bytes 3932160 | tf_op jit(solution)/shard_map/reduce_scatter | solution.py:410
  2021.2 294.1 %all-reduce.16.cloned.1.call-start = ((), (), s32[]{:S(2)}) async-start(), calls=%async_computation.16 | async-start | bytes 6291456 | tf_op jit(solution)/shard_map/psum | solution.py:427
  2243.5 274.8 %all-reduce.18.cloned.1.call-start = ((), (), s32[]{:S(2)}) async-start(), calls=%async_computation.17 | async-start | bytes 16777216 | tf_op jit(solution)/shard_map/psum | solution.py:270
  (119 other events, 1219.5 us)
Sparse Core Ops, SparseCore 0:
  38.6 83.4 all-gather.12
  123.7 79.2 all-gather.14
  204.6 79.2 all-gather.8
  285.4 79.2 all-gather.10
  824.7 106.3 all-reduce.21
  998.3 108.2 all-reduce.19
  1488.3 141.7 reduce-scatter.8
  1850.8 142.0 reduce-scatter.6
  1995.3 27.8 reduce-scatter.12
  2025.4 75.4 reduce-scatter.16
  2103.1 77.2 reduce-scatter.14
  2182.7 60.7 reduce-scatter.10
  2246.3 69.0 all-reduce.15
  2318.6 199.6 all-reduce.17
where the time goes:
time: 2640 us; the launch traced here: 2630 us
  waiting for transfers between devices  948 us (36%)
  local copies, waits for them, and re-layouts  736 us (28%)
  matrix products  442 us (17%)
  other arithmetic  421 us (16%)
  blocking collectives  61.2 us (2%)
    another operation x26, local copies, waits for them, and re-layouts  226 us
    psum x1, waiting for transfers between devices, local(): lax.psum(jnp.dot(activated, down_weight, preferred_element_type=jnp.float...  194 us
    scatter-add x2, other arithmetic, local(): jax.ops.segment_sum(picked_grads.reshape(batch_seqs * picked_rows, 2 * he...  165 us
    all_gather x2, waiting for transfers between devices, fetch_rows(): lax.all_gather(values, 'seq', axis=1, tiled=True)  162 us
    gather x4, local copies, waits for them, and re-layouts, fetch_rows(): jnp.take_along_axis(source, take_index, axis=1)  147 us
    psum x1, waiting for transfers between devices, local(): lax.psum(jnp.einsum('rf,df->rd', pre_grad, up_weight, preferred_element_t...  107 us
    psum x1, waiting for transfers between devices, local(): lax.psum(jnp.dot(attended_low, out_weight, preferred_element_type=jnp.flo...  107 us
    reduce_scatter x1, waiting for transfers between devices, local(): lax.psum_scatter(up_total.astype(jnp.bfloat16), 'seq', scatter_dimension=...  79.6 us
  transfers between devices with their start and end apart: 14, of which 12 were waited for; matrix products, arithmetic and copies ran while one was open for 23% of the time, Pallas kernels for 0%

commit v1 on v0

--- a/solution.py
+++ b/solution.py
@@ -1,21 +1,23 @@
+import functools
+
 import jax
 import jax.numpy as jnp
 from jax import lax
+from jax.experimental import pallas as pl
+from jax.experimental.pallas import tpu as pltpu
 from jax.sharding import PartitionSpec as P
 
 BLOCK = 64
 GLOB = 2
 WIN = 3
-NBLK = 64
-MB = 2
 HD = 64
 LIST = 8
-LEN = 4096
-
 
 NEG = -1e30
 EPS = 1e-05
-HIGH = lax.Precision.HIGHEST
+F32 = jnp.float32
+BF16 = jnp.bfloat16
+VMEM_LIMIT = 60 * 1024 * 1024
 
 
 def norm_stats(rows):
@@ -34,11 +36,573 @@
     )
 
 
+def block_lists(blocks, randoms, block_count):
+    leading = randoms.shape[:-1]
+    globals_part = jnp.broadcast_to(jnp.arange(GLOB, dtype=jnp.int32), leading + (GLOB,))
+    window_part = jnp.broadcast_to(
+        blocks[:, None] + jnp.arange(WIN, dtype=jnp.int32) - WIN // 2, leading + (WIN,)
+    )
+    block_list = jnp.concatenate([globals_part, window_part, randoms], axis=-1)
+    inside = (block_list >= 0) & (block_list < block_count)
+    same_entry = block_list[..., :, None] == block_list[..., None, :]
+    order_ids = jnp.arange(LIST)
+    earlier = order_ids[None, :] < order_ids[:, None]
+    repeated = jnp.any(same_entry & earlier, axis=-1)
+    admitted = inside & jnp.logical_not(repeated)
+    return (jnp.clip(block_list, 0, block_count - 1), admitted.astype(jnp.int32))
+
+
+def segment_at(places, ends_ref):
+    total = jnp.zeros(places.shape, jnp.int32)
+    for doc in range(ends_ref.shape[0]):
+        total = total + (places >= ends_ref[doc]).astype(jnp.int32)
+    return total
+
+
+def head_spread(rows, heads):
+    lane_head = lax.broadcasted_iota(jnp.int32, rows.shape, 1) // HD
+    return jnp.concatenate(
+        [rows * (lane_head == head).astype(rows.dtype) for head in range(heads)], axis=0
+    )
+
+
+def head_fold(wide, heads):
+    rows = wide.shape[0] // heads
+    lane_head = lax.broadcasted_iota(jnp.int32, (rows, wide.shape[1]), 1) // HD
+    folded = jnp.zeros((rows, wide.shape[1]), wide.dtype)
+    for head in range(heads):
+        folded = jnp.where(lane_head == head, wide[head * rows : (head + 1) * rows], folded)
+    return folded
+
+
+def fill_segments(key_segs, ends_ref):
+    def fill(block, _):
+        places = block * BLOCK + lax.broadcasted_iota(jnp.int32, (BLOCK, key_segs.shape[1]), 0)
+        key_segs[pl.ds(pl.multiple_of(block * BLOCK, BLOCK), BLOCK), :] = segment_at(places, ends_ref)
+        return 0
+
+    lax.fori_loop(0, key_segs.shape[0] // BLOCK, fill, 0)
+
+
+def query_segments(block, heads, ends_ref):
+    lanes = lax.broadcasted_iota(jnp.int32, (8, heads * BLOCK), 1)
+    return segment_at(block * BLOCK + lanes % BLOCK, ends_ref)[0:1]
+
+
+def block_rows(ref, block):
+    return ref[pl.ds(pl.multiple_of(block * BLOCK, BLOCK), BLOCK), :]
+
+
+def dot_nt(left, right):
+    return lax.dot_general(left, right, (((1,), (1,)), ((), ())), preferred_element_type=F32)
+
+
+def dot_tn(left, right):
+    return lax.dot_general(left, right, (((0,), (0,)), ((), ())), preferred_element_type=F32)
+
+
+def dot_nn(left, right):
+    return lax.dot_general(left, right, (((1,), (0,)), ((), ())), preferred_element_type=F32)
+
+
+def listed_scores(block, starts, keeps, query_wide, k_ref, key_segs, seg_row):
+    keys = jnp.concatenate([block_rows(k_ref, start) for start in starts], axis=0)
+    scores = dot_nt(keys, query_wide)
+    pieces = []
+    for entry in range(LIST):
+        wanted = jnp.where(keeps[entry] > 0, seg_row, -1)
+        keep = block_rows(key_segs, starts[entry]) == wanted
+        pieces.append(jnp.where(keep, scores[entry * BLOCK : (entry + 1) * BLOCK], NEG))
+    return keys, jnp.concatenate(pieces, axis=0)
+
+
+def forward_kernel(
+    heads, ends_ref, lists_ref, admit_ref, q_ref, k_ref, v_ref, o_ref, lse_ref, key_segs, held
+):
+    scale = HD ** (-0.5)
+    rows_total = q_ref.shape[0]
+    blocks = rows_total // BLOCK
+    chunk = LIST * BLOCK
+    fill_segments(key_segs, ends_ref)
+
+    def store(block, wide, top, total):
+        out = head_fold(wide, heads)
+        places = block * BLOCK + lax.broadcasted_iota(jnp.int32, out.shape, 0)
+        out = jnp.where(places < ends_ref[ends_ref.shape[0] - 1], out, 0.0)
+        o_ref[pl.ds(pl.multiple_of(block * BLOCK, BLOCK), BLOCK), :] = out.astype(BF16)
+        lse_ref[block] = jnp.broadcast_to(top + jnp.log(total), lse_ref.shape[1:])
+
+    def global_block(block, _):
+        query_wide = head_spread(block_rows(q_ref, block) * scale, heads)
+        seg_row = query_segments(block, heads, ends_ref)
+
+        def score(part, top):
+            here = pl.ds(pl.multiple_of(part * chunk, chunk), chunk)
+            scores = dot_nt(k_ref[here, :], query_wide)
+            scores = jnp.where(key_segs[here, :] == seg_row, scores, NEG)
+            held[here, :] = scores
+            return jnp.maximum(top, jnp.max(scores, axis=0, keepdims=True))
+
+        top = lax.fori_loop(
+            0, rows_total // chunk, score, jnp.full((1, heads * BLOCK), NEG, F32)
+        )
+
+        def weigh(part, total):
+            here = pl.ds(pl.multiple_of(part * chunk, chunk), chunk)
+            weights = jnp.exp(held[here, :] - top)
+            held[here, :] = weights
+            return total + jnp.sum(weights, axis=0, keepdims=True)
+
+        total = lax.fori_loop(
+            0, rows_total // chunk, weigh, jnp.zeros((1, heads * BLOCK), F32)
+        )
+        inverse = 1.0 / total
+
+        def gather(part, wide):
+            here = pl.ds(pl.multiple_of(part * chunk, chunk), chunk)
+            probs = (held[here, :] * inverse).astype(BF16)
+            return wide + dot_tn(probs, v_ref[here, :])
+
+        wide = lax.fori_loop(
+            0,
+            rows_total // chunk,
+            gather,
+            jnp.zeros((heads * BLOCK, q_ref.shape[1]), F32),
+        )
+        store(block, wide, top, total)
+        return 0
+
+    lax.fori_loop(0, GLOB, global_block, 0)
+
+    def listed_block(block):
+        query_wide = head_spread(block_rows(q_ref, block) * scale, heads)
+        seg_row = query_segments(block, heads, ends_ref)
+        starts = [lists_ref[block * LIST + entry] for entry in range(LIST)]
+        keeps = [admit_ref[block * LIST + entry] for entry in range(LIST)]
+        _, scores = listed_scores(block, starts, keeps, query_wide, k_ref, key_segs, seg_row)
+        top = jnp.max(scores, axis=0, keepdims=True)
+        weights = jnp.exp(scores - top)
+        total = jnp.sum(weights, axis=0, keepdims=True)
+        probs = (weights * (1.0 / total)).astype(BF16)
+        values = jnp.concatenate([block_rows(v_ref, start) for start in starts], axis=0)
+        store(block, dot_tn(probs, values), top, total)
+
+    def listed_pair(pair, _):
+        listed_block(GLOB + 2 * pair)
+        listed_block(GLOB + 2 * pair + 1)
+        return 0
+
+    lax.fori_loop(0, (blocks - GLOB) // 2, listed_pair, 0)
+
+
+def backward_kernel(
+    heads,
+    ends_ref,
+    lists_ref,
+    admit_ref,
+    q_ref,
+    k_ref,
+    v_ref,
+    o_ref,
+    do_ref,
+    lse_ref,
+    out_ref,
+    key_segs,
+    dk_ref,
+    dv_ref,
+    dq_ref,
+):
+    scale = HD ** (-0.5)
+    rows_total, cols = q_ref.shape
+    blocks = rows_total // BLOCK
+    chunk = LIST * BLOCK
+    fill_segments(key_segs, ends_ref)
+
+    def clear(block, _):
+        here = pl.ds(pl.multiple_of(block * BLOCK, BLOCK), BLOCK)
+        dk_ref[here, :] = jnp.zeros((BLOCK, cols), F32)
+        dv_ref[here, :] = jnp.zeros((BLOCK, cols), F32)
+        return 0
+
+    lax.fori_loop(0, blocks, clear, 0)
+
+    def query_side(block):
+        query_wide = head_spread(block_rows(q_ref, block) * scale, heads)
+        grad_rows = block_rows(do_ref, block)
+        grad_wide = head_spread(grad_rows, heads)
+        product = grad_rows.astype(F32) * block_rows(o_ref, block).astype(F32)
+        spread = head_spread(product, heads).astype(BF16)
+        delta = dot_nt(jnp.ones((8, cols), BF16), spread)[0:1]
+        return query_wide, grad_wide, delta, lse_ref[block, 0:1]
+
+    def grads(scores, keys, values, query_wide, grad_wide, delta, lse):
+        probs = jnp.exp(scores - lse)
+        prob_grad = dot_nt(values, grad_wide)
+        score_grad = (probs * (prob_grad - delta)).astype(BF16)
+        dk = dot_nn(score_grad, query_wide)
+        dv = dot_nn(probs.astype(BF16), grad_wide)
+        dq = dot_tn(score_grad, keys)
+        return dk, dv, dq
+
+    def store_query(block, wide):
+        here = pl.ds(pl.multiple_of(block * BLOCK, BLOCK), BLOCK)
+        out_ref[here, 0:cols] = (head_fold(wide, heads) * scale).astype(BF16)
+
+    def global_block(block, _):
+        query_wide, grad_wide, delta, lse = query_side(block)
+        seg_row = query_segments(block, heads, ends_ref)
+        dq_ref[...] = jnp.zeros_like(dq_ref)
+
+        def part_of(part, _):
+            here = pl.ds(pl.multiple_of(part * chunk, chunk), chunk)
+            keys = k_ref[here, :]
+            scores = jnp.where(key_segs[here, :] == seg_row, dot_nt(keys, query_wide), NEG)
+            dk, dv, dq = grads(scores, keys, v_ref[here, :], query_wide, grad_wide, delta, lse)
+            dk_ref[here, :] += dk
+            dv_ref[here, :] += dv
+            dq_ref[...] += dq
+            return 0
+
+        lax.fori_loop(0, rows_total // chunk, part_of, 0)
+        store_query(block, dq_ref[...])
+        return 0
+
+    lax.fori_loop(0, GLOB, global_block, 0)
+
+    def listed_block(block):
+        query_wide, grad_wide, delta, lse = query_side(block)
+        seg_row = query_segments(block, heads, ends_ref)
+        starts = [lists_ref[block * LIST + entry] for entry in range(LIST)]
+        keeps = [admit_ref[block * LIST + entry] for entry in range(LIST)]
+        keys, scores = listed_scores(block, starts, keeps, query_wide, k_ref, key_segs, seg_row)
+        values = jnp.concatenate([block_rows(v_ref, start) for start in starts], axis=0)
+        dk, dv, dq = grads(scores, keys, values, query_wide, grad_wide, delta, lse)
+        store_query(block, dq)
+        for entry in range(LIST):
+            here = pl.ds(pl.multiple_of(starts[entry] * BLOCK, BLOCK), BLOCK)
+            dk_ref[here, :] += dk[entry * BLOCK : (entry + 1) * BLOCK]
+            dv_ref[here, :] += dv[entry * BLOCK : (entry + 1) * BLOCK]
+
+    def listed_pair(pair, _):
+        listed_block(GLOB + 2 * pair)
+        listed_block(GLOB + 2 * pair + 1)
+        return 0
+
+    lax.fori_loop(0, (blocks - GLOB) // 2, listed_pair, 0)
+
+    def finish(block, _):
+        here = pl.ds(pl.multiple_of(block * BLOCK, BLOCK), BLOCK)
+        out_ref[here, cols : 2 * cols] = dk_ref[here, :].astype(BF16)
+        out_ref[here, 2 * cols : 3 * cols] = dv_ref[here, :].astype(BF16)
+        return 0
+
+    lax.fori_loop(0, blocks, finish, 0)
+
+
+def smem():
+    return pl.BlockSpec(memory_space=pltpu.SMEM)
+
+
+def column(rows, cols, index):
+    return pl.BlockSpec((rows, cols), lambda step: (0, index))
+
+
+def attention_forward(qkv, doc_ends, lists, admits, cols):
+    rows = qkv.shape[0]
+    heads = cols // HD
+    blocks = rows // BLOCK
+    return pl.pallas_call(
+        functools.partial(forward_kernel, heads),
+        grid=(1,),
+        in_specs=[smem(), smem(), smem()] + [column(rows, cols, part) for part in range(3)],
+        out_specs=[
+            column(rows, cols, 0),
+            pl.BlockSpec((blocks, 8, heads * BLOCK), lambda step: (0, 0, 0)),
+        ],
+        out_shape=[
+            jax.ShapeDtypeStruct((rows, cols), BF16),
+            jax.ShapeDtypeStruct((blocks, 8, heads * BLOCK), F32),
+        ],
+        scratch_shapes=[
+            pltpu.VMEM((rows, heads * BLOCK), jnp.int32),
+            pltpu.VMEM((rows, heads * BLOCK), F32),
+        ],
+        compiler_params=pltpu.CompilerParams(vmem_limit_bytes=VMEM_LIMIT),
+        cost_estimate=pl.CostEstimate(
+            flops=8 * rows * 10 * LIST * BLOCK * cols * heads,
+            bytes_accessed=8 * rows * cols,
+            transcendentals=0,
+        ),
+    )(doc_ends, lists, admits, qkv, qkv, qkv)
+
+
+def attention_backward(qkv, attended, attended_grad, lse, doc_ends, lists, admits, cols):
+    rows = qkv.shape[0]
+    heads = cols // HD
+    blocks = rows // BLOCK
+    return pl.pallas_call(
+        functools.partial(backward_kernel, heads),
+        grid=(1,),
+        in_specs=[smem(), smem(), smem()]
+        + [column(rows, cols, part) for part in range(3)]
+        + [
+            column(rows, cols, 0),
+            column(rows, cols, 0),
+            pl.BlockSpec((blocks, 8, heads * BLOCK), lambda step: (0, 0, 0)),
+        ],
+        out_specs=column(rows, 3 * cols, 0),
+        out_shape=jax.ShapeDtypeStruct((rows, 3 * cols), BF16),
+        scratch_shapes=[
+            pltpu.VMEM((rows, heads * BLOCK), jnp.int32),
+            pltpu.VMEM((rows, cols), F32),
+            pltpu.VMEM((rows, cols), F32),
+            pltpu.VMEM((heads * BLOCK, cols), F32),
+        ],
+        compiler_params=pltpu.CompilerParams(vmem_limit_bytes=VMEM_LIMIT),
+        cost_estimate=pl.CostEstimate(
+            flops=20 * rows * 10 * LIST * BLOCK * cols * heads,
+            bytes_accessed=20 * rows * cols,
+            transcendentals=0,
+        ),
+    )(doc_ends, lists, admits, qkv, qkv, qkv, attended, attended_grad, lse)
+
+
+def swap(value, axis, distance=1):
+    size = lax.axis_size(axis)
+    return lax.ppermute(value, axis, [(j, j ^ distance) for j in range(size)])
+
+
+def all_to_all(value):
+    return lax.all_to_all(value, "seq", 0, 0, tiled=True)
+
+
+def batch_levels():
+    return [1 << level for level in range(lax.axis_size("batch").bit_length() - 1)]
+
+
+def pick(value, index, count):
+    size = value.shape[0] // count
+    return lax.dynamic_slice_in_dim(value, index * size, size, 0)
+
+
+def fetch_other(weight):
+    parity = lax.axis_index("batch") % 2
+    first = swap(pick(weight, parity, 2), "mp")
+    return first, swap(first, "batch")
+
+
+def narrow_add(mine, received):
+    return (mine.astype(F32) + received.astype(F32)).astype(BF16)
+
+
+def halve(value, distance):
+    side = (lax.axis_index("batch") // distance) % 2
+    return narrow_add(pick(value, side, 2), swap(pick(value, 1 - side, 2), "batch", distance))
+
+
+def unhalve(value, distance):
+    side = (lax.axis_index("batch") // distance) % 2
+    other = swap(value, "batch", distance)
+    low = jnp.where(side == 0, value, other)
+    high = jnp.where(side == 0, other, value)
+    return jnp.concatenate([low, high], axis=0)
+
+
+def reduce_units(own, near, far):
+    levels = batch_levels()
+    near = narrow_add(near, swap(far, "batch"))
+    for distance in levels:
+        own = halve(own, distance)
+    for distance in levels[1:]:
+        near = halve(near, distance)
+    own = narrow_add(own, swap(near, "mp"))
+    own = lax.psum_scatter(own, "seq", scatter_dimension=1, tiled=True)
+    for distance in reversed(levels):
+        own = unhalve(own, distance)
+    return own.astype(F32)
+
+
+def both_sequences(own):
+    place = lax.axis_index("mp")
+    other = swap(own, "mp").astype(F32)
+    mine = own.astype(F32)
+    return jnp.concatenate(
+        [jnp.where(place == 0, mine, other), jnp.where(place == 0, other, mine)], axis=0
+    )
+
+
+def local(
+    layer_input,
+    lengths,
+    random_blocks,
+    first_gain,
+    first_bias,
+    qkv_weight,
+    out_weight,
+    second_gain,
+    second_bias,
+    up_weight,
+    up_bias,
+    down_weight,
+    down_bias,
+    cotangent,
+):
+    seq_count = lax.axis_size("seq")
+    seq_index = lax.axis_index("seq")
+    mp_index = lax.axis_index("mp")
+    parity = lax.axis_index("batch") % 2
+    _, local_rows, width = layer_input.shape
+    rows_total = local_rows * seq_count
+    blocks = rows_total // BLOCK
+    half_cols = qkv_weight.shape[2]
+    cols = width // seq_count
+    units = up_weight.shape[1]
+
+    rows_in = lax.dynamic_index_in_dim(layer_input, mp_index, 0, keepdims=False)
+    grad_rows = lax.dynamic_index_in_dim(cotangent, mp_index, 0, keepdims=False)
+    doc_ends = jnp.cumsum(lax.dynamic_index_in_dim(lengths, mp_index, 0, keepdims=False))
+    randoms = lax.dynamic_index_in_dim(random_blocks, mp_index, 0, keepdims=False)
+    randoms = lax.all_gather(randoms, "seq", axis=0, tiled=True)
+    lists, admits = block_lists(jnp.arange(blocks, dtype=jnp.int32), randoms, blocks)
+    lists, admits = lists.reshape(-1), admits.reshape(-1)
+    places = seq_index * local_rows + jnp.arange(local_rows, dtype=jnp.int32)
+    valid = (places < doc_ends[-1])[:, None]
+
+    own_half = (seq_index * cols) // half_cols
+    candidate = lax.dynamic_slice_in_dim(qkv_weight, (seq_index * cols) % half_cols, cols, 2)
+    pairs = []
+    for place in range(seq_count):
+        source = (place * cols) // half_cols
+        pairs.append((place * 2 + source, place * 2 + 1 - source))
+    fetched = lax.ppermute(candidate, ("seq", "mp"), pairs)
+    qkv_own = jnp.where(mp_index == own_half, candidate, fetched).reshape(width, 3 * cols)
+    up_own = up_weight.T
+    up_near, up_far = fetch_other(up_own)
+    down_near, down_far = fetch_other(down_weight)
+    out_full = lax.all_gather(out_weight, "mp", axis=0, tiled=True)
+    bias_near, bias_far = fetch_other(up_bias)
+    up_parts = (up_own, up_near, up_far)
+    down_parts = (down_weight, down_near, down_far)
+    bias_parts = (up_bias, bias_near, bias_far)
+
+    normed_one, inverse_one = norm_stats(rows_in)
+    first_low = (normed_one * first_gain + first_bias).astype(BF16)
+    first_all = lax.all_gather(first_low, "seq", axis=0, tiled=True)
+    qkv = jnp.dot(first_all, qkv_own, preferred_element_type=F32).astype(BF16)
+    attended, lse = attention_forward(qkv, doc_ends, lists, admits, cols)
+    attended_low = all_to_all(attended.reshape(seq_count, local_rows, cols))
+    attended_low = attended_low.transpose(1, 0, 2).reshape(local_rows, width)
+    hidden = rows_in + jnp.dot(attended_low, out_full, preferred_element_type=F32)
+    normed_two, inverse_two = norm_stats(hidden)
+    second_low = (normed_two * second_gain + second_bias).astype(BF16)
+    grad_low = grad_rows.astype(BF16)
+    ffn = jnp.zeros((local_rows, width), F32)
+    second_grad = jnp.zeros((local_rows, width), F32)
+    activations, pre_grads, bias_sums = [], [], []
+    for up_part, down_part, bias_part in zip(up_parts, down_parts, bias_parts):
+        pre_act = dot_nt(second_low, up_part) + bias_part
+        activated = jax.nn.gelu(pre_act, approximate=True).astype(BF16)
+        activations.append(activated)
+        ffn = ffn + jnp.dot(activated, down_part, preferred_element_type=F32)
+        act_grad = dot_nt(grad_low, down_part)
+        _, gelu_pull = jax.vjp(lambda inner: jax.nn.gelu(inner, approximate=True), pre_act)
+        pre_grad = gelu_pull(act_grad)[0].astype(BF16)
+        pre_grads.append(pre_grad)
+        bias_sums.append(jnp.sum(pre_grad.astype(F32), axis=0))
+        second_grad = second_grad + jnp.dot(pre_grad, up_part, preferred_element_type=F32)
+    output_low = lax.optimization_barrier((hidden + ffn + down_bias).astype(BF16))
+    layer_output = both_sequences(output_low[None])
+
+    hidden_grad = grad_rows + norm_back(second_grad, normed_two, inverse_two, second_gain)
+    hidden_low = hidden_grad.astype(BF16)
+    attended_grad = dot_nt(hidden_low, out_full).astype(BF16)
+    attended_grad = jnp.where(valid, attended_grad, jnp.zeros_like(attended_grad))
+    grad_all = all_to_all(attended_grad.reshape(local_rows, seq_count, cols).transpose(1, 0, 2))
+    grad_all = grad_all.reshape(rows_total, cols)
+    down_grads = [dot_tn(activated, grad_low).astype(BF16) for activated in activations]
+    up_grads = [dot_tn(pre_grad, second_low).astype(BF16) for pre_grad in pre_grads]
+    down_grad = reduce_units(*down_grads)
+    up_grad = reduce_units(*up_grads)
+    out_sum = dot_tn(attended_low, hidden_low).astype(BF16)
+    out_other = pick(out_sum, 1 - mp_index, 2)
+    out_grad = reduce_units(
+        pick(out_sum, mp_index, 2), pick(out_other, parity, 2), pick(out_other, 1 - parity, 2)
+    )
+    bias_other = jnp.where(
+        parity == 0,
+        jnp.concatenate([bias_sums[1], bias_sums[2]]),
+        jnp.concatenate([bias_sums[2], bias_sums[1]]),
+    )
+    bias_all = jnp.where(
+        mp_index == 0,
+        jnp.concatenate([bias_sums[0], bias_other]),
+        jnp.concatenate([bias_other, bias_sums[0]]),
+    )
+    early = lax.psum(
+        jnp.concatenate(
+            [
+                jnp.sum(grad_rows, axis=0),
+                jnp.sum(second_grad * normed_two, axis=0),
+                jnp.sum(second_grad, axis=0),
+                bias_all,
+            ]
+        ),
+        ("seq", "batch", "mp"),
+    )
+
+    qkv_low_grad = attention_backward(
+        qkv, attended, grad_all, lse, doc_ends, lists, admits, cols
+    )
+    first_part = dot_nt(qkv_low_grad, qkv_own).astype(BF16)
+    first_grad = lax.psum_scatter(first_part, "seq", scatter_dimension=0, tiled=True).astype(F32)
+    qkv_sum = dot_tn(first_all, qkv_low_grad).astype(BF16)
+    qkv_sum = qkv_sum.reshape(seq_count, -1, 3 * cols).transpose(1, 0, 2)
+    levels = batch_levels()
+    for distance in levels:
+        qkv_sum = halve(qkv_sum, distance)
+    qkv_sum = narrow_add(qkv_sum, swap(qkv_sum, "mp"))
+    qkv_sum = all_to_all(qkv_sum.transpose(1, 0, 2))
+    qkv_sum = pick(qkv_sum, mp_index, 2)
+    qkv_sum = qkv_sum.reshape(seq_count // 2, -1, 3, cols).transpose(1, 2, 0, 3)
+    qkv_sum = qkv_sum.reshape(-1, 3, half_cols)
+    for distance in reversed(levels):
+        qkv_sum = unhalve(qkv_sum, distance)
+    qkv_grad = qkv_sum.astype(F32)
+
+    late = lax.psum(
+        jnp.concatenate([jnp.sum(first_grad * normed_one, axis=0), jnp.sum(first_grad, axis=0)]),
+        ("seq", "batch", "mp"),
+    )
+    input_low = hidden_grad + norm_back(first_grad, normed_one, inverse_one, first_gain)
+    input_grad = both_sequences(lax.optimization_barrier(input_low.astype(BF16))[None])
+    up_bias_grad = lax.dynamic_slice_in_dim(early, 3 * width + mp_index * units, units)
+    return (
+        layer_output,
+        input_grad,
+        late[:width],
+        late[width:],
+        qkv_grad,
+        out_grad,
+        early[width : 2 * width],
+        early[2 * width : 3 * width],
+        up_grad.T,
+        up_bias_grad,
+        down_grad,
+        early[:width],
+    )
+
+
+MB = 2
+NBLK = 64
+LEN = 4096
+HIGH = lax.Precision.HIGHEST
+
+
 def segment_of(places, doc_ends):
     return jnp.sum((places[..., None] >= doc_ends).astype(jnp.int32), axis=-1)
 
 
-def block_lists(blocks, randoms):
+def block_lists_by_index(blocks, randoms):
     leading = randoms.shape[:-1]
     globals_part = jnp.broadcast_to(jnp.arange(GLOB, dtype=jnp.int32), leading + (GLOB,))
     window_part = jnp.broadcast_to(
@@ -133,7 +697,7 @@
     )
 
 
-def local(
+def local_by_blocks(
     layer_input,
     lengths,
     random_blocks,
@@ -166,7 +730,7 @@
     valid_rows = (places[None, :] < doc_ends[:, -1:]).astype(jnp.float32)
     glob_flag = (places < glob_rows)[None, :, None]
     query_blocks = seq_index * blocks_dev + jnp.arange(blocks_dev, dtype=jnp.int32)
-    block_list, admitted = block_lists(query_blocks, random_blocks)
+    block_list, admitted = block_lists_by_index(query_blocks, random_blocks)
     key_places = block_list[..., None] * BLOCK + jnp.arange(BLOCK, dtype=jnp.int32)
     key_segs = segment_of(key_places, doc_ends[:, None, None, None, :]).reshape(
         local_seqs, blocks_dev, LIST * BLOCK
@@ -473,8 +1037,9 @@
         P(),
         P("batch", "seq", None),
     )
+    by_heads = (1024 // mesh.shape["seq"]) % 128 == 0
     return jax.shard_map(
-        local,
+        local if by_heads else local_by_blocks,
         mesh=mesh,
         in_specs=placed,
         out_specs=(

time: 2640 us -> 968 us (0.37)
  local copies, waits for them, and re-layouts: 736 us -> 62.2 us
  waiting for transfers between devices: 948 us -> 367 us
  other arithmetic: 421 us -> 88.9 us
  matrix products: 442 us -> 175 us
  Pallas kernels: 0 us -> 110 us
  starting transfers between devices: 1.9 us -> 50.1 us
  blocking collectives: 61.2 us -> 90.7 us
    psum x4 -> x0, waiting for transfers between devices: 466 us -> none  [the longest x1 194 us: local(): lax.psum(jnp.dot(activated, down_weight, preferred_element_type=jnp.float...]
    another operation x32 -> x0, local copies, waits for them, and re-layouts: 240 us -> none
    dot_general x48 -> x24, matrix products: 413 us -> 175 us  [the longest x8 62.4 us: dot_nt(): lax.dot_general(left, right, (((1,), (1,)), ((), ())), preferred_element_...]
    ppermute x0 -> x35, waiting for transfers between devices: none -> 172 us  [the longest x34 162 us: swap(): return lax.ppermute(value, axis, [(j, j ^ distance) for j in range(size)])]
    reduce_scatter x6 -> x4, waiting for transfers between devices: 241 us -> 74.1 us  [the longest x1 74.1 us: local(): lax.psum_scatter(first_part, 'seq', scatter_dimension=0, tiled=True)]
    scatter-add x2 -> x0, other arithmetic: 165 us -> none  [local(): jax.ops.segment_sum(picked_grads.reshape(batch_seqs * picked_rows, 2 * he...]
    reshape x12 -> x5, local copies, waits for them, and re-layouts: 160 us -> 8.09 us  [the longest x1 3.94 us: local(): attended_low = all_to_all(attended.reshape(seq_count, local_rows, cols))]
    gather x4 -> x0, local copies, waits for them, and re-layouts: 147 us -> none  [fetch_rows(): jnp.take_along_axis(source, take_index, axis=1)]
  transfers between devices with their start and end apart: 14 -> 44, of which waited for: 12 -> 14; matrix products, arithmetic and copies ran while one was open for 23% -> 25% of each run, Pallas kernels for 0% -> 6%
where the time goes in v1:
time: 968 us; the launch traced here: 961 us
  waiting for transfers between devices  367 us (38%)
  matrix products  175 us (18%)
  Pallas kernels  110 us (11%)
  blocking collectives  90.7 us (9%)
  other arithmetic  88.9 us (9%)
  local copies, waits for them, and re-layouts  62.2 us (6%)
  starting transfers between devices  50.1 us (5%)
  between operations  17 us (2%)
    ppermute x34, waiting for transfers between devices, swap(): return lax.ppermute(value, axis, [(j, j ^ distance) for j in range(size)])  162 us
    all_gather x1, waiting for transfers between devices, local(): first_all = lax.all_gather(first_low, 'seq', axis=0, tiled=True)  111 us
    reduce_scatter x1, waiting for transfers between devices, local(): lax.psum_scatter(first_part, 'seq', scatter_dimension=0, tiled=True)  74.1 us
    psum x1, blocking collectives, local(): lax.psum(jnp.concatenate([jnp.sum(first_grad * normed_one, axis=0), jnp.s...  71.6 us
    dot_general x8, matrix products, dot_nt(): lax.dot_general(left, right, (((1,), (1,)), ((), ())), preferred_element_...  62.4 us
    pallas_call x1, Pallas kernels, attention_forward(): pl.pallas_call(functools.partial(forward_kernel, heads), grid=(1,), in_sp...  55.7 us
    pallas_call x1, Pallas kernels, attention_backward(): pl.pallas_call(functools.partial(backward_kernel, heads), grid=(1,), in_s...  54.7 us
    dot_general x8, matrix products, dot_tn(): lax.dot_general(left, right, (((0,), (0,)), ((), ())), preferred_element_...  49.6 us
  transfers between devices with their start and end apart: 44, of which 14 were waited for; matrix products, arithmetic and copies ran while one was open for 25% of the time, Pallas kernels for 6%

profile of v1, /device:TPU:0, one launch (start us, length us, event | category | flops | bytes accessed | tf_op | source)
XLA Modules:
  0.0 960.7 jit_solution(16883305800325579789)
XLA Ops:
  32.7 19.1 %all-gather = s32[1,64,3]{2,0,1:T(1,128)S(1)} all-gather(s32[1,16,3]{2,0,1:T(1,128)S(1)} %copy.129), channel_id=2, replica_groups=mesh['seq'=4,'batch'=4,'mp'=2] {'seq'}, dimensions={1}, use_global_device_ids=true | all-gather | bytes 960 | tf_op jit(solution)/shard_map/all_gather | solution.py:465
  54.3 10.7 %collective-permute-done = bf16[1024,3,256]{0,2,1:T(8,128)(2,1)} collective-permute-done((bf16[1024,3,256]{0,2,1:T(8,128)(2,1)S(1)}, bf16[1024,3,256]{0,2,1:T(8,128)(2,1)}, u32[]{:S(2)}, u32[]{:S(2)}) %collective-permute-start) | collective-permute-done | bytes 1572896 | tf_op jit(solution)/shard_map/ppermute | solution.py:477
  65.2 111.0 %all-gather.4.cloned.1.call-done = bf16[4096,1024]{0,1:T(8,128)(2,1)} async-done(((bf16[1024,1024]{0,1:T(8,128)(2,1)}), bf16[4096,1024]{0,1:T(8,128)(2,1)}) %all-gather.4.cloned.1.call-update) | async-done | bytes 8388624 | tf_op jit(solution)/shard_map/all_gather | solution.py:490
  176.2 12.2 %convolution_convert_fusion.1.q_ref.k_ref.v_ref = bf16[4096,768]{1,0:T(8,128)(2,1)} fusion(bf16[4096,1024]{0,1:T(8,128)(2,1)} %all-gather.4.cloned.1.call-done, bf16[1024,768]{0,1:T(8,128)(2,1)S(1)} %bitcast.95), kind=kOutput, calls=%fused_computation.14 | convolution fusion | flops 6445596672 | bytes 16252928 | tf_op jit(solution)/shard_map/dot_general | solution.py:491
  188.4 55.7 %shard_map.229 = (bf16[4096,256]{1,0:T(8,128)(2,1)}, f32[64,8,256]{2,1,0:T(8,128)}) custom-call(s32[4]{0:T(128)} %bitcast.101, s32[512]{0:T(512)} %min.12.lists_ref, s32[512]{0:T(512)} %reshape.155.admit_ref, bf16[4096,768]{1,0:T(8,128)(2,1)} %convolution_convert_fusion.1.q_ref.k_ref.v_ref, bf16[4096,768]{1,0:T(8,128)(2,1)} %convolution_convert_fusion.1.q_ref.k_ref.v_ref, ...), custom_call_target="tpu_custom_call" | custom-call | flops 171798691840 | bytes 8388608 | tf_op jit(solution)/shard_map/pallas_call | solution.py:314
  276.3 95.2 %collective-permute-done.2 = f32[1024]{0:T(1024)S(1)} collective-permute-done((f32[1024]{0:T(1024)S(1)}, f32[1024]{0:T(1024)S(1)}, u32[]{:S(2)}, u32[]{:S(2)}) %collective-permute-start.2) | collective-permute-done | bytes 4128 | tf_op jit(solution)/shard_map/ppermute | solution.py:372
  389.1 10.2 %convolution_convert_fusion.2 = bf16[2048,1024]{1,0:T(8,128)(2,1)S(1)} fusion(bf16[1024,1024]{0,1:T(8,128)(2,1)S(1)} %bitcast_convert_fusion, f32[1024,2048]{1,0:T(8,128)} %fusion.47, f32[2048]{0:T(1024)S(1)} %copy-done.41), kind=kOutput, calls=%fused_computation.71 | convolution fusion | flops 4318035968 | bytes 14688256 | tf_op jit(solution)/shard_map/dot_general | solution.py:101
  399.3 15.8 %convert_reduce_fusion = (f32[2048]{0:T(1024)}, bf16[1024,2048]{1,0:T(8,128)(2,1)}) fusion(f32[1024,2048]{1,0:T(8,128)} %fusion.47, f32[2048]{0:T(1024)S(1)} %copy-done.41, bf16[1024,1024]{0,1:T(8,128)(2,1)S(1)} %bitcast_convert_fusion, bf16[2048,1024]{1,0:T(8,128)(2,1)S(1)} %copy-done.23), kind=kOutput, calls=%fused_computation.11 | convolution fusion | flops 4343199744 | bytes 18890752 | tf_op jit(solution)/shard_map/dot_general | solution.py:97
  531.8 14.7 %collective-permute-done.29 = bf16[512,1024]{1,0:T(8,128)(2,1)} collective-permute-done((bf16[512,1024]{1,0:T(8,128)(2,1)}, bf16[512,1024]{1,0:T(8,128)(2,1)}, u32[]{:S(2)}, u32[]{:S(2)}) %collective-permute-start.29) | collective-permute-done | bytes 1048608 | tf_op jit(solution)/shard_map/ppermute | solution.py:372
  554.9 14.1 %collective-permute-done.24 = bf16[512,1024]{1,0:T(8,128)(2,1)} collective-permute-done((bf16[512,1024]{1,0:T(8,128)(2,1)}, bf16[512,1024]{1,0:T(8,128)(2,1)}, u32[]{:S(2)}, u32[]{:S(2)}) %collective-permute-start.24) | collective-permute-done | bytes 1048608 | tf_op jit(solution)/shard_map/ppermute | solution.py:372
  572.2 18.5 %collective-permute-done.22 = bf16[512,1024]{1,0:T(8,128)(2,1)S(1)} collective-permute-done((bf16[512,1024]{1,0:T(8,128)(2,1)S(1)}, bf16[512,1024]{1,0:T(8,128)(2,1)S(1)}, u32[]{:S(2)}, u32[]{:S(2)}) %collective-permute-start.22) | collective-permute-done | bytes 1048608 | tf_op jit(solution)/shard_map/ppermute | solution.py:372
  596.2 54.7 %shard_map.230 = bf16[4096,768]{1,0:T(8,128)(2,1)} custom-call(s32[4]{0:T(128)} %bitcast.102, s32[512]{0:T(512)} %min.12.lists_ref, s32[512]{0:T(512)} %reshape.155.admit_ref, bf16[4096,768]{1,0:T(8,128)(2,1)} %convolution_convert_fusion.1.q_ref.k_ref.v_ref, bf16[4096,768]{1,0:T(8,128)(2,1)} %convolution_convert_fusion.1.q_ref.k_ref.v_ref, ...), custom_call_target="tpu_custom_call" | custom-call | flops 429496729600 | bytes 20971520 | tf_op jit(solution)/shard_map/pallas_call | solution.py:343
  650.9 11.8 %convolution_convert_fusion = bf16[4096,1024]{0,1:T(8,128)(2,1)} fusion(bf16[4096,768]{1,0:T(8,128)(2,1)} %shard_map.230, bf16[1024,768]{0,1:T(8,128)(2,1)S(1)} %bitcast.96), kind=kOutput, calls=%fused_computation.13 | convolution fusion | flops 6446645248 | bytes 16252928 | tf_op jit(solution)/shard_map/dot_general | solution.py:97
  662.7 11.1 %convolution_convert_fusion.7 = bf16[1024,768]{1,0:T(8,128)(2,1)S(1)} fusion(bf16[4096,1024]{0,1:T(8,128)(2,1)} %all-gather.4.cloned.1.call-done, bf16[4096,768]{1,0:T(8,128)(2,1)} %shard_map.230), kind=kOutput, calls=%fused_computation.86 | convolution fusion | flops 6443237376 | bytes 16252928 | tf_op jit(solution)/shard_map/dot_general | solution.py:101
  677.9 11.5 %fusion.38 = f32[1024,1024]{0,1:T(8,128)} fusion(bf16[2048,1024]{1,0:T(8,128)(2,1)} %param.25, f32[1024,2048]{1,0:T(8,128)} %fusion.47, f32[2048]{0:T(1024)S(1)} %copy-done.42), kind=kOutput, calls=%fused_computation.164 | convolution fusion | flops 4315938816 | bytes 16785408 | tf_op jit(solution)/shard_map/dot_general | solution.py:506
  706.6 11.0 %add_convert_fusion.4 = bf16[1024,1024]{0,1:T(8,128)(2,1)} fusion(f32[1024,1024]{0,1:T(8,128)} %copy-done.4, f32[1024,1024]{0,1:T(8,128)} %fusion.38, f32[1024,1024]{0,1:T(8,128)} %fusion.37, f32[1024]{0:T(1024)S(1)} %copy-done.45, bf16[1024,1024]{1,0:T(8,128)(2,1)} %collective-permute-done.6, f32[1024,1024]{1,0:T(8,128)} %copy-done.52, f32[1024]{0:T(1024)S(1)} %copy-done.49), kind=kOutput, calls=%fused_computation.62 | convolution fusion | flops 2163212288 | bytes 20979712 | tf_op jit(solution)/shard_map/dot_general | solution.py:506
  720.1 8.9 all-to-all-done.2
  740.4 74.1 %reduce-scatter.5.cloned.1.call-done = bf16[1024,1024]{0,1:T(8,128)(2,1)} async-done(((bf16[4096,1024]{0,1:T(8,128)(2,1)}), bf16[1024,1024]{0,1:T(8,128)(2,1)}) %reduce-scatter.5.cloned.1.call-update) | async-done | bytes 2097168 | tf_op jit(solution)/shard_map/reduce_scatter | solution.py:557
  834.4 71.6 %all-reduce = (f32[2048]{0:T(1024)S(1)}, f32[7168]{0:T(1024)S(1)}) all-reduce(f32[2048]{0:T(1024)S(1)} %pad_maximum_fusion.7, f32[7168]{0:T(1024)S(1)} %pad_maximum_fusion.6), channel_id=1, replica_groups=mesh['seq'=4,'batch'=4,'mp'=2] {'seq','batch','mp'}, use_global_device_ids=true, to_apply=%region_13.14 | all-reduce | flops 9216 | bytes 73728 | tf_op jit(solution)/shard_map/psum | solution.py:572
  907.2 11.4 %convert_select_fusion.1 = (f32[1,1024,1024]{1,2,0:T(8,128)}, f32[1,1024,1024]{1,2,0:T(8,128)}, f32[1,1024,1024]{1,2,0:T(8,128)}, f32[1,1024,1024]{1,2,0:T(8,128)}) fusion(bf16[1,1024,1024]{1,2,0:T(8,128)(2,1)} %collective-permute-done.8, pred[]{:T(512)S(6)} %eq.69, bf16[1024,1024]{0,1:T(8,128)(2,1)} %fusion.13, bf16[1024,1024]{0,1:T(8,128)(2,1)} %add_convert_fusion.4, ...), kind=kLoop, calls=%fused_computation.26 | loop fusion | flops 8388608 | bytes 25165824 | tf_op jit(solution)/shard_map/jit(_where)/select_n | solution.py:430
  918.6 8.5 pad_maximum_fusion.1
  927.1 8.7 copy.120
  935.8 8.4 pad_maximum_fusion
  944.3 8.8 copy.119
  (317 shorter events, 265.8 us)
Async XLA Ops:
  8.0 168.2 %all-gather.4.cloned.1.call-start = ((), (), s32[]{:S(2)}) async-start(), calls=%async_computation.7 | async-start | bytes 10485760 | tf_op jit(solution)/shard_map/all_gather | solution.py:490
  26.5 38.5 %collective-permute-start = (bf16[1024,3,256]{0,2,1:T(8,128)(2,1)S(1)}, bf16[1024,3,256]{0,2,1:T(8,128)(2,1)}, u32[]{:S(2)}, u32[]{:S(2)}) collective-permute-start(bf16[1024,3,256]{0,2,1:T(8,128)(2,1)S(1)} %copy.130), channel_id=1, source_target_pairs={{0,1},{8,9},{17,16},{25,24},{2,3},{10,11},{19,18},{27,26},{4,5},{1... | collective-permute-start | bytes 4718600 | tf_op jit(solution)/shard_map/ppermute | solution.py:477
  248.1 124.0 %all-to-all-start = ((bf16[4,1024,256]{1,2,0:T(8,128)(2,1)}), bf16[4,1024,256]{1,2,0:T(8,128)(2,1)}, u32[]{:S(2)}, u32[]{:S(2)}) async-start(bf16[4,1024,256]{1,2,0:T(8,128)(2,1)} %copy.108), calls=%async_computation | async-start | bytes 4194304 | tf_op jit(solution)/shard_map/all_to_all | solution.py:376
  252.6 119.5 %all-gather.6.cloned.1.call-start = ((), (), s32[]{:S(2)}) async-start(), calls=%async_computation.8 | async-start | bytes 3145728 | tf_op jit(solution)/shard_map/all_gather | solution.py:482
  256.1 115.4 %collective-permute-start.1 = (bf16[1024,1024]{0,1:T(8,128)(2,1)}, bf16[1024,1024]{0,1:T(8,128)(2,1)}, u32[]{:S(2)}, u32[]{:S(2)}) collective-permute-start(bf16[1024,1024]{0,1:T(8,128)(2,1)} %dynamic-slice_bitcast_fusion), channel_id=1, source_target_pairs={{0,1},{1,0},{2,3},{3,2},{4,5},{5,4},{6,7},{7,6},{8,9},{9,8},{10,11... | collective-permute-start | bytes 6291464 | tf_op jit(solution)/shard_map/ppermute | solution.py:372
  259.3 112.8 %collective-permute-start.3 = (bf16[1024,1024]{1,0:T(8,128)(2,1)}, bf16[1024,1024]{1,0:T(8,128)(2,1)}, u32[]{:S(2)}, u32[]{:S(2)}) collective-permute-start(bf16[1024,1024]{1,0:T(8,128)(2,1)} %constant_dynamic-slice_fusion.13), channel_id=1, source_target_pairs={{0,1},{1,0},{2,3},{3,2},{4,5},{5,4},{6,7},{7,6},{8,9},{9,8},{10,11... | collective-permute-start | bytes 6291464 | tf_op jit(solution)/shard_map/ppermute | solution.py:372
  259.8 111.7 %collective-permute-start.2 = (f32[1024]{0:T(1024)S(1)}, f32[1024]{0:T(1024)S(1)}, u32[]{:S(2)}, u32[]{:S(2)}) collective-permute-start(f32[1024]{0:T(1024)S(1)} %dynamic_slice.124), channel_id=1, source_target_pairs={{0,1},{1,0},{2,3},{3,2},{4,5},{5,4},{6,7},{7,6},{8,9},{9,8},{10,11... | collective-permute-start | bytes 12296 | tf_op jit(solution)/shard_map/ppermute | solution.py:372
  371.5 47.7 %collective-permute-start.5 = (f32[1024]{0:T(1024)S(1)}, f32[1024]{0:T(1024)S(1)}, u32[]{:S(2)}, u32[]{:S(2)}) collective-permute-start(f32[1024]{0:T(1024)S(1)} %collective-permute-done.2), channel_id=1, source_target_pairs={{0,2},{2,0},{4,6},{6,4},{1,3},{3,1},{5,7},{7,5},{8,10},{10,8},{12,... | collective-permute-start | bytes 12296 | tf_op jit(solution)/shard_map/ppermute | solution.py:372
  371.5 43.6 %collective-permute-start.4 = (bf16[1024,1024]{0,1:T(8,128)(2,1)}, bf16[1024,1024]{0,1:T(8,128)(2,1)}, u32[]{:S(2)}, u32[]{:S(2)}) collective-permute-start(bf16[1024,1024]{0,1:T(8,128)(2,1)} %collective-permute-done.1), channel_id=1, source_target_pairs={{0,2},{2,0},{4,6},{6,4},{1,3},{3,1},{5,7},{7,5},{8,10},{10,8},{12,... | collective-permute-start | bytes 6291464 | tf_op jit(solution)/shard_map/ppermute | solution.py:372
  372.0 73.0 %collective-permute-start.6 = (bf16[1024,1024]{1,0:T(8,128)(2,1)}, bf16[1024,1024]{1,0:T(8,128)(2,1)}, u32[]{:S(2)}, u32[]{:S(2)}) collective-permute-start(bf16[1024,1024]{1,0:T(8,128)(2,1)} %collective-permute-done.3), channel_id=1, source_target_pairs={{0,2},{2,0},{4,6},{6,4},{1,3},{3,1},{5,7},{7,5},{8,10},{10,8},{12,... | collective-permute-start | bytes 6291464 | tf_op jit(solution)/shard_map/ppermute | solution.py:372
  423.8 64.5 %collective-permute-start.30 = (bf16[1024,1024]{1,0:T(8,128)(2,1)}, bf16[1024,1024]{1,0:T(8,128)(2,1)}, u32[]{:S(2)}, u32[]{:S(2)}) collective-permute-start(bf16[1024,1024]{1,0:T(8,128)(2,1)} %convolution_convert_fusion.4), channel_id=1, source_target_pairs={{0,2},{2,0},{4,6},{6,4},{1,3},{3,1},{5,7},{7,5},{8,10},{10,8},{12,... | collective-permute-start | bytes 6291464 | tf_op jit(solution)/shard_map/ppermute | solution.py:372
  425.9 82.1 %collective-permute-start.28 = (bf16[1024,1024]{1,0:T(8,128)(2,1)}, bf16[1024,1024]{1,0:T(8,128)(2,1)}, u32[]{:S(2)}, u32[]{:S(2)}) collective-permute-start(bf16[1024,1024]{1,0:T(8,128)(2,1)} %constant_dynamic-slice_fusion.2), channel_id=1, source_target_pairs={{0,2},{2,0},{4,6},{6,4},{1,3},{3,1},{5,7},{7,5},{8,10},{10,8},{12,... | collective-permute-start | bytes 6291464 | tf_op jit(solution)/shard_map/ppermute | solution.py:372
  434.8 115.0 %collective-permute-start.21 = (bf16[1024,1024]{1,0:T(8,128)(2,1)}, bf16[1024,1024]{1,0:T(8,128)(2,1)}, u32[]{:S(2)}, u32[]{:S(2)}) collective-permute-start(bf16[1024,1024]{1,0:T(8,128)(2,1)} %constant_dynamic-slice_fusion.5), channel_id=1, source_target_pairs={{0,2},{2,0},{4,6},{6,4},{1,3},{3,1},{5,7},{7,5},{8,10},{10,8},{12,... | collective-permute-start | bytes 6291464 | tf_op jit(solution)/shard_map/ppermute | solution.py:372
  500.6 95.5 %all-to-all-start.1 = ((bf16[4,1024,256]{2,1,0:T(8,128)(2,1)}), bf16[4,1024,256]{2,1,0:T(8,128)(2,1)}, u32[]{:S(2)}, u32[]{:S(2)}) async-start(bf16[4,1024,256]{2,1,0:T(8,128)(2,1)} %bitcast.13), calls=%async_computation.1 | async-start | bytes 4194304 | tf_op jit(solution)/shard_map/all_to_all | solution.py:376
  505.4 213.8 %reduce-scatter.7.cloned.1.call-start = ((), (), s32[]{:S(2)}) async-start(), calls=%async_computation.10 | async-start | bytes 327680 | tf_op jit(solution)/shard_map/reduce_scatter | solution.py:419
  530.5 38.5 %collective-permute-start.24 = (bf16[512,1024]{1,0:T(8,128)(2,1)}, bf16[512,1024]{1,0:T(8,128)(2,1)}, u32[]{:S(2)}, u32[]{:S(2)}) collective-permute-start(bf16[512,1024]{1,0:T(8,128)(2,1)} %constant_dynamic-slice_fusion.3), channel_id=1, source_target_pairs={{0,4},{2,6},{4,0},{6,2},{1,5},{3,7},{5,1},{7,3},{8,12},{10,14},{12... | collective-permute-start | bytes 3145736 | tf_op jit(solution)/shard_map/ppermute | solution.py:372
  531.7 206.6 %reduce-scatter.11.cloned.1.call-start = ((), (), s32[]{:S(2)}) async-start(), calls=%async_computation.12 | async-start | bytes 1310720 | tf_op jit(solution)/shard_map/reduce_scatter | solution.py:419
  549.7 190.3 %reduce-scatter.9.cloned.1.call-start = ((), (), s32[]{:S(2)}) async-start(), calls=%async_computation.11 | async-start | bytes 1310720 | tf_op jit(solution)/shard_map/reduce_scatter | solution.py:419
  553.2 37.5 %collective-permute-start.22 = (bf16[512,1024]{1,0:T(8,128)(2,1)S(1)}, bf16[512,1024]{1,0:T(8,128)(2,1)S(1)}, u32[]{:S(2)}, u32[]{:S(2)}) collective-permute-start(bf16[512,1024]{1,0:T(8,128)(2,1)S(1)} %constant_dynamic-slice_fusion.4), channel_id=1, source_target_pairs={{0,4},{2,6},{4,0},{6,2},{1,5},{3,7},{5,1},{7,3},{8,12},{10,14},{12... | collective-permute-start | bytes 3145736 | tf_op jit(solution)/shard_map/ppermute | solution.py:372
  596.1 218.4 %reduce-scatter.5.cloned.1.call-start = ((), (), s32[]{:S(2)}) async-start(), calls=%async_computation.9 | async-start | bytes 10485760 | tf_op jit(solution)/shard_map/reduce_scatter | solution.py:557
  717.6 189.7 %collective-permute-start.7 = (bf16[1,1024,1024]{1,2,0:T(8,128)(2,1)}, bf16[1,1024,1024]{1,2,0:T(8,128)(2,1)}, u32[]{:S(2)}, u32[]{:S(2)}) collective-permute-start(bf16[1,1024,1024]{1,2,0:T(8,128)(2,1)} %bitcast.9), channel_id=1, source_target_pairs={{0,1},{1,0},{2,3},{3,2},{4,5},{5,4},{6,7},{7,6},{8,9},{9,8},{10,11... | collective-permute-start | bytes 6291464 | tf_op jit(solution)/shard_map/ppermute | solution.py:372
  738.3 89.8 %collective-permute-start.33 = (bf16[512,256]{1,0:T(8,128)(2,1)}, bf16[512,256]{1,0:T(8,128)(2,1)S(1)}, u32[]{:S(2)}, u32[]{:S(2)}) collective-permute-start(bf16[512,256]{1,0:T(8,128)(2,1)} %reduce-scatter.11.cloned.1.call-done), channel_id=1, source_target_pairs={{0,4},{2,6},{4,0},{6,2},{1,5},{3,7},{5,1},{7,3},{8,12},{10,14},{12... | collective-permute-start | bytes 786440 | tf_op jit(solution)/shard_map/ppermute | solution.py:372
  739.9 85.7 %collective-permute-start.26 = (bf16[512,256]{1,0:T(8,128)(2,1)}, bf16[512,256]{1,0:T(8,128)(2,1)}, u32[]{:S(2)}, u32[]{:S(2)}) collective-permute-start(bf16[512,256]{1,0:T(8,128)(2,1)} %reduce-scatter.9.cloned.1.call-done), channel_id=1, source_target_pairs={{0,4},{2,6},{4,0},{6,2},{1,5},{3,7},{5,1},{7,3},{8,12},{10,14},{12... | collective-permute-start | bytes 786440 | tf_op jit(solution)/shard_map/ppermute | solution.py:372
  824.2 83.1 %collective-permute-start.8 = (bf16[1,1024,1024]{1,2,0:T(8,128)(2,1)}, bf16[1,1024,1024]{1,2,0:T(8,128)(2,1)}, u32[]{:S(2)}, u32[]{:S(2)}) collective-permute-start(bf16[1,1024,1024]{1,2,0:T(8,128)(2,1)} %bitcast.15), channel_id=1, source_target_pairs={{0,1},{1,0},{2,3},{3,2},{4,5},{5,4},{6,7},{7,6},{8,9},{9,8},{10,11... | collective-permute-start | bytes 6291464 | tf_op jit(solution)/shard_map/ppermute | solution.py:372
  (79 other events, 1708.4 us)
Sparse Core Ops, SparseCore 0:
  23.7 152.5 all-gather.3
  531.9 27.0 reduce-scatter.6
  561.3 25.9 reduce-scatter.10
  596.2 27.9 reduce-scatter.8
  662.9 151.6 reduce-scatter.4
Sparse Core Ops, SparseCore 1:
  259.9 56.9 all-gather.5

commit v2 on v0

--- a/solution.py
+++ b/solution.py
@@ -1,21 +1,23 @@
+import functools
+
 import jax
 import jax.numpy as jnp
 from jax import lax
+from jax.experimental import pallas as pl
+from jax.experimental.pallas import tpu as pltpu
 from jax.sharding import PartitionSpec as P
 
 BLOCK = 64
 GLOB = 2
 WIN = 3
-NBLK = 64
-MB = 2
 HD = 64
 LIST = 8
-LEN = 4096
-
 
 NEG = -1e30
 EPS = 1e-05
-HIGH = lax.Precision.HIGHEST
+F32 = jnp.float32
+BF16 = jnp.bfloat16
+VMEM_LIMIT = 60 * 1024 * 1024
 
 
 def norm_stats(rows):
@@ -34,11 +36,1353 @@
     )
 
 
+def block_lists(blocks, randoms, block_count):
+    leading = randoms.shape[:-1]
+    globals_part = jnp.broadcast_to(jnp.arange(GLOB, dtype=jnp.int32), leading + (GLOB,))
+    window_part = jnp.broadcast_to(
+        blocks[:, None] + jnp.arange(WIN, dtype=jnp.int32) - WIN // 2, leading + (WIN,)
+    )
+    block_list = jnp.concatenate([globals_part, window_part, randoms], axis=-1)
+    inside = (block_list >= 0) & (block_list < block_count)
+    same_entry = block_list[..., :, None] == block_list[..., None, :]
+    order_ids = jnp.arange(LIST)
+    earlier = order_ids[None, :] < order_ids[:, None]
+    repeated = jnp.any(same_entry & earlier, axis=-1)
+    admitted = inside & jnp.logical_not(repeated)
+    return (jnp.clip(block_list, 0, block_count - 1), admitted.astype(jnp.int32))
+
+
+def segment_at(places, ends_ref):
+    total = jnp.zeros(places.shape, jnp.int32)
+    for doc in range(ends_ref.shape[0]):
+        total = total + (places >= ends_ref[doc]).astype(jnp.int32)
+    return total
+
+
+def head_spread(rows, heads):
+    lane_head = lax.broadcasted_iota(jnp.int32, (1, rows.shape[1]), 1) // HD
+    return jnp.concatenate(
+        [rows * (lane_head == head).astype(F32).astype(rows.dtype) for head in range(heads)], axis=0
+    )
+
+
+def head_fold(wide, heads):
+    rows = wide.shape[0] // heads
+    lane_head = lax.broadcasted_iota(jnp.int32, (rows, wide.shape[1]), 1) // HD
+    folded = jnp.zeros((rows, wide.shape[1]), wide.dtype)
+    for head in range(heads):
+        folded = jnp.where(lane_head == head, wide[head * rows : (head + 1) * rows], folded)
+    return folded
+
+
+def block_at(block):
+    return pl.ds(pl.multiple_of(block * BLOCK, BLOCK), BLOCK)
+
+
+def fill_segments(token_segs, ends_ref):
+    def fill(block, _):
+        places = block * BLOCK + lax.broadcasted_iota(jnp.int32, (BLOCK, token_segs.shape[1]), 0)
+        token_segs[block_at(block), :] = segment_at(places, ends_ref)
+        return 0
+
+    lax.fori_loop(0, token_segs.shape[0] // BLOCK, fill, 0)
+
+
+def query_segments(block, heads, ends_ref):
+    lanes = lax.broadcasted_iota(jnp.int32, (8, heads * BLOCK), 1)
+    return segment_at(block * BLOCK + lanes % BLOCK, ends_ref)[0:1]
+
+
+def key_segments(starts, keeps, ends_ref):
+    lanes = lax.broadcasted_iota(jnp.int32, (8, 2 * BLOCK), 1)
+    first = lanes < BLOCK
+    pieces = []
+    for entry in range(0, LIST, 2):
+        places = lanes + jnp.where(
+            first, starts[entry] * BLOCK, (starts[entry + 1] - 1) * BLOCK
+        )
+        keep = jnp.where(first, keeps[entry], keeps[entry + 1]) > 0
+        pieces.append(jnp.where(keep, segment_at(places, ends_ref), -1))
+    return jnp.concatenate(pieces, axis=1)[0:1]
+
+
+def gathered(ref, starts):
+    return jnp.concatenate([ref[block_at(start), :] for start in starts], axis=0)
+
+
+def block_parts(wide):
+    return [wide[start : start + BLOCK] for start in range(0, wide.shape[0], BLOCK)]
+
+
+def dot_nt(left, right):
+    return lax.dot_general(left, right, (((1,), (1,)), ((), ())), preferred_element_type=F32)
+
+
+def dot_tn(left, right):
+    return lax.dot_general(left, right, (((0,), (0,)), ((), ())), preferred_element_type=F32)
+
+
+def dot_nn(left, right):
+    return lax.dot_general(left, right, (((1,), (0,)), ((), ())), preferred_element_type=F32)
+
+
+def as_row(tall):
+    count = tall.shape[0]
+    row_ids = lax.broadcasted_iota(jnp.int32, (count, count), 0)
+    lane_ids = lax.broadcasted_iota(jnp.int32, (count, count), 1)
+    return jnp.sum(jnp.where(row_ids == lane_ids, tall, 0.0), axis=0, keepdims=True)
+
+
+def together(running):
+    while running:
+        still = []
+        for each in running:
+            if next(each, 0) is None:
+                still.append(each)
+        running = still
+
+
+def forward_kernel(
+    heads, ends_ref, lists_ref, admit_ref, q_ref, k_ref, v_ref, o_ref, lse_ref, token_segs, held
+):
+    scale = HD ** (-0.5)
+    rows_total = q_ref.shape[0]
+    blocks = rows_total // BLOCK
+    chunk = LIST * BLOCK
+    fill_segments(token_segs, ends_ref)
+
+    def store(block, wide, top, total):
+        out = head_fold(wide, heads)
+        places = block * BLOCK + lax.broadcasted_iota(jnp.int32, out.shape, 0)
+        out = jnp.where(places < ends_ref[ends_ref.shape[0] - 1], out, 0.0)
+        o_ref[block_at(block), :] = out.astype(BF16)
+        lse_ref[block] = jnp.broadcast_to(as_row(top + jnp.log(total)), lse_ref.shape[1:])
+
+    def kept(block, key_segs):
+        own = token_segs[block_at(block), :]
+        return jnp.concatenate([own] * (chunk // own.shape[1]), axis=1) == key_segs
+
+    def global_blocks():
+        query_wide = jnp.concatenate(
+            [head_spread(q_ref[block_at(block), :] * scale, heads) for block in range(GLOB)], axis=0
+        )
+        wide_rows = GLOB * heads * BLOCK
+
+        def score(part, top):
+            here = pl.ds(pl.multiple_of(part * chunk, chunk), chunk)
+            places = part * chunk + lax.broadcasted_iota(jnp.int32, (8, chunk), 1)
+            key_segs = segment_at(places, ends_ref)[0:1]
+            keeps = [kept(block, key_segs) for block in range(GLOB)]
+            scores = dot_nt(query_wide, k_ref[here, :])
+            tops = []
+            for place, rows in enumerate(block_parts(scores)):
+                rows = jnp.where(keeps[place // heads], rows, NEG)
+                held[place * BLOCK : (place + 1) * BLOCK, here] = rows
+                tops.append(jnp.max(rows, axis=1, keepdims=True))
+            return jnp.maximum(top, jnp.concatenate(tops, axis=0))
+
+        top = lax.fori_loop(0, rows_total // chunk, score, jnp.full((wide_rows, 1), NEG, F32))
+
+        def gather(part, carried):
+            total, wide = carried
+            here = pl.ds(pl.multiple_of(part * chunk, chunk), chunk)
+            totals, weights = [], []
+            for place, part_top in enumerate(block_parts(top)):
+                weight = jnp.exp(held[place * BLOCK : (place + 1) * BLOCK, here] - part_top)
+                totals.append(jnp.sum(weight, axis=1, keepdims=True))
+                weights.append(weight.astype(BF16))
+            wide = wide + dot_nn(jnp.concatenate(weights, axis=0), v_ref[here, :])
+            return total + jnp.concatenate(totals, axis=0), wide
+
+        total, wide = lax.fori_loop(
+            0,
+            rows_total // chunk,
+            gather,
+            (jnp.zeros((wide_rows, 1), F32), jnp.zeros((wide_rows, q_ref.shape[1]), F32)),
+        )
+        wide = wide * (1.0 / total)
+        for block in range(GLOB):
+            own = slice(block * heads * BLOCK, (block + 1) * heads * BLOCK)
+            store(block, wide[own], top[own], total[own])
+
+    global_blocks()
+
+    def listed_block(block):
+        query_wide = head_spread(q_ref[block_at(block), :] * scale, heads)
+        starts = [lists_ref[block * LIST + entry] for entry in range(LIST)]
+        keeps = [admit_ref[block * LIST + entry] for entry in range(LIST)]
+        keep = kept(block, key_segments(starts, keeps, ends_ref))
+        scores = dot_nt(query_wide, gathered(k_ref, starts))
+        yield
+        tops, totals, probs = [], [], []
+        for rows in block_parts(scores):
+            rows = jnp.where(keep, rows, NEG)
+            top = jnp.max(rows, axis=1, keepdims=True)
+            weights = jnp.exp(rows - top)
+            total = jnp.sum(weights, axis=1, keepdims=True)
+            probs.append((weights * (1.0 / total)).astype(BF16))
+            tops.append(top)
+            totals.append(total)
+            yield
+        wide = dot_nn(jnp.concatenate(probs, axis=0), gathered(v_ref, starts))
+        store(block, wide, jnp.concatenate(tops, axis=0), jnp.concatenate(totals, axis=0))
+
+    def listed_group(group, _):
+        together([listed_block(GLOB + 4 * group + place) for place in range(4)])
+        return 0
+
+    lax.fori_loop(0, (blocks - GLOB) // 4, listed_group, 0)
+    together([listed_block(blocks - 1 - place) for place in range((blocks - GLOB) % 4)])
+
+
+def backward_kernel(
+    heads,
+    ends_ref,
+    lists_ref,
+    admit_ref,
+    q_ref,
+    k_ref,
+    v_ref,
+    o_ref,
+    do_ref,
+    lse_ref,
+    out_ref,
+    token_segs,
+    dk_ref,
+    dv_ref,
+    dq_ref,
+):
+    scale = HD ** (-0.5)
+    rows_total, cols = q_ref.shape
+    blocks = rows_total // BLOCK
+    pair_rows = 2 * BLOCK
+    fill_segments(token_segs, ends_ref)
+
+    def prepare(pair, _):
+        here = pl.ds(pl.multiple_of(pair * pair_rows, pair_rows), pair_rows)
+        dk_ref[here, :] = jnp.zeros((pair_rows, cols), F32)
+        dv_ref[here, :] = jnp.zeros((pair_rows, cols), F32)
+        return 0
+
+    lax.fori_loop(0, blocks // 2, prepare, 0)
+
+    def query_side(block):
+        query_wide = head_spread(q_ref[block_at(block), :] * scale, heads)
+        grad_rows = do_ref[block_at(block), :]
+        grad_wide = head_spread(grad_rows, heads)
+        product = grad_rows.astype(F32) * o_ref[block_at(block), :].astype(F32)
+        spread = head_spread(product.astype(BF16), heads)
+        delta = dot_nt(jnp.ones((8, cols), BF16), spread)[0:1]
+        seg_row = query_segments(block, heads, ends_ref)
+        return query_wide, grad_wide, delta, lse_ref[block, 0:1], seg_row
+
+    def unit(starts, keeps, query_wide, grad_wide, delta, lse, seg_row, finish_query):
+        keys = gathered(k_ref, starts)
+        scores = block_parts(dot_nt(keys, query_wide))
+        prob_grads = block_parts(dot_nt(gathered(v_ref, starts), grad_wide))
+        yield
+        probs, score_grads = [], []
+        for entry in range(LIST):
+            wanted = seg_row if keeps is None else jnp.where(keeps[entry] > 0, seg_row, -1)
+            own = token_segs[block_at(starts[entry]), :]
+            keep = jnp.concatenate([own] * (seg_row.shape[1] // own.shape[1]), axis=1) == wanted
+            prob = jnp.exp(jnp.where(keep, scores[entry], NEG) - lse)
+            probs.append(prob.astype(BF16))
+            score_grads.append((prob * (prob_grads[entry] - delta)).astype(BF16))
+            if entry % 2:
+                yield
+        score_grad = jnp.concatenate(score_grads, axis=0)
+        finish_query(dot_tn(score_grad, keys))
+        dk = dot_nn(score_grad, query_wide)
+        dv = dot_nn(jnp.concatenate(probs, axis=0), grad_wide)
+        yield
+        for entry in range(LIST):
+            here = block_at(starts[entry])
+            dk_ref[here, :] += dk[entry * BLOCK : (entry + 1) * BLOCK]
+            dv_ref[here, :] += dv[entry * BLOCK : (entry + 1) * BLOCK]
+        yield
+
+    def store_query(block, wide):
+        out_ref[block_at(block), 0:cols] = (head_fold(wide, heads) * scale).astype(BF16)
+
+    def global_blocks():
+        sides = [query_side(block) for block in range(GLOB)]
+        side = [jnp.concatenate(both, axis=axis) for both, axis in zip(zip(*sides), (0, 0, 1, 1, 1))]
+        dq_ref[...] = jnp.zeros_like(dq_ref)
+
+        def part_of(part, _):
+            def add_query(wide):
+                dq_ref[...] += wide
+
+            together([unit([part * LIST + entry for entry in range(LIST)], None, *side, add_query)])
+            return 0
+
+        lax.fori_loop(0, blocks // LIST, part_of, 0)
+        for block in range(GLOB):
+            store_query(block, dq_ref[block * heads * BLOCK : (block + 1) * heads * BLOCK])
+
+    global_blocks()
+
+    def listed_block(block):
+        starts = [lists_ref[block * LIST + entry] for entry in range(LIST)]
+        keeps = [admit_ref[block * LIST + entry] for entry in range(LIST)]
+        return unit(starts, keeps, *query_side(block), functools.partial(store_query, block))
+
+    def listed_group(group, _):
+        together([listed_block(GLOB + 4 * group + place) for place in range(4)])
+        return 0
+
+    lax.fori_loop(0, (blocks - GLOB) // 4, listed_group, 0)
+    together([listed_block(blocks - 1 - place) for place in range((blocks - GLOB) % 4)])
+
+    def finish(block, _):
+        here = block_at(block)
+        out_ref[here, cols : 2 * cols] = dk_ref[here, :].astype(BF16)
+        out_ref[here, 2 * cols : 3 * cols] = dv_ref[here, :].astype(BF16)
+        return 0
+
+    lax.fori_loop(0, blocks, finish, 0)
+
+
+def smem():
+    return pl.BlockSpec(memory_space=pltpu.SMEM)
+
+
+def column(rows, cols, index):
+    return pl.BlockSpec((rows, cols), lambda step: (0, index))
+
+
+def attention_forward(qkv, doc_ends, lists, admits, cols):
+    rows = qkv.shape[0]
+    heads = cols // HD
+    blocks = rows // BLOCK
+    return pl.pallas_call(
+        functools.partial(forward_kernel, heads),
+        grid=(1,),
+        in_specs=[smem(), smem(), smem()] + [column(rows, cols, part) for part in range(3)],
+        out_specs=[
+            column(rows, cols, 0),
+            pl.BlockSpec((blocks, 8, heads * BLOCK), lambda step: (0, 0, 0)),
+        ],
+        out_shape=[
+            jax.ShapeDtypeStruct((rows, cols), BF16),
+            jax.ShapeDtypeStruct((blocks, 8, heads * BLOCK), F32),
+        ],
+        scratch_shapes=[
+            pltpu.VMEM((rows, 2 * BLOCK), jnp.int32),
+            pltpu.VMEM((GLOB * heads * BLOCK, rows), F32),
+        ],
+        compiler_params=pltpu.CompilerParams(vmem_limit_bytes=VMEM_LIMIT),
+        cost_estimate=pl.CostEstimate(
+            flops=rows * LIST * BLOCK * cols * heads * 5,
+            bytes_accessed=8 * rows * cols,
+            transcendentals=0,
+        ),
+    )(doc_ends, lists, admits, qkv, qkv, qkv)
+
+
+def attention_backward(qkv, attended, attended_grad, lse, doc_ends, lists, admits, cols):
+    rows = qkv.shape[0]
+    heads = cols // HD
+    blocks = rows // BLOCK
+    return pl.pallas_call(
+        functools.partial(backward_kernel, heads),
+        grid=(1,),
+        in_specs=[smem(), smem(), smem()]
+        + [column(rows, cols, part) for part in range(3)]
+        + [
+            column(rows, cols, 0),
+            column(rows, cols, 0),
+            pl.BlockSpec((blocks, 8, heads * BLOCK), lambda step: (0, 0, 0)),
+        ],
+        out_specs=column(rows, 3 * cols, 0),
+        out_shape=jax.ShapeDtypeStruct((rows, 3 * cols), BF16),
+        scratch_shapes=[
+            pltpu.VMEM((rows, 2 * BLOCK), jnp.int32),
+            pltpu.VMEM((rows, cols), F32),
+            pltpu.VMEM((rows, cols), F32),
+            pltpu.VMEM((GLOB * heads * BLOCK, cols), F32),
+        ],
+        compiler_params=pltpu.CompilerParams(vmem_limit_bytes=VMEM_LIMIT),
+        cost_estimate=pl.CostEstimate(
+            flops=rows * LIST * BLOCK * cols * heads * 15,
+            bytes_accessed=20 * rows * cols,
+            transcendentals=0,
+        ),
+    )(doc_ends, lists, admits, qkv, qkv, qkv, attended, attended_grad, lse)
+
+
+def row_stats(rows):
+    mean = jnp.mean(rows, axis=-1, keepdims=True)
+    centre = rows - mean
+    spread = jnp.mean(centre * centre, axis=-1, keepdims=True)
+    inverse = lax.rsqrt(spread + EPS)
+    return centre * inverse, inverse
+
+
+def gelu_pair(inner):
+    root = 0.7978845608028654
+    cube = 0.044715
+    square = inner * inner
+    bent = jnp.tanh(inner * (root + (root * cube) * square))
+    half = 0.5 + 0.5 * bent
+    value = inner * half
+    return value, half + value * (1.0 - bent) * (root + (3.0 * root * cube) * square)
+
+
+def token_kernel(
+    tile,
+    where_ref,
+    att_ref,
+    x_ref,
+    grad_ref,
+    out_own_ref,
+    out_other_ref,
+    up_own_ref,
+    up_near_ref,
+    up_far_ref,
+    down_own_ref,
+    down_near_ref,
+    down_far_ref,
+    up_bias_ref,
+    gain_ref,
+    bias_ref,
+    down_bias_ref,
+    act_in,
+    pre_in,
+    second_in,
+    hidden_in,
+    grad_in,
+    output_ref,
+    hidden_grad_ref,
+    datt_ref,
+    act_ref,
+    pre_ref,
+    second_ref,
+    hidden_low_ref,
+    grad_low_ref,
+    sums_ref,
+    unit_sums_ref,
+    hidden,
+    normed,
+    inverse,
+    ffn,
+    second_grad,
+    up_slots,
+    down_slots,
+    slot_sems,
+):
+    step = pl.program_id(0)
+    steps = pl.num_programs(0)
+    rows = hidden.shape[0]
+    parts = att_ref.shape[0]
+    tiles = [slice(start, start + tile) for start in range(0, rows, tile)]
+    chunk = up_slots.shape[2]
+    own_steps = up_own_ref.shape[1] // chunk
+    near_steps = up_near_ref.shape[1] // chunk
+
+    def copies(up_from, down_from, index, slot):
+        here = pl.ds(pl.multiple_of(index * chunk, chunk), chunk)
+        return (
+            pltpu.make_async_copy(up_from.at[:, here], up_slots.at[slot], slot_sems.at[0, slot]),
+            pltpu.make_async_copy(down_from.at[here], down_slots.at[slot], slot_sems.at[1, slot]),
+        )
+
+    def fetch(index):
+        def begin(up_from, down_from, first):
+            for copy in copies(up_from, down_from, index - first, index % 2):
+                copy.start()
+
+        @pl.when(index < own_steps)
+        def _():
+            begin(up_own_ref, down_own_ref, 0)
+
+        @pl.when((index >= own_steps) & (index < own_steps + near_steps))
+        def _():
+            begin(up_near_ref, down_near_ref, own_steps)
+
+        @pl.when(index >= own_steps + near_steps)
+        def _():
+            begin(up_far_ref, down_far_ref, own_steps + near_steps)
+
+    half = parts // 2
+    own_place = where_ref[0] * half
+    other_place = (1 - where_ref[0]) * half
+    out_parts = [(own_place + part, out_own_ref, part) for part in range(half)]
+    out_parts += [(other_place + part, out_other_ref, part) for part in range(half)]
+
+    @pl.when(step == 0)
+    def _():
+        fetch(step)
+
+    @pl.when(step + 1 < steps)
+    def _():
+        fetch(step + 1)
+
+    @pl.when(step == 0)
+    def _():
+        for here in tiles:
+            total = x_ref[0, here, :]
+            for part, weight_ref, index in out_parts:
+                total = total + dot_nn(att_ref[part, here, :], weight_ref[index])
+            hidden[here, :] = total
+            unit, scale = row_stats(total)
+            normed[here, :] = unit
+            inverse[here, :] = jnp.broadcast_to(scale, (tile, inverse.shape[1]))
+            second_ref[here, :] = (unit * gain_ref[...] + bias_ref[...]).astype(BF16)
+            grad_low_ref[here, :] = grad_ref[0, here, :].astype(BF16)
+            ffn[here, :] = jnp.zeros((tile, ffn.shape[1]), F32)
+            second_grad[here, :] = jnp.zeros((tile, ffn.shape[1]), F32)
+
+    slot = step % 2
+    for copy in copies(up_own_ref, down_own_ref, 0, slot):
+        copy.wait()
+    up_ref = up_slots.at[slot]
+    down_ref = down_slots.at[slot]
+    unit_sum = jnp.zeros((1, chunk), F32)
+    for here in tiles:
+        inner = dot_nn(second_ref[here, :], up_ref[...]) + up_bias_ref[...]
+        act_grad = dot_nt(grad_low_ref[here, :], down_ref[...])
+        value, slope = gelu_pair(inner)
+        value = value.astype(BF16)
+        pre_grad = (act_grad * slope).astype(BF16)
+        act_ref[here, :] = value
+        pre_ref[here, :] = pre_grad
+        unit_sum = unit_sum + jnp.sum(pre_grad.astype(F32), axis=0, keepdims=True)
+        ffn[here, :] += dot_nn(value, down_ref[...])
+        second_grad[here, :] += dot_nt(pre_grad, up_ref[...])
+    unit_sums_ref[...] = jnp.broadcast_to(unit_sum, unit_sums_ref.shape)
+
+    @pl.when(step == steps - 1)
+    def _():
+        width = ffn.shape[1]
+        grad_sum = jnp.zeros((1, width), F32)
+        gain_sum = jnp.zeros((1, width), F32)
+        bias_sum = jnp.zeros((1, width), F32)
+        for index, here in enumerate(tiles):
+            output_ref[here, :] = (hidden[here, :] + ffn[here, :] + down_bias_ref[...]).astype(BF16)
+            grad = grad_ref[0, here, :]
+            back = second_grad[here, :]
+            unit = normed[here, :]
+            scaled = back * gain_ref[...]
+            through = (
+                scaled
+                - jnp.mean(scaled, axis=-1, keepdims=True)
+                - unit * jnp.mean(scaled * unit, axis=-1, keepdims=True)
+            )
+            total = grad + inverse[here, 0:1] * through
+            hidden_grad_ref[here, :] = total
+            low = total.astype(BF16)
+            hidden_low_ref[here, :] = low
+            grad_sum = grad_sum + jnp.sum(grad, axis=0, keepdims=True)
+            gain_sum = gain_sum + jnp.sum(back * unit, axis=0, keepdims=True)
+            bias_sum = bias_sum + jnp.sum(back, axis=0, keepdims=True)
+            for part, weight_ref, piece in out_parts:
+                spread = dot_nt(low, weight_ref[piece])
+                places = where_ref[1] + index * tile + lax.broadcasted_iota(jnp.int32, spread.shape, 0)
+                datt_ref[part, here, :] = jnp.where(places < where_ref[2], spread, 0.0).astype(BF16)
+        sums_ref[...] = jnp.concatenate(
+            [grad_sum, gain_sum, bias_sum, jnp.zeros((5, width), F32)], axis=0
+        )
+
+
+def token_part(
+    index, where, att, layer_input, cotangent, outs, ups, downs, up_bias, gain, bias, down_bias, kept
+):
+    parts, rows, cols = att.shape
+    width = layer_input.shape[2]
+    units = up_bias.shape[1]
+    chunk = min(512, units // 4)
+    whole = 2 * rows
+    shapes = [(whole, units), (whole, units), (whole, width), (whole, width), (whole, width)]
+    if kept is None:
+        kept = [jnp.zeros((8, 128), BF16)] * len(shapes)
+        aliases = {}
+    else:
+        aliases = {16 + place: 3 + place for place in range(len(shapes))}
+    half = lambda step, where_ref: (index, 0)
+    fixed = lambda step, where_ref: (0, 0)
+    any_spec = pl.BlockSpec(memory_space=pl.ANY)
+    rows_spec = pl.BlockSpec((1, rows, width), lambda step, where_ref: (where_ref[0], index, 0))
+    cube = lambda step, where_ref: (0, 0, 0)
+    vector = pl.BlockSpec((1, width), fixed)
+    return pl.pallas_call(
+        functools.partial(token_kernel, min(256, rows)),
+        grid_spec=pltpu.PrefetchScalarGridSpec(
+            num_scalar_prefetch=1,
+            grid=(units // chunk,),
+            in_specs=[
+                pl.BlockSpec((parts, rows, cols), cube),
+                rows_spec,
+                rows_spec,
+                pl.BlockSpec((parts // 2, cols, width), cube),
+                pl.BlockSpec((parts // 2, cols, width), cube),
+            ]
+            + [any_spec] * 6
+            + [
+                pl.BlockSpec((1, chunk), lambda step, where_ref: (0, step)),
+                vector,
+                vector,
+                vector,
+            ]
+            + [any_spec] * len(shapes),
+            out_specs=[
+                pl.BlockSpec((rows, width), fixed),
+                pl.BlockSpec((rows, width), fixed),
+                pl.BlockSpec((parts, rows, cols), cube),
+                pl.BlockSpec((rows, chunk), lambda step, where_ref: (index, step)),
+                pl.BlockSpec((rows, chunk), lambda step, where_ref: (index, step)),
+                pl.BlockSpec((rows, width), half),
+                pl.BlockSpec((rows, width), half),
+                pl.BlockSpec((rows, width), half),
+                pl.BlockSpec((8, width), fixed),
+                pl.BlockSpec((8, chunk), lambda step, where_ref: (0, step)),
+            ],
+            scratch_shapes=[
+                pltpu.VMEM((rows, width), F32),
+                pltpu.VMEM((rows, width), F32),
+                pltpu.VMEM((rows, 128), F32),
+                pltpu.VMEM((rows, width), F32),
+                pltpu.VMEM((rows, width), F32),
+                pltpu.VMEM((2, width, chunk), BF16),
+                pltpu.VMEM((2, chunk, width), BF16),
+                pltpu.SemaphoreType.DMA((2, 2)),
+            ],
+        ),
+        out_shape=[
+            jax.ShapeDtypeStruct((rows, width), BF16),
+            jax.ShapeDtypeStruct((rows, width), F32),
+            jax.ShapeDtypeStruct((parts, rows, cols), BF16),
+        ]
+        + [jax.ShapeDtypeStruct(shape, BF16) for shape in shapes]
+        + [jax.ShapeDtypeStruct((8, width), F32), jax.ShapeDtypeStruct((8, units), F32)],
+        input_output_aliases=aliases,
+        compiler_params=pltpu.CompilerParams(vmem_limit_bytes=VMEM_LIMIT),
+        cost_estimate=pl.CostEstimate(
+            flops=rows * width * (8 * units + 4 * width),
+            bytes_accessed=8 * units * width,
+            transcendentals=0,
+        ),
+    )(where, att, layer_input, cotangent, *outs, *ups, *downs, up_bias, gain, bias, down_bias, *kept)
+
+
+MESH = pl.DeviceIdType.MESH
+
+
+def greet(me, count, partner=None):
+    barrier = pltpu.get_barrier_semaphore()
+
+    @pl.when(me > 0)
+    def _():
+        pl.semaphore_signal(barrier, inc=1, device_id={"seq": me - 1}, device_id_type=MESH)
+
+    @pl.when(me < count - 1)
+    def _():
+        pl.semaphore_signal(barrier, inc=1, device_id={"seq": me + 1}, device_id_type=MESH)
+
+    peers = jnp.minimum(me, 1) + jnp.minimum(count - 1 - me, 1)
+    if partner is not None:
+        pl.semaphore_signal(barrier, inc=1, device_id={"mp": partner}, device_id_type=MESH)
+        peers = peers + 1
+    pl.semaphore_wait(barrier, peers)
+
+
+def gather_kernel(
+    count,
+    chunks,
+    half_cols,
+    x_ref,
+    gain_ref,
+    bias_ref,
+    weight_ref,
+    all_ref,
+    qkv_ref,
+    own_ref,
+    rows_in,
+    shards,
+    results,
+    weight,
+    weight_sems,
+    load_sems,
+    send_sems,
+    recv_sems,
+    all_sems,
+    qkv_sems,
+):
+    me = lax.axis_index("seq")
+    place = lax.axis_index("mp")
+    step = rows_in.shape[0] // chunks
+    cols = weight.shape[1] // 3
+
+    def at(chunk):
+        return pl.ds(pl.multiple_of(chunk * step, step), step)
+
+    def load(chunk):
+        return pltpu.make_async_copy(
+            x_ref.at[place, at(chunk)], rows_in.at[at(chunk)], load_sems.at[chunk]
+        )
+
+    def send(side, hop, chunk):
+        shard = me - hop if side == 0 else me + hop
+        target = me + 1 if side == 0 else me - 1
+        return pltpu.make_async_remote_copy(
+            src_ref=shards.at[shard, at(chunk)],
+            dst_ref=shards.at[shard, at(chunk)],
+            send_sem=send_sems.at[side, hop, chunk],
+            recv_sem=recv_sems.at[side, hop, chunk],
+            device_id={"seq": target},
+            device_id_type=MESH,
+        )
+
+    def keep_all(shard, chunk):
+        return pltpu.make_async_copy(
+            shards.at[shard, at(chunk)], all_ref.at[shard, at(chunk)], all_sems.at[shard, chunk]
+        )
+
+    def keep_qkv(shard, chunk):
+        return pltpu.make_async_copy(
+            results.at[shard, at(chunk)], qkv_ref.at[shard, at(chunk)], qkv_sems.at[shard, chunk]
+        )
+
+    def over_chunks(body):
+        def run(chunk, _):
+            body(chunk)
+            return 0
+
+        lax.fori_loop(0, chunks, run, 0)
+
+    over_chunks(lambda chunk: load(chunk).start())
+    greet(me, count, 1 - place)
+
+    here = (me * cols) // half_cols == place
+    fetch = pltpu.make_async_remote_copy(
+        src_ref=weight_ref,
+        dst_ref=weight,
+        send_sem=weight_sems.at[0],
+        recv_sem=weight_sems.at[1],
+        device_id={"mp": 1 - place},
+        device_id_type=MESH,
+    )
+    copy = pltpu.make_async_copy(weight_ref, weight, weight_sems.at[2])
+
+    @pl.when(here)
+    def _():
+        fetch.start()
+        copy.start()
+
+    def norm(chunk):
+        load(chunk).wait()
+        unit, _ = row_stats(rows_in[at(chunk), :])
+        shards[me, at(chunk), :] = (unit * gain_ref[...] + bias_ref[...]).astype(BF16)
+        keep_all(me, chunk).start()
+
+        @pl.when(me < count - 1)
+        def _():
+            send(0, 0, chunk).start()
+
+        @pl.when(me > 0)
+        def _():
+            send(1, 0, chunk).start()
+
+    over_chunks(norm)
+
+    def project(shard, chunk):
+        rows = dot_nn(shards[shard, at(chunk), :], weight[...])
+        results[shard, at(chunk), :] = rows.astype(BF16)
+        keep_qkv(shard, chunk).start()
+
+    def receive(hop, chunk):
+        @pl.when(me >= hop + 1)
+        def _():
+            send(0, hop, chunk).wait_recv()
+            if hop + 1 < count - 1:
+
+                @pl.when(me < count - 1)
+                def _():
+                    send(0, hop + 1, chunk).start()
+
+            keep_all(me - hop - 1, chunk).start()
+
+        @pl.when(me + hop + 1 < count)
+        def _():
+            send(1, hop, chunk).wait_recv()
+            if hop + 1 < count - 1:
+
+                @pl.when(me > 0)
+                def _():
+                    send(1, hop + 1, chunk).start()
+
+            keep_all(me + hop + 1, chunk).start()
+
+    for hop in range(count - 2):
+        over_chunks(functools.partial(receive, hop))
+
+    @pl.when(here)
+    def _():
+        copy.wait()
+
+    @pl.when(jnp.logical_not(here))
+    def _():
+        fetch.wait_recv()
+
+    keep_weight = pltpu.make_async_copy(weight, own_ref, weight_sems.at[3])
+    keep_weight.start()
+
+    def last(chunk):
+        project(me, chunk)
+        for hop in range(count - 1):
+            if hop == count - 2:
+                receive(hop, chunk)
+
+            @pl.when(me >= hop + 1)
+            def _():
+                project(me - hop - 1, chunk)
+
+            @pl.when(me + hop + 1 < count)
+            def _():
+                project(me + hop + 1, chunk)
+
+    over_chunks(last)
+
+    def finish(chunk):
+        for hop in range(count - 1):
+
+            @pl.when((me >= hop) & (me < count - 1))
+            def _():
+                send(0, hop, chunk).wait_send()
+
+            @pl.when((me + hop < count) & (me > 0))
+            def _():
+                send(1, hop, chunk).wait_send()
+
+        for shard in range(count):
+            keep_all(shard, chunk).wait()
+            keep_qkv(shard, chunk).wait()
+
+    over_chunks(finish)
+    keep_weight.wait()
+
+    @pl.when(here)
+    def _():
+        fetch.wait_send()
+
+
+def gather_project(layer_input, gain, bias, weight, half_cols):
+    count = lax.axis_size("seq")
+    _, rows, width = layer_input.shape
+    cols = weight.shape[1]
+    chunks = max(1, rows // 128)
+    any_spec = pl.BlockSpec(memory_space=pl.ANY)
+    vmem = pl.BlockSpec(memory_space=pltpu.VMEM)
+    dma = pltpu.SemaphoreType.DMA
+    return pl.pallas_call(
+        functools.partial(gather_kernel, count, chunks, half_cols),
+        in_specs=[any_spec, vmem, vmem, vmem],
+        out_specs=[any_spec, any_spec, any_spec],
+        out_shape=[
+            jax.ShapeDtypeStruct((count, rows, width), BF16),
+            jax.ShapeDtypeStruct((count, rows, cols), BF16),
+            jax.ShapeDtypeStruct((width, cols), BF16),
+        ],
+        scratch_shapes=[
+            pltpu.VMEM((rows, width), F32),
+            pltpu.VMEM((count, rows, width), BF16),
+            pltpu.VMEM((count, rows, cols), BF16),
+            pltpu.VMEM((width, cols), BF16),
+            dma((4,)),
+            dma((chunks,)),
+            dma((2, count - 1, chunks)),
+            dma((2, count - 1, chunks)),
+            dma((count, chunks)),
+            dma((count, chunks)),
+        ],
+        compiler_params=pltpu.CompilerParams(
+            collective_id=0, has_side_effects=True, vmem_limit_bytes=VMEM_LIMIT
+        ),
+        cost_estimate=pl.CostEstimate(
+            flops=150_000_000_000, bytes_accessed=1, transcendentals=0
+        ),
+    )(layer_input, gain, bias, weight)
+
+
+def return_kernel(
+    count,
+    chunks,
+    lag,
+    offset,
+    parts_ref,
+    weight_ref,
+    x_ref,
+    hidden_grad_ref,
+    gain_ref,
+    input_ref,
+    sums_ref,
+    rows_in,
+    sending,
+    received,
+    load_sem,
+    send_sems,
+    recv_sems,
+):
+    me = lax.axis_index("seq")
+    place = lax.axis_index("mp")
+    rows = hidden_grad_ref.shape[0]
+    step = rows // chunks
+    width = gain_ref.shape[1]
+    steps = (count - 1) * chunks
+
+    def at(chunk):
+        return pl.ds(pl.multiple_of(chunk * step, step), step)
+
+    load = pltpu.make_async_copy(x_ref.at[place, pl.ds(offset, rows)], rows_in, load_sem.at[0])
+    load.start()
+    greet(me, count)
+
+    def send(side, message, chunk):
+        return pltpu.make_async_remote_copy(
+            src_ref=sending.at[side, message, at(chunk)],
+            dst_ref=received.at[side, message, at(chunk)],
+            send_sem=send_sems.at[side, message, chunk],
+            recv_sem=recv_sems.at[side, message, chunk],
+            device_id={"seq": me + 1 - 2 * side},
+            device_id_type=MESH,
+        )
+
+    def flow(side, index):
+        message = index // chunks
+        chunk = index % chunks
+        target = (1 - side) * (count - 1 - message) + side * message
+
+        @pl.when((target - me) * (1 - 2 * side) > 0)
+        def _():
+            total = dot_nt(parts_ref[target, at(chunk), :], weight_ref[...])
+            first = (1 - side) * me + side * (count - 1 - me)
+
+            @pl.when(first == 0)
+            def _():
+                sending[side, message, at(chunk), :] = total.astype(BF16)
+
+            @pl.when(first > 0)
+            def _():
+                send(side, message, chunk).wait_recv()
+                come = received[side, message, at(chunk), :].astype(F32)
+                sending[side, message, at(chunk), :] = (total + come).astype(BF16)
+
+            send(side, message, chunk).start()
+
+    near = me // (count // 2)
+
+    def advance(index, _):
+        @pl.when(index < steps)
+        def _():
+            flow(near, index)
+
+        @pl.when(index >= lag)
+        def _():
+            flow(1 - near, index - lag)
+
+        return 0
+
+    lax.fori_loop(0, steps + lag, advance, 0)
+    load.wait()
+
+    def own(chunk, carried):
+        here = at(chunk)
+        rows_in_now = rows_in[here, :]
+        total = dot_nt(parts_ref[me, here, :], weight_ref[...])
+
+        @pl.when(me > 0)
+        def _():
+            send(0, count - 1 - me, chunk).wait_recv()
+
+        @pl.when(me < count - 1)
+        def _():
+            send(1, me, chunk).wait_recv()
+
+        left = received[0, jnp.minimum(count - 1 - me, count - 2), here, :].astype(F32)
+        right = received[1, jnp.minimum(me, count - 2), here, :].astype(F32)
+        total = total + jnp.where(me > 0, left, 0.0) + jnp.where(me < count - 1, right, 0.0)
+        unit, inverse = row_stats(rows_in_now)
+        scaled = total * gain_ref[...]
+        through = (
+            scaled
+            - jnp.mean(scaled, axis=-1, keepdims=True)
+            - unit * jnp.mean(scaled * unit, axis=-1, keepdims=True)
+        )
+        input_ref[here, :] = (hidden_grad_ref[here, :] + inverse * through).astype(BF16)
+        gain_sum, bias_sum = carried
+        return (
+            gain_sum + jnp.sum(total * unit, axis=0, keepdims=True),
+            bias_sum + jnp.sum(total, axis=0, keepdims=True),
+        )
+
+    zero = jnp.zeros((1, width), F32)
+    gain_sum, bias_sum = lax.fori_loop(0, chunks, own, (zero, zero))
+    sums_ref[...] = jnp.concatenate([gain_sum, bias_sum, jnp.zeros((6, width), F32)], axis=0)
+
+    def finish(index, _):
+        message = index // chunks
+        chunk = index % chunks
+
+        @pl.when(count - 1 - message > me)
+        def _():
+            send(0, message, chunk).wait_send()
+
+        @pl.when(message < me)
+        def _():
+            send(1, message, chunk).wait_send()
+
+        return 0
+
+    lax.fori_loop(0, steps, finish, 0)
+
+
+def return_part(index, parts, weight, layer_input, hidden_grad, gain):
+    count, rows, cols = parts.shape
+    rows = rows // 2
+    width = weight.shape[0]
+    chunks = max(1, rows // 128)
+    any_spec = pl.BlockSpec(memory_space=pl.ANY)
+    dma = pltpu.SemaphoreType.DMA
+    fixed = lambda step: (0, 0)
+    return pl.pallas_call(
+        functools.partial(return_kernel, count, chunks, 2, index * rows),
+        grid=(1,),
+        in_specs=[
+            pl.BlockSpec((count, rows, cols), lambda step: (0, index, 0)),
+            pl.BlockSpec((width, cols), fixed),
+            any_spec,
+            pl.BlockSpec((rows, width), fixed),
+            pl.BlockSpec((1, width), fixed),
+        ],
+        out_specs=[pl.BlockSpec((rows, width), fixed), pl.BlockSpec((8, width), fixed)],
+        out_shape=[
+            jax.ShapeDtypeStruct((rows, width), BF16),
+            jax.ShapeDtypeStruct((8, width), F32),
+        ],
+        scratch_shapes=[
+            pltpu.VMEM((rows, width), F32),
+            pltpu.VMEM((2, count - 1, rows, width), BF16),
+            pltpu.VMEM((2, count - 1, rows, width), BF16),
+            dma((1,)),
+            dma((2, count - 1, chunks)),
+            dma((2, count - 1, chunks)),
+        ],
+        compiler_params=pltpu.CompilerParams(
+            collective_id=1 + index, has_side_effects=True, vmem_limit_bytes=VMEM_LIMIT
+        ),
+        cost_estimate=pl.CostEstimate(flops=80_000_000_000, bytes_accessed=1, transcendentals=0),
+    )(parts, weight, layer_input, hidden_grad, gain)
+
+
+def swap(value, axis, distance=1):
+    size = lax.axis_size(axis)
+    return lax.ppermute(value, axis, [(j, j ^ distance) for j in range(size)])
+
+
+def after(value, *earlier):
+    return lax.optimization_barrier((value,) + earlier)[0]
+
+
+def all_to_all(value):
+    return lax.all_to_all(value, "seq", 0, 0, tiled=True)
+
+
+def halves(value):
+    return jnp.split(value, 2, axis=1)
+
+
+def levels_of(axis):
+    return [1 << level for level in range(lax.axis_size(axis).bit_length() - 1)]
+
+
+def sum_everywhere(value):
+    for axis in ("batch", "seq", "mp"):
+        for distance in levels_of(axis):
+            value = value + swap(value, axis, distance)
+    return value
+
+
+def gather_small(value):
+    place = lax.axis_index("seq")
+    count = lax.axis_size("seq")
+    parts = [value] + [swap(value, "seq", distance) for distance in range(1, count)]
+    stacked = jnp.stack(parts)
+    order = jnp.arange(count, dtype=jnp.int32) ^ place
+    return jnp.take(stacked, order, axis=0).reshape((-1,) + value.shape[1:])
+
+
+def pick(value, index, count, axis=0):
+    size = value.shape[axis] // count
+    return lax.dynamic_slice_in_dim(value, index * size, size, axis)
+
+
+def fetch_near(weight, axis):
+    return swap(pick(weight, lax.axis_index("batch") % 2, 2, axis), "mp")
+
+
+def narrow_add(mine, received):
+    return (mine.astype(F32) + received.astype(F32)).astype(BF16)
+
+
+def halve(value, distance, axis):
+    side = (lax.axis_index("batch") // distance) % 2
+    return narrow_add(
+        pick(value, side, 2, axis), swap(pick(value, 1 - side, 2, axis), "batch", distance)
+    )
+
+
+def unhalve(value, distance, axis):
+    side = (lax.axis_index("batch") // distance) % 2
+    other = swap(value, "batch", distance)
+    low = jnp.where(side == 0, value, other)
+    high = jnp.where(side == 0, other, value)
+    return jnp.concatenate([low, high], axis=axis)
+
+
+def sum_cores(own, near, far, axis):
+    return halve(own, 1, axis), narrow_add(near, swap(far, "batch"))
+
+
+def sum_chips(own, near, axis):
+    for distance in levels_of("batch")[1:]:
+        own = halve(own, distance, axis)
+        near = halve(near, distance, axis)
+    return own, near
+
+
+def scatter_rows_of(own, axis):
+    return lax.psum_scatter(own, "seq", scatter_dimension=1 - axis, tiled=True)
+
+
+def spread_batch(value, axis):
+    for distance in reversed(levels_of("batch")):
+        value = unhalve(value, distance, axis)
+    return value.astype(F32)
+
+
+def place_kernel(place_ref, own_first, own_second, other_first, other_second, out_ref):
+    place = place_ref[0]
+
+    @pl.when(pl.program_id(0) == 0)
+    def _():
+        out_ref[place] = own_first[...].astype(F32)
+        out_ref[1 - place] = other_first[...].astype(F32)
+
+    @pl.when(pl.program_id(0) == 1)
+    def _():
+        out_ref[place] = own_second[...].astype(F32)
+        out_ref[1 - place] = other_second[...].astype(F32)
+
+
+def both_sequences(own):
+    other = [swap(part, "mp") for part in own]
+    rows, width = own[0].shape
+    step = min(256, rows)
+    steps = rows // step
+    first = pl.BlockSpec(
+        (step, width), lambda half, index, place_ref: (index * (1 - half) + (steps - 1) * half, 0)
+    )
+    second = pl.BlockSpec((step, width), lambda half, index, place_ref: (index * half, 0))
+    return pl.pallas_call(
+        place_kernel,
+        grid_spec=pltpu.PrefetchScalarGridSpec(
+            num_scalar_prefetch=1,
+            grid=(2, steps),
+            in_specs=[first, second, first, second],
+            out_specs=pl.BlockSpec(
+                (2, step, width), lambda half, index, place_ref: (0, half * steps + index, 0)
+            ),
+        ),
+        out_shape=jax.ShapeDtypeStruct((2, 2 * rows, width), F32),
+    )(lax.axis_index("mp").astype(jnp.int32)[None], *own, *other)
+
+
+def local(
+    layer_input,
+    lengths,
+    random_blocks,
+    first_gain,
+    first_bias,
+    qkv_weight,
+    out_weight,
+    second_gain,
+    second_bias,
+    up_weight,
+    up_bias,
+    down_weight,
+    down_bias,
+    cotangent,
+):
+    seq_count = lax.axis_size("seq")
+    seq_index = lax.axis_index("seq")
+    mp_index = lax.axis_index("mp")
+    parity = lax.axis_index("batch") % 2
+    _, local_rows, width = layer_input.shape
+    rows_total = local_rows * seq_count
+    blocks = rows_total // BLOCK
+    half_cols = qkv_weight.shape[2]
+    cols = width // seq_count
+    units = up_weight.shape[1]
+
+    doc_ends = jnp.cumsum(lax.dynamic_index_in_dim(lengths, mp_index, 0, keepdims=False))
+    randoms = lax.dynamic_index_in_dim(random_blocks, mp_index, 0, keepdims=False)
+    randoms = gather_small(randoms)
+    lists, admits = block_lists(jnp.arange(blocks, dtype=jnp.int32), randoms, blocks)
+    lists, admits = lists.reshape(-1), admits.reshape(-1)
+
+    qkv_near = lax.dynamic_slice_in_dim(qkv_weight, (seq_index * cols) % half_cols, cols, 2)
+    qkv_near = qkv_near.reshape(width, 3 * cols)
+    up_near = fetch_near(up_weight, 1)
+    bias_near = fetch_near(up_bias, 0)
+    out_other = swap(out_weight, "mp")
+
+    first_all, qkv, qkv_own = gather_project(
+        layer_input, first_gain[None], first_bias[None], qkv_near, half_cols
+    )
+    first_all = first_all.reshape(rows_total, width)
+    qkv, up_near, out_other, bias_near, lists, down_cut = lax.optimization_barrier(
+        (qkv.reshape(rows_total, 3 * cols), up_near, out_other, bias_near, lists, down_weight)
+    )
+    up_far, bias_far = swap(up_near, "batch"), swap(bias_near, "batch")
+    down_near = fetch_near(down_cut, 0)
+    attended, lse = attention_forward(qkv, doc_ends, lists, admits, cols)
+    attended, up_far, down_near, bias_far = lax.optimization_barrier(
+        (attended, up_far, down_near, bias_far)
+    )
+    down_far = swap(down_near, "batch")
+    bias_full = jnp.concatenate([up_bias, bias_near, bias_far])[None]
+    half_rows = local_rows // 2
+    attended_halves = [
+        all_to_all(part) for part in halves(attended.reshape(seq_count, local_rows, cols))
+    ]
+    outs = [part.reshape(seq_count // 2, cols, width) for part in (out_weight, out_other)]
+    kept, results = None, []
+    for index, att in enumerate(attended_halves):
+        where = jnp.stack(
+            [mp_index, seq_index * local_rows + index * half_rows, doc_ends[-1]]
+        ).astype(jnp.int32)
+        result = token_part(
+            index,
+            where,
+            att,
+            layer_input,
+            cotangent,
+            outs,
+            (up_weight, up_near, up_far),
+            (down_weight, down_near, down_far),
+            bias_full,
+            second_gain[None],
+            second_bias[None],
+            down_bias[None],
+            kept,
+        )
+        kept = result[3:8]
+        results.append(result[:3] + result[8:])
+    activated, pre_grad, second_low, hidden_low, grad_low = kept
+    sums = results[0][3][:3] + results[1][3][:3]
+    unit_sums = results[0][4][0] + results[1][4][0]
+    bias_sums = [unit_sums[:units], unit_sums[units : units * 3 // 2], unit_sums[units * 3 // 2 :]]
+    layer_output = both_sequences([result[0] for result in results])
+    grad_all = jnp.concatenate([all_to_all(result[2]) for result in results], axis=1)
+    grad_all = grad_all.reshape(rows_total, cols)
+
+    down_sum = dot_tn(activated, grad_low).astype(BF16)
+    up_sum = dot_tn(second_low, pre_grad).astype(BF16)
+    attended_low = jnp.concatenate(attended_halves, axis=1)
+    out_sum = jnp.einsum(
+        "zrc,rd->zcd", attended_low, hidden_low, preferred_element_type=F32
+    ).astype(BF16).reshape(width, width)
+    cuts = [units, units * 3 // 2]
+    down_sum = sum_cores(*jnp.split(down_sum, cuts, axis=0), 0)
+    up_sum = sum_cores(*jnp.split(up_sum, cuts, axis=1), 1)
+    out_theirs = pick(out_sum, 1 - mp_index, 2)
+    out_sum = sum_cores(
+        pick(out_sum, mp_index, 2), pick(out_theirs, parity, 2), pick(out_theirs, 1 - parity, 2), 0
+    )
+    bias_other = jnp.where(
+        parity == 0,
+        jnp.concatenate([bias_sums[1], bias_sums[2]]),
+        jnp.concatenate([bias_sums[2], bias_sums[1]]),
+    )
+    bias_all = jnp.where(
+        mp_index == 0,
+        jnp.concatenate([bias_sums[0], bias_other]),
+        jnp.concatenate([bias_other, bias_sums[0]]),
+    )
+    early = sum_everywhere(jnp.concatenate([sums.reshape(-1), bias_all]))
+    grad_all, down_sum, up_sum, out_sum = lax.optimization_barrier(
+        (grad_all, down_sum, up_sum, out_sum)
+    )
+    down_sum, up_sum, out_sum = sum_chips(*down_sum, 0), sum_chips(*up_sum, 1), sum_chips(*out_sum, 0)
+    qkv_low_grad = attention_backward(
+        qkv, attended, grad_all, lse, doc_ends, lists, admits, cols
+    )
+    qkv_sum = dot_tn(first_all, qkv_low_grad).astype(BF16)
+    qkv_sum = qkv_sum.reshape(seq_count, -1, 3 * cols).transpose(1, 0, 2)
+    levels = levels_of("batch")
+    sums_now = [down_sum, up_sum, out_sum]
+    qkv_low_grad, qkv_sum, sums_now = lax.optimization_barrier((qkv_low_grad, qkv_sum, sums_now))
+    near_sums = [swap(near, "mp") for _, near in sums_now]
+    qkv_part = halve(qkv_sum, levels[0], 0)
+    parts = qkv_low_grad.reshape(seq_count, local_rows, 3 * cols)
+    input_first, first_sums = return_part(
+        0, parts, qkv_own, layer_input, results[0][1], first_gain[None]
+    )
+    input_first, near_sums, qkv_part = lax.optimization_barrier((input_first, near_sums, qkv_part))
+    own_sums = [narrow_add(own, near) for (own, _), near in zip(sums_now, near_sums)]
+    second_grad, input_first, own_sums = lax.optimization_barrier(
+        (results[1][1], input_first, own_sums)
+    )
+    down_grad, up_grad, out_grad = [
+        scatter_rows_of(own, axis) for own, axis in zip(own_sums, (0, 1, 0))
+    ]
+    for distance in levels[1:]:
+        qkv_part = halve(qkv_part, distance, 0)
+    input_second, second_sums = return_part(
+        1, parts, qkv_own, layer_input, second_grad, first_gain[None]
+    )
+    input_second, qkv_part, down_grad, up_grad, out_grad = lax.optimization_barrier(
+        (input_second, qkv_part, down_grad, up_grad, out_grad)
+    )
+    late = sum_everywhere((first_sums + second_sums)[:2])
+    qkv_part = narrow_add(qkv_part, swap(qkv_part, "mp"))
+    qkv_part = all_to_all(qkv_part.transpose(1, 0, 2))
+    qkv_part = pick(qkv_part, mp_index, 2)
+    qkv_part = qkv_part.reshape(seq_count // 2, -1, 3, cols).transpose(1, 2, 0, 3)
+    qkv_grad = spread_batch(qkv_part.reshape(-1, 3, half_cols), 0)
+    down_grad = spread_batch(down_grad, 0)
+    up_grad = spread_batch(up_grad, 1)
+    out_grad = spread_batch(out_grad, 0)
+    input_grad = both_sequences([input_first, input_second])
+    up_bias_grad = lax.dynamic_slice_in_dim(early, 3 * width + mp_index * units, units)
+    return (
+        layer_output,
+        input_grad,
+        late[0],
+        late[1],
+        qkv_grad,
+        out_grad,
+        early[width : 2 * width],
+        early[2 * width : 3 * width],
+        up_grad,
+        up_bias_grad,
+        down_grad,
+        early[:width],
+    )
+
+
+MB = 2
+NBLK = 64
+LEN = 4096
+HIGH = lax.Precision.HIGHEST
+
+
 def segment_of(places, doc_ends):
     return jnp.sum((places[..., None] >= doc_ends).astype(jnp.int32), axis=-1)
 
 
-def block_lists(blocks, randoms):
+def block_lists_by_index(blocks, randoms):
     leading = randoms.shape[:-1]
     globals_part = jnp.broadcast_to(jnp.arange(GLOB, dtype=jnp.int32), leading + (GLOB,))
     window_part = jnp.broadcast_to(
@@ -133,7 +1477,7 @@
     )
 
 
-def local(
+def local_by_blocks(
     layer_input,
     lengths,
     random_blocks,
@@ -166,7 +1510,7 @@
     valid_rows = (places[None, :] < doc_ends[:, -1:]).astype(jnp.float32)
     glob_flag = (places < glob_rows)[None, :, None]
     query_blocks = seq_index * blocks_dev + jnp.arange(blocks_dev, dtype=jnp.int32)
-    block_list, admitted = block_lists(query_blocks, random_blocks)
+    block_list, admitted = block_lists_by_index(query_blocks, random_blocks)
     key_places = block_list[..., None] * BLOCK + jnp.arange(BLOCK, dtype=jnp.int32)
     key_segs = segment_of(key_places, doc_ends[:, None, None, None, :]).reshape(
         local_seqs, blocks_dev, LIST * BLOCK
@@ -473,8 +1817,9 @@
         P(),
         P("batch", "seq", None),
     )
+    by_heads = (1024 // mesh.shape["seq"]) % 128 == 0
     return jax.shard_map(
-        local,
+        local if by_heads else local_by_blocks,
         mesh=mesh,
         in_specs=placed,
         out_specs=(

time: 2640 us -> 817 us (0.31)
  waiting for transfers between devices: 948 us -> 114 us
  local copies, waits for them, and re-layouts: 736 us -> 42.3 us
  Pallas kernels: 0 us -> 478 us
  matrix products: 442 us -> 38 us
  other arithmetic: 421 us -> 51.1 us
  starting transfers between devices: 1.9 us -> 71 us
  blocking collectives: 61.2 us -> 0 us
    pallas_call x0 -> x9, Pallas kernels: none -> 478 us  [the longest x2 179 us: return_part(): pl.pallas_call(functools.partial(return_kernel, count, chunks, 2, index *...]
    psum x4 -> x0, waiting for transfers between devices: 466 us -> none  [the longest x1 194 us: local(): lax.psum(jnp.dot(activated, down_weight, preferred_element_type=jnp.float...]
    dot_general x48 -> x4, matrix products: 413 us -> 38 us  [the longest x3 35.6 us: dot_tn(): lax.dot_general(left, right, (((0,), (0,)), ((), ())), preferred_element_...]
    reduce_scatter x6 -> x3, waiting for transfers between devices: 241 us -> 0.06 us  [scatter_rows_of(): return lax.psum_scatter(own, 'seq', scatter_dimension=1 - axis, tiled=True)]
    another operation x32 -> x0, local copies, waits for them, and re-layouts: 240 us -> none
    all_gather x4 -> x0, waiting for transfers between devices: 240 us -> none  [the longest x2 162 us: fetch_rows(): lax.all_gather(values, 'seq', axis=1, tiled=True)]
    scatter-add x2 -> x0, other arithmetic: 165 us -> none  [local(): jax.ops.segment_sum(picked_grads.reshape(batch_seqs * picked_rows, 2 * he...]
    reshape x12 -> x5, local copies, waits for them, and re-layouts: 160 us -> 1.8 us  [the longest x1 1.57 us: local(): qkv_near = qkv_near.reshape(width, 3 * cols)]
  transfers between devices with their start and end apart: 14 -> 58, of which waited for: 12 -> 16; matrix products, arithmetic and copies ran while one was open for 23% -> 13% of each run, Pallas kernels for 0% -> 55%
where the time goes in v2:
time: 817 us; the launch traced here: 810 us
  Pallas kernels  478 us (59%)
  waiting for transfers between devices  114 us (14%)
  starting transfers between devices  71 us (9%)
  other arithmetic  51.1 us (6%)
  local copies, waits for them, and re-layouts  42.3 us (5%)
  matrix products  38 us (5%)
  between operations  15.1 us (2%)
    pallas_call x2, Pallas kernels, return_part(): pl.pallas_call(functools.partial(return_kernel, count, chunks, 2, index *...  179 us
    pallas_call x1, Pallas kernels, gather_project(): pl.pallas_call(functools.partial(gather_kernel, count, chunks, half_cols)...  141 us
    ppermute x50, waiting for transfers between devices, swap(): return lax.ppermute(value, axis, [(j, j ^ distance) for j in range(size)])  83.7 us
    pallas_call x2, Pallas kernels, token_part(): pl.pallas_call(functools.partial(token_kernel, min(256, rows)), grid_spec...  66.3 us
    ppermute x50, starting transfers between devices, swap(): return lax.ppermute(value, axis, [(j, j ^ distance) for j in range(size)])  48.4 us
    pallas_call x1, Pallas kernels, attention_backward(): pl.pallas_call(functools.partial(backward_kernel, heads), grid=(1,), in_s...  46.9 us
    dot_general x3, matrix products, dot_tn(): lax.dot_general(left, right, (((0,), (0,)), ((), ())), preferred_element_...  35.6 us
    convert_element_type x16, other arithmetic, narrow_add(): return (mine.astype(F32) + received.astype(F32)).astype(BF16)  32.7 us
  transfers between devices with their start and end apart: 58, of which 16 were waited for; matrix products, arithmetic and copies ran while one was open for 13% of the time, Pallas kernels for 55%

profile of v2, /device:TPU:0, one launch (start us, length us, event | category | flops | bytes accessed | tf_op | source)
XLA Modules:
  0.0 809.9 jit_solution(17804676382662351128)
XLA Ops:
  23.9 140.7 %shard_map.229 = (bf16[4,1024,1024]{2,1,0:T(8,128)(2,1)}, bf16[4,1024,768]{2,1,0:T(8,128)(2,1)}, bf16[1024,768]{1,0:T(8,128)(2,1)}) custom-call(f32[2,1024,1024]{2,1,0:T(8,128)} %x_ref.9, f32[1,1024]{1,0:T(1,128)} %bitcast.79, f32[1,1024]{1,0:T(1,128)} %bitcast.72, bf16[1024,768]{1,0:T(8,128)(2,1)} %copy.54.weight_ref), custom_call_target="tpu_custom_call" | custom-call | flops 149999992832 | bytes 1 | tf_op jit(solution)/shard_map/pallas_call | solution.py:878
  173.8 31.9 %shard_map.230 = (bf16[4096,256]{1,0:T(8,128)(2,1)}, f32[64,8,256]{2,1,0:T(8,128)}) custom-call(s32[4]{0:T(128)} %bitcast.91, s32[512]{0:T(512)} %min.12.lists_ref, s32[512]{0:T(512)} %reshape.146.admit_ref, bf16[4096,768]{1,0:T(8,128)(2,1)} %bitcast.83, bf16[4096,768]{1,0:T(8,128)(2,1)} %bitcast.84, bf16[4096,768]{1,0:T(8,128)(2,1)} %bitcast.85), custom_call_target="tpu_custom_call" | custom-call | flops 10737418240 | bytes 8388608 | tf_op jit(solution)/shard_map/pallas_call | solution.py:359
  205.7 9.5 %collective-permute-done.7.down_near_ref = bf16[1024,1024]{1,0:T(8,128)(2,1)} collective-permute-done((bf16[1024,1024]{1,0:T(8,128)(2,1)S(1)}, bf16[1024,1024]{1,0:T(8,128)(2,1)}, u32[]{:S(2)}, u32[]{:S(2)}) %collective-permute-start.7) | collective-permute-done | bytes 2097184 | tf_op jit(solution)/shard_map/ppermute | solution.py:1080
  218.2 4.9 all-to-all-start
  226.7 22.8 %all-to-all-done.att_ref = bf16[4,512,256]{2,1,0:T(8,128)(2,1)S(1)} async-done(((bf16[4,512,256]{2,1,0:T(8,128)(2,1)}), bf16[4,512,256]{2,1,0:T(8,128)(2,1)S(1)}, u32[]{:S(2)}, u32[]{:S(2)}) %all-to-all-start) | async-done | bytes 1048608 | tf_op jit(solution)/shard_map/all_to_all | solution.py:1088
  253.8 33.1 %shard_map.231 = (bf16[512,1024]{1,0:T(8,128)(2,1)}, f32[512,1024]{1,0:T(8,128)}, bf16[4,512,256]{2,1,0:T(8,128)(2,1)}, bf16[1024,4096]{1,0:T(8,128)(2,1)}, bf16...) custom-call(s32[3]{0:T(128)} %add_add_fusion.1.where_ref, ...), custom_call_target="tpu_custom_call" | custom-call | flops 19327352832 | bytes 33554432 | tf_op jit(solution)/shard_map/pallas_call | solution.py:609
  287.8 33.3 %shard_map.232 = (bf16[512,1024]{1,0:T(8,128)(2,1)}, f32[512,1024]{1,0:T(8,128)}, bf16[4,512,256]{2,1,0:T(8,128)(2,1)}, bf16[1024,4096]{1,0:T(8,128)(2,1)}, bf16...) custom-call(s32[3]{0:T(128)} %add_add_fusion.2.where_ref, ...), custom_call_target="tpu_custom_call", output_to_operand_aliasing={{3}: (16, {}), {4}: (17, {}), {5}: (18, {}), {6}: (19, {}),... | custom-call | flops 19327352832 | bytes 33554432 | tf_op jit(solution)/shard_map/pallas_call | solution.py:609
  321.1 5.7 all-to-all-start.3
  326.8 11.4 %convolution_convert_fusion = bf16[1024,4096]{1,0:T(8,128)(2,1)S(1)} fusion(bf16[1024,1024]{1,0:T(8,128)(2,1)S(1)} %copy-done.30, bf16[1024,4096]{1,0:T(8,128)(2,1)} %get-tuple-element.106), kind=kOutput, calls=%fused_computation.1 | convolution fusion | flops 8594128896 | bytes 18874368 | tf_op jit(solution)/shard_map/dot_general | solution.py:122
  351.8 4.6 all-to-all-start.2
  356.4 13.1 %convolution_convert_fusion.1 = bf16[4096,1024]{1,0:T(8,128)(2,1)S(1)} fusion(bf16[1024,4096]{1,0:T(8,128)(2,1)} %get-tuple-element.103, bf16[1024,1024]{1,0:T(8,128)(2,1)} %get-tuple-element.104), kind=kOutput, calls=%fused_computation.2 | convolution fusion | flops 8594128896 | bytes 18874368 | tf_op jit(solution)/shard_map/dot_general | solution.py:122
  376.6 4.5 collective-permute-done.17
  396.0 4.4 add_convert_fusion.3
  409.4 46.9 %shard_map.234 = bf16[4096,768]{1,0:T(8,128)(2,1)} custom-call(s32[4]{0:T(128)} %bitcast.92, s32[512]{0:T(512)} %min.12.lists_ref, s32[512]{0:T(512)} %reshape.146.admit_ref, bf16[4096,768]{1,0:T(8,128)(2,1)} %bitcast.86, bf16[4096,768]{1,0:T(8,128)(2,1)} %bitcast.87, bf16[4096,768]{1,0:T(8,128)(2,1)} %bitcast.88, ...), custom_call_target="tpu_custom_call" | custom-call | flops 32212254720 | bytes 20971520 | tf_op jit(solution)/shard_map/pallas_call | solution.py:388
  456.4 11.2 %convolution_convert_fusion.2 = bf16[1024,768]{1,0:T(8,128)(2,1)S(1)} fusion(bf16[4096,1024]{1,0:T(8,128)(2,1)} %bitcast.82, bf16[4096,768]{1,0:T(8,128)(2,1)} %shard_map.234), kind=kOutput, calls=%fused_computation.20 | convolution fusion | flops 6443237376 | bytes 16252928 | tf_op jit(solution)/shard_map/dot_general | solution.py:122
  474.2 8.6 %collective-permute-done.19 = bf16[512,1024]{1,0:T(8,128)(2,1)} collective-permute-done((bf16[512,1024]{1,0:T(8,128)(2,1)}, bf16[512,1024]{1,0:T(8,128)(2,1)}, u32[]{:S(2)}, u32[]{:S(2)}) %collective-permute-start.19) | collective-permute-done | bytes 1048608 | tf_op jit(solution)/shard_map/ppermute | solution.py:1080
  485.4 19.1 %collective-permute-done.18 = bf16[512,1024]{1,0:T(8,128)(2,1)S(1)} collective-permute-done((bf16[512,1024]{1,0:T(8,128)(2,1)S(1)}, bf16[512,1024]{1,0:T(8,128)(2,1)S(1)}, u32[]{:S(2)}, u32[]{:S(2)}) %collective-permute-start.18) | collective-permute-done | bytes 1048608 | tf_op jit(solution)/shard_map/ppermute | solution.py:1080
  507.7 74.1 %shard_map.235 = (bf16[512,1024]{1,0:T(8,128)(2,1)}, f32[8,1024]{1,0:T(8,128)}) custom-call(bf16[4,1024,768]{2,1,0:T(8,128)(2,1)} %bitcast.89, bf16[1024,768]{1,0:T(8,128)(2,1)} %get-tuple-element.118.weight_ref, f32[2,1024,1024]{2,1,0:T(8,128)} %x_ref.9, f32[512,1024]{1,0:T(8,128)} %get-tuple-element.119.hidden_grad_ref, f32[1,1024]{1,0:T(1,128)} %bitcast.80), custom_call_target="tpu_custom_call" | custom-call | flops 80000000000 | bytes 1 | tf_op jit(solution)/shard_map/pallas_call | solution.py:1048
  606.7 105.1 %shard_map.236 = (bf16[512,1024]{1,0:T(8,128)(2,1)}, f32[8,1024]{1,0:T(8,128)}) custom-call(bf16[4,1024,768]{2,1,0:T(8,128)(2,1)} %bitcast.90, bf16[1024,768]{1,0:T(8,128)(2,1)} %get-tuple-element.118.weight_ref, f32[2,1024,1024]{2,1,0:T(8,128)} %x_ref.9, f32[512,1024]{1,0:T(8,128)} %get-tuple-element.133.hidden_grad_ref, f32[1,1024]{1,0:T(1,128)} %bitcast.81), custom_call_target="tpu_custom_call" | custom-call | flops 80000000000 | bytes 1 | tf_op jit(solution)/shard_map/pallas_call | solution.py:1048
  730.7 6.4 shard_map.233
  743.8 4.2 collective-permute-done.48
  748.1 23.7 %collective-permute-done.36 = bf16[64,4,768]{2,0,1:T(8,128)(2,1)S(1)} collective-permute-done((bf16[64,4,768]{2,0,1:T(8,128)(2,1)S(1)}, bf16[64,4,768]{2,0,1:T(8,128)(2,1)S(1)}, u32[]{:S(2)}, u32[]{:S(2)}) %collective-permute-start.36) | collective-permute-done | bytes 393248 | tf_op jit(solution)/shard_map/ppermute | solution.py:1080
  778.3 6.7 all-to-all-done.4
  793.8 6.6 shard_map.237
  (280 shorter events, 162.7 us)
Async XLA Ops:
  8.6 156.2 %collective-permute-start.3 = (s32[16,3]{0,1:T(4,128)}, s32[16,3]{0,1:T(4,128)}, u32[]{:S(2)}, u32[]{:S(2)}) collective-permute-start(s32[16,3]{0,1:T(4,128)} %bitcast.47.clone.2), channel_id=1, source_target_pairs={{0,8},{8,0},{16,24},{24,16},{1,9},{9,1},{17,25},{25,17},{2,10},{10... | collective-permute-start | bytes 584 | tf_op jit(solution)/shard_map/ppermute | solution.py:1080
  11.7 154.6 %collective-permute-start.4 = (s32[16,3]{0,1:T(4,128)}, s32[16,3]{0,1:T(4,128)}, u32[]{:S(2)}, u32[]{:S(2)}) collective-permute-start(s32[16,3]{0,1:T(4,128)} %bitcast.47.clone.2), channel_id=1, source_target_pairs={{0,16},{8,24},{16,0},{24,8},{1,17},{9,25},{17,1},{25,9},{2,18},{10... | collective-permute-start | bytes 584 | tf_op jit(solution)/shard_map/ppermute | solution.py:1080
  14.2 152.1 %collective-permute-start.5 = (s32[16,3]{0,1:T(4,128)}, s32[16,3]{0,1:T(4,128)}, u32[]{:S(2)}, u32[]{:S(2)}) collective-permute-start(s32[16,3]{0,1:T(4,128)} %bitcast.47.clone.2), channel_id=1, source_target_pairs={{0,24},{8,16},{16,8},{24,0},{1,25},{9,17},{17,9},{25,1},{2,26},{10... | collective-permute-start | bytes 584 | tf_op jit(solution)/shard_map/ppermute | solution.py:1080
  17.3 151.2 %collective-permute-start = (bf16[1024,1024]{1,0:T(8,128)(2,1)}, bf16[1024,1024]{1,0:T(8,128)(2,1)}, u32[]{:S(2)}, u32[]{:S(2)}) collective-permute-start(bf16[1024,1024]{1,0:T(8,128)(2,1)} %constant_dynamic-slice_fusion.15), channel_id=1, source_target_pairs={{0,1},{1,0},{2,3},{3,2},{4,5},{5,4},{6,7},{7,6},{8,9},{9,8},{10,11... | collective-permute-start | bytes 6291464 | tf_op jit(solution)/shard_map/ppermute | solution.py:1080
  19.1 149.4 %collective-permute-start.1 = (bf16[512,1024]{1,0:T(8,128)(2,1)}, bf16[512,1024]{1,0:T(8,128)(2,1)}, u32[]{:S(2)}, u32[]{:S(2)}) collective-permute-start(bf16[512,1024]{1,0:T(8,128)(2,1)} %param.20), channel_id=1, source_target_pairs={{0,1},{1,0},{2,3},{3,2},{4,5},{5,4},{6,7},{7,6},{8,9},{9,8},{10,11... | collective-permute-start | bytes 3145736 | tf_op jit(solution)/shard_map/ppermute | solution.py:1080
  170.3 44.9 %collective-permute-start.7 = (bf16[1024,1024]{1,0:T(8,128)(2,1)S(1)}, bf16[1024,1024]{1,0:T(8,128)(2,1)}, u32[]{:S(2)}, u32[]{:S(2)}) collective-permute-start(bf16[1024,1024]{1,0:T(8,128)(2,1)S(1)} %constant_dynamic-slice_fusion.13), channel_id=1, source_target_pairs={{0,1},{1,0},{2,3},{3,2},{4,5},{5,4},{6,7},{7,6},{8,9},{9,8},{10,11... | collective-permute-start | bytes 6291464 | tf_op jit(solution)/shard_map/ppermute | solution.py:1080
  356.4 372.4 %reduce-scatter.8.cloned.1.call-start = ((), (), s32[]{:S(2)}) async-start(), calls=%async_computation.10 | async-start | bytes 327680 | tf_op jit(solution)/shard_map/reduce_scatter | solution.py:1155
  400.5 67.2 %collective-permute-start.23 = (bf16[128,1024]{1,0:T(8,128)(2,1)S(1)}, bf16[128,1024]{1,0:T(8,128)(2,1)}, u32[]{:S(2)}, u32[]{:S(2)}) collective-permute-start(bf16[128,1024]{1,0:T(8,128)(2,1)S(1)} %constant_dynamic-slice_fusion.3), channel_id=1, source_target_pairs={{0,4},{2,6},{4,0},{6,2},{1,5},{3,7},{5,1},{7,3},{8,12},{10,14},{12... | collective-permute-start | bytes 786440 | tf_op jit(solution)/shard_map/ppermute | solution.py:1080
  402.1 67.7 %collective-permute-start.22 = (bf16[128,1024]{1,0:T(8,128)(2,1)S(1)}, bf16[128,1024]{1,0:T(8,128)(2,1)S(1)}, u32[]{:S(2)}, u32[]{:S(2)}) collective-permute-start(bf16[128,1024]{1,0:T(8,128)(2,1)S(1)} %constant_dynamic-slice_fusion.4), channel_id=1, source_target_pairs={{0,4},{2,6},{4,0},{6,2},{1,5},{3,7},{5,1},{7,3},{8,12},{10,14},{12... | collective-permute-start | bytes 786440 | tf_op jit(solution)/shard_map/ppermute | solution.py:1080
  403.8 66.1 %collective-permute-start.21 = (bf16[1024,512]{1,0:T(8,128)(2,1)}, bf16[1024,512]{1,0:T(8,128)(2,1)}, u32[]{:S(2)}, u32[]{:S(2)}) collective-permute-start(bf16[1024,512]{1,0:T(8,128)(2,1)} %constant_dynamic-slice_fusion.5), channel_id=1, source_target_pairs={{0,4},{2,6},{4,0},{6,2},{1,5},{3,7},{5,1},{7,3},{8,12},{10,14},{12... | collective-permute-start | bytes 3145736 | tf_op jit(solution)/shard_map/ppermute | solution.py:1080
  406.3 66.1 %collective-permute-start.20 = (bf16[1024,512]{1,0:T(8,128)(2,1)}, bf16[1024,512]{1,0:T(8,128)(2,1)}, u32[]{:S(2)}, u32[]{:S(2)}) collective-permute-start(bf16[1024,512]{1,0:T(8,128)(2,1)} %constant_dynamic-slice_fusion.6), channel_id=1, source_target_pairs={{0,4},{2,6},{4,0},{6,2},{1,5},{3,7},{5,1},{7,3},{8,12},{10,14},{12... | collective-permute-start | bytes 3145736 | tf_op jit(solution)/shard_map/ppermute | solution.py:1080
  407.9 74.9 %collective-permute-start.19 = (bf16[512,1024]{1,0:T(8,128)(2,1)}, bf16[512,1024]{1,0:T(8,128)(2,1)}, u32[]{:S(2)}, u32[]{:S(2)}) collective-permute-start(bf16[512,1024]{1,0:T(8,128)(2,1)} %constant_dynamic-slice_fusion.7), channel_id=1, source_target_pairs={{0,4},{2,6},{4,0},{6,2},{1,5},{3,7},{5,1},{7,3},{8,12},{10,14},{12... | collective-permute-start | bytes 3145736 | tf_op jit(solution)/shard_map/ppermute | solution.py:1080
  505.0 76.8 %collective-permute-start.27 = (bf16[128,4,768]{2,0,1:T(8,128)(2,1)S(1)}, bf16[128,4,768]{2,0,1:T(8,128)(2,1)}, u32[]{:S(2)}, u32[]{:S(2)}) collective-permute-start(bf16[128,4,768]{2,0,1:T(8,128)(2,1)S(1)} %constant_dynamic-slice_fusion.2), channel_id=1, source_target_pairs={{0,2},{2,0},{4,6},{6,4},{1,3},{3,1},{5,7},{7,5},{8,10},{10,8},{12,... | collective-permute-start | bytes 2359304 | tf_op jit(solution)/shard_map/ppermute | solution.py:1080
  505.1 78.3 %collective-permute-start.24 = (bf16[512,1024]{1,0:T(8,128)(2,1)}, bf16[512,1024]{1,0:T(8,128)(2,1)}, u32[]{:S(2)}, u32[]{:S(2)}) collective-permute-start(bf16[512,1024]{1,0:T(8,128)(2,1)} %add_convert_fusion.8), channel_id=1, source_target_pairs={{0,1},{1,0},{2,3},{3,2},{4,5},{5,4},{6,7},{7,6},{8,9},{9,8},{10,11... | collective-permute-start | bytes 3145736 | tf_op jit(solution)/shard_map/ppermute | solution.py:1080
  505.7 77.7 %collective-permute-start.25 = (bf16[1024,512]{1,0:T(8,128)(2,1)}, bf16[1024,512]{1,0:T(8,128)(2,1)}, u32[]{:S(2)}, u32[]{:S(2)}) collective-permute-start(bf16[1024,512]{1,0:T(8,128)(2,1)} %add_convert_fusion.6), channel_id=1, source_target_pairs={{0,1},{1,0},{2,3},{3,2},{4,5},{5,4},{6,7},{7,6},{8,9},{9,8},{10,11... | collective-permute-start | bytes 3145736 | tf_op jit(solution)/shard_map/ppermute | solution.py:1080
  507.2 76.2 %collective-permute-start.26 = (bf16[128,1024]{1,0:T(8,128)(2,1)S(1)}, bf16[128,1024]{1,0:T(8,128)(2,1)S(1)}, u32[]{:S(2)}, u32[]{:S(2)}) collective-permute-start(bf16[128,1024]{1,0:T(8,128)(2,1)S(1)} %add_convert_fusion.16), channel_id=1, source_target_pairs={{0,1},{1,0},{2,3},{3,2},{4,5},{5,4},{6,7},{7,6},{8,9},{9,8},{10,11... | collective-permute-start | bytes 786440 | tf_op jit(solution)/shard_map/ppermute | solution.py:1080
  589.4 139.4 %reduce-scatter.4.cloned.1.call-start = ((), (), s32[]{:S(2)}) async-start(), calls=%async_computation.8 | async-start | bytes 1310720 | tf_op jit(solution)/shard_map/reduce_scatter | solution.py:1155
  590.1 138.7 %reduce-scatter.6.cloned.1.call-start = ((), (), s32[]{:S(2)}) async-start(), calls=%async_computation.9 | async-start | bytes 1310720 | tf_op jit(solution)/shard_map/reduce_scatter | solution.py:1155
  600.2 130.5 %collective-permute-start.11 = (bf16[512,1024]{1,0:T(8,128)(2,1)}, bf16[512,1024]{1,0:T(8,128)(2,1)}, u32[]{:S(2)}, u32[]{:S(2)}) collective-permute-start(bf16[512,1024]{1,0:T(8,128)(2,1)} %get-tuple-element.99.own_second), channel_id=1, source_target_pairs={{0,1},{1,0},{2,3},{3,2},{4,5},{5,4},{6,7},{7,6},{8,9},{9,8},{10,11... | collective-permute-start | bytes 3145736 | tf_op jit(solution)/shard_map/ppermute | solution.py:1080
  601.6 129.0 %collective-permute-start.10 = (bf16[512,1024]{1,0:T(8,128)(2,1)S(1)}, bf16[512,1024]{1,0:T(8,128)(2,1)}, u32[]{:S(2)}, u32[]{:S(2)}) collective-permute-start(bf16[512,1024]{1,0:T(8,128)(2,1)S(1)} %copy-done.15), channel_id=1, source_target_pairs={{0,1},{1,0},{2,3},{3,2},{4,5},{5,4},{6,7},{7,6},{8,9},{9,8},{10,11... | collective-permute-start | bytes 3145736 | tf_op jit(solution)/shard_map/ppermute | solution.py:1080
  602.4 110.2 %collective-permute-start.44 = (f32[7168]{0:T(1024)S(1)}, f32[7168]{0:T(1024)S(1)}, u32[]{:S(2)}, u32[]{:S(2)}) collective-permute-start(f32[7168]{0:T(1024)S(1)} %add.301), channel_id=1, source_target_pairs={{0,16},{8,24},{16,0},{24,8},{1,17},{9,25},{17,1},{25,9},{2,18},{10... | collective-permute-start | bytes 86024 | tf_op jit(solution)/shard_map/ppermute | solution.py:1080
  605.1 123.6 %collective-permute-start.28 = (bf16[64,4,768]{2,0,1:T(8,128)(2,1)S(1)}, bf16[64,4,768]{2,0,1:T(8,128)(2,1)S(1)}, u32[]{:S(2)}, u32[]{:S(2)}) collective-permute-start(bf16[64,4,768]{2,0,1:T(8,128)(2,1)S(1)} %constant_dynamic-slice_fusion.1), channel_id=1, source_target_pairs={{0,4},{2,6},{4,0},{6,2},{1,5},{3,7},{5,1},{7,3},{8,12},{10,14},{12... | collective-permute-start | bytes 1179656 | tf_op jit(solution)/shard_map/ppermute | solution.py:1080
  737.1 56.7 %collective-permute-start.29 = (bf16[512,1024]{1,0:T(8,128)(2,1)}, bf16[512,1024]{1,0:T(8,128)(2,1)}, u32[]{:S(2)}, u32[]{:S(2)}) collective-permute-start(bf16[512,1024]{1,0:T(8,128)(2,1)} %get-tuple-element.132.own_first), channel_id=1, source_target_pairs={{0,1},{1,0},{2,3},{3,2},{4,5},{5,4},{6,7},{7,6},{8,9},{9,8},{10,11... | collective-permute-start | bytes 3145736 | tf_op jit(solution)/shard_map/ppermute | solution.py:1080
  741.9 51.9 %collective-permute-start.30 = (bf16[512,1024]{1,0:T(8,128)(2,1)}, bf16[512,1024]{1,0:T(8,128)(2,1)}, u32[]{:S(2)}, u32[]{:S(2)}) collective-permute-start(bf16[512,1024]{1,0:T(8,128)(2,1)} %get-tuple-element.139.own_second), channel_id=1, source_target_pairs={{0,1},{1,0},{2,3},{3,2},{4,5},{5,4},{6,7},{7,6},{8,9},{9,8},{10,11... | collective-permute-start | bytes 3145736 | tf_op jit(solution)/shard_map/ppermute | solution.py:1080
  (65 other events, 990.2 us)
Sparse Core Ops, SparseCore 0:
  589.5 22.1 reduce-scatter.7
  614.6 41.5 reduce-scatter.3
  659.1 42.6 reduce-scatter.5

commit v3 on v2

--- a/solution.py
+++ b/solution.py
@@ -52,6 +52,56 @@
     return (jnp.clip(block_list, 0, block_count - 1), admitted.astype(jnp.int32))
 
 
+MESH = pl.DeviceIdType.MESH
+
+
+class Trade:
+    def __init__(self, source, target, send_sems, recv_sems, own_sem):
+        self.source, self.target = source, target
+        self.send_sems, self.recv_sems, self.own_sem = send_sems, recv_sems, own_sem
+        self.count = source.shape[0]
+        self.me = lax.axis_index("seq")
+
+    def greet(self, others):
+        barrier = pltpu.get_barrier_semaphore()
+        for distance in range(1, self.count):
+            other = lax.rem(self.me + distance, self.count)
+            pl.semaphore_signal(barrier, inc=1, device_id={"seq": other}, device_id_type=MESH)
+        pl.semaphore_wait(barrier, self.count - 1 + others)
+
+    def copy(self, distance):
+        other = lax.rem(self.me + distance, self.count)
+        return pltpu.make_async_remote_copy(
+            src_ref=self.source.at[other],
+            dst_ref=self.target.at[self.me],
+            send_sem=self.send_sems.at[distance - 1],
+            recv_sem=self.recv_sems.at[distance - 1],
+            device_id={"seq": other},
+            device_id_type=MESH,
+        )
+
+    def own(self):
+        return pltpu.make_async_copy(
+            self.source.at[self.me], self.target.at[self.me], self.own_sem.at[0]
+        )
+
+    def start(self, others=0):
+        self.greet(others)
+        for distance in range(1, self.count):
+            self.copy(distance).start()
+        self.own().start()
+
+    def finish(self):
+        for distance in range(1, self.count):
+            self.copy(distance).wait()
+        self.own().wait()
+
+
+def trade_scratch(count):
+    dma = pltpu.SemaphoreType.DMA
+    return [dma((count - 1,)), dma((count - 1,)), dma((1,))]
+
+
 def segment_at(places, ends_ref):
     total = jnp.zeros(places.shape, jnp.int32)
     for doc in range(ends_ref.shape[0]):
@@ -142,21 +192,30 @@
         running = still
 
 
-def forward_kernel(
-    heads, ends_ref, lists_ref, admit_ref, q_ref, k_ref, v_ref, o_ref, lse_ref, token_segs, held
-):
+def unit_block(unit, half, parts, rows_total):
+    per = rows_total // parts // BLOCK // 2
+    part = unit // per
+    inside = unit - part * per
+    return part, inside, part * 2 * per + half * per + inside
+
+
+def forward_kernel(heads, half, ends_ref, lists_ref, admit_ref, q_ref, k_ref, v_ref, *rest):
+    o_ref, lse_ref, token_segs, *held = rest
+    held = held[0] if held else None
     scale = HD ** (-0.5)
     rows_total = q_ref.shape[0]
-    blocks = rows_total // BLOCK
+    units = o_ref.shape[0] * o_ref.shape[1] // BLOCK
+    first_unit = GLOB if half == 0 else 0
     chunk = LIST * BLOCK
     fill_segments(token_segs, ends_ref)
 
-    def store(block, wide, top, total):
+    def store(unit, wide, top, total):
+        part, inside, block = unit_block(unit, half, o_ref.shape[0], rows_total)
         out = head_fold(wide, heads)
         places = block * BLOCK + lax.broadcasted_iota(jnp.int32, out.shape, 0)
         out = jnp.where(places < ends_ref[ends_ref.shape[0] - 1], out, 0.0)
-        o_ref[block_at(block), :] = out.astype(BF16)
-        lse_ref[block] = jnp.broadcast_to(as_row(top + jnp.log(total)), lse_ref.shape[1:])
+        o_ref[part, block_at(inside), :] = out.astype(BF16)
+        lse_ref[unit] = jnp.broadcast_to(as_row(top + jnp.log(total)), lse_ref.shape[1:])
 
     def kept(block, key_segs):
         own = token_segs[block_at(block), :]
@@ -205,9 +264,11 @@
             own = slice(block * heads * BLOCK, (block + 1) * heads * BLOCK)
             store(block, wide[own], top[own], total[own])
 
-    global_blocks()
-
-    def listed_block(block):
+    if half == 0:
+        global_blocks()
+
+    def listed_block(unit):
+        _, _, block = unit_block(unit, half, o_ref.shape[0], rows_total)
         query_wide = head_spread(q_ref[block_at(block), :] * scale, heads)
         starts = [lists_ref[block * LIST + entry] for entry in range(LIST)]
         keeps = [admit_ref[block * LIST + entry] for entry in range(LIST)]
@@ -225,14 +286,14 @@
             totals.append(total)
             yield
         wide = dot_nn(jnp.concatenate(probs, axis=0), gathered(v_ref, starts))
-        store(block, wide, jnp.concatenate(tops, axis=0), jnp.concatenate(totals, axis=0))
+        store(unit, wide, jnp.concatenate(tops, axis=0), jnp.concatenate(totals, axis=0))
 
     def listed_group(group, _):
-        together([listed_block(GLOB + 4 * group + place) for place in range(4)])
+        together([listed_block(first_unit + 4 * group + place) for place in range(4)])
         return 0
 
-    lax.fori_loop(0, (blocks - GLOB) // 4, listed_group, 0)
-    together([listed_block(blocks - 1 - place) for place in range((blocks - GLOB) % 4)])
+    lax.fori_loop(0, (units - first_unit) // 4, listed_group, 0)
+    together([listed_block(units - 1 - place) for place in range((units - first_unit) % 4)])
 
 
 def backward_kernel(
@@ -243,9 +304,12 @@
     q_ref,
     k_ref,
     v_ref,
-    o_ref,
-    do_ref,
-    lse_ref,
+    o_first,
+    o_second,
+    do_first,
+    do_second,
+    lse_first,
+    lse_second,
     out_ref,
     token_segs,
     dk_ref,
@@ -266,15 +330,20 @@
 
     lax.fori_loop(0, blocks // 2, prepare, 0)
 
-    def query_side(block):
+    parts = o_first.shape[0]
+    halves_of = ((o_first, do_first, lse_first), (o_second, do_second, lse_second))
+
+    def query_side(unit, half):
+        o_ref, do_ref, lse_ref = halves_of[half]
+        part, inside, block = unit_block(unit, half, parts, rows_total)
         query_wide = head_spread(q_ref[block_at(block), :] * scale, heads)
-        grad_rows = do_ref[block_at(block), :]
+        grad_rows = do_ref[part, block_at(inside), :]
         grad_wide = head_spread(grad_rows, heads)
-        product = grad_rows.astype(F32) * o_ref[block_at(block), :].astype(F32)
+        product = grad_rows.astype(F32) * o_ref[part, block_at(inside), :].astype(F32)
         spread = head_spread(product.astype(BF16), heads)
         delta = dot_nt(jnp.ones((8, cols), BF16), spread)[0:1]
         seg_row = query_segments(block, heads, ends_ref)
-        return query_wide, grad_wide, delta, lse_ref[block, 0:1], seg_row
+        return query_wide, grad_wide, delta, lse_ref[unit, 0:1], seg_row
 
     def unit(starts, keeps, query_wide, grad_wide, delta, lse, seg_row, finish_query):
         keys = gathered(k_ref, starts)
@@ -306,7 +375,7 @@
         out_ref[block_at(block), 0:cols] = (head_fold(wide, heads) * scale).astype(BF16)
 
     def global_blocks():
-        sides = [query_side(block) for block in range(GLOB)]
+        sides = [query_side(block, 0) for block in range(GLOB)]
         side = [jnp.concatenate(both, axis=axis) for both, axis in zip(zip(*sides), (0, 0, 1, 1, 1))]
         dq_ref[...] = jnp.zeros_like(dq_ref)
 
@@ -323,17 +392,23 @@
 
     global_blocks()
 
-    def listed_block(block):
+    def listed_block(place, half):
+        _, _, block = unit_block(place, half, parts, rows_total)
         starts = [lists_ref[block * LIST + entry] for entry in range(LIST)]
         keeps = [admit_ref[block * LIST + entry] for entry in range(LIST)]
-        return unit(starts, keeps, *query_side(block), functools.partial(store_query, block))
-
-    def listed_group(group, _):
-        together([listed_block(GLOB + 4 * group + place) for place in range(4)])
-        return 0
-
-    lax.fori_loop(0, (blocks - GLOB) // 4, listed_group, 0)
-    together([listed_block(blocks - 1 - place) for place in range((blocks - GLOB) % 4)])
+        return unit(
+            starts, keeps, *query_side(place, half), functools.partial(store_query, block)
+        )
+
+    for half, first_unit in ((0, GLOB), (1, 0)):
+        units = blocks // 2
+
+        def listed_group(group, _):
+            together([listed_block(first_unit + 4 * group + place, half) for place in range(4)])
+            return 0
+
+        lax.fori_loop(0, (units - first_unit) // 4, listed_group, 0)
+        together([listed_block(units - 1 - place, half) for place in range((units - first_unit) % 4)])
 
     def finish(block, _):
         here = block_at(block)
@@ -352,26 +427,22 @@
     return pl.BlockSpec((rows, cols), lambda step: (0, index))
 
 
-def attention_forward(qkv, doc_ends, lists, admits, cols):
+def attention_forward(half, qkv, doc_ends, lists, admits, parts):
     rows = qkv.shape[0]
+    cols = qkv.shape[1] // 3
     heads = cols // HD
     blocks = rows // BLOCK
+    out = jax.ShapeDtypeStruct((parts, rows // parts // 2, cols), BF16)
+    lse = jax.ShapeDtypeStruct((blocks // 2, 8, heads * BLOCK), F32)
+    cube = lambda step: (0, 0, 0)
     return pl.pallas_call(
-        functools.partial(forward_kernel, heads),
+        functools.partial(forward_kernel, heads, half),
         grid=(1,),
         in_specs=[smem(), smem(), smem()] + [column(rows, cols, part) for part in range(3)],
-        out_specs=[
-            column(rows, cols, 0),
-            pl.BlockSpec((blocks, 8, heads * BLOCK), lambda step: (0, 0, 0)),
-        ],
-        out_shape=[
-            jax.ShapeDtypeStruct((rows, cols), BF16),
-            jax.ShapeDtypeStruct((blocks, 8, heads * BLOCK), F32),
-        ],
-        scratch_shapes=[
-            pltpu.VMEM((rows, 2 * BLOCK), jnp.int32),
-            pltpu.VMEM((GLOB * heads * BLOCK, rows), F32),
-        ],
+        out_specs=[pl.BlockSpec(out.shape, cube), pl.BlockSpec(lse.shape, cube)],
+        out_shape=[out, lse],
+        scratch_shapes=[pltpu.VMEM((rows, 2 * BLOCK), jnp.int32)]
+        + ([] if half else [pltpu.VMEM((GLOB * heads * BLOCK, rows), F32)]),
         compiler_params=pltpu.CompilerParams(vmem_limit_bytes=VMEM_LIMIT),
         cost_estimate=pl.CostEstimate(
             flops=rows * LIST * BLOCK * cols * heads * 5,
@@ -381,20 +452,17 @@
     )(doc_ends, lists, admits, qkv, qkv, qkv)
 
 
-def attention_backward(qkv, attended, attended_grad, lse, doc_ends, lists, admits, cols):
+def attention_backward(qkv, attended, attended_grad, lse, doc_ends, lists, admits):
     rows = qkv.shape[0]
+    cols = qkv.shape[1] // 3
     heads = cols // HD
-    blocks = rows // BLOCK
+    cube = lambda step: (0, 0, 0)
     return pl.pallas_call(
         functools.partial(backward_kernel, heads),
         grid=(1,),
         in_specs=[smem(), smem(), smem()]
         + [column(rows, cols, part) for part in range(3)]
-        + [
-            column(rows, cols, 0),
-            column(rows, cols, 0),
-            pl.BlockSpec((blocks, 8, heads * BLOCK), lambda step: (0, 0, 0)),
-        ],
+        + [pl.BlockSpec(part.shape, cube) for part in (*attended, *attended_grad, *lse)],
         out_specs=column(rows, 3 * cols, 0),
         out_shape=jax.ShapeDtypeStruct((rows, 3 * cols), BF16),
         scratch_shapes=[
@@ -409,7 +477,7 @@
             bytes_accessed=20 * rows * cols,
             transcendentals=0,
         ),
-    )(doc_ends, lists, admits, qkv, qkv, qkv, attended, attended_grad, lse)
+    )(doc_ends, lists, admits, qkv, qkv, qkv, *attended, *attended_grad, *lse)
 
 
 def row_stats(rows):
@@ -432,10 +500,11 @@
 
 def token_kernel(
     tile,
-    where_ref,
+    index,
+    ends_ref,
     att_ref,
     x_ref,
-    grad_ref,
+    cotangent_ref,
     out_own_ref,
     out_other_ref,
     up_own_ref,
@@ -448,11 +517,13 @@
     gain_ref,
     bias_ref,
     down_bias_ref,
+    trade_source,
     act_in,
     pre_in,
     second_in,
     hidden_in,
     grad_in,
+    att_in,
     output_ref,
     hidden_grad_ref,
     datt_ref,
@@ -461,16 +532,21 @@
     second_ref,
     hidden_low_ref,
     grad_low_ref,
+    att_rows_ref,
     sums_ref,
     unit_sums_ref,
+    trade_target,
     hidden,
     normed,
     inverse,
     ffn,
     second_grad,
+    grad_rows,
     up_slots,
     down_slots,
     slot_sems,
+    row_sems,
+    *trade_sems,
 ):
     step = pl.program_id(0)
     steps = pl.num_programs(0)
@@ -506,14 +582,25 @@
             begin(up_far_ref, down_far_ref, own_steps + near_steps)
 
     half = parts // 2
-    own_place = where_ref[0] * half
-    other_place = (1 - where_ref[0]) * half
+    me = lax.axis_index("seq")
+    place = lax.axis_index("mp")
+    own_place = place * half
+    other_place = (1 - place) * half
+    first_row = index * rows
+    row_copies = [
+        pltpu.make_async_copy(source.at[place, pl.ds(first_row, rows)], target, row_sems.at[which])
+        for which, (source, target) in enumerate(((x_ref, hidden), (cotangent_ref, grad_rows)))
+    ]
+    trade = Trade(trade_source, trade_target, *trade_sems)
     out_parts = [(own_place + part, out_own_ref, part) for part in range(half)]
     out_parts += [(other_place + part, out_other_ref, part) for part in range(half)]
 
     @pl.when(step == 0)
     def _():
+        for copy in row_copies:
+            copy.start()
         fetch(step)
+        trade.start()
 
     @pl.when(step + 1 < steps)
     def _():
@@ -521,16 +608,21 @@
 
     @pl.when(step == 0)
     def _():
+        for copy in row_copies:
+            copy.wait()
         for here in tiles:
-            total = x_ref[0, here, :]
+            total = hidden[here, :]
             for part, weight_ref, index in out_parts:
                 total = total + dot_nn(att_ref[part, here, :], weight_ref[index])
+            for part in range(parts):
+                cols = att_ref.shape[2]
+                att_rows_ref[here, part * cols : (part + 1) * cols] = att_ref[part, here, :]
             hidden[here, :] = total
             unit, scale = row_stats(total)
             normed[here, :] = unit
             inverse[here, :] = jnp.broadcast_to(scale, (tile, inverse.shape[1]))
             second_ref[here, :] = (unit * gain_ref[...] + bias_ref[...]).astype(BF16)
-            grad_low_ref[here, :] = grad_ref[0, here, :].astype(BF16)
+            grad_low_ref[here, :] = grad_rows[here, :].astype(BF16)
             ffn[here, :] = jnp.zeros((tile, ffn.shape[1]), F32)
             second_grad[here, :] = jnp.zeros((tile, ffn.shape[1]), F32)
 
@@ -559,9 +651,9 @@
         grad_sum = jnp.zeros((1, width), F32)
         gain_sum = jnp.zeros((1, width), F32)
         bias_sum = jnp.zeros((1, width), F32)
-        for index, here in enumerate(tiles):
+        for number, here in enumerate(tiles):
             output_ref[here, :] = (hidden[here, :] + ffn[here, :] + down_bias_ref[...]).astype(BF16)
-            grad = grad_ref[0, here, :]
+            grad = grad_rows[here, :]
             back = second_grad[here, :]
             unit = normed[here, :]
             scaled = back * gain_ref[...]
@@ -579,94 +671,111 @@
             bias_sum = bias_sum + jnp.sum(back, axis=0, keepdims=True)
             for part, weight_ref, piece in out_parts:
                 spread = dot_nt(low, weight_ref[piece])
-                places = where_ref[1] + index * tile + lax.broadcasted_iota(jnp.int32, spread.shape, 0)
-                datt_ref[part, here, :] = jnp.where(places < where_ref[2], spread, 0.0).astype(BF16)
+                places = me * 2 * rows + first_row + number * tile
+                places = places + lax.broadcasted_iota(jnp.int32, spread.shape, 0)
+                inside = places < ends_ref[ends_ref.shape[0] - 1]
+                datt_ref[part, here, :] = jnp.where(inside, spread, 0.0).astype(BF16)
         sums_ref[...] = jnp.concatenate(
             [grad_sum, gain_sum, bias_sum, jnp.zeros((5, width), F32)], axis=0
         )
+        trade.finish()
 
 
 def token_part(
-    index, where, att, layer_input, cotangent, outs, ups, downs, up_bias, gain, bias, down_bias, kept
+    index, doc_ends, att, layer_input, cotangent, outs, ups, downs, up_bias, gain, bias, down_bias, source, kept
 ):
     parts, rows, cols = att.shape
     width = layer_input.shape[2]
     units = up_bias.shape[1]
     chunk = min(512, units // 4)
     whole = 2 * rows
-    shapes = [(whole, units), (whole, units), (whole, width), (whole, width), (whole, width)]
+    shapes = [(whole, units)] * 2 + [(whole, width)] * 4
     if kept is None:
         kept = [jnp.zeros((8, 128), BF16)] * len(shapes)
         aliases = {}
     else:
-        aliases = {16 + place: 3 + place for place in range(len(shapes))}
-    half = lambda step, where_ref: (index, 0)
-    fixed = lambda step, where_ref: (0, 0)
+        aliases = {17 + place: 3 + place for place in range(len(shapes))}
+    half = lambda step: (index, 0)
+    fixed = lambda step: (0, 0)
     any_spec = pl.BlockSpec(memory_space=pl.ANY)
-    rows_spec = pl.BlockSpec((1, rows, width), lambda step, where_ref: (where_ref[0], index, 0))
-    cube = lambda step, where_ref: (0, 0, 0)
+    cube = lambda step: (0, 0, 0)
     vector = pl.BlockSpec((1, width), fixed)
     return pl.pallas_call(
-        functools.partial(token_kernel, min(256, rows)),
-        grid_spec=pltpu.PrefetchScalarGridSpec(
-            num_scalar_prefetch=1,
-            grid=(units // chunk,),
-            in_specs=[
-                pl.BlockSpec((parts, rows, cols), cube),
-                rows_spec,
-                rows_spec,
-                pl.BlockSpec((parts // 2, cols, width), cube),
-                pl.BlockSpec((parts // 2, cols, width), cube),
-            ]
-            + [any_spec] * 6
-            + [
-                pl.BlockSpec((1, chunk), lambda step, where_ref: (0, step)),
-                vector,
-                vector,
-                vector,
-            ]
-            + [any_spec] * len(shapes),
-            out_specs=[
-                pl.BlockSpec((rows, width), fixed),
-                pl.BlockSpec((rows, width), fixed),
-                pl.BlockSpec((parts, rows, cols), cube),
-                pl.BlockSpec((rows, chunk), lambda step, where_ref: (index, step)),
-                pl.BlockSpec((rows, chunk), lambda step, where_ref: (index, step)),
-                pl.BlockSpec((rows, width), half),
-                pl.BlockSpec((rows, width), half),
-                pl.BlockSpec((rows, width), half),
-                pl.BlockSpec((8, width), fixed),
-                pl.BlockSpec((8, chunk), lambda step, where_ref: (0, step)),
-            ],
-            scratch_shapes=[
-                pltpu.VMEM((rows, width), F32),
-                pltpu.VMEM((rows, width), F32),
-                pltpu.VMEM((rows, 128), F32),
-                pltpu.VMEM((rows, width), F32),
-                pltpu.VMEM((rows, width), F32),
-                pltpu.VMEM((2, width, chunk), BF16),
-                pltpu.VMEM((2, chunk, width), BF16),
-                pltpu.SemaphoreType.DMA((2, 2)),
-            ],
-        ),
+        functools.partial(token_kernel, min(256, rows), index),
+        grid=(units // chunk,),
+        in_specs=[
+            smem(),
+            pl.BlockSpec((parts, rows, cols), cube),
+            any_spec,
+            any_spec,
+            pl.BlockSpec((parts // 2, cols, width), cube),
+            pl.BlockSpec((parts // 2, cols, width), cube),
+        ]
+        + [any_spec] * 6
+        + [pl.BlockSpec((1, chunk), lambda step: (0, step)), vector, vector, vector]
+        + [any_spec] * (1 + len(shapes)),
+        out_specs=[
+            pl.BlockSpec((rows, width), fixed),
+            pl.BlockSpec((rows, width), fixed),
+            pl.BlockSpec((parts, rows, cols), cube),
+            pl.BlockSpec((rows, chunk), lambda step: (index, step)),
+            pl.BlockSpec((rows, chunk), lambda step: (index, step)),
+            pl.BlockSpec((rows, width), half),
+            pl.BlockSpec((rows, width), half),
+            pl.BlockSpec((rows, width), half),
+            pl.BlockSpec((rows, width), half),
+            pl.BlockSpec((8, width), fixed),
+            pl.BlockSpec((8, chunk), lambda step: (0, step)),
+            any_spec,
+        ],
+        scratch_shapes=[
+            pltpu.VMEM((rows, width), F32),
+            pltpu.VMEM((rows, width), F32),
+            pltpu.VMEM((rows, 128), F32),
+            pltpu.VMEM((rows, width), F32),
+            pltpu.VMEM((rows, width), F32),
+            pltpu.VMEM((rows, width), F32),
+            pltpu.VMEM((2, width, chunk), BF16),
+            pltpu.VMEM((2, chunk, width), BF16),
+            pltpu.SemaphoreType.DMA((2, 2)),
+            pltpu.SemaphoreType.DMA((2,)),
+        ]
+        + trade_scratch(parts),
         out_shape=[
             jax.ShapeDtypeStruct((rows, width), BF16),
             jax.ShapeDtypeStruct((rows, width), F32),
             jax.ShapeDtypeStruct((parts, rows, cols), BF16),
         ]
         + [jax.ShapeDtypeStruct(shape, BF16) for shape in shapes]
-        + [jax.ShapeDtypeStruct((8, width), F32), jax.ShapeDtypeStruct((8, units), F32)],
+        + [
+            jax.ShapeDtypeStruct((8, width), F32),
+            jax.ShapeDtypeStruct((8, units), F32),
+            jax.ShapeDtypeStruct((parts, rows, cols), BF16),
+        ],
         input_output_aliases=aliases,
-        compiler_params=pltpu.CompilerParams(vmem_limit_bytes=VMEM_LIMIT),
+        compiler_params=pltpu.CompilerParams(
+            collective_id=5 + index, has_side_effects=True, vmem_limit_bytes=VMEM_LIMIT
+        ),
         cost_estimate=pl.CostEstimate(
             flops=rows * width * (8 * units + 4 * width),
             bytes_accessed=8 * units * width,
             transcendentals=0,
         ),
-    )(where, att, layer_input, cotangent, *outs, *ups, *downs, up_bias, gain, bias, down_bias, *kept)
-
-
-MESH = pl.DeviceIdType.MESH
+    )(
+        doc_ends,
+        att,
+        layer_input,
+        cotangent,
+        *outs,
+        *ups,
+        *downs,
+        up_bias,
+        gain,
+        bias,
+        down_bias,
+        source,
+        *kept,
+    )
 
 
 def greet(me, count, partner=None):
@@ -1075,6 +1184,173 @@
     )(parts, weight, layer_input, hidden_grad, gain)
 
 
+def weight_grad_kernel(
+    tile,
+    second_ref,
+    grad_ref,
+    hidden_ref,
+    pre_ref,
+    act_ref,
+    att_ref,
+    trade_source,
+    up_own,
+    up_near,
+    down_own,
+    down_near,
+    out_own,
+    out_near,
+    trade_target,
+    turned,
+    slots,
+    sending,
+    received,
+    slot_sems,
+    send_sems,
+    recv_sems,
+    out_sems,
+    *trade_sems,
+):
+    rows, width = second_ref.shape
+    units = pre_ref.shape[1]
+    me = lax.axis_index("batch")
+    place = lax.axis_index("mp")
+    parity = me % 2
+    mate = me + 1 - 2 * parity
+    barrier = pltpu.get_barrier_semaphore()
+    pl.semaphore_signal(barrier, inc=1, device_id={"batch": mate}, device_id_type=MESH)
+    trade = Trade(trade_source, trade_target, *trade_sems)
+    trade.start(1)
+
+    piece = units // 4
+    head_piece = width // 4
+    jobs = []
+    for matrix, source, own, near in ((0, pre_ref, up_own, up_near), (1, act_ref, down_own, down_near)):
+        for start in range(0, piece, tile):
+            jobs.append(
+                (matrix, source, tile, (1 - parity) * piece + start, parity * piece + start, own, start)
+            )
+        for start in range(0, piece, tile):
+            jobs.append((matrix, source, tile, 3 * piece + start, 2 * piece + start, near, start))
+    for side, target in ((place, out_own), (1 - place, out_near)):
+        first = 2 * side * head_piece
+        jobs.append(
+            (
+                2,
+                att_ref,
+                head_piece,
+                first + (1 - parity) * head_piece,
+                first + parity * head_piece,
+                target,
+                0,
+            )
+        )
+    count = len(jobs)
+    order = [(job, 3) for job in range(count)] + [(job, 4) for job in range(count)]
+
+    def fetch(index):
+        job, which = order[index]
+        _, source, size, *_ = jobs[job]
+        start = jobs[job][which]
+        return pltpu.make_async_copy(
+            source.at[:, pl.ds(pl.multiple_of(start, 128), size)],
+            slots.at[index % 2, :, pl.ds(0, size)],
+            slot_sems.at[index % 2],
+        )
+
+    def exchange(job):
+        size = jobs[job][2]
+        return pltpu.make_async_remote_copy(
+            src_ref=sending.at[job, :, pl.ds(0, size)],
+            dst_ref=received.at[job, :, pl.ds(0, size)],
+            send_sem=send_sems.at[job],
+            recv_sem=recv_sems.at[job],
+            device_id={"batch": mate},
+            device_id_type=MESH,
+        )
+
+    def put(job):
+        size, target, start = jobs[job][2], jobs[job][5], jobs[job][6]
+        return pltpu.make_async_copy(
+            received.at[job, :, pl.ds(0, size)], target.at[:, pl.ds(start, size)], out_sems.at[job]
+        )
+
+    fetch(0).start()
+    block = min(256, width)
+    for matrix, source in enumerate((second_ref, grad_ref, hidden_ref)):
+
+        def turn(index, _):
+            here = pl.ds(pl.multiple_of(index * 128, 128), 128)
+            turned[matrix, :, here] = source[here, :].T
+            return 0
+
+        lax.fori_loop(0, rows // 128, turn, 0)
+
+    for index, (job, which) in enumerate(order):
+        matrix, _, size, *_ = jobs[job]
+        fetch(index).wait()
+        if index + 1 < len(order):
+            fetch(index + 1).start()
+        if which == 4:
+            exchange(job).wait_recv()
+
+        def multiply(part, _):
+            here = pl.ds(pl.multiple_of(part * block, block), block)
+            total = dot_nn(turned[matrix, here, :], slots[index % 2, :, 0:size])
+            if which == 3:
+                sending[job, here, 0:size] = total.astype(BF16)
+            else:
+                total = total + received[job, here, 0:size].astype(F32)
+                received[job, here, 0:size] = total.astype(BF16)
+            return 0
+
+        lax.fori_loop(0, width // block, multiply, 0)
+        if which == 3:
+            exchange(job).start()
+        else:
+            put(job).start()
+    for job in range(count):
+        exchange(job).wait_send()
+        put(job).wait()
+    trade.finish()
+
+
+def weight_grads(second_low, grad_low, hidden_low, pre_grad, activated, attended, source):
+    rows, width = second_low.shape
+    units = pre_grad.shape[1]
+    piece = units // 4
+    tile = min(512, piece)
+    jobs = 4 * (piece // tile) + 2
+    any_spec = pl.BlockSpec(memory_space=pl.ANY)
+    vmem = pl.BlockSpec(memory_space=pltpu.VMEM)
+    dma = pltpu.SemaphoreType.DMA
+    shapes = [(width, piece)] * 4 + [(width, width // 4)] * 2
+    return pl.pallas_call(
+        functools.partial(weight_grad_kernel, tile),
+        in_specs=[vmem] * 3 + [any_spec] * 4,
+        out_specs=[any_spec] * 7,
+        out_shape=[jax.ShapeDtypeStruct(shape, BF16) for shape in shapes + [source.shape]],
+        scratch_shapes=[
+            pltpu.VMEM((3, width, rows), BF16),
+            pltpu.VMEM((2, rows, tile), BF16),
+            pltpu.VMEM((jobs, width, tile), BF16),
+            pltpu.VMEM((jobs, width, tile), BF16),
+            dma((2,)),
+            dma((jobs,)),
+            dma((jobs,)),
+            dma((jobs,)),
+        ]
+        + trade_scratch(source.shape[0]),
+        compiler_params=pltpu.CompilerParams(
+            collective_id=3, has_side_effects=True, vmem_limit_bytes=VMEM_LIMIT
+        ),
+        cost_estimate=pl.CostEstimate(
+            flops=2 * rows * width * (2 * units + width),
+            bytes_accessed=4 * rows * units,
+            transcendentals=0,
+        ),
+    )(second_low, grad_low, hidden_low, pre_grad, activated, attended, source)
+
+
 def swap(value, axis, distance=1):
     size = lax.axis_size(axis)
     return lax.ppermute(value, axis, [(j, j ^ distance) for j in range(size)])
@@ -1090,6 +1366,23 @@
 
 def halves(value):
     return jnp.split(value, 2, axis=1)
+
+
+def trade_pieces(value):
+    place, count = lax.axis_index("seq"), lax.axis_size("seq")
+    pieces = [pick(value, place, count)]
+    for distance in range(1, count):
+        pairs = [(j, (j + distance) % count) for j in range(count)]
+        pieces.append(
+            lax.ppermute(pick(value, (place + distance) % count, count), "seq", pairs)
+        )
+    return pieces
+
+
+def place_pieces(pieces):
+    place, count = lax.axis_index("seq"), len(pieces)
+    whole = jnp.concatenate(pieces, axis=0)
+    return jnp.roll(whole[::-1], place + 1, axis=0)
 
 
 def levels_of(axis):
@@ -1138,21 +1431,6 @@
     low = jnp.where(side == 0, value, other)
     high = jnp.where(side == 0, other, value)
     return jnp.concatenate([low, high], axis=axis)
-
-
-def sum_cores(own, near, far, axis):
-    return halve(own, 1, axis), narrow_add(near, swap(far, "batch"))
-
-
-def sum_chips(own, near, axis):
-    for distance in levels_of("batch")[1:]:
-        own = halve(own, distance, axis)
-        near = halve(near, distance, axis)
-    return own, near
-
-
-def scatter_rows_of(own, axis):
-    return lax.psum_scatter(own, "seq", scatter_dimension=1 - axis, tiled=True)
 
 
 def spread_batch(value, axis):
@@ -1246,25 +1524,23 @@
     )
     up_far, bias_far = swap(up_near, "batch"), swap(bias_near, "batch")
     down_near = fetch_near(down_cut, 0)
-    attended, lse = attention_forward(qkv, doc_ends, lists, admits, cols)
-    attended, up_far, down_near, bias_far = lax.optimization_barrier(
-        (attended, up_far, down_near, bias_far)
+    attended_first, lse_first = attention_forward(0, qkv, doc_ends, lists, admits, seq_count)
+    att_pieces = trade_pieces(attended_first)
+    attended_second, lse_second = attention_forward(1, qkv, doc_ends, lists, admits, seq_count)
+    *att_pieces, attended_second = lax.optimization_barrier((*att_pieces, attended_second))
+    att_first = place_pieces(att_pieces)
+    att_first, up_far, down_near, bias_far = lax.optimization_barrier(
+        (att_first, up_far, down_near, bias_far)
     )
     down_far = swap(down_near, "batch")
     bias_full = jnp.concatenate([up_bias, bias_near, bias_far])[None]
-    half_rows = local_rows // 2
-    attended_halves = [
-        all_to_all(part) for part in halves(attended.reshape(seq_count, local_rows, cols))
-    ]
     outs = [part.reshape(seq_count // 2, cols, width) for part in (out_weight, out_other)]
     kept, results = None, []
-    for index, att in enumerate(attended_halves):
-        where = jnp.stack(
-            [mp_index, seq_index * local_rows + index * half_rows, doc_ends[-1]]
-        ).astype(jnp.int32)
+    att, source = att_first, attended_second
+    for index in range(2):
         result = token_part(
             index,
-            where,
+            doc_ends,
             att,
             layer_input,
             cotangent,
@@ -1275,30 +1551,20 @@
             second_gain[None],
             second_bias[None],
             down_bias[None],
+            source,
             kept,
         )
-        kept = result[3:8]
-        results.append(result[:3] + result[8:])
-    activated, pre_grad, second_low, hidden_low, grad_low = kept
+        kept = result[3:9]
+        results.append(result[:3] + result[9:])
+        att, source = result[11], result[2]
+    grad_first = att
+    activated, pre_grad, second_low, hidden_low, grad_low, attended_low = kept
     sums = results[0][3][:3] + results[1][3][:3]
     unit_sums = results[0][4][0] + results[1][4][0]
     bias_sums = [unit_sums[:units], unit_sums[units : units * 3 // 2], unit_sums[units * 3 // 2 :]]
     layer_output = both_sequences([result[0] for result in results])
-    grad_all = jnp.concatenate([all_to_all(result[2]) for result in results], axis=1)
-    grad_all = grad_all.reshape(rows_total, cols)
-
-    down_sum = dot_tn(activated, grad_low).astype(BF16)
-    up_sum = dot_tn(second_low, pre_grad).astype(BF16)
-    attended_low = jnp.concatenate(attended_halves, axis=1)
-    out_sum = jnp.einsum(
-        "zrc,rd->zcd", attended_low, hidden_low, preferred_element_type=F32
-    ).astype(BF16).reshape(width, width)
-    cuts = [units, units * 3 // 2]
-    down_sum = sum_cores(*jnp.split(down_sum, cuts, axis=0), 0)
-    up_sum = sum_cores(*jnp.split(up_sum, cuts, axis=1), 1)
-    out_theirs = pick(out_sum, 1 - mp_index, 2)
-    out_sum = sum_cores(
-        pick(out_sum, mp_index, 2), pick(out_theirs, parity, 2), pick(out_theirs, 1 - parity, 2), 0
+    up_own, up_near, down_own, down_near, out_own, out_near, grad_second = weight_grads(
+        second_low, grad_low, hidden_low, pre_grad, activated, attended_low, source
     )
     bias_other = jnp.where(
         parity == 0,
@@ -1311,31 +1577,40 @@
         jnp.concatenate([bias_other, bias_sums[0]]),
     )
     early = sum_everywhere(jnp.concatenate([sums.reshape(-1), bias_all]))
-    grad_all, down_sum, up_sum, out_sum = lax.optimization_barrier(
-        (grad_all, down_sum, up_sum, out_sum)
-    )
-    down_sum, up_sum, out_sum = sum_chips(*down_sum, 0), sum_chips(*up_sum, 1), sum_chips(*out_sum, 0)
+    levels = levels_of("batch")
+    for distance in levels[1:]:
+        up_own, up_near = halve(up_own, distance, 1), halve(up_near, distance, 1)
+        out_own, out_near = halve(out_own, distance, 1), halve(out_near, distance, 1)
+    down_own = narrow_add(down_own, swap(down_near, "mp"))
     qkv_low_grad = attention_backward(
-        qkv, attended, grad_all, lse, doc_ends, lists, admits, cols
+        qkv,
+        (attended_first, attended_second),
+        (grad_first, grad_second),
+        (lse_first, lse_second),
+        doc_ends,
+        lists,
+        admits,
     )
     qkv_sum = dot_tn(first_all, qkv_low_grad).astype(BF16)
     qkv_sum = qkv_sum.reshape(seq_count, -1, 3 * cols).transpose(1, 0, 2)
-    levels = levels_of("batch")
-    sums_now = [down_sum, up_sum, out_sum]
-    qkv_low_grad, qkv_sum, sums_now = lax.optimization_barrier((qkv_low_grad, qkv_sum, sums_now))
-    near_sums = [swap(near, "mp") for _, near in sums_now]
+    qkv_low_grad, qkv_sum, up_own, up_near, down_own, out_own, out_near = lax.optimization_barrier(
+        (qkv_low_grad, qkv_sum, up_own, up_near, down_own, out_own, out_near)
+    )
+    up_own = narrow_add(up_own, swap(up_near, "mp"))
+    out_own = narrow_add(out_own, swap(out_near, "mp"))
+    for distance in levels[1:]:
+        down_own = halve(down_own, distance, 1)
     qkv_part = halve(qkv_sum, levels[0], 0)
     parts = qkv_low_grad.reshape(seq_count, local_rows, 3 * cols)
     input_first, first_sums = return_part(
         0, parts, qkv_own, layer_input, results[0][1], first_gain[None]
     )
-    input_first, near_sums, qkv_part = lax.optimization_barrier((input_first, near_sums, qkv_part))
-    own_sums = [narrow_add(own, near) for (own, _), near in zip(sums_now, near_sums)]
-    second_grad, input_first, own_sums = lax.optimization_barrier(
-        (results[1][1], input_first, own_sums)
-    )
-    down_grad, up_grad, out_grad = [
-        scatter_rows_of(own, axis) for own, axis in zip(own_sums, (0, 1, 0))
+    second_grad, input_first, up_own, down_own, out_own, qkv_part = lax.optimization_barrier(
+        (results[1][1], input_first, up_own, down_own, out_own, qkv_part)
+    )
+    up_grad, down_grad, out_grad = [
+        lax.psum_scatter(own, "seq", scatter_dimension=0, tiled=True)
+        for own in (up_own, down_own, out_own)
     ]
     for distance in levels[1:]:
         qkv_part = halve(qkv_part, distance, 0)
@@ -1351,9 +1626,9 @@
     qkv_part = pick(qkv_part, mp_index, 2)
     qkv_part = qkv_part.reshape(seq_count // 2, -1, 3, cols).transpose(1, 2, 0, 3)
     qkv_grad = spread_batch(qkv_part.reshape(-1, 3, half_cols), 0)
-    down_grad = spread_batch(down_grad, 0)
-    up_grad = spread_batch(up_grad, 1)
-    out_grad = spread_batch(out_grad, 0)
+    up_grad, down_grad, out_grad = [
+        spread_batch(grad, 1) for grad in (up_grad, down_grad, out_grad)
+    ]
     input_grad = both_sequences([input_first, input_second])
     up_bias_grad = lax.dynamic_slice_in_dim(early, 3 * width + mp_index * units, units)
     return (
@@ -1362,12 +1637,12 @@
         late[0],
         late[1],
         qkv_grad,
-        out_grad,
+        out_grad.T,
         early[width : 2 * width],
         early[2 * width : 3 * width],
         up_grad,
         up_bias_grad,
-        down_grad,
+        down_grad.T,
         early[:width],
     )
 

time: 817 us -> 740 us (0.906)
  waiting for transfers between devices: 114 us -> 55.7 us
  Pallas kernels: 478 us -> 531 us
  matrix products: 38 us -> 11.2 us
  starting transfers between devices: 71 us -> 53.6 us
  other arithmetic: 51.1 us -> 36.2 us
  local copies, waits for them, and re-layouts: 42.3 us -> 29.9 us
    pallas_call x3 -> x5, Pallas kernels: 98.2 us -> 153 us  [the longest x2 72.3 us: token_part(): pl.pallas_call(functools.partial(token_kernel, min(256, rows), index), gr...]
    ppermute x50 -> x43, waiting for transfers between devices: 83.7 us -> 46.4 us  [swap(): return lax.ppermute(value, axis, [(j, j ^ distance) for j in range(size)])]
    dot_general x3 -> x1, matrix products: 35.6 us -> 11.2 us  [dot_tn(): lax.dot_general(left, right, (((0,), (0,)), ((), ())), preferred_element_...]
    all_to_all x5 -> x1, waiting for transfers between devices: 30 us -> 5.93 us  [all_to_all(): return lax.all_to_all(value, 'seq', 0, 0, tiled=True)]
    all_to_all x5 -> x1, starting transfers between devices: 22.3 us -> 3.46 us  [all_to_all(): return lax.all_to_all(value, 'seq', 0, 0, tiled=True)]
    convert_element_type x16 -> x10, other arithmetic: 32.7 us -> 17.6 us  [narrow_add(): return (mine.astype(F32) + received.astype(F32)).astype(BF16)]
    ppermute x50 -> x43, starting transfers between devices: 48.4 us -> 45.7 us  [swap(): return lax.ppermute(value, axis, [(j, j ^ distance) for j in range(size)])]
  transfers between devices with their start and end apart: 58 -> 50, of which waited for: 16 -> 13; matrix products, arithmetic and copies ran while one was open for 13% -> 8% of each run, Pallas kernels for 55% -> 57%
where the time goes in v3:
time: 740 us; the launch traced here: 733 us
  Pallas kernels  531 us (72%)
  waiting for transfers between devices  55.7 us (8%)
  starting transfers between devices  53.6 us (7%)
  other arithmetic  36.2 us (5%)
  local copies, waits for them, and re-layouts  29.9 us (4%)
  between operations  15 us (2%)
  matrix products  11.2 us (2%)
    pallas_call x2, Pallas kernels, return_part(): pl.pallas_call(functools.partial(return_kernel, count, chunks, 2, index *...  178 us
    pallas_call x1, Pallas kernels, gather_project(): pl.pallas_call(functools.partial(gather_kernel, count, chunks, half_cols)...  142 us
    pallas_call x2, Pallas kernels, token_part(): pl.pallas_call(functools.partial(token_kernel, min(256, rows), index), gr...  72.3 us
    pallas_call x1, Pallas kernels, attention_backward(): pl.pallas_call(functools.partial(backward_kernel, heads), grid=(1,), in_s...  46.8 us
    ppermute x43, waiting for transfers between devices, swap(): return lax.ppermute(value, axis, [(j, j ^ distance) for j in range(size)])  46.4 us
    ppermute x43, starting transfers between devices, swap(): return lax.ppermute(value, axis, [(j, j ^ distance) for j in range(size)])  45.7 us
    pallas_call x1, Pallas kernels, weight_grads(): pl.pallas_call(functools.partial(weight_grad_kernel, tile), in_specs=[vme...  43.5 us
    pallas_call x2, Pallas kernels, attention_forward(): pl.pallas_call(functools.partial(forward_kernel, heads, half), grid=(1,),...  36.8 us
  transfers between devices with their start and end apart: 50, of which 13 were waited for; matrix products, arithmetic and copies ran while one was open for 8% of the time, Pallas kernels for 57%

profile of v3, /device:TPU:0, one launch (start us, length us, event | category | flops | bytes accessed | tf_op | source)
XLA Modules:
  0.0 733.0 jit_solution(425892588738318659)
XLA Ops:
  8.7 5.0 collective-permute-start.5
  23.9 141.5 %shard_map.229 = (bf16[4,1024,1024]{2,1,0:T(8,128)(2,1)}, bf16[4,1024,768]{2,1,0:T(8,128)(2,1)}, bf16[1024,768]{1,0:T(8,128)(2,1)}) custom-call(f32[2,1024,1024]{2,1,0:T(8,128)} %x_ref.9, f32[1,1024]{1,0:T(1,128)} %bitcast.64, f32[1,1024]{1,0:T(1,128)} %bitcast.57, bf16[1024,768]{1,0:T(8,128)(2,1)} %copy.58.weight_ref), custom_call_target="tpu_custom_call" | custom-call | flops 149999992832 | bytes 1 | tf_op jit(solution)/shard_map/pallas_call | solution.py:987
  170.9 3.1 constant_dynamic-slice_fusion.8
  174.7 22.2 %shard_map.230 = (bf16[4,512,256]{2,1,0:T(8,128)(2,1)}, f32[32,8,256]{2,1,0:T(8,128)}) custom-call(s32[4]{0:T(128)} %bitcast.79, s32[512]{0:T(512)} %min.12.lists_ref, s32[512]{0:T(512)} %reshape.153.admit_ref, bf16[4096,768]{1,0:T(8,128)(2,1)} %bitcast.68, bf16[4096,768]{1,0:T(8,128)(2,1)} %bitcast.69, bf16[4096,768]{1,0:T(8,128)(2,1)} %bitcast.70), custom_call_target="tpu_custom_call" | custom-call | flops 10737418240 | bytes 8388608 | tf_op jit(solution)/shard_map/pallas_call | solution.py:438
  198.2 3.2 collective-permute-start.7
  202.5 14.6 %shard_map.231 = (bf16[4,512,256]{2,1,0:T(8,128)(2,1)}, f32[32,8,256]{2,1,0:T(8,128)}) custom-call(s32[4]{0:T(128)} %bitcast.80, s32[512]{0:T(512)} %min.12.lists_ref, s32[512]{0:T(512)} %reshape.153.admit_ref, bf16[4096,768]{1,0:T(8,128)(2,1)} %bitcast.71, bf16[4096,768]{1,0:T(8,128)(2,1)} %bitcast.72, bf16[4096,768]{1,0:T(8,128)(2,1)} %bitcast.73), custom_call_target="tpu_custom_call" | custom-call | flops 10737418240 | bytes 8388608 | tf_op jit(solution)/shard_map/pallas_call | solution.py:438
  222.1 3.7 collective-permute-done.12.down_far_ref
  227.1 37.5 %shard_map.232 = (bf16[512,1024]{1,0:T(8,128)(2,1)}, f32[512,1024]{1,0:T(8,128)}, bf16[4,512,256]{2,1,0:T(8,128)(2,1)}, bf16[1024,4096]{1,0:T(8,128)(2,1)}, bf16...) custom-call(s32[4]{0:T(128)} %bitcast.81, ...), custom_call_target="tpu_custom_call" | custom-call | flops 19327352832 | bytes 33554432 | tf_op jit(solution)/shard_map/pallas_call | solution.py:703
  264.6 34.8 %shard_map.233 = (bf16[512,1024]{1,0:T(8,128)(2,1)}, f32[512,1024]{1,0:T(8,128)}, bf16[4,512,256]{2,1,0:T(8,128)(2,1)}, bf16[1024,4096]{1,0:T(8,128)(2,1)}, bf16...) custom-call(s32[4]{0:T(128)} %bitcast.82, ...), custom_call_target="tpu_custom_call", output_to_operand_aliasing={{3}: (17, {}), {4}: (18, {}), {5}: (19, {}), {6}: (20, {}),... | custom-call | flops 19327352832 | bytes 33554432 | tf_op jit(solution)/shard_map/pallas_call | solution.py:703
  299.4 43.5 %shard_map.235 = (bf16[1024,1024]{1,0:T(8,128)(2,1)}, bf16[1024,1024]{1,0:T(8,128)(2,1)}, bf16[1024,1024]{1,0:T(8,128)(2,1)}, bf16[1024,1024]{1,0:T(8,128)(2,1)}...) custom-call(bf16[1024,1024]{1,0:T(8,128)(2,1)} %get-tuple-element.117.second_ref, ...), custom_call_target="tpu_custom_call" | custom-call | flops 19327352832 | bytes 16777216 | tf_op jit(solution)/shard_map/pallas_call | solution.py:1327
  353.1 46.8 %shard_map.236 = bf16[4096,768]{1,0:T(8,128)(2,1)} custom-call(s32[4]{0:T(128)} %bitcast.83, s32[512]{0:T(512)} %min.12.lists_ref, s32[512]{0:T(512)} %reshape.153.admit_ref, bf16[4096,768]{1,0:T(8,128)(2,1)} %bitcast.74, bf16[4096,768]{1,0:T(8,128)(2,1)} %bitcast.75, bf16[4096,768]{1,0:T(8,128)(2,1)} %bitcast.76, ...), custom_call_target="tpu_custom_call" | custom-call | flops 32212254720 | bytes 20971520 | tf_op jit(solution)/shard_map/pallas_call | solution.py:460
  399.9 11.2 %convolution_convert_fusion = bf16[1024,768]{1,0:T(8,128)(2,1)S(1)} fusion(bf16[4096,1024]{1,0:T(8,128)(2,1)} %bitcast.67, bf16[4096,768]{1,0:T(8,128)(2,1)} %shard_map.236), kind=kOutput, calls=%fused_computation.9 | convolution fusion | flops 6443237376 | bytes 16252928 | tf_op jit(solution)/shard_map/dot_general | solution.py:172
  426.0 72.9 %shard_map.237 = (bf16[512,1024]{1,0:T(8,128)(2,1)}, f32[8,1024]{1,0:T(8,128)}) custom-call(bf16[4,1024,768]{2,1,0:T(8,128)(2,1)} %bitcast.77, bf16[1024,768]{1,0:T(8,128)(2,1)} %get-tuple-element.135.weight_ref, f32[2,1024,1024]{2,1,0:T(8,128)} %x_ref.9, f32[512,1024]{1,0:T(8,128)} %get-tuple-element.136.hidden_grad_ref, f32[1,1024]{1,0:T(1,128)} %bitcast.65), custom_call_target="tpu_custom_call" | custom-call | flops 80000000000 | bytes 1 | tf_op jit(solution)/shard_map/pallas_call | solution.py:1157
  511.0 3.3 collective-permute-done.38
  514.3 3.6 collective-permute-start.39
  524.0 104.7 %shard_map.238 = (bf16[512,1024]{1,0:T(8,128)(2,1)}, f32[8,1024]{1,0:T(8,128)}) custom-call(bf16[4,1024,768]{2,1,0:T(8,128)(2,1)} %bitcast.78, bf16[1024,768]{1,0:T(8,128)(2,1)} %get-tuple-element.135.weight_ref, f32[2,1024,1024]{2,1,0:T(8,128)} %x_ref.9, f32[512,1024]{1,0:T(8,128)} %get-tuple-element.145.hidden_grad_ref, f32[1,1024]{1,0:T(1,128)} %bitcast.66), custom_call_target="tpu_custom_call" | custom-call | flops 80000000000 | bytes 1 | tf_op jit(solution)/shard_map/pallas_call | solution.py:1157
  634.3 3.6 collective-permute-start.29
  649.2 6.4 shard_map.234
  662.6 3.9 collective-permute-done.44
  666.7 23.7 %collective-permute-done.32 = bf16[64,4,768]{2,0,1:T(8,128)(2,1)S(1)} collective-permute-done((bf16[64,4,768]{2,0,1:T(8,128)(2,1)S(1)}, bf16[64,4,768]{2,0,1:T(8,128)(2,1)S(1)}, u32[]{:S(2)}, u32[]{:S(2)}) %collective-permute-start.32) | collective-permute-done | bytes 393248 | tf_op jit(solution)/shard_map/ppermute | solution.py:1356
  691.2 3.5 all-to-all-start
  697.6 5.9 all-to-all-done
  705.6 4.1 collective-permute-done.33
  717.0 6.6 shard_map.239
  (228 shorter events, 108.9 us)
Async XLA Ops:
  7.2 638.0 %reduce-scatter.8.cloned.1.call-start = ((), (), s32[]{:S(2)}) async-start(), calls=%async_computation.6 | async-start | bytes 327680 | tf_op jit(solution)/shard_map/reduce_scatter | solution.py:1612
  8.7 157.8 %collective-permute-start.5 = (s32[16,3]{0,1:T(4,128)}, s32[16,3]{0,1:T(4,128)}, u32[]{:S(2)}, u32[]{:S(2)}) collective-permute-start(s32[16,3]{0,1:T(4,128)} %bitcast.40.clone.2), channel_id=1, source_target_pairs={{0,24},{8,16},{16,8},{24,0},{1,25},{9,17},{17,9},{25,1},{2,26},{10... | collective-permute-start | bytes 584 | tf_op jit(solution)/shard_map/ppermute | solution.py:1356
  13.7 154.2 %collective-permute-start.3 = (s32[16,3]{0,1:T(4,128)}, s32[16,3]{0,1:T(4,128)}, u32[]{:S(2)}, u32[]{:S(2)}) collective-permute-start(s32[16,3]{0,1:T(4,128)} %bitcast.40.clone.2), channel_id=1, source_target_pairs={{0,8},{8,0},{16,24},{24,16},{1,9},{9,1},{17,25},{25,17},{2,10},{10... | collective-permute-start | bytes 584 | tf_op jit(solution)/shard_map/ppermute | solution.py:1356
  13.7 154.2 %collective-permute-start.4 = (s32[16,3]{0,1:T(4,128)}, s32[16,3]{0,1:T(4,128)}, u32[]{:S(2)}, u32[]{:S(2)}) collective-permute-start(s32[16,3]{0,1:T(4,128)} %bitcast.40.clone.2), channel_id=1, source_target_pairs={{0,16},{8,24},{16,0},{24,8},{1,17},{9,25},{17,1},{25,9},{2,18},{10... | collective-permute-start | bytes 584 | tf_op jit(solution)/shard_map/ppermute | solution.py:1356
  17.4 153.5 %collective-permute-start = (bf16[1024,1024]{1,0:T(8,128)(2,1)}, bf16[1024,1024]{1,0:T(8,128)(2,1)}, u32[]{:S(2)}, u32[]{:S(2)}) collective-permute-start(bf16[1024,1024]{1,0:T(8,128)(2,1)} %constant_dynamic-slice_fusion.14), channel_id=1, source_target_pairs={{0,1},{1,0},{2,3},{3,2},{4,5},{5,4},{6,7},{7,6},{8,9},{9,8},{10,11... | collective-permute-start | bytes 6291464 | tf_op jit(solution)/shard_map/ppermute | solution.py:1356
  19.1 151.8 %collective-permute-start.1 = (bf16[512,1024]{1,0:T(8,128)(2,1)}, bf16[512,1024]{1,0:T(8,128)(2,1)}, u32[]{:S(2)}, u32[]{:S(2)}) collective-permute-start(bf16[512,1024]{1,0:T(8,128)(2,1)} %param.20), channel_id=1, source_target_pairs={{0,1},{1,0},{2,3},{3,2},{4,5},{5,4},{6,7},{7,6},{8,9},{9,8},{10,11... | collective-permute-start | bytes 3145736 | tf_op jit(solution)/shard_map/ppermute | solution.py:1356
  174.0 47.3 %collective-permute-start.10 = (bf16[1024,1024]{1,0:T(8,128)(2,1)}, bf16[1024,1024]{1,0:T(8,128)(2,1)}, u32[]{:S(2)}, u32[]{:S(2)}) collective-permute-start(bf16[1024,1024]{1,0:T(8,128)(2,1)} %constant_dynamic-slice_fusion.8), channel_id=1, source_target_pairs={{0,1},{1,0},{2,3},{3,2},{4,5},{5,4},{6,7},{7,6},{8,9},{9,8},{10,11... | collective-permute-start | bytes 6291464 | tf_op jit(solution)/shard_map/ppermute | solution.py:1356
  344.0 67.1 %collective-permute-start.19 = (bf16[1024,128]{1,0:T(8,128)(2,1)S(1)}, bf16[1024,128]{1,0:T(8,128)(2,1)}, u32[]{:S(2)}, u32[]{:S(2)}) collective-permute-start(bf16[1024,128]{1,0:T(8,128)(2,1)S(1)} %constant_dynamic-slice_fusion.4), channel_id=1, source_target_pairs={{0,4},{2,6},{4,0},{6,2},{1,5},{3,7},{5,1},{7,3},{8,12},{10,14},{12... | collective-permute-start | bytes 786440 | tf_op jit(solution)/shard_map/ppermute | solution.py:1356
  346.6 65.8 %collective-permute-start.18 = (bf16[1024,128]{1,0:T(8,128)(2,1)S(1)}, bf16[1024,128]{1,0:T(8,128)(2,1)}, u32[]{:S(2)}, u32[]{:S(2)}) collective-permute-start(bf16[1024,128]{1,0:T(8,128)(2,1)S(1)} %constant_dynamic-slice_fusion.5), channel_id=1, source_target_pairs={{0,4},{2,6},{4,0},{6,2},{1,5},{3,7},{5,1},{7,3},{8,12},{10,14},{12... | collective-permute-start | bytes 786440 | tf_op jit(solution)/shard_map/ppermute | solution.py:1356
  347.2 70.6 %collective-permute-start.17 = (bf16[1024,1024]{1,0:T(8,128)(2,1)}, bf16[1024,1024]{1,0:T(8,128)(2,1)}, u32[]{:S(2)}, u32[]{:S(2)}) collective-permute-start(bf16[1024,1024]{1,0:T(8,128)(2,1)} %get-tuple-element.131), channel_id=1, source_target_pairs={{0,1},{1,0},{2,3},{3,2},{4,5},{5,4},{6,7},{7,6},{8,9},{9,8},{10,11... | collective-permute-start | bytes 6291464 | tf_op jit(solution)/shard_map/ppermute | solution.py:1356
  350.9 62.5 %collective-permute-start.16 = (bf16[1024,512]{1,0:T(8,128)(2,1)}, bf16[1024,512]{1,0:T(8,128)(2,1)}, u32[]{:S(2)}, u32[]{:S(2)}) collective-permute-start(bf16[1024,512]{1,0:T(8,128)(2,1)} %constant_dynamic-slice_fusion.6), channel_id=1, source_target_pairs={{0,4},{2,6},{4,0},{6,2},{1,5},{3,7},{5,1},{7,3},{8,12},{10,14},{12... | collective-permute-start | bytes 3145736 | tf_op jit(solution)/shard_map/ppermute | solution.py:1356
  352.5 63.6 %collective-permute-start.15 = (bf16[1024,512]{1,0:T(8,128)(2,1)S(1)}, bf16[1024,512]{1,0:T(8,128)(2,1)}, u32[]{:S(2)}, u32[]{:S(2)}) collective-permute-start(bf16[1024,512]{1,0:T(8,128)(2,1)S(1)} %constant_dynamic-slice_fusion.7), channel_id=1, source_target_pairs={{0,4},{2,6},{4,0},{6,2},{1,5},{3,7},{5,1},{7,3},{8,12},{10,14},{12... | collective-permute-start | bytes 3145736 | tf_op jit(solution)/shard_map/ppermute | solution.py:1356
  421.5 78.3 %collective-permute-start.23 = (bf16[128,4,768]{2,0,1:T(8,128)(2,1)}, bf16[128,4,768]{2,0,1:T(8,128)(2,1)}, u32[]{:S(2)}, u32[]{:S(2)}) collective-permute-start(bf16[128,4,768]{2,0,1:T(8,128)(2,1)} %constant_dynamic-slice_fusion.2), channel_id=1, source_target_pairs={{0,2},{2,0},{4,6},{6,4},{1,3},{3,1},{5,7},{7,5},{8,10},{10,8},{12,... | collective-permute-start | bytes 2359304 | tf_op jit(solution)/shard_map/ppermute | solution.py:1356
  421.5 77.5 %collective-permute-start.22 = (bf16[1024,128]{1,0:T(8,128)(2,1)S(1)}, bf16[1024,128]{1,0:T(8,128)(2,1)S(1)}, u32[]{:S(2)}, u32[]{:S(2)}) collective-permute-start(bf16[1024,128]{1,0:T(8,128)(2,1)S(1)} %add_convert_fusion.9), channel_id=1, source_target_pairs={{0,1},{1,0},{2,3},{3,2},{4,5},{5,4},{6,7},{7,6},{8,9},{9,8},{10,11... | collective-permute-start | bytes 786440 | tf_op jit(solution)/shard_map/ppermute | solution.py:1356
  423.1 79.1 %collective-permute-start.21 = (bf16[1024,512]{1,0:T(8,128)(2,1)}, bf16[1024,512]{1,0:T(8,128)(2,1)}, u32[]{:S(2)}, u32[]{:S(2)}) collective-permute-start(bf16[1024,512]{1,0:T(8,128)(2,1)} %constant_dynamic-slice_fusion.3), channel_id=1, source_target_pairs={{0,4},{2,6},{4,0},{6,2},{1,5},{3,7},{5,1},{7,3},{8,12},{10,14},{12... | collective-permute-start | bytes 3145736 | tf_op jit(solution)/shard_map/ppermute | solution.py:1356
  424.6 80.1 %collective-permute-start.20 = (bf16[1024,512]{1,0:T(8,128)(2,1)}, bf16[1024,512]{1,0:T(8,128)(2,1)}, u32[]{:S(2)}, u32[]{:S(2)}) collective-permute-start(bf16[1024,512]{1,0:T(8,128)(2,1)} %add_convert_fusion.3), channel_id=1, source_target_pairs={{0,1},{1,0},{2,3},{3,2},{4,5},{5,4},{6,7},{7,6},{8,9},{9,8},{10,11... | collective-permute-start | bytes 3145736 | tf_op jit(solution)/shard_map/ppermute | solution.py:1356
  507.3 137.9 %reduce-scatter.4.cloned.1.call-start = ((), (), s32[]{:S(2)}) async-start(), calls=%async_computation.4 | async-start | bytes 1310720 | tf_op jit(solution)/shard_map/reduce_scatter | solution.py:1612
  508.1 137.2 %reduce-scatter.6.cloned.1.call-start = ((), (), s32[]{:S(2)}) async-start(), calls=%async_computation.5 | async-start | bytes 1310720 | tf_op jit(solution)/shard_map/reduce_scatter | solution.py:1612
  517.9 130.4 %collective-permute-start.14 = (bf16[512,1024]{1,0:T(8,128)(2,1)}, bf16[512,1024]{1,0:T(8,128)(2,1)S(1)}, u32[]{:S(2)}, u32[]{:S(2)}) collective-permute-start(bf16[512,1024]{1,0:T(8,128)(2,1)} %get-tuple-element.114.own_second), channel_id=1, source_target_pairs={{0,1},{1,0},{2,3},{3,2},{4,5},{5,4},{6,7},{7,6},{8,9},{9,8},{10,11... | collective-permute-start | bytes 3145736 | tf_op jit(solution)/shard_map/ppermute | solution.py:1356
  518.5 129.8 %collective-permute-start.13 = (bf16[512,1024]{1,0:T(8,128)(2,1)}, bf16[512,1024]{1,0:T(8,128)(2,1)}, u32[]{:S(2)}, u32[]{:S(2)}) collective-permute-start(bf16[512,1024]{1,0:T(8,128)(2,1)} %get-tuple-element.105.own_first), channel_id=1, source_target_pairs={{0,1},{1,0},{2,3},{3,2},{4,5},{5,4},{6,7},{7,6},{8,9},{9,8},{10,11... | collective-permute-start | bytes 3145736 | tf_op jit(solution)/shard_map/ppermute | solution.py:1356
  520.2 109.3 %collective-permute-start.40 = (f32[7168]{0:T(1024)S(1)}, f32[7168]{0:T(1024)S(1)}, u32[]{:S(2)}, u32[]{:S(2)}) collective-permute-start(f32[7168]{0:T(1024)S(1)} %add.280), channel_id=1, source_target_pairs={{0,16},{8,24},{16,0},{24,8},{1,17},{9,25},{17,1},{25,9},{2,18},{10... | collective-permute-start | bytes 86024 | tf_op jit(solution)/shard_map/ppermute | solution.py:1356
  523.0 122.1 %collective-permute-start.24 = (bf16[64,4,768]{2,0,1:T(8,128)(2,1)S(1)}, bf16[64,4,768]{2,0,1:T(8,128)(2,1)S(1)}, u32[]{:S(2)}, u32[]{:S(2)}) collective-permute-start(bf16[64,4,768]{2,0,1:T(8,128)(2,1)S(1)} %constant_dynamic-slice_fusion.1), channel_id=1, source_target_pairs={{0,4},{2,6},{4,0},{6,2},{1,5},{3,7},{5,1},{7,3},{8,12},{10,14},{12... | collective-permute-start | bytes 1179656 | tf_op jit(solution)/shard_map/ppermute | solution.py:1356
  655.6 61.3 %collective-permute-start.25 = (bf16[512,1024]{1,0:T(8,128)(2,1)}, bf16[512,1024]{1,0:T(8,128)(2,1)}, u32[]{:S(2)}, u32[]{:S(2)}) collective-permute-start(bf16[512,1024]{1,0:T(8,128)(2,1)} %get-tuple-element.144.own_first), channel_id=1, source_target_pairs={{0,1},{1,0},{2,3},{3,2},{4,5},{5,4},{6,7},{7,6},{8,9},{9,8},{10,11... | collective-permute-start | bytes 3145736 | tf_op jit(solution)/shard_map/ppermute | solution.py:1356
  660.4 56.5 %collective-permute-start.26 = (bf16[512,1024]{1,0:T(8,128)(2,1)}, bf16[512,1024]{1,0:T(8,128)(2,1)}, u32[]{:S(2)}, u32[]{:S(2)}) collective-permute-start(bf16[512,1024]{1,0:T(8,128)(2,1)} %get-tuple-element.151.own_second), channel_id=1, source_target_pairs={{0,1},{1,0},{2,3},{3,2},{4,5},{5,4},{6,7},{7,6},{8,9},{9,8},{10,11... | collective-permute-start | bytes 3145736 | tf_op jit(solution)/shard_map/ppermute | solution.py:1356
  (46 other events, 751.6 us)
Sparse Core Ops, SparseCore 0:
  507.4 20.1 reduce-scatter.7
  530.7 41.8 reduce-scatter.3
  575.5 42.6 reduce-scatter.5

commit v4 on v3

--- a/solution.py
+++ b/solution.py
@@ -56,8 +56,8 @@
 
 
 class Trade:
-    def __init__(self, source, target, send_sems, recv_sems, own_sem):
-        self.source, self.target = source, target
+    def __init__(self, source, target, send_sems, recv_sems, own_sem, pair=None):
+        self.source, self.target, self.pair = source, target, pair
         self.send_sems, self.recv_sems, self.own_sem = send_sems, recv_sems, own_sem
         self.count = source.shape[0]
         self.me = lax.axis_index("seq")
@@ -67,6 +67,10 @@
         for distance in range(1, self.count):
             other = lax.rem(self.me + distance, self.count)
             pl.semaphore_signal(barrier, inc=1, device_id={"seq": other}, device_id_type=MESH)
+        if self.pair is not None:
+            partner = 1 - lax.axis_index("mp")
+            pl.semaphore_signal(barrier, inc=1, device_id={"mp": partner}, device_id_type=MESH)
+            others = others + 1
         pl.semaphore_wait(barrier, self.count - 1 + others)
 
     def copy(self, distance):
@@ -80,6 +84,17 @@
             device_id_type=MESH,
         )
 
+    def pair_copy(self):
+        source, target, sems = self.pair
+        return pltpu.make_async_remote_copy(
+            src_ref=source,
+            dst_ref=target,
+            send_sem=sems.at[0],
+            recv_sem=sems.at[1],
+            device_id={"mp": 1 - lax.axis_index("mp")},
+            device_id_type=MESH,
+        )
+
     def own(self):
         return pltpu.make_async_copy(
             self.source.at[self.me], self.target.at[self.me], self.own_sem.at[0]
@@ -89,11 +104,15 @@
         self.greet(others)
         for distance in range(1, self.count):
             self.copy(distance).start()
+        if self.pair is not None:
+            self.pair_copy().start()
         self.own().start()
 
     def finish(self):
         for distance in range(1, self.count):
             self.copy(distance).wait()
+        if self.pair is not None:
+            self.pair_copy().wait()
         self.own().wait()
 
 
@@ -518,6 +537,7 @@
     bias_ref,
     down_bias_ref,
     trade_source,
+    pair_source,
     act_in,
     pre_in,
     second_in,
@@ -536,6 +556,7 @@
     sums_ref,
     unit_sums_ref,
     trade_target,
+    pair_target,
     hidden,
     normed,
     inverse,
@@ -546,6 +567,7 @@
     down_slots,
     slot_sems,
     row_sems,
+    pair_sems,
     *trade_sems,
 ):
     step = pl.program_id(0)
@@ -591,7 +613,8 @@
         pltpu.make_async_copy(source.at[place, pl.ds(first_row, rows)], target, row_sems.at[which])
         for which, (source, target) in enumerate(((x_ref, hidden), (cotangent_ref, grad_rows)))
     ]
-    trade = Trade(trade_source, trade_target, *trade_sems)
+    pair = (pair_source, pair_target, pair_sems) if index else None
+    trade = Trade(trade_source, trade_target, *trade_sems, pair)
     out_parts = [(own_place + part, out_own_ref, part) for part in range(half)]
     out_parts += [(other_place + part, out_other_ref, part) for part in range(half)]
 
@@ -682,7 +705,7 @@
 
 
 def token_part(
-    index, doc_ends, att, layer_input, cotangent, outs, ups, downs, up_bias, gain, bias, down_bias, source, kept
+    index, doc_ends, att, layer_input, cotangent, outs, ups, downs, up_bias, gain, bias, down_bias, source, pair, kept
 ):
     parts, rows, cols = att.shape
     width = layer_input.shape[2]
@@ -694,7 +717,7 @@
         kept = [jnp.zeros((8, 128), BF16)] * len(shapes)
         aliases = {}
     else:
-        aliases = {17 + place: 3 + place for place in range(len(shapes))}
+        aliases = {18 + place: 3 + place for place in range(len(shapes))}
     half = lambda step: (index, 0)
     fixed = lambda step: (0, 0)
     any_spec = pl.BlockSpec(memory_space=pl.ANY)
@@ -713,7 +736,7 @@
         ]
         + [any_spec] * 6
         + [pl.BlockSpec((1, chunk), lambda step: (0, step)), vector, vector, vector]
-        + [any_spec] * (1 + len(shapes)),
+        + [any_spec] * (2 + len(shapes)),
         out_specs=[
             pl.BlockSpec((rows, width), fixed),
             pl.BlockSpec((rows, width), fixed),
@@ -727,6 +750,7 @@
             pl.BlockSpec((8, width), fixed),
             pl.BlockSpec((8, chunk), lambda step: (0, step)),
             any_spec,
+            any_spec,
         ],
         scratch_shapes=[
             pltpu.VMEM((rows, width), F32),
@@ -738,6 +762,7 @@
             pltpu.VMEM((2, width, chunk), BF16),
             pltpu.VMEM((2, chunk, width), BF16),
             pltpu.SemaphoreType.DMA((2, 2)),
+            pltpu.SemaphoreType.DMA((2,)),
             pltpu.SemaphoreType.DMA((2,)),
         ]
         + trade_scratch(parts),
@@ -751,6 +776,7 @@
             jax.ShapeDtypeStruct((8, width), F32),
             jax.ShapeDtypeStruct((8, units), F32),
             jax.ShapeDtypeStruct((parts, rows, cols), BF16),
+            jax.ShapeDtypeStruct(pair.shape, BF16),
         ],
         input_output_aliases=aliases,
         compiler_params=pltpu.CompilerParams(
@@ -774,6 +800,7 @@
         bias,
         down_bias,
         source,
+        pair,
         *kept,
     )
 
@@ -1014,25 +1041,331 @@
     )(layer_input, gain, bias, weight)
 
 
+class VectorSum:
+    def __init__(self, group, line, sems):
+        self.group, self.line, self.sems = group, line, sems
+        self.me, self.count = lax.axis_index("seq"), lax.axis_size("seq")
+        self.pairs = lax.axis_size("mp")
+        self.members = lax.axis_size("batch") * self.pairs
+        self.mine = lax.axis_index("batch") * self.pairs + lax.axis_index("mp")
+
+    def member(self, distance):
+        other = lax.rem(self.mine + distance, self.members)
+        return {"batch": other // self.pairs, "mp": lax.rem(other, self.pairs)}
+
+    def along(self, distance):
+        return {"seq": lax.rem(self.me + distance, self.count)}
+
+    def greet(self):
+        barrier = pltpu.get_barrier_semaphore()
+        for distance in range(1, self.members):
+            pl.semaphore_signal(
+                barrier, inc=1, device_id=self.member(distance), device_id_type=MESH
+            )
+        for distance in range(1, self.count):
+            pl.semaphore_signal(barrier, inc=1, device_id=self.along(distance), device_id_type=MESH)
+        pl.semaphore_wait(barrier, self.members + self.count - 2)
+
+    def share(self, distance, along):
+        buffer, place = (self.line, self.me) if along else (self.group, self.mine)
+        which = distance - 1 + (self.members - 1 if along else 0)
+        return pltpu.make_async_remote_copy(
+            src_ref=buffer.at[place],
+            dst_ref=buffer.at[place],
+            send_sem=self.sems.at[0, which],
+            recv_sem=self.sems.at[1, which],
+            device_id=self.along(distance) if along else self.member(distance),
+            device_id_type=MESH,
+        )
+
+    def start(self, value):
+        self.group[self.mine] = value
+        for distance in range(1, self.members):
+            self.share(distance, False).start()
+
+    def middle(self):
+        for distance in range(1, self.members):
+            self.share(distance, False).wait()
+        total = self.group[0]
+        for place in range(1, self.members):
+            total = total + self.group[place]
+        self.line[self.me] = total
+        for distance in range(1, self.count):
+            self.share(distance, True).start()
+
+    def finish(self):
+        for distance in range(1, self.count):
+            self.share(distance, True).wait()
+        total = self.line[0]
+        for place in range(1, self.count):
+            total = total + self.line[place]
+        return total
+
+
+class Extra:
+    def __init__(self, kind, source, target, sems):
+        self.source, self.target, self.sems = source, target, sems
+        batch, place, me = lax.axis_index("batch"), lax.axis_index("mp"), lax.axis_index("seq")
+        self.local = None
+        if kind == "mp":
+            self.moves = [(source, target, {"mp": 1 - place})]
+        elif kind == "chip":
+            side = (batch // 2) % 2
+            size = source.shape[1] // 2
+            there = pl.ds(pl.multiple_of((1 - side) * size, 128), size)
+            self.moves = [(source.at[:, there], target, {"batch": batch + 2 - 4 * side})]
+        else:
+            count = source.shape[0]
+            pairs = lax.axis_size("mp")
+            mine = me if kind == "line" else batch * pairs + place
+            self.moves = []
+            for distance in range(1, count):
+                other = lax.rem(mine + distance, count)
+                device = {"batch": other // pairs, "mp": lax.rem(other, pairs)}
+                if kind == "line":
+                    device = {"seq": other}
+                self.moves.append((source.at[other], target.at[mine], device))
+            self.local = (source.at[mine], target.at[mine])
+
+    def copies(self):
+        for index, (source, target, device) in enumerate(self.moves):
+            yield pltpu.make_async_remote_copy(
+                src_ref=source,
+                dst_ref=target,
+                send_sem=self.sems.at[0, index],
+                recv_sem=self.sems.at[1, index],
+                device_id=device,
+                device_id_type=MESH,
+            )
+        if self.local is not None:
+            yield pltpu.make_async_copy(*self.local, self.sems.at[0, len(self.moves)])
+
+    def start(self):
+        for copy in self.copies():
+            copy.start()
+
+    def finish(self):
+        for copy in self.copies():
+            copy.wait()
+
+
+def extra_target(kind, source):
+    rows, *rest = source.shape
+    return (rows, rest[0] // 2) if kind == "chip" else source.shape
+
+
+def extra_moves(kind, source):
+    return 1 if kind in ("mp", "chip") else source.shape[0]
+
+
+def in_rows(vectors, width):
+    pieces = []
+    for row in range(vectors.shape[0]):
+        for start in range(0, vectors.shape[1], width):
+            pieces.append(vectors[row : row + 1, start : start + width])
+    return jnp.concatenate(pieces, axis=0)
+
+
+class WeightChain:
+    def __init__(self, terms, qkv_terms, gathered, heads_ref, sending, received, result, head_sum, heads_in, sems):
+        self.up, self.up_come, self.out, self.out_come, self.down, self.down_come = terms
+        self.qkv_terms, self.gathered, self.heads_ref = qkv_terms, gathered, heads_ref
+        self.sending, self.received, self.result = sending, received, result
+        self.head_sum, self.heads_in, self.sems = head_sum, heads_in, sems
+        self.me, self.count = lax.axis_index("seq"), lax.axis_size("seq")
+        self.batch, self.place = lax.axis_index("batch"), lax.axis_index("mp")
+        self.rows = result.shape[1]
+        self.chunks = 2
+        self.step = self.rows // self.chunks
+        self.steps = (self.count - 1) * self.chunks
+        self.members = qkv_terms.shape[0]
+        self.mine = self.batch * 2 + self.place
+        self.used = 2 * self.steps
+
+    def at(self, chunk):
+        return pl.ds(pl.multiple_of(chunk * self.step, self.step), self.step)
+
+    def term(self, target, chunk):
+        here = pl.ds(pl.multiple_of(target * self.rows + chunk * self.step, self.step), self.step)
+        size = self.down.shape[1] // 2
+        kept = pl.ds(pl.multiple_of((self.batch // 2) % 2 * size, 128), size)
+        pairs = (
+            (self.up[here, :], self.up_come[here, :]),
+            (self.down[here, kept], self.down_come[here, :]),
+            (self.out[here, :], self.out_come[here, :]),
+        )
+        return jnp.concatenate([own.astype(F32) + come.astype(F32) for own, come in pairs], axis=1)
+
+    def send(self, side, message, chunk):
+        which = (side * (self.count - 1) + message) * self.chunks + chunk
+        return pltpu.make_async_remote_copy(
+            src_ref=self.sending.at[side, message, self.at(chunk)],
+            dst_ref=self.received.at[side, message, self.at(chunk)],
+            send_sem=self.sems.at[0, which],
+            recv_sem=self.sems.at[1, which],
+            device_id={"seq": self.me + 1 - 2 * side},
+            device_id_type=MESH,
+        )
+
+    def flow(self, side, index):
+        message, chunk = index // self.chunks, index % self.chunks
+        target = (1 - side) * (self.count - 1 - message) + side * message
+
+        @pl.when((target - self.me) * (1 - 2 * side) > 0)
+        def _():
+            total = self.term(target, chunk)
+            first = (1 - side) * self.me + side * (self.count - 1 - self.me)
+
+            @pl.when(first == 0)
+            def _():
+                self.sending[side, message, self.at(chunk), :] = total.astype(BF16)
+
+            @pl.when(first > 0)
+            def _():
+                self.send(side, message, chunk).wait_recv()
+                come = self.received[side, message, self.at(chunk), :].astype(F32)
+                self.sending[side, message, self.at(chunk), :] = (total + come).astype(BF16)
+
+            self.send(side, message, chunk).start()
+
+    def heads_line(self, distance):
+        other = lax.rem(self.me + distance, self.count)
+        which = self.used + distance - 1
+        return pltpu.make_async_remote_copy(
+            src_ref=self.head_sum.at[other],
+            dst_ref=self.heads_in.at[self.me],
+            send_sem=self.sems.at[0, which],
+            recv_sem=self.sems.at[1, which],
+            device_id={"seq": other},
+            device_id_type=MESH,
+        )
+
+    def heads_member(self, distance):
+        other = lax.rem(self.mine + distance, self.members)
+        which = self.used + self.count - 1 + distance - 1
+        parts = self.count // 2
+        return pltpu.make_async_remote_copy(
+            src_ref=self.heads_in.at[pl.ds(lax.rem(other, 2) * parts, parts)],
+            dst_ref=self.heads_ref.at[self.mine],
+            send_sem=self.sems.at[0, which],
+            recv_sem=self.sems.at[1, which],
+            device_id={"batch": other // 2, "mp": lax.rem(other, 2)},
+            device_id_type=MESH,
+        )
+
+    def heads_own(self):
+        parts = self.count // 2
+        return pltpu.make_async_copy(
+            self.heads_in.at[pl.ds(self.place * parts, parts)],
+            self.heads_ref.at[self.mine],
+            self.sems.at[0, self.used + self.count + self.members - 2],
+        )
+
+    def piece(self, index):
+        which = self.used + self.count + self.members - 1 + index
+        side = (self.batch // 2) % 2
+        parity = self.batch % 2
+        other = self.batch + 1 - 2 * parity if index else self.batch + 2 - 4 * side
+        source = max(index - 1, 0)
+        return pltpu.make_async_remote_copy(
+            src_ref=self.result.at[source],
+            dst_ref=self.result.at[source + (2 if index else 1)],
+            send_sem=self.sems.at[0, which],
+            recv_sem=self.sems.at[1, which],
+            device_id={"batch": other},
+            device_id_type=MESH,
+        )
+
+    def start(self):
+        total = self.qkv_terms[0].astype(F32)
+        for member in range(1, self.members):
+            total = total + self.qkv_terms[member].astype(F32)
+        self.head_sum[...] = total.astype(BF16)
+        self.heads_in[self.me] = self.head_sum[self.me]
+        for distance in range(1, self.count):
+            self.heads_line(distance).start()
+
+    def own(self):
+        for chunk in range(self.chunks):
+            here = self.at(chunk)
+            total = self.term(self.me, chunk)
+
+            @pl.when(self.me > 0)
+            def _():
+                self.send(0, self.count - 1 - self.me, chunk).wait_recv()
+
+            @pl.when(self.me < self.count - 1)
+            def _():
+                self.send(1, self.me, chunk).wait_recv()
+
+            left = self.received[0, jnp.minimum(self.count - 1 - self.me, self.count - 2), here, :]
+            right = self.received[1, jnp.minimum(self.me, self.count - 2), here, :]
+            total = total + jnp.where(self.me > 0, left.astype(F32), 0.0)
+            total = total + jnp.where(self.me < self.count - 1, right.astype(F32), 0.0)
+            self.result[0, here, :] = total.astype(BF16)
+        self.piece(0).start()
+        for distance in range(1, self.count):
+            self.heads_line(distance).wait()
+        for distance in range(1, self.members):
+            self.heads_member(distance).start()
+        self.heads_own().start()
+
+    def spread(self):
+        self.piece(0).wait()
+        self.piece(1).start()
+        self.piece(2).start()
+
+    def finish(self):
+        for index in range(self.steps):
+            message, chunk = index // self.chunks, index % self.chunks
+
+            @pl.when(self.count - 1 - message > self.me)
+            def _():
+                self.send(0, message, chunk).wait_send()
+
+            @pl.when(message < self.me)
+            def _():
+                self.send(1, message, chunk).wait_send()
+
+        self.piece(1).wait()
+        self.piece(2).wait()
+        self.heads_own().wait()
+        for distance in range(1, self.members):
+            self.heads_member(distance).wait()
+        copy = pltpu.make_async_copy(
+            self.result, self.gathered, self.sems.at[0, self.used + self.count + self.members + 2]
+        )
+        copy.start()
+        copy.wait()
+
+
 def return_kernel(
     count,
     chunks,
     lag,
-    offset,
+    index_of,
+    kinds,
     parts_ref,
     weight_ref,
     x_ref,
     hidden_grad_ref,
     gain_ref,
-    input_ref,
-    sums_ref,
-    rows_in,
-    sending,
-    received,
-    load_sem,
-    send_sems,
-    recv_sems,
+    vectors_ref,
+    *rest,
 ):
+    extras = len(kinds)
+    sources, rest = rest[:extras], rest[extras:]
+    if index_of:
+        *weight_terms, qkv_terms = rest[:7]
+        rest = rest[7:]
+    input_ref, sums_ref, total_ref, other_ref, *rest = rest
+    targets, rest = rest[:extras], rest[extras:]
+    if index_of:
+        gathered, heads_ref, *rest = rest
+    rows_in, sending, received, group, line, load_sem, *rest = rest
+    send_sems, recv_sems, pair_send_sems, pair_recv_sems, vector_sems, *extra_sems = rest
+    late = extra_sems[extras:]
+    extras = [Extra(*each) for each in zip(kinds, sources, targets, extra_sems)]
     me = lax.axis_index("seq")
     place = lax.axis_index("mp")
     rows = hidden_grad_ref.shape[0]
@@ -1043,9 +1376,14 @@
     def at(chunk):
         return pl.ds(pl.multiple_of(chunk * step, step), step)
 
-    load = pltpu.make_async_copy(x_ref.at[place, pl.ds(offset, rows)], rows_in, load_sem.at[0])
+    load = pltpu.make_async_copy(x_ref.at[place, pl.ds(index_of * rows, rows)], rows_in, load_sem.at[0])
     load.start()
-    greet(me, count)
+    vector_sum = VectorSum(group, line, vector_sems)
+    vector_sum.greet()
+    if index_of == 0:
+        vector_sum.start(vectors_ref[...])
+    for extra in extras:
+        extra.start()
 
     def send(side, message, chunk):
         return pltpu.make_async_remote_copy(
@@ -1079,25 +1417,26 @@
 
             send(side, message, chunk).start()
 
+    if index_of:
+        chain = WeightChain(weight_terms, qkv_terms, gathered, heads_ref, *late)
+        chain.start()
+    else:
+        chain = None
+    ahead = chain.steps if chain else 0
     near = me // (count // 2)
 
-    def advance(index, _):
-        @pl.when(index < steps)
-        def _():
-            flow(near, index)
-
-        @pl.when(index >= lag)
-        def _():
-            flow(1 - near, index - lag)
-
-        return 0
-
-    lax.fori_loop(0, steps + lag, advance, 0)
-    load.wait()
-
-    def own(chunk, carried):
+    def pair(chunk):
+        return pltpu.make_async_remote_copy(
+            src_ref=input_ref.at[at(chunk)],
+            dst_ref=other_ref.at[at(chunk)],
+            send_sem=pair_send_sems.at[chunk],
+            recv_sem=pair_recv_sems.at[chunk],
+            device_id={"mp": 1 - place},
+            device_id_type=MESH,
+        )
+
+    def own(chunk):
         here = at(chunk)
-        rows_in_now = rows_in[here, :]
         total = dot_nt(parts_ref[me, here, :], weight_ref[...])
 
         @pl.when(me > 0)
@@ -1111,7 +1450,7 @@
         left = received[0, jnp.minimum(count - 1 - me, count - 2), here, :].astype(F32)
         right = received[1, jnp.minimum(me, count - 2), here, :].astype(F32)
         total = total + jnp.where(me > 0, left, 0.0) + jnp.where(me < count - 1, right, 0.0)
-        unit, inverse = row_stats(rows_in_now)
+        unit, inverse = row_stats(rows_in[here, :])
         scaled = total * gain_ref[...]
         through = (
             scaled
@@ -1119,15 +1458,56 @@
             - unit * jnp.mean(scaled * unit, axis=-1, keepdims=True)
         )
         input_ref[here, :] = (hidden_grad_ref[here, :] + inverse * through).astype(BF16)
-        gain_sum, bias_sum = carried
-        return (
-            gain_sum + jnp.sum(total * unit, axis=0, keepdims=True),
-            bias_sum + jnp.sum(total, axis=0, keepdims=True),
-        )
-
-    zero = jnp.zeros((1, width), F32)
-    gain_sum, bias_sum = lax.fori_loop(0, chunks, own, (zero, zero))
-    sums_ref[...] = jnp.concatenate([gain_sum, bias_sum, jnp.zeros((6, width), F32)], axis=0)
+        if index_of:
+            pair(chunk).start()
+        sums_ref[0:1, :] += jnp.sum(total * unit, axis=0, keepdims=True)
+        sums_ref[1:2, :] += jnp.sum(total, axis=0, keepdims=True)
+
+    sums_ref[...] = jnp.zeros_like(sums_ref)
+    load.wait()
+    wait_for = ahead + ((count - 2) * chunks + lag + 1 if index_of else steps + lag)
+    steps_all = ahead + steps
+
+    def flow_of(side, index):
+        if chain is not None:
+
+            @pl.when(index < ahead)
+            def _():
+                chain.flow(side, index)
+
+        @pl.when(index >= ahead)
+        def _():
+            flow(side, index - ahead)
+
+    def advance(index, _):
+        @pl.when(index < steps_all)
+        def _():
+            flow_of(near, index)
+
+        @pl.when((index >= lag) & (index < steps_all + lag))
+        def _():
+            flow_of(1 - near, index - lag)
+
+        if chain is not None:
+
+            @pl.when(index == ahead + lag + 2)
+            def _():
+                chain.own()
+
+            @pl.when(index == ahead + lag + 6)
+            def _():
+                chain.spread()
+
+        @pl.when(index >= wait_for)
+        def _():
+            own(index - wait_for)
+
+        return 0
+
+    lax.fori_loop(0, wait_for + chunks, advance, 0)
+    if index_of:
+        vector_sum.start(in_rows(sums_ref[0:2, :] + vectors_ref[0:2, :], group.shape[2]))
+    vector_sum.middle()
 
     def finish(index, _):
         message = index // chunks
@@ -1145,17 +1525,51 @@
 
     lax.fori_loop(0, steps, finish, 0)
 
-
-def return_part(index, parts, weight, layer_input, hidden_grad, gain):
+    def finish_pair(chunk, _):
+        pair(chunk).wait()
+        return 0
+
+    if index_of:
+        lax.fori_loop(0, chunks, finish_pair, 0)
+    total_ref[...] = vector_sum.finish()
+    if chain is not None:
+        chain.finish()
+    for extra in extras:
+        extra.finish()
+
+
+def return_part(
+    index, parts, weight, layer_input, hidden_grad, gain, vectors, extras, weight_terms=(), qkv_terms=None
+):
     count, rows, cols = parts.shape
     rows = rows // 2
     width = weight.shape[0]
     chunks = max(1, rows // 128)
+    members = lax.axis_size("batch") * lax.axis_size("mp")
+    small = (8, 2 * width // 8) if index else vectors.shape
+    kinds, sources = [kind for kind, _ in extras], [source for _, source in extras]
+    late_in, late_out, late_scratch = [], [], []
+    if index:
+        late_in = [*weight_terms, qkv_terms]
+        up, _, out, *_ = weight_terms
+        part = (width // count, 2 * up.shape[1] + out.shape[1])
+        batches = lax.axis_size("batch")
+        head = qkv_terms.shape[2:]
+        late_out = [(batches,) + part, (members, count // 2) + head]
+        messages = (2, count - 1) + part
+        late_scratch = [
+            pltpu.VMEM(messages, BF16),
+            pltpu.VMEM(messages, BF16),
+            pltpu.VMEM((batches,) + part, BF16),
+            pltpu.VMEM((count,) + head, BF16),
+            pltpu.VMEM((count,) + head, BF16),
+            pltpu.SemaphoreType.DMA((2, 4 * (count - 1) + count + members + 3)),
+        ]
     any_spec = pl.BlockSpec(memory_space=pl.ANY)
     dma = pltpu.SemaphoreType.DMA
     fixed = lambda step: (0, 0)
     return pl.pallas_call(
-        functools.partial(return_kernel, count, chunks, 2, index * rows),
+        functools.partial(return_kernel, count, chunks, 2, index, kinds),
         grid=(1,),
         in_specs=[
             pl.BlockSpec((count, rows, cols), lambda step: (0, index, 0)),
@@ -1163,25 +1577,45 @@
             any_spec,
             pl.BlockSpec((rows, width), fixed),
             pl.BlockSpec((1, width), fixed),
-        ],
-        out_specs=[pl.BlockSpec((rows, width), fixed), pl.BlockSpec((8, width), fixed)],
+            pl.BlockSpec(vectors.shape, fixed),
+        ]
+        + [any_spec] * len(extras)
+        + [pl.BlockSpec(memory_space=pltpu.VMEM)] * len(late_in),
+        out_specs=[
+            pl.BlockSpec((rows, width), fixed),
+            pl.BlockSpec((8, width), fixed),
+            pl.BlockSpec(small, fixed),
+            any_spec,
+        ]
+        + [any_spec] * (len(extras) + len(late_out)),
         out_shape=[
             jax.ShapeDtypeStruct((rows, width), BF16),
             jax.ShapeDtypeStruct((8, width), F32),
-        ],
+            jax.ShapeDtypeStruct(small, F32),
+            jax.ShapeDtypeStruct((rows, width), BF16),
+        ]
+        + [jax.ShapeDtypeStruct(extra_target(*extra), BF16) for extra in extras]
+        + [jax.ShapeDtypeStruct(shape, BF16) for shape in late_out],
         scratch_shapes=[
             pltpu.VMEM((rows, width), F32),
             pltpu.VMEM((2, count - 1, rows, width), BF16),
             pltpu.VMEM((2, count - 1, rows, width), BF16),
+            pltpu.VMEM((members,) + small, F32),
+            pltpu.VMEM((count,) + small, F32),
             dma((1,)),
             dma((2, count - 1, chunks)),
             dma((2, count - 1, chunks)),
-        ],
+            dma((chunks,)),
+            dma((chunks,)),
+            dma((2, members + count - 2)),
+        ]
+        + [dma((2, extra_moves(*extra))) for extra in extras]
+        + late_scratch,
         compiler_params=pltpu.CompilerParams(
             collective_id=1 + index, has_side_effects=True, vmem_limit_bytes=VMEM_LIMIT
         ),
         cost_estimate=pl.CostEstimate(flops=80_000_000_000, bytes_accessed=1, transcendentals=0),
-    )(parts, weight, layer_input, hidden_grad, gain)
+    )(parts, weight, layer_input, hidden_grad, gain, vectors, *sources, *late_in)
 
 
 def weight_grad_kernel(
@@ -1193,6 +1627,7 @@
     act_ref,
     att_ref,
     trade_source,
+    pair_source,
     up_own,
     up_near,
     down_own,
@@ -1200,6 +1635,7 @@
     out_own,
     out_near,
     trade_target,
+    pair_target,
     turned,
     slots,
     sending,
@@ -1208,6 +1644,7 @@
     send_sems,
     recv_sems,
     out_sems,
+    pair_sems,
     *trade_sems,
 ):
     rows, width = second_ref.shape
@@ -1218,7 +1655,7 @@
     mate = me + 1 - 2 * parity
     barrier = pltpu.get_barrier_semaphore()
     pl.semaphore_signal(barrier, inc=1, device_id={"batch": mate}, device_id_type=MESH)
-    trade = Trade(trade_source, trade_target, *trade_sems)
+    trade = Trade(trade_source, trade_target, *trade_sems, (pair_source, pair_target, pair_sems))
     trade.start(1)
 
     piece = units // 4
@@ -1314,7 +1751,7 @@
     trade.finish()
 
 
-def weight_grads(second_low, grad_low, hidden_low, pre_grad, activated, attended, source):
+def weight_grads(second_low, grad_low, hidden_low, pre_grad, activated, attended, source, pair):
     rows, width = second_low.shape
     units = pre_grad.shape[1]
     piece = units // 4
@@ -1326,9 +1763,11 @@
     shapes = [(width, piece)] * 4 + [(width, width // 4)] * 2
     return pl.pallas_call(
         functools.partial(weight_grad_kernel, tile),
-        in_specs=[vmem] * 3 + [any_spec] * 4,
-        out_specs=[any_spec] * 7,
-        out_shape=[jax.ShapeDtypeStruct(shape, BF16) for shape in shapes + [source.shape]],
+        in_specs=[vmem] * 3 + [any_spec] * 5,
+        out_specs=[any_spec] * 8,
+        out_shape=[
+            jax.ShapeDtypeStruct(shape, BF16) for shape in shapes + [source.shape, pair.shape]
+        ],
         scratch_shapes=[
             pltpu.VMEM((3, width, rows), BF16),
             pltpu.VMEM((2, rows, tile), BF16),
@@ -1338,6 +1777,7 @@
             dma((jobs,)),
             dma((jobs,)),
             dma((jobs,)),
+            dma((2,)),
         ]
         + trade_scratch(source.shape[0]),
         compiler_params=pltpu.CompilerParams(
@@ -1348,7 +1788,7 @@
             bytes_accessed=4 * rows * units,
             transcendentals=0,
         ),
-    )(second_low, grad_low, hidden_low, pre_grad, activated, attended, source)
+    )(second_low, grad_low, hidden_low, pre_grad, activated, attended, source, pair)
 
 
 def swap(value, axis, distance=1):
@@ -1389,13 +1829,6 @@
     return [1 << level for level in range(lax.axis_size(axis).bit_length() - 1)]
 
 
-def sum_everywhere(value):
-    for axis in ("batch", "seq", "mp"):
-        for distance in levels_of(axis):
-            value = value + swap(value, axis, distance)
-    return value
-
-
 def gather_small(value):
     place = lax.axis_index("seq")
     count = lax.axis_size("seq")
@@ -1425,18 +1858,56 @@
     )
 
 
-def unhalve(value, distance, axis):
-    side = (lax.axis_index("batch") // distance) % 2
-    other = swap(value, "batch", distance)
-    low = jnp.where(side == 0, value, other)
-    high = jnp.where(side == 0, other, value)
-    return jnp.concatenate([low, high], axis=axis)
-
-
-def spread_batch(value, axis):
-    for distance in reversed(levels_of("batch")):
-        value = unhalve(value, distance, axis)
-    return value.astype(F32)
+def assemble_kernel(unit_cols, pieces, heads, up_ref, down_ref, out_ref, qkv_ref):
+    batch = lax.axis_index("batch")
+    batches = pieces.shape[0]
+    levels = batches.bit_length() - 1
+    for index in range(batches):
+        source = jnp.bitwise_xor(batch, index // 2 + 2 * (index % 2))
+        slot = 0
+        for level in range(levels):
+            slot = slot + ((source >> level) % 2) * (batches >> (level + 1))
+        start = 0
+        for size, target, turn in (
+            (unit_cols, up_ref, False),
+            (unit_cols, down_ref, True),
+            (pieces.shape[2] - 2 * unit_cols, out_ref, True),
+        ):
+            value = pieces[index, :, start : start + size].astype(F32)
+            here = pl.ds(pl.multiple_of(slot * size, 128), size)
+            if turn:
+                target[here, :] = value.T
+            else:
+                target[:, here] = value
+            start = start + size
+    members, parts, rows, cols = heads.shape
+    cols = cols // 3
+    for member in range(members):
+        for matrix in range(3):
+            for part in range(parts):
+                start = (matrix * parts + part) * cols
+                qkv_ref[member * rows : (member + 1) * rows, start : start + cols] = heads[
+                    member, part, :, matrix * cols : (matrix + 1) * cols
+                ].astype(F32)
+
+
+def assemble(unit_cols, pieces, heads):
+    batches, rows, all_cols = pieces.shape
+    out_cols = all_cols - 2 * unit_cols
+    shapes = [
+        (rows, batches * unit_cols),
+        (batches * unit_cols, rows),
+        (batches * out_cols, rows),
+        (heads.shape[0] * heads.shape[2], heads.shape[1] * heads.shape[3]),
+    ]
+    vmem = pl.BlockSpec(memory_space=pltpu.VMEM)
+    return pl.pallas_call(
+        functools.partial(assemble_kernel, unit_cols),
+        in_specs=[vmem] * 2,
+        out_specs=[vmem] * 4,
+        out_shape=[jax.ShapeDtypeStruct(shape, F32) for shape in shapes],
+        compiler_params=pltpu.CompilerParams(vmem_limit_bytes=VMEM_LIMIT),
+    )(pieces, heads)
 
 
 def place_kernel(place_ref, own_first, own_second, other_first, other_second, out_ref):
@@ -1453,8 +1924,7 @@
         out_ref[1 - place] = other_second[...].astype(F32)
 
 
-def both_sequences(own):
-    other = [swap(part, "mp") for part in own]
+def both_sequences(own, other):
     rows, width = own[0].shape
     step = min(256, rows)
     steps = rows // step
@@ -1536,7 +2006,7 @@
     bias_full = jnp.concatenate([up_bias, bias_near, bias_far])[None]
     outs = [part.reshape(seq_count // 2, cols, width) for part in (out_weight, out_other)]
     kept, results = None, []
-    att, source = att_first, attended_second
+    att, source, pair = att_first, attended_second, jnp.zeros((8, 128), BF16)
     for index in range(2):
         result = token_part(
             index,
@@ -1552,20 +2022,22 @@
             second_bias[None],
             down_bias[None],
             source,
+            pair,
             kept,
         )
         kept = result[3:9]
         results.append(result[:3] + result[9:])
-        att, source = result[11], result[2]
+        att, source, pair = result[11], result[2], result[0]
+        other_output = result[12]
     grad_first = att
     activated, pre_grad, second_low, hidden_low, grad_low, attended_low = kept
     sums = results[0][3][:3] + results[1][3][:3]
     unit_sums = results[0][4][0] + results[1][4][0]
     bias_sums = [unit_sums[:units], unit_sums[units : units * 3 // 2], unit_sums[units * 3 // 2 :]]
-    layer_output = both_sequences([result[0] for result in results])
-    up_own, up_near, down_own, down_near, out_own, out_near, grad_second = weight_grads(
-        second_low, grad_low, hidden_low, pre_grad, activated, attended_low, source
-    )
+    up_own, up_near, down_own, down_near, out_own, out_near, grad_second, other_second = weight_grads(
+        second_low, grad_low, hidden_low, pre_grad, activated, attended_low, source, pair
+    )
+    outputs, other_outputs = [result[0] for result in results], [other_output, other_second]
     bias_other = jnp.where(
         parity == 0,
         jnp.concatenate([bias_sums[1], bias_sums[2]]),
@@ -1576,7 +2048,6 @@
         jnp.concatenate([bias_sums[0], bias_other]),
         jnp.concatenate([bias_other, bias_sums[0]]),
     )
-    early = sum_everywhere(jnp.concatenate([sums.reshape(-1), bias_all]))
     levels = levels_of("batch")
     for distance in levels[1:]:
         up_own, up_near = halve(up_own, distance, 1), halve(up_near, distance, 1)
@@ -1592,57 +2063,53 @@
         admits,
     )
     qkv_sum = dot_tn(first_all, qkv_low_grad).astype(BF16)
-    qkv_sum = qkv_sum.reshape(seq_count, -1, 3 * cols).transpose(1, 0, 2)
+    members = lax.axis_size("batch") * 2
+    mine = lax.axis_index("batch") * 2 + mp_index
+    qkv_sum = qkv_sum.reshape(seq_count, members, -1, 3 * cols).transpose(1, 0, 2, 3)
     qkv_low_grad, qkv_sum, up_own, up_near, down_own, out_own, out_near = lax.optimization_barrier(
         (qkv_low_grad, qkv_sum, up_own, up_near, down_own, out_own, out_near)
     )
-    up_own = narrow_add(up_own, swap(up_near, "mp"))
-    out_own = narrow_add(out_own, swap(out_near, "mp"))
-    for distance in levels[1:]:
-        down_own = halve(down_own, distance, 1)
-    qkv_part = halve(qkv_sum, levels[0], 0)
     parts = qkv_low_grad.reshape(seq_count, local_rows, 3 * cols)
-    input_first, first_sums = return_part(
-        0, parts, qkv_own, layer_input, results[0][1], first_gain[None]
-    )
-    second_grad, input_first, up_own, down_own, out_own, qkv_part = lax.optimization_barrier(
-        (results[1][1], input_first, up_own, down_own, out_own, qkv_part)
-    )
-    up_grad, down_grad, out_grad = [
-        lax.psum_scatter(own, "seq", scatter_dimension=0, tiled=True)
-        for own in (up_own, down_own, out_own)
-    ]
-    for distance in levels[1:]:
-        qkv_part = halve(qkv_part, distance, 0)
-    input_second, second_sums = return_part(
-        1, parts, qkv_own, layer_input, second_grad, first_gain[None]
-    )
-    input_second, qkv_part, down_grad, up_grad, out_grad = lax.optimization_barrier(
-        (input_second, qkv_part, down_grad, up_grad, out_grad)
-    )
-    late = sum_everywhere((first_sums + second_sums)[:2])
-    qkv_part = narrow_add(qkv_part, swap(qkv_part, "mp"))
-    qkv_part = all_to_all(qkv_part.transpose(1, 0, 2))
-    qkv_part = pick(qkv_part, mp_index, 2)
-    qkv_part = qkv_part.reshape(seq_count // 2, -1, 3, cols).transpose(1, 2, 0, 3)
-    qkv_grad = spread_batch(qkv_part.reshape(-1, 3, half_cols), 0)
-    up_grad, down_grad, out_grad = [
-        spread_batch(grad, 1) for grad in (up_grad, down_grad, out_grad)
-    ]
-    input_grad = both_sequences([input_first, input_second])
+    early = jnp.concatenate([sums, bias_all.reshape(-1, width)], axis=0)
+    input_first, first_sums, early, _, up_come, out_come, down_come, qkv_terms = return_part(
+        0,
+        parts,
+        qkv_own,
+        layer_input,
+        results[0][1],
+        first_gain[None],
+        early.reshape(8, -1),
+        [("mp", up_near), ("mp", out_near), ("chip", down_own), ("group", qkv_sum)],
+    )
+    input_second, _, late, other_second, other_first, weights_back, qkv_back = return_part(
+        1,
+        parts,
+        qkv_own,
+        layer_input,
+        results[1][1],
+        first_gain[None],
+        first_sums,
+        [("mp", input_first)],
+        (up_own, up_come, out_own, out_come, down_own, down_come),
+        qkv_terms,
+    )
+    layer_output = both_sequences(outputs, other_outputs)
+    input_grad = both_sequences([input_first, input_second], [other_first, other_second])
+    up_grad, down_grad, out_grad, qkv_grad = assemble(up_own.shape[1], weights_back, qkv_back)
+    early, late = early.reshape(-1), late.reshape(-1)
     up_bias_grad = lax.dynamic_slice_in_dim(early, 3 * width + mp_index * units, units)
     return (
         layer_output,
         input_grad,
-        late[0],
-        late[1],
-        qkv_grad,
-        out_grad.T,
+        late[:width],
+        late[width:],
+        qkv_grad.reshape(-1, 3, half_cols),
+        out_grad,
         early[width : 2 * width],
         early[2 * width : 3 * width],
         up_grad,
         up_bias_grad,
-        down_grad.T,
+        down_grad,
         early[:width],
     )
 
@@ -2092,7 +2559,8 @@
         P(),
         P("batch", "seq", None),
     )
-    by_heads = (1024 // mesh.shape["seq"]) % 128 == 0
+    sizes = mesh.shape
+    by_heads = (1024 // sizes["seq"]) % 128 == 0 and sizes["batch"] == 4 and sizes["mp"] == 2
     return jax.shard_map(
         local if by_heads else local_by_blocks,
         mesh=mesh,

time: 740 us -> 667 us (0.901)
  waiting for transfers between devices: 55.7 us -> 6.44 us
  Pallas kernels: 531 us -> 574 us
  starting transfers between devices: 53.6 us -> 19.7 us
  other arithmetic: 36.2 us -> 17.7 us
  between operations: 15 us -> 1.57 us
    ppermute x43 -> x15, waiting for transfers between devices: 46.4 us -> 3.72 us  [swap(): return lax.ppermute(value, axis, [(j, j ^ distance) for j in range(size)])]
    pallas_call x2 -> x3, Pallas kernels: 178 us -> 219 us  [the longest x2 214 us: return_part(): pl.pallas_call(functools.partial(return_kernel, count, chunks, 2, index,...]
    ppermute x43 -> x15, starting transfers between devices: 45.7 us -> 15.4 us  [swap(): return lax.ppermute(value, axis, [(j, j ^ distance) for j in range(size)])]
    convert_element_type x10 -> x5, other arithmetic: 17.6 us -> 13 us  [narrow_add(): return (mine.astype(F32) + received.astype(F32)).astype(BF16)]
  transfers between devices with their start and end apart: 50 -> 18, of which waited for: 13 -> 2; matrix products, arithmetic and copies ran while one was open for 8% -> 6% of each run, Pallas kernels for 57% -> 35%
where the time goes in v4:
time: 667 us; the launch traced here: 660 us
  Pallas kernels  574 us (86%)
  local copies, waits for them, and re-layouts  30.2 us (5%)
  starting transfers between devices  19.7 us (3%)
  other arithmetic  17.7 us (3%)
  matrix products  11.1 us (2%)
    pallas_call x2, Pallas kernels, return_part(): pl.pallas_call(functools.partial(return_kernel, count, chunks, 2, index,...  214 us
    pallas_call x1, Pallas kernels, gather_project(): pl.pallas_call(functools.partial(gather_kernel, count, chunks, half_cols)...  142 us
    pallas_call x2, Pallas kernels, token_part(): pl.pallas_call(functools.partial(token_kernel, min(256, rows), index), gr...  72.4 us
    pallas_call x1, Pallas kernels, attention_backward(): pl.pallas_call(functools.partial(backward_kernel, heads), grid=(1,), in_s...  46.8 us
    pallas_call x1, Pallas kernels, weight_grads(): pl.pallas_call(functools.partial(weight_grad_kernel, tile), in_specs=[vme...  43.5 us
    pallas_call x2, Pallas kernels, attention_forward(): pl.pallas_call(functools.partial(forward_kernel, heads, half), grid=(1,),...  36.8 us
    ppermute x15, starting transfers between devices, swap(): return lax.ppermute(value, axis, [(j, j ^ distance) for j in range(size)])  15.4 us
  transfers between devices with their start and end apart: 18, of which 2 were waited for; matrix products, arithmetic and copies ran while one was open for 6% of the time, Pallas kernels for 35%

profile of v4, /device:TPU:0, one launch (start us, length us, event | category | flops | bytes accessed | tf_op | source)
XLA Modules:
  0.0 660.2 jit_solution(833234802232498477)
XLA Ops:
  2.1 5.0 collective-permute-start.5
  7.7 3.1 constant_dynamic-slice_fusion.10
  17.4 141.5 %shard_map.229 = (bf16[4,1024,1024]{2,1,0:T(8,128)(2,1)}, bf16[4,1024,768]{2,1,0:T(8,128)(2,1)}, bf16[1024,768]{1,0:T(8,128)(2,1)}) custom-call(f32[2,1024,1024]{2,1,0:T(8,128)} %x_ref.9, f32[1,1024]{1,0:T(1,128)} %bitcast.57, f32[1,1024]{1,0:T(1,128)} %bitcast.50, bf16[1024,768]{1,0:T(8,128)(2,1)} %copy.47.weight_ref), custom_call_target="tpu_custom_call" | custom-call | flops 149999992832 | bytes 1 | tf_op jit(solution)/shard_map/pallas_call | solution.py:1014
  164.3 3.1 constant_dynamic-slice_fusion.4
  168.1 22.2 %shard_map.230 = (bf16[4,512,256]{2,1,0:T(8,128)(2,1)}, f32[32,8,256]{2,1,0:T(8,128)}) custom-call(s32[4]{0:T(128)} %bitcast.72, s32[512]{0:T(512)} %min.12.lists_ref, s32[512]{0:T(512)} %reshape.175.admit_ref, bf16[4096,768]{1,0:T(8,128)(2,1)} %bitcast.61, bf16[4096,768]{1,0:T(8,128)(2,1)} %bitcast.62, bf16[4096,768]{1,0:T(8,128)(2,1)} %bitcast.63), custom_call_target="tpu_custom_call" | custom-call | flops 10737418240 | bytes 8388608 | tf_op jit(solution)/shard_map/pallas_call | solution.py:457
  191.6 3.2 collective-permute-start.7
  195.9 14.6 %shard_map.231 = (bf16[4,512,256]{2,1,0:T(8,128)(2,1)}, f32[32,8,256]{2,1,0:T(8,128)}) custom-call(s32[4]{0:T(128)} %bitcast.73, s32[512]{0:T(512)} %min.12.lists_ref, s32[512]{0:T(512)} %reshape.175.admit_ref, bf16[4096,768]{1,0:T(8,128)(2,1)} %bitcast.64, bf16[4096,768]{1,0:T(8,128)(2,1)} %bitcast.65, bf16[4096,768]{1,0:T(8,128)(2,1)} %bitcast.66), custom_call_target="tpu_custom_call" | custom-call | flops 10737418240 | bytes 8388608 | tf_op jit(solution)/shard_map/pallas_call | solution.py:457
  210.5 2.7 collective-permute-done.7
  215.5 3.7 collective-permute-done.12.down_far_ref
  220.5 37.5 %shard_map.232 = (bf16[512,1024]{1,0:T(8,128)(2,1)}, f32[512,1024]{1,0:T(8,128)}, bf16[4,512,256]{2,1,0:T(8,128)(2,1)}, bf16[1024,4096]{1,0:T(8,128)(2,1)}, bf16...) custom-call(s32[4]{0:T(128)} %bitcast.74, ...), custom_call_target="tpu_custom_call" | custom-call | flops 19327352832 | bytes 33554432 | tf_op jit(solution)/shard_map/pallas_call | solution.py:726
  258.0 34.9 %shard_map.233 = (bf16[512,1024]{1,0:T(8,128)(2,1)}, f32[512,1024]{1,0:T(8,128)}, bf16[4,512,256]{2,1,0:T(8,128)(2,1)}, bf16[1024,4096]{1,0:T(8,128)(2,1)}, bf16...) custom-call(s32[4]{0:T(128)} %bitcast.75, ...), custom_call_target="tpu_custom_call", output_to_operand_aliasing={{3}: (18, {}), {4}: (19, {}), {5}: (20, {}), {6}: (21, {}),... | custom-call | flops 19327352832 | bytes 33554432 | tf_op jit(solution)/shard_map/pallas_call | solution.py:726
  292.9 43.5 %shard_map.234 = (bf16[1024,1024]{1,0:T(8,128)(2,1)}, bf16[1024,1024]{1,0:T(8,128)(2,1)}, bf16[1024,1024]{1,0:T(8,128)(2,1)}, bf16[1024,1024]{1,0:T(8,128)(2,1)}...) custom-call(bf16[1024,1024]{1,0:T(8,128)(2,1)} %get-tuple-element.12, ...), custom_call_target="tpu_custom_call" | custom-call | flops 19327352832 | bytes 16777216 | tf_op jit(solution)/shard_map/pallas_call | solution.py:1764
  342.7 2.3 constant_dynamic-slice_fusion.2
  348.2 46.8 %shard_map.236 = bf16[4096,768]{1,0:T(8,128)(2,1)} custom-call(s32[4]{0:T(128)} %bitcast.76, s32[512]{0:T(512)} %min.12.lists_ref, s32[512]{0:T(512)} %reshape.175.admit_ref, bf16[4096,768]{1,0:T(8,128)(2,1)} %bitcast.67, bf16[4096,768]{1,0:T(8,128)(2,1)} %bitcast.68, bf16[4096,768]{1,0:T(8,128)(2,1)} %bitcast.69, ...), custom_call_target="tpu_custom_call" | custom-call | flops 32212254720 | bytes 20971520 | tf_op jit(solution)/shard_map/pallas_call | solution.py:479
  395.0 11.1 %convolution_convert_fusion = bf16[1024,768]{1,0:T(8,128)(2,1)S(1)} fusion(bf16[4096,1024]{1,0:T(8,128)(2,1)} %bitcast.60, bf16[4096,768]{1,0:T(8,128)(2,1)} %shard_map.236), kind=kOutput, calls=%fused_computation.6 | convolution fusion | flops 6443237376 | bytes 16252928 | tf_op jit(solution)/shard_map/dot_general | solution.py:191
  408.2 6.6 shard_map.235
  416.5 1.9 add_convert_fusion.4.rest_3_
  418.5 2.8 add_convert_fusion.1.rest_0_
  421.3 2.7 add_convert_fusion.2.rest_1_
  424.0 3.9 add_convert_fusion.rest_2_.rest_5_
  427.9 81.8 %shard_map.237 = (bf16[512,1024]{1,0:T(8,128)(2,1)}, f32[8,1024]{1,0:T(8,128)}, f32[8,896]{1,0:T(8,128)}, bf16[512,1024]{1,0:T(8,128)(2,1)}, bf16[1024,512]{1,0:...) custom-call(bf16[4,1024,768]{2,1,0:T(8,128)(2,1)} %bitcast.70, ...), custom_call_target="tpu_custom_call" | custom-call | flops 80000000000 | bytes 1 | tf_op jit(solution)/shard_map/pallas_call | solution.py:1571
  509.7 132.7 %shard_map.238 = (bf16[512,1024]{1,0:T(8,128)(2,1)}, f32[8,1024]{1,0:T(8,128)}, f32[8,256]{1,0:T(8,128)}, bf16[512,1024]{1,0:T(8,128)(2,1)}, bf16[512,1024]{1,0:...) custom-call(bf16[4,1024,768]{2,1,0:T(8,128)(2,1)} %bitcast.71, ...), custom_call_target="tpu_custom_call" | custom-call | flops 80000000000 | bytes 1 | tf_op jit(solution)/shard_map/pallas_call | solution.py:1571
  642.4 5.0 shard_map.240
  653.3 6.5 shard_map.239
  (116 shorter events, 39.7 us)
Async XLA Ops:
  0.6 12.2 %copy-start = (bf16[1024,3,512]{2,0,1:T(8,128)(2,1)S(1)}, bf16[1024,3,512]{2,0,1:T(8,128)(2,1)}, u32[]{:S(2)}) copy-start(bf16[1024,3,512]{2,0,1:T(8,128)(2,1)} %param.19) | copy-start | bytes 9437188
  2.1 157.8 %collective-permute-start.5 = (s32[16,3]{0,1:T(4,128)}, s32[16,3]{0,1:T(4,128)}, u32[]{:S(2)}, u32[]{:S(2)}) collective-permute-start(s32[16,3]{0,1:T(4,128)} %bitcast.35.clone.2), channel_id=1, source_target_pairs={{0,24},{8,16},{16,8},{24,0},{1,25},{9,17},{17,9},{25,1},{2,26},{10... | collective-permute-start | bytes 584 | tf_op jit(solution)/shard_map/ppermute | solution.py:1796
  7.1 154.2 %collective-permute-start.3 = (s32[16,3]{0,1:T(4,128)}, s32[16,3]{0,1:T(4,128)}, u32[]{:S(2)}, u32[]{:S(2)}) collective-permute-start(s32[16,3]{0,1:T(4,128)} %bitcast.35.clone.2), channel_id=1, source_target_pairs={{0,8},{8,0},{16,24},{24,16},{1,9},{9,1},{17,25},{25,17},{2,10},{10... | collective-permute-start | bytes 584 | tf_op jit(solution)/shard_map/ppermute | solution.py:1796
  7.1 154.2 %collective-permute-start.4 = (s32[16,3]{0,1:T(4,128)}, s32[16,3]{0,1:T(4,128)}, u32[]{:S(2)}, u32[]{:S(2)}) collective-permute-start(s32[16,3]{0,1:T(4,128)} %bitcast.35.clone.2), channel_id=1, source_target_pairs={{0,16},{8,24},{16,0},{24,8},{1,17},{9,25},{17,1},{25,9},{2,18},{10... | collective-permute-start | bytes 584 | tf_op jit(solution)/shard_map/ppermute | solution.py:1796
  10.8 153.5 %collective-permute-start = (bf16[1024,1024]{1,0:T(8,128)(2,1)}, bf16[1024,1024]{1,0:T(8,128)(2,1)}, u32[]{:S(2)}, u32[]{:S(2)}) collective-permute-start(bf16[1024,1024]{1,0:T(8,128)(2,1)} %constant_dynamic-slice_fusion.10), channel_id=1, source_target_pairs={{0,1},{1,0},{2,3},{3,2},{4,5},{5,4},{6,7},{7,6},{8,9},{9,8},{10,11... | collective-permute-start | bytes 6291464 | tf_op jit(solution)/shard_map/ppermute | solution.py:1796
  12.5 151.8 %collective-permute-start.1 = (bf16[512,1024]{1,0:T(8,128)(2,1)}, bf16[512,1024]{1,0:T(8,128)(2,1)}, u32[]{:S(2)}, u32[]{:S(2)}) collective-permute-start(bf16[512,1024]{1,0:T(8,128)(2,1)} %param.20), channel_id=1, source_target_pairs={{0,1},{1,0},{2,3},{3,2},{4,5},{5,4},{6,7},{7,6},{8,9},{9,8},{10,11... | collective-permute-start | bytes 3145736 | tf_op jit(solution)/shard_map/ppermute | solution.py:1796
  17.3 141.6 %copy-start.12 = (s32[2,4]{1,0:T(2,128)S(1)}, s32[2,4]{1,0:T(2,128)}, u32[]{:S(2)}) copy-start(s32[2,4]{1,0:T(2,128)} %param.15) | copy-start | bytes 100
  17.4 141.6 %copy-start.7 = (f32[2048]{0:T(1024)S(1)}, f32[2048]{0:T(1024)}, u32[]{:S(2)}) copy-start(f32[2048]{0:T(1024)} %param.24) | copy-start | bytes 24580
  159.9 4.4 collective-permute-start.2
  167.4 47.3 %collective-permute-start.10 = (bf16[1024,1024]{1,0:T(8,128)(2,1)}, bf16[1024,1024]{1,0:T(8,128)(2,1)}, u32[]{:S(2)}, u32[]{:S(2)}) collective-permute-start(bf16[1024,1024]{1,0:T(8,128)(2,1)} %constant_dynamic-slice_fusion.4), channel_id=1, source_target_pairs={{0,1},{1,0},{2,3},{3,2},{4,5},{5,4},{6,7},{7,6},{8,9},{9,8},{10,11... | collective-permute-start | bytes 6291464 | tf_op jit(solution)/shard_map/ppermute | solution.py:1796
  168.1 46.7 %collective-permute-start.9 = (bf16[1024,1024]{1,0:T(8,128)(2,1)}, bf16[1024,1024]{1,0:T(8,128)(2,1)}, u32[]{:S(2)}, u32[]{:S(2)}) collective-permute-start(bf16[1024,1024]{1,0:T(8,128)(2,1)} %collective-permute-done.up_near_ref), channel_id=1, source_target_pairs={{0,2},{2,0},{4,6},{6,4},{1,3},{3,1},{5,7},{7,5},{8,10},{10,8},{12,... | collective-permute-start | bytes 6291464 | tf_op jit(solution)/shard_map/ppermute | solution.py:1796
  191.5 18.9 %collective-permute-start.6 = (bf16[1,512,256]{2,1,0:T(8,128)(2,1)S(1)}, bf16[1,512,256]{2,1,0:T(8,128)(2,1)S(1)}, u32[]{:S(2)}, u32[]{:S(2)}) collective-permute-start(bf16[1,512,256]{2,1,0:T(8,128)(2,1)S(1)} %get-tuple-element.212), channel_id=1, source_target_pairs={{0,8},{8,16},{16,24},{24,0},{1,9},{9,17},{17,25},{25,1},{2,10},{10... | collective-permute-start | bytes 786440 | tf_op jit(solution)/shard_map/ppermute | solution.py:1817
  191.6 21.6 %collective-permute-start.7 = (bf16[1,512,256]{2,1,0:T(8,128)(2,1)S(1)}, bf16[1,512,256]{2,1,0:T(8,128)(2,1)S(1)}, u32[]{:S(2)}, u32[]{:S(2)}) collective-permute-start(bf16[1,512,256]{2,1,0:T(8,128)(2,1)S(1)} %get-tuple-element.211), channel_id=1, source_target_pairs={{0,16},{8,24},{16,0},{24,8},{1,17},{9,25},{17,1},{25,9},{2,18},{10... | collective-permute-start | bytes 786440 | tf_op jit(solution)/shard_map/ppermute | solution.py:1817
  194.8 18.4 %collective-permute-start.8 = (bf16[1,512,256]{2,1,0:T(8,128)(2,1)S(1)}, bf16[1,512,256]{2,1,0:T(8,128)(2,1)S(1)}, u32[]{:S(2)}, u32[]{:S(2)}) collective-permute-start(bf16[1,512,256]{2,1,0:T(8,128)(2,1)S(1)} %get-tuple-element.210), channel_id=1, source_target_pairs={{0,24},{8,0},{16,8},{24,16},{1,25},{9,1},{17,9},{25,17},{2,26},{10... | collective-permute-start | bytes 786440 | tf_op jit(solution)/shard_map/ppermute | solution.py:1817
  210.4 4.3 collective-permute-start.11
  214.8 4.4 collective-permute-start.12
  336.4 10.1 %copy-start.3 = (bf16[1024,1024]{1,0:T(8,128)(2,1)S(1)}, bf16[1024,1024]{1,0:T(8,128)(2,1)}, u32[]{:S(2)}) copy-start(bf16[1024,1024]{1,0:T(8,128)(2,1)} %get-tuple-element.133) | copy-start | bytes 6291460
  338.3 76.5 %collective-permute-start.17 = (bf16[1024,128]{1,0:T(8,128)(2,1)}, bf16[1024,128]{1,0:T(8,128)(2,1)}, u32[]{:S(2)}, u32[]{:S(2)}) collective-permute-start(bf16[1024,128]{1,0:T(8,128)(2,1)} %constant_dynamic-slice_fusion), channel_id=1, source_target_pairs={{0,4},{2,6},{4,0},{6,2},{1,5},{3,7},{5,1},{7,3},{8,12},{10,14},{12... | collective-permute-start | bytes 786440 | tf_op jit(solution)/shard_map/ppermute | solution.py:1796
  340.7 75.8 %collective-permute-start.16 = (bf16[1024,128]{1,0:T(8,128)(2,1)S(1)}, bf16[1024,128]{1,0:T(8,128)(2,1)}, u32[]{:S(2)}, u32[]{:S(2)}) collective-permute-start(bf16[1024,128]{1,0:T(8,128)(2,1)S(1)} %constant_dynamic-slice_fusion.1), channel_id=1, source_target_pairs={{0,4},{2,6},{4,0},{6,2},{1,5},{3,7},{5,1},{7,3},{8,12},{10,14},{12... | collective-permute-start | bytes 786440 | tf_op jit(solution)/shard_map/ppermute | solution.py:1796
  341.3 82.7 %collective-permute-start.15 = (bf16[1024,1024]{1,0:T(8,128)(2,1)}, bf16[1024,1024]{1,0:T(8,128)(2,1)}, u32[]{:S(2)}, u32[]{:S(2)}) collective-permute-start(bf16[1024,1024]{1,0:T(8,128)(2,1)} %get-tuple-element.136), channel_id=1, source_target_pairs={{0,1},{1,0},{2,3},{3,2},{4,5},{5,4},{6,7},{7,6},{8,9},{9,8},{10,11... | collective-permute-start | bytes 6291464 | tf_op jit(solution)/shard_map/ppermute | solution.py:1796
  345.0 73.5 %collective-permute-start.14 = (bf16[1024,512]{1,0:T(8,128)(2,1)}, bf16[1024,512]{1,0:T(8,128)(2,1)}, u32[]{:S(2)}, u32[]{:S(2)}) collective-permute-start(bf16[1024,512]{1,0:T(8,128)(2,1)} %constant_dynamic-slice_fusion.2), channel_id=1, source_target_pairs={{0,4},{2,6},{4,0},{6,2},{1,5},{3,7},{5,1},{7,3},{8,12},{10,14},{12... | collective-permute-start | bytes 3145736 | tf_op jit(solution)/shard_map/ppermute | solution.py:1796
  346.6 74.6 %collective-permute-start.13 = (bf16[1024,512]{1,0:T(8,128)(2,1)S(1)}, bf16[1024,512]{1,0:T(8,128)(2,1)}, u32[]{:S(2)}, u32[]{:S(2)}) collective-permute-start(bf16[1024,512]{1,0:T(8,128)(2,1)S(1)} %constant_dynamic-slice_fusion.3), channel_id=1, source_target_pairs={{0,4},{2,6},{4,0},{6,2},{1,5},{3,7},{5,1},{7,3},{8,12},{10,14},{12... | collective-permute-start | bytes 3145736 | tf_op jit(solution)/shard_map/ppermute | solution.py:1796
  395.0 11.2 %copy-start.8 = (f32[8,1024]{1,0:T(8,128)S(1)}, f32[8,1024]{1,0:T(8,128)}, u32[]{:S(2)}) copy-start(f32[8,1024]{1,0:T(8,128)} %get-tuple-element.142) | copy-start | bytes 98308
  395.0 11.2 %copy-start.9 = (f32[8,1024]{1,0:T(8,128)S(1)}, f32[8,1024]{1,0:T(8,128)}, u32[]{:S(2)}) copy-start(f32[8,1024]{1,0:T(8,128)} %get-tuple-element.143) | copy-start | bytes 98308
  (7 other events, 26.4 us)

commit v5 on v4

--- a/solution.py
+++ b/solution.py
@@ -1105,25 +1105,18 @@
 class Extra:
     def __init__(self, kind, source, target, sems):
         self.source, self.target, self.sems = source, target, sems
-        batch, place, me = lax.axis_index("batch"), lax.axis_index("mp"), lax.axis_index("seq")
+        batch, place = lax.axis_index("batch"), lax.axis_index("mp")
         self.local = None
         if kind == "mp":
             self.moves = [(source, target, {"mp": 1 - place})]
-        elif kind == "chip":
-            side = (batch // 2) % 2
-            size = source.shape[1] // 2
-            there = pl.ds(pl.multiple_of((1 - side) * size, 128), size)
-            self.moves = [(source.at[:, there], target, {"batch": batch + 2 - 4 * side})]
         else:
             count = source.shape[0]
             pairs = lax.axis_size("mp")
-            mine = me if kind == "line" else batch * pairs + place
+            mine = batch * pairs + place
             self.moves = []
             for distance in range(1, count):
                 other = lax.rem(mine + distance, count)
                 device = {"batch": other // pairs, "mp": lax.rem(other, pairs)}
-                if kind == "line":
-                    device = {"seq": other}
                 self.moves.append((source.at[other], target.at[mine], device))
             self.local = (source.at[mine], target.at[mine])
 
@@ -1149,13 +1142,8 @@
             copy.wait()
 
 
-def extra_target(kind, source):
-    rows, *rest = source.shape
-    return (rows, rest[0] // 2) if kind == "chip" else source.shape
-
-
 def extra_moves(kind, source):
-    return 1 if kind in ("mp", "chip") else source.shape[0]
+    return 1 if kind == "mp" else source.shape[0]
 
 
 def in_rows(vectors, width):
@@ -1166,9 +1154,66 @@
     return jnp.concatenate(pieces, axis=0)
 
 
+class WeightBegin:
+    def __init__(self, terms, targets, near_sum, own_sum, down_sum, sems):
+        self.terms, self.targets, self.sems = terms, targets, sems
+        self.near_sum, self.own_sum, self.down_sum = near_sum, own_sum, down_sum
+
+    def copies(self):
+        own_out, near_target, down_out, down_target = self.targets
+        batch, place = lax.axis_index("batch"), lax.axis_index("mp")
+        side = (batch // 2) % 2
+        size = self.down_sum.shape[1] // 2
+        kept = pl.ds(pl.multiple_of(side * size, 128), size)
+        there = pl.ds(pl.multiple_of((1 - side) * size, 128), size)
+        return [
+            pltpu.make_async_remote_copy(
+                src_ref=self.near_sum,
+                dst_ref=near_target,
+                send_sem=self.sems.at[0],
+                recv_sem=self.sems.at[1],
+                device_id={"mp": 1 - place},
+                device_id_type=MESH,
+            ),
+            pltpu.make_async_remote_copy(
+                src_ref=self.down_sum.at[:, there],
+                dst_ref=down_target,
+                send_sem=self.sems.at[2],
+                recv_sem=self.sems.at[3],
+                device_id={"batch": batch + 2 - 4 * side},
+                device_id_type=MESH,
+            ),
+            pltpu.make_async_copy(self.own_sum, own_out, self.sems.at[4]),
+            pltpu.make_async_copy(self.down_sum.at[:, kept], down_out, self.sems.at[5]),
+        ]
+
+    def start(self):
+        keep, come, down, down_come = self.terms
+        rows = keep.shape[1]
+        step = min(128, rows)
+
+        def add(index, _):
+            here = pl.ds(pl.multiple_of(index * step, step), step)
+            near = keep[1, here, :].astype(F32) + come[1, here, :].astype(F32)
+            own = keep[0, here, :].astype(F32) + come[0, here, :].astype(F32)
+            low = down[here, :].astype(F32) + down_come[here, :].astype(F32)
+            self.near_sum[here, :] = near.astype(BF16)
+            self.own_sum[here, :] = own.astype(BF16)
+            self.down_sum[here, :] = low.astype(BF16)
+            return 0
+
+        lax.fori_loop(0, rows // step, add, 0)
+        for copy in self.copies():
+            copy.start()
+
+    def finish(self):
+        for copy in self.copies():
+            copy.wait()
+
+
 class WeightChain:
     def __init__(self, terms, qkv_terms, gathered, heads_ref, sending, received, result, head_sum, heads_in, sems):
-        self.up, self.up_come, self.out, self.out_come, self.down, self.down_come = terms
+        self.terms = terms
         self.qkv_terms, self.gathered, self.heads_ref = qkv_terms, gathered, heads_ref
         self.sending, self.received, self.result = sending, received, result
         self.head_sum, self.heads_in, self.sems = head_sum, heads_in, sems
@@ -1187,14 +1232,8 @@
 
     def term(self, target, chunk):
         here = pl.ds(pl.multiple_of(target * self.rows + chunk * self.step, self.step), self.step)
-        size = self.down.shape[1] // 2
-        kept = pl.ds(pl.multiple_of((self.batch // 2) % 2 * size, 128), size)
-        pairs = (
-            (self.up[here, :], self.up_come[here, :]),
-            (self.down[here, kept], self.down_come[here, :]),
-            (self.out[here, :], self.out_come[here, :]),
-        )
-        return jnp.concatenate([own.astype(F32) + come.astype(F32) for own, come in pairs], axis=1)
+        own, own_come, down, down_come = (term[here, :].astype(F32) for term in self.terms)
+        return jnp.concatenate([own + own_come, down + down_come], axis=1)
 
     def send(self, side, message, chunk):
         which = (side * (self.count - 1) + message) * self.chunks + chunk
@@ -1347,6 +1386,7 @@
     kinds,
     parts_ref,
     weight_ref,
+    edge_weight_ref,
     x_ref,
     hidden_grad_ref,
     gain_ref,
@@ -1355,14 +1395,13 @@
 ):
     extras = len(kinds)
     sources, rest = rest[:extras], rest[extras:]
+    weight_terms, rest = rest[:4], rest[4:]
     if index_of:
-        *weight_terms, qkv_terms = rest[:7]
-        rest = rest[7:]
+        qkv_terms, *rest = rest
     input_ref, sums_ref, total_ref, other_ref, *rest = rest
     targets, rest = rest[:extras], rest[extras:]
-    if index_of:
-        gathered, heads_ref, *rest = rest
-    rows_in, sending, received, group, line, load_sem, *rest = rest
+    late_out, rest = (rest[:2], rest[2:]) if index_of else (rest[:4], rest[4:])
+    rows_in, sending, received, edge_in, summed, group, line, load_sem, *rest = rest
     send_sems, recv_sems, pair_send_sems, pair_recv_sems, vector_sems, *extra_sems = rest
     late = extra_sems[extras:]
     extras = [Extra(*each) for each in zip(kinds, sources, targets, extra_sems)]
@@ -1395,6 +1434,17 @@
             device_id_type=MESH,
         )
 
+    def send_edge(side, message, chunk):
+        target = (1 - side) * (count - 1 - message) + side * message
+        return pltpu.make_async_remote_copy(
+            src_ref=parts_ref.at[target, at(chunk)],
+            dst_ref=edge_in.at[message, at(chunk)],
+            send_sem=send_sems.at[side, message, chunk],
+            recv_sem=recv_sems.at[side, message, chunk],
+            device_id={"seq": me + 1 - 2 * side},
+            device_id_type=MESH,
+        )
+
     def flow(side, index):
         message = index // chunks
         chunk = index % chunks
@@ -1402,26 +1452,35 @@
 
         @pl.when((target - me) * (1 - 2 * side) > 0)
         def _():
-            total = dot_nt(parts_ref[target, at(chunk), :], weight_ref[...])
             first = (1 - side) * me + side * (count - 1 - me)
 
             @pl.when(first == 0)
             def _():
+                send_edge(side, message, chunk).start()
+
+            @pl.when(first == 1)
+            def _():
+                send_edge(side, message, chunk).wait_recv()
+                total = dot_nt(parts_ref[target, at(chunk), :], weight_ref[...])
+                total = total + dot_nt(edge_in[message, at(chunk), :], edge_weight_ref[...])
                 sending[side, message, at(chunk), :] = total.astype(BF16)
-
-            @pl.when(first > 0)
+                send(side, message, chunk).start()
+
+            @pl.when(first > 1)
             def _():
+                total = dot_nt(parts_ref[target, at(chunk), :], weight_ref[...])
                 send(side, message, chunk).wait_recv()
                 come = received[side, message, at(chunk), :].astype(F32)
                 sending[side, message, at(chunk), :] = (total + come).astype(BF16)
-
-            send(side, message, chunk).start()
+                send(side, message, chunk).start()
 
     if index_of:
-        chain = WeightChain(weight_terms, qkv_terms, gathered, heads_ref, *late)
+        chain = WeightChain(weight_terms, qkv_terms, *late_out, *late)
         chain.start()
+        begin = None
     else:
         chain = None
+        begin = WeightBegin(weight_terms, late_out, *late)
     ahead = chain.steps if chain else 0
     near = me // (count // 2)
 
@@ -1437,19 +1496,22 @@
 
     def own(chunk):
         here = at(chunk)
-        total = dot_nt(parts_ref[me, here, :], weight_ref[...])
-
-        @pl.when(me > 0)
-        def _():
-            send(0, count - 1 - me, chunk).wait_recv()
-
-        @pl.when(me < count - 1)
-        def _():
-            send(1, me, chunk).wait_recv()
-
-        left = received[0, jnp.minimum(count - 1 - me, count - 2), here, :].astype(F32)
-        right = received[1, jnp.minimum(me, count - 2), here, :].astype(F32)
-        total = total + jnp.where(me > 0, left, 0.0) + jnp.where(me < count - 1, right, 0.0)
+        summed[...] = dot_nt(parts_ref[me, here, :], weight_ref[...])
+        for side in range(2):
+            first = me if side == 0 else count - 1 - me
+            message = count - 1 - me if side == 0 else me
+
+            @pl.when(first == 1)
+            def _():
+                send_edge(side, message, chunk).wait_recv()
+                summed[...] += dot_nt(edge_in[message, here, :], edge_weight_ref[...])
+
+            @pl.when(first > 1)
+            def _():
+                send(side, message, chunk).wait_recv()
+                summed[...] += received[side, message, here, :].astype(F32)
+
+        total = summed[...]
         unit, inverse = row_stats(rows_in[here, :])
         scaled = total * gain_ref[...]
         through = (
@@ -1488,6 +1550,11 @@
         def _():
             flow_of(1 - near, index - lag)
 
+        if begin is not None:
+            @pl.when(index == 2)
+            def _():
+                begin.start()
+
         if chain is not None:
 
             @pl.when(index == ahead + lag + 2)
@@ -1513,13 +1580,21 @@
         message = index // chunks
         chunk = index % chunks
 
-        @pl.when(count - 1 - message > me)
+        @pl.when((count - 1 - message > me) & (me > 0))
         def _():
             send(0, message, chunk).wait_send()
 
-        @pl.when(message < me)
+        @pl.when((count - 1 - message > me) & (me == 0))
+        def _():
+            send_edge(0, message, chunk).wait_send()
+
+        @pl.when((message < me) & (me < count - 1))
         def _():
             send(1, message, chunk).wait_send()
+
+        @pl.when((message < me) & (me == count - 1))
+        def _():
+            send_edge(1, message, chunk).wait_send()
 
         return 0
 
@@ -1534,12 +1609,14 @@
     total_ref[...] = vector_sum.finish()
     if chain is not None:
         chain.finish()
+    else:
+        begin.finish()
     for extra in extras:
         extra.finish()
 
 
 def return_part(
-    index, parts, weight, layer_input, hidden_grad, gain, vectors, extras, weight_terms=(), qkv_terms=None
+    index, parts, weight, edge_weight, layer_input, hidden_grad, gain, vectors, extras, weight_terms, qkv_terms=None
 ):
     count, rows, cols = parts.shape
     rows = rows // 2
@@ -1548,11 +1625,20 @@
     members = lax.axis_size("batch") * lax.axis_size("mp")
     small = (8, 2 * width // 8) if index else vectors.shape
     kinds, sources = [kind for kind, _ in extras], [source for _, source in extras]
-    late_in, late_out, late_scratch = [], [], []
-    if index:
-        late_in = [*weight_terms, qkv_terms]
-        up, _, out, *_ = weight_terms
-        part = (width // count, 2 * up.shape[1] + out.shape[1])
+    late_in = [*weight_terms]
+    if not index:
+        keep, _, down, _ = weight_terms
+        half = (width, down.shape[1] // 2)
+        late_out = [keep.shape[1:], keep.shape[1:], half, half]
+        late_scratch = [
+            pltpu.VMEM(keep.shape[1:], BF16),
+            pltpu.VMEM(keep.shape[1:], BF16),
+            pltpu.VMEM(down.shape, BF16),
+            pltpu.SemaphoreType.DMA((6,)),
+        ]
+    else:
+        late_in = late_in + [qkv_terms]
+        part = (width // count, weight_terms[0].shape[1] + weight_terms[2].shape[1])
         batches = lax.axis_size("batch")
         head = qkv_terms.shape[2:]
         late_out = [(batches,) + part, (members, count // 2) + head]
@@ -1574,6 +1660,7 @@
         in_specs=[
             pl.BlockSpec((count, rows, cols), lambda step: (0, index, 0)),
             pl.BlockSpec((width, cols), fixed),
+            pl.BlockSpec((width, cols), fixed),
             any_spec,
             pl.BlockSpec((rows, width), fixed),
             pl.BlockSpec((1, width), fixed),
@@ -1594,12 +1681,14 @@
             jax.ShapeDtypeStruct(small, F32),
             jax.ShapeDtypeStruct((rows, width), BF16),
         ]
-        + [jax.ShapeDtypeStruct(extra_target(*extra), BF16) for extra in extras]
+        + [jax.ShapeDtypeStruct(source.shape, BF16) for source in sources]
         + [jax.ShapeDtypeStruct(shape, BF16) for shape in late_out],
         scratch_shapes=[
             pltpu.VMEM((rows, width), F32),
             pltpu.VMEM((2, count - 1, rows, width), BF16),
             pltpu.VMEM((2, count - 1, rows, width), BF16),
+            pltpu.VMEM((count - 1, rows, cols), BF16),
+            pltpu.VMEM((rows // chunks, width), F32),
             pltpu.VMEM((members,) + small, F32),
             pltpu.VMEM((count,) + small, F32),
             dma((1,)),
@@ -1615,7 +1704,7 @@
             collective_id=1 + index, has_side_effects=True, vmem_limit_bytes=VMEM_LIMIT
         ),
         cost_estimate=pl.CostEstimate(flops=80_000_000_000, bytes_accessed=1, transcendentals=0),
-    )(parts, weight, layer_input, hidden_grad, gain, vectors, *sources, *late_in)
+    )(parts, weight, edge_weight, layer_input, hidden_grad, gain, vectors, *sources, *late_in)
 
 
 def weight_grad_kernel(
@@ -1628,12 +1717,10 @@
     att_ref,
     trade_source,
     pair_source,
-    up_own,
-    up_near,
+    keep,
+    away,
     down_own,
     down_near,
-    out_own,
-    out_near,
     trade_target,
     pair_target,
     turned,
@@ -1658,18 +1745,32 @@
     trade = Trade(trade_source, trade_target, *trade_sems, (pair_source, pair_target, pair_sems))
     trade.start(1)
 
+    depth = slots.shape[0]
     piece = units // 4
     head_piece = width // 4
+    side = (me // 2) % 2
     jobs = []
-    for matrix, source, own, near in ((0, pre_ref, up_own, up_near), (1, act_ref, down_own, down_near)):
+    for half, first_sent, first_kept in (
+        (0, (1 - parity) * piece, parity * piece),
+        (1, 3 * piece, 2 * piece),
+    ):
+        for target, start in ((away, (1 - side) * tile), (keep, side * tile)):
+            puts = [(0, tile, target.at[half], 0)]
+            jobs.append((0, pre_ref, tile, first_sent + start, first_kept + start, puts))
+    for target, first_sent, first_kept in (
+        (down_near, 3 * piece, 2 * piece),
+        (down_own, (1 - parity) * piece, parity * piece),
+    ):
         for start in range(0, piece, tile):
-            jobs.append(
-                (matrix, source, tile, (1 - parity) * piece + start, parity * piece + start, own, start)
-            )
-        for start in range(0, piece, tile):
-            jobs.append((matrix, source, tile, 3 * piece + start, 2 * piece + start, near, start))
-    for side, target in ((place, out_own), (1 - place, out_near)):
-        first = 2 * side * head_piece
+            puts = [(0, tile, target, start)]
+            jobs.append((1, act_ref, tile, first_sent + start, first_kept + start, puts))
+    for half, owner in ((0, place), (1, 1 - place)):
+        first = 2 * owner * head_piece
+        size = head_piece // 2
+        puts = [
+            (side * size, size, keep.at[half], tile),
+            ((1 - side) * size, size, away.at[half], tile),
+        ]
         jobs.append(
             (
                 2,
@@ -1677,8 +1778,7 @@
                 head_piece,
                 first + (1 - parity) * head_piece,
                 first + parity * head_piece,
-                target,
-                0,
+                puts,
             )
         )
     count = len(jobs)
@@ -1690,8 +1790,8 @@
         start = jobs[job][which]
         return pltpu.make_async_copy(
             source.at[:, pl.ds(pl.multiple_of(start, 128), size)],
-            slots.at[index % 2, :, pl.ds(0, size)],
-            slot_sems.at[index % 2],
+            slots.at[index % depth, :, pl.ds(0, size)],
+            slot_sems.at[index % depth],
         )
 
     def exchange(job):
@@ -1706,13 +1806,21 @@
         )
 
     def put(job):
-        size, target, start = jobs[job][2], jobs[job][5], jobs[job][6]
-        return pltpu.make_async_copy(
-            received.at[job, :, pl.ds(0, size)], target.at[:, pl.ds(start, size)], out_sems.at[job]
-        )
-
-    fetch(0).start()
-    block = min(256, width)
+        copies = []
+        for which, (first, size, target, start) in enumerate(jobs[job][5]):
+            from_here = pl.ds(first if isinstance(first, int) else pl.multiple_of(first, 128), size)
+            copies.append(
+                pltpu.make_async_copy(
+                    received.at[job, :, from_here],
+                    target.at[:, pl.ds(start, size)],
+                    out_sems.at[which, job],
+                )
+            )
+        return copies
+
+    for index in range(depth - 1):
+        fetch(index).start()
+    block = min(1024, width)
     for matrix, source in enumerate((second_ref, grad_ref, hidden_ref)):
 
         def turn(index, _):
@@ -1725,14 +1833,14 @@
     for index, (job, which) in enumerate(order):
         matrix, _, size, *_ = jobs[job]
         fetch(index).wait()
-        if index + 1 < len(order):
-            fetch(index + 1).start()
+        if index + depth - 1 < len(order):
+            fetch(index + depth - 1).start()
         if which == 4:
             exchange(job).wait_recv()
 
         def multiply(part, _):
             here = pl.ds(pl.multiple_of(part * block, block), block)
-            total = dot_nn(turned[matrix, here, :], slots[index % 2, :, 0:size])
+            total = dot_nn(turned[matrix, here, :], slots[index % depth, :, 0:size])
             if which == 3:
                 sending[job, here, 0:size] = total.astype(BF16)
             else:
@@ -1744,10 +1852,12 @@
         if which == 3:
             exchange(job).start()
         else:
-            put(job).start()
+            for copy in put(job):
+                copy.start()
     for job in range(count):
         exchange(job).wait_send()
-        put(job).wait()
+        for copy in put(job):
+            copy.wait()
     trade.finish()
 
 
@@ -1755,28 +1865,28 @@
     rows, width = second_low.shape
     units = pre_grad.shape[1]
     piece = units // 4
-    tile = min(512, piece)
-    jobs = 4 * (piece // tile) + 2
+    tile = piece // 2
+    jobs = 10
     any_spec = pl.BlockSpec(memory_space=pl.ANY)
     vmem = pl.BlockSpec(memory_space=pltpu.VMEM)
     dma = pltpu.SemaphoreType.DMA
-    shapes = [(width, piece)] * 4 + [(width, width // 4)] * 2
+    shapes = [(2, width, tile + width // 8)] * 2 + [(width, piece)] * 2
     return pl.pallas_call(
         functools.partial(weight_grad_kernel, tile),
         in_specs=[vmem] * 3 + [any_spec] * 5,
-        out_specs=[any_spec] * 8,
+        out_specs=[any_spec] * 6,
         out_shape=[
             jax.ShapeDtypeStruct(shape, BF16) for shape in shapes + [source.shape, pair.shape]
         ],
         scratch_shapes=[
             pltpu.VMEM((3, width, rows), BF16),
-            pltpu.VMEM((2, rows, tile), BF16),
+            pltpu.VMEM((3, rows, tile), BF16),
             pltpu.VMEM((jobs, width, tile), BF16),
             pltpu.VMEM((jobs, width, tile), BF16),
-            dma((2,)),
+            dma((3,)),
             dma((jobs,)),
             dma((jobs,)),
-            dma((jobs,)),
+            dma((2, jobs)),
             dma((2,)),
         ]
         + trade_scratch(source.shape[0]),
@@ -1851,13 +1961,6 @@
     return (mine.astype(F32) + received.astype(F32)).astype(BF16)
 
 
-def halve(value, distance, axis):
-    side = (lax.axis_index("batch") // distance) % 2
-    return narrow_add(
-        pick(value, side, 2, axis), swap(pick(value, 1 - side, 2, axis), "batch", distance)
-    )
-
-
 def assemble_kernel(unit_cols, pieces, heads, up_ref, down_ref, out_ref, qkv_ref):
     batch = lax.axis_index("batch")
     batches = pieces.shape[0]
@@ -1870,8 +1973,8 @@
         start = 0
         for size, target, turn in (
             (unit_cols, up_ref, False),
+            (pieces.shape[2] - 2 * unit_cols, out_ref, True),
             (unit_cols, down_ref, True),
-            (pieces.shape[2] - 2 * unit_cols, out_ref, True),
         ):
             value = pieces[index, :, start : start + size].astype(F32)
             here = pl.ds(pl.multiple_of(slot * size, 128), size)
@@ -2034,7 +2137,7 @@
     sums = results[0][3][:3] + results[1][3][:3]
     unit_sums = results[0][4][0] + results[1][4][0]
     bias_sums = [unit_sums[:units], unit_sums[units : units * 3 // 2], unit_sums[units * 3 // 2 :]]
-    up_own, up_near, down_own, down_near, out_own, out_near, grad_second, other_second = weight_grads(
+    keep, away, down_own, down_near, grad_second, other_second = weight_grads(
         second_low, grad_low, hidden_low, pre_grad, activated, attended_low, source, pair
     )
     outputs, other_outputs = [result[0] for result in results], [other_output, other_second]
@@ -2048,11 +2151,10 @@
         jnp.concatenate([bias_sums[0], bias_other]),
         jnp.concatenate([bias_other, bias_sums[0]]),
     )
-    levels = levels_of("batch")
-    for distance in levels[1:]:
-        up_own, up_near = halve(up_own, distance, 1), halve(up_near, distance, 1)
-        out_own, out_near = halve(out_own, distance, 1), halve(out_near, distance, 1)
-    down_own = narrow_add(down_own, swap(down_near, "mp"))
+    qkv_cut, grad_second = lax.optimization_barrier((qkv_own, grad_second))
+    qkv_edge = lax.ppermute(qkv_cut, "seq", [(0, 1), (seq_count - 1, seq_count - 2)])
+
+    come, down_come = swap(away, "batch", 2), swap(down_near, "mp")
     qkv_low_grad = attention_backward(
         qkv,
         (attended_first, attended_second),
@@ -2066,36 +2168,39 @@
     members = lax.axis_size("batch") * 2
     mine = lax.axis_index("batch") * 2 + mp_index
     qkv_sum = qkv_sum.reshape(seq_count, members, -1, 3 * cols).transpose(1, 0, 2, 3)
-    qkv_low_grad, qkv_sum, up_own, up_near, down_own, out_own, out_near = lax.optimization_barrier(
-        (qkv_low_grad, qkv_sum, up_own, up_near, down_own, out_own, out_near)
+    qkv_low_grad, qkv_sum, come, down_come = lax.optimization_barrier(
+        (qkv_low_grad, qkv_sum, come, down_come)
     )
     parts = qkv_low_grad.reshape(seq_count, local_rows, 3 * cols)
     early = jnp.concatenate([sums, bias_all.reshape(-1, width)], axis=0)
-    input_first, first_sums, early, _, up_come, out_come, down_come, qkv_terms = return_part(
+    input_first, first_sums, early, _, qkv_terms, *weight_terms = return_part(
         0,
         parts,
         qkv_own,
+        qkv_edge,
         layer_input,
         results[0][1],
         first_gain[None],
         early.reshape(8, -1),
-        [("mp", up_near), ("mp", out_near), ("chip", down_own), ("group", qkv_sum)],
+        [("group", qkv_sum)],
+        (keep, come, down_own, down_come),
     )
     input_second, _, late, other_second, other_first, weights_back, qkv_back = return_part(
         1,
         parts,
         qkv_own,
+        qkv_edge,
         layer_input,
         results[1][1],
         first_gain[None],
         first_sums,
         [("mp", input_first)],
-        (up_own, up_come, out_own, out_come, down_own, down_come),
+        weight_terms,
         qkv_terms,
     )
     layer_output = both_sequences(outputs, other_outputs)
     input_grad = both_sequences([input_first, input_second], [other_first, other_second])
-    up_grad, down_grad, out_grad, qkv_grad = assemble(up_own.shape[1], weights_back, qkv_back)
+    up_grad, down_grad, out_grad, qkv_grad = assemble(units // 4, weights_back, qkv_back)
     early, late = early.reshape(-1), late.reshape(-1)
     up_bias_grad = lax.dynamic_slice_in_dim(early, 3 * width + mp_index * units, units)
     return (
@@ -2560,7 +2665,7 @@
         P("batch", "seq", None),
     )
     sizes = mesh.shape
-    by_heads = (1024 // sizes["seq"]) % 128 == 0 and sizes["batch"] == 4 and sizes["mp"] == 2
+    by_heads = sizes["seq"] in (4, 8) and sizes["batch"] == 4 and sizes["mp"] == 2
     return jax.shard_map(
         local if by_heads else local_by_blocks,
         mesh=mesh,

time: 667 us -> 621 us (0.931)
  Pallas kernels: 574 us -> 544 us
  other arithmetic: 17.7 us -> 5.42 us
    pallas_call x2, Pallas kernels: 214 us -> 193 us  [return_part(): pl.pallas_call(functools.partial(return_kernel, count, chunks, 2, index,...]
    convert_element_type x5 -> x0, other arithmetic: 13 us -> none  [narrow_add(): return (mine.astype(F32) + received.astype(F32)).astype(BF16)]
    pallas_call x1, Pallas kernels: 43.5 us -> 35.7 us  [weight_grads(): pl.pallas_call(functools.partial(weight_grad_kernel, tile), in_specs=[vme...]
    ppermute x15 -> x12, starting transfers between devices: 15.4 us -> 12.8 us  [swap(): return lax.ppermute(value, axis, [(j, j ^ distance) for j in range(size)])]
  transfers between devices with their start and end apart: 18 -> 16, of which waited for: 2 -> 2; matrix products, arithmetic and copies ran while one was open for 6% -> 4% of each run, Pallas kernels for 35% -> 38%
where the time goes in v5:
time: 621 us; the launch traced here: 614 us
  Pallas kernels  544 us (88%)
  local copies, waits for them, and re-layouts  25 us (4%)
  starting transfers between devices  20.5 us (3%)
  matrix products  11 us (2%)
  waiting for transfers between devices  6.76 us (1%)
    pallas_call x2, Pallas kernels, return_part(): pl.pallas_call(functools.partial(return_kernel, count, chunks, 2, index,...  193 us
    pallas_call x1, Pallas kernels, gather_project(): pl.pallas_call(functools.partial(gather_kernel, count, chunks, half_cols)...  142 us
    pallas_call x2, Pallas kernels, token_part(): pl.pallas_call(functools.partial(token_kernel, min(256, rows), index), gr...  72.6 us
    pallas_call x1, Pallas kernels, attention_backward(): pl.pallas_call(functools.partial(backward_kernel, heads), grid=(1,), in_s...  46.8 us
    pallas_call x2, Pallas kernels, attention_forward(): pl.pallas_call(functools.partial(forward_kernel, heads, half), grid=(1,),...  36.8 us
    pallas_call x1, Pallas kernels, weight_grads(): pl.pallas_call(functools.partial(weight_grad_kernel, tile), in_specs=[vme...  35.7 us
    ppermute x12, starting transfers between devices, swap(): return lax.ppermute(value, axis, [(j, j ^ distance) for j in range(size)])  12.8 us
    pallas_call x2, Pallas kernels, both_sequences(): pl.pallas_call(place_kernel, grid_spec=pltpu.PrefetchScalarGridSpec(num_s...  12.8 us
  transfers between devices with their start and end apart: 16, of which 2 were waited for; matrix products, arithmetic and copies ran while one was open for 4% of the time, Pallas kernels for 38%

profile of v5, /device:TPU:0, one launch (start us, length us, event | category | flops | bytes accessed | tf_op | source)
XLA Modules:
  0.0 614.0 jit_solution(9480984104491664415)
XLA Ops:
  2.1 5.0 collective-permute-start.5
  7.7 3.1 constant_dynamic-slice_fusion.6
  10.8 1.7 collective-permute-start
  14.1 1.7 copy.55
  17.4 141.5 %shard_map.229 = (bf16[4,1024,1024]{2,1,0:T(8,128)(2,1)}, bf16[4,1024,768]{2,1,0:T(8,128)(2,1)}, bf16[1024,768]{1,0:T(8,128)(2,1)}) custom-call(f32[2,1024,1024]{2,1,0:T(8,128)} %x_ref.9, f32[1,1024]{1,0:T(1,128)} %bitcast.57, f32[1,1024]{1,0:T(1,128)} %bitcast.50, bf16[1024,768]{1,0:T(8,128)(2,1)} %copy.47.weight_ref), custom_call_target="tpu_custom_call" | custom-call | flops 149999992832 | bytes 1 | tf_op jit(solution)/shard_map/pallas_call | solution.py:1014
  164.3 3.1 constant_dynamic-slice_fusion
  168.1 22.2 %shard_map.230 = (bf16[4,512,256]{2,1,0:T(8,128)(2,1)}, f32[32,8,256]{2,1,0:T(8,128)}) custom-call(s32[4]{0:T(128)} %bitcast.72, s32[512]{0:T(512)} %min.12.lists_ref, s32[512]{0:T(512)} %reshape.175.admit_ref, bf16[4096,768]{1,0:T(8,128)(2,1)} %bitcast.61, bf16[4096,768]{1,0:T(8,128)(2,1)} %bitcast.62, bf16[4096,768]{1,0:T(8,128)(2,1)} %bitcast.63), custom_call_target="tpu_custom_call" | custom-call | flops 10737418240 | bytes 8388608 | tf_op jit(solution)/shard_map/pallas_call | solution.py:457
  191.6 3.2 collective-permute-start.7
  195.6 14.6 %shard_map.231 = (bf16[4,512,256]{2,1,0:T(8,128)(2,1)}, f32[32,8,256]{2,1,0:T(8,128)}) custom-call(s32[4]{0:T(128)} %bitcast.73, s32[512]{0:T(512)} %min.12.lists_ref, s32[512]{0:T(512)} %reshape.175.admit_ref, bf16[4096,768]{1,0:T(8,128)(2,1)} %bitcast.64, bf16[4096,768]{1,0:T(8,128)(2,1)} %bitcast.65, bf16[4096,768]{1,0:T(8,128)(2,1)} %bitcast.66), custom_call_target="tpu_custom_call" | custom-call | flops 10737418240 | bytes 8388608 | tf_op jit(solution)/shard_map/pallas_call | solution.py:457
  210.2 3.0 collective-permute-done.7
  215.5 3.7 collective-permute-done.12.down_far_ref
  220.5 37.5 %shard_map.232 = (bf16[512,1024]{1,0:T(8,128)(2,1)}, f32[512,1024]{1,0:T(8,128)}, bf16[4,512,256]{2,1,0:T(8,128)(2,1)}, bf16[1024,4096]{1,0:T(8,128)(2,1)}, bf16...) custom-call(s32[4]{0:T(128)} %bitcast.74, ...), custom_call_target="tpu_custom_call" | custom-call | flops 19327352832 | bytes 33554432 | tf_op jit(solution)/shard_map/pallas_call | solution.py:726
  258.1 35.1 %shard_map.233 = (bf16[512,1024]{1,0:T(8,128)(2,1)}, f32[512,1024]{1,0:T(8,128)}, bf16[4,512,256]{2,1,0:T(8,128)(2,1)}, bf16[1024,4096]{1,0:T(8,128)(2,1)}, bf16...) custom-call(s32[4]{0:T(128)} %bitcast.75, ...), custom_call_target="tpu_custom_call", output_to_operand_aliasing={{3}: (18, {}), {4}: (19, {}), {5}: (20, {}), {6}: (21, {}),... | custom-call | flops 19327352832 | bytes 33554432 | tf_op jit(solution)/shard_map/pallas_call | solution.py:726
  295.7 35.7 %shard_map.234 = (bf16[2,1024,640]{2,1,0:T(8,128)(2,1)}, bf16[2,1024,640]{2,1,0:T(8,128)(2,1)}, bf16[1024,1024]{1,0:T(8,128)(2,1)}, bf16[1024,1024]{1,0:T(8,128)...) custom-call(bf16[1024,1024]{1,0:T(8,128)(2,1)} %get-tuple-element.118.second_ref, ...), custom_call_target="tpu_custom_call" | custom-call | flops 19327352832 | bytes 16777216 | tf_op jit(solution)/shard_map/pallas_call | solution.py:1874
  334.5 3.6 collective-permute-start.15
  338.1 46.8 %shard_map.236 = bf16[4096,768]{1,0:T(8,128)(2,1)} custom-call(s32[4]{0:T(128)} %bitcast.76, s32[512]{0:T(512)} %min.12.lists_ref, s32[512]{0:T(512)} %reshape.175.admit_ref, bf16[4096,768]{1,0:T(8,128)(2,1)} %bitcast.67, bf16[4096,768]{1,0:T(8,128)(2,1)} %bitcast.68, bf16[4096,768]{1,0:T(8,128)(2,1)} %bitcast.69, ...), custom_call_target="tpu_custom_call" | custom-call | flops 32212254720 | bytes 20971520 | tf_op jit(solution)/shard_map/pallas_call | solution.py:479
  384.9 11.0 %convolution_convert_fusion = bf16[1024,768]{1,0:T(8,128)(2,1)S(1)} fusion(bf16[4096,1024]{1,0:T(8,128)(2,1)} %bitcast.60, bf16[4096,768]{1,0:T(8,128)(2,1)} %shard_map.236), kind=kOutput, calls=%fused_computation.3 | convolution fusion | flops 6443237376 | bytes 16252928 | tf_op jit(solution)/shard_map/dot_general | solution.py:191
  397.2 6.3 %shard_map.235 = f32[2,1024,1024]{2,1,0:T(8,128)} custom-call(s32[1]{0:T(128)} %bitcast.place_ref, bf16[512,1024]{1,0:T(8,128)(2,1)} %get-tuple-element.107.pair_source.own_first, bf16[512,1024]{1,0:T(8,128)(2,1)} %get-tuple-element.116.pair_source.own_second, bf16[512,1024]{1,0:T(8,128)(2,1)} %get-tuple-element.117.other_first, ...), custom_call_target="tpu_custom_call" | custom-call | tf_op jit(solution)/shard_map/pallas_call | solution.py:2038
  403.5 68.6 %shard_map.237 = (bf16[512,1024]{1,0:T(8,128)(2,1)}, f32[8,1024]{1,0:T(8,128)}, f32[8,896]{1,0:T(8,128)}, bf16[512,1024]{1,0:T(8,128)(2,1)}, bf16[8,4,32,768]{3,...) custom-call(bf16[4,1024,768]{2,1,0:T(8,128)(2,1)} %bitcast.70, ...), custom_call_target="tpu_custom_call" | custom-call | flops 80000000000 | bytes 1 | tf_op jit(solution)/shard_map/pallas_call | solution.py:1657
  472.1 124.0 %shard_map.238 = (bf16[512,1024]{1,0:T(8,128)(2,1)}, f32[8,1024]{1,0:T(8,128)}, f32[8,256]{1,0:T(8,128)}, bf16[512,1024]{1,0:T(8,128)(2,1)}, bf16[512,1024]{1,0:...) custom-call(bf16[4,1024,768]{2,1,0:T(8,128)(2,1)} %bitcast.71, ...), custom_call_target="tpu_custom_call" | custom-call | flops 80000000000 | bytes 1 | tf_op jit(solution)/shard_map/pallas_call | solution.py:1657
  596.1 5.0 shard_map.240
  601.1 1.9 copy.53
  603.0 1.6 copy.54
  607.0 6.5 %shard_map.239 = f32[2,1024,1024]{2,1,0:T(8,128)} custom-call(s32[1]{0:T(128)} %bitcast.place_ref, bf16[512,1024]{1,0:T(8,128)(2,1)} %get-tuple-element.147.rest_0_.own_first, bf16[512,1024]{1,0:T(8,128)(2,1)} %get-tuple-element.155.own_second, bf16[512,1024]{1,0:T(8,128)(2,1)} %get-tuple-element.156.other_first, ...), custom_call_target="tpu_custom_call" | custom-call | tf_op jit(solution)/shard_map/pallas_call | solution.py:2038
  (95 shorter events, 26.0 us)
Async XLA Ops:
  0.6 12.2 %copy-start = (bf16[1024,3,512]{2,0,1:T(8,128)(2,1)S(1)}, bf16[1024,3,512]{2,0,1:T(8,128)(2,1)}, u32[]{:S(2)}) copy-start(bf16[1024,3,512]{2,0,1:T(8,128)(2,1)} %param.19) | copy-start | bytes 9437188
  2.1 157.8 %collective-permute-start.5 = (s32[16,3]{0,1:T(4,128)}, s32[16,3]{0,1:T(4,128)}, u32[]{:S(2)}, u32[]{:S(2)}) collective-permute-start(s32[16,3]{0,1:T(4,128)} %bitcast.35.clone.2), channel_id=1, source_target_pairs={{0,24},{8,16},{16,8},{24,0},{1,25},{9,17},{17,9},{25,1},{2,26},{10... | collective-permute-start | bytes 584 | tf_op jit(solution)/shard_map/ppermute | solution.py:1906
  7.1 154.2 %collective-permute-start.3 = (s32[16,3]{0,1:T(4,128)}, s32[16,3]{0,1:T(4,128)}, u32[]{:S(2)}, u32[]{:S(2)}) collective-permute-start(s32[16,3]{0,1:T(4,128)} %bitcast.35.clone.2), channel_id=1, source_target_pairs={{0,8},{8,0},{16,24},{24,16},{1,9},{9,1},{17,25},{25,17},{2,10},{10... | collective-permute-start | bytes 584 | tf_op jit(solution)/shard_map/ppermute | solution.py:1906
  7.1 154.2 %collective-permute-start.4 = (s32[16,3]{0,1:T(4,128)}, s32[16,3]{0,1:T(4,128)}, u32[]{:S(2)}, u32[]{:S(2)}) collective-permute-start(s32[16,3]{0,1:T(4,128)} %bitcast.35.clone.2), channel_id=1, source_target_pairs={{0,16},{8,24},{16,0},{24,8},{1,17},{9,25},{17,1},{25,9},{2,18},{10... | collective-permute-start | bytes 584 | tf_op jit(solution)/shard_map/ppermute | solution.py:1906
  10.8 153.5 %collective-permute-start = (bf16[1024,1024]{1,0:T(8,128)(2,1)}, bf16[1024,1024]{1,0:T(8,128)(2,1)}, u32[]{:S(2)}, u32[]{:S(2)}) collective-permute-start(bf16[1024,1024]{1,0:T(8,128)(2,1)} %constant_dynamic-slice_fusion.6), channel_id=1, source_target_pairs={{0,1},{1,0},{2,3},{3,2},{4,5},{5,4},{6,7},{7,6},{8,9},{9,8},{10,11... | collective-permute-start | bytes 6291464 | tf_op jit(solution)/shard_map/ppermute | solution.py:1906
  12.5 151.8 %collective-permute-start.1 = (bf16[512,1024]{1,0:T(8,128)(2,1)}, bf16[512,1024]{1,0:T(8,128)(2,1)}, u32[]{:S(2)}, u32[]{:S(2)}) collective-permute-start(bf16[512,1024]{1,0:T(8,128)(2,1)} %param.20), channel_id=1, source_target_pairs={{0,1},{1,0},{2,3},{3,2},{4,5},{5,4},{6,7},{7,6},{8,9},{9,8},{10,11... | collective-permute-start | bytes 3145736 | tf_op jit(solution)/shard_map/ppermute | solution.py:1906
  17.3 141.6 %copy-start.8 = (s32[2,4]{1,0:T(2,128)S(1)}, s32[2,4]{1,0:T(2,128)}, u32[]{:S(2)}) copy-start(s32[2,4]{1,0:T(2,128)} %param.15) | copy-start | bytes 100
  17.4 141.6 %copy-start.3 = (f32[2048]{0:T(1024)S(1)}, f32[2048]{0:T(1024)}, u32[]{:S(2)}) copy-start(f32[2048]{0:T(1024)} %param.24) | copy-start | bytes 24580
  159.9 4.4 collective-permute-start.2
  167.4 47.3 %collective-permute-start.10 = (bf16[1024,1024]{1,0:T(8,128)(2,1)}, bf16[1024,1024]{1,0:T(8,128)(2,1)}, u32[]{:S(2)}, u32[]{:S(2)}) collective-permute-start(bf16[1024,1024]{1,0:T(8,128)(2,1)} %constant_dynamic-slice_fusion), channel_id=1, source_target_pairs={{0,1},{1,0},{2,3},{3,2},{4,5},{5,4},{6,7},{7,6},{8,9},{9,8},{10,11... | collective-permute-start | bytes 6291464 | tf_op jit(solution)/shard_map/ppermute | solution.py:1906
  168.1 46.7 %collective-permute-start.9 = (bf16[1024,1024]{1,0:T(8,128)(2,1)}, bf16[1024,1024]{1,0:T(8,128)(2,1)}, u32[]{:S(2)}, u32[]{:S(2)}) collective-permute-start(bf16[1024,1024]{1,0:T(8,128)(2,1)} %collective-permute-done.up_near_ref), channel_id=1, source_target_pairs={{0,2},{2,0},{4,6},{6,4},{1,3},{3,1},{5,7},{7,5},{8,10},{10,8},{12,... | collective-permute-start | bytes 6291464 | tf_op jit(solution)/shard_map/ppermute | solution.py:1906
  191.5 18.7 %collective-permute-start.6 = (bf16[1,512,256]{2,1,0:T(8,128)(2,1)S(1)}, bf16[1,512,256]{2,1,0:T(8,128)(2,1)S(1)}, u32[]{:S(2)}, u32[]{:S(2)}) collective-permute-start(bf16[1,512,256]{2,1,0:T(8,128)(2,1)S(1)} %get-tuple-element.208), channel_id=1, source_target_pairs={{0,8},{8,16},{16,24},{24,0},{1,9},{9,17},{17,25},{25,1},{2,10},{10... | collective-permute-start | bytes 786440 | tf_op jit(solution)/shard_map/ppermute | solution.py:1927
  191.6 21.6 %collective-permute-start.7 = (bf16[1,512,256]{2,1,0:T(8,128)(2,1)S(1)}, bf16[1,512,256]{2,1,0:T(8,128)(2,1)S(1)}, u32[]{:S(2)}, u32[]{:S(2)}) collective-permute-start(bf16[1,512,256]{2,1,0:T(8,128)(2,1)S(1)} %get-tuple-element.207), channel_id=1, source_target_pairs={{0,16},{8,24},{16,0},{24,8},{1,17},{9,25},{17,1},{25,9},{2,18},{10... | collective-permute-start | bytes 786440 | tf_op jit(solution)/shard_map/ppermute | solution.py:1927
  194.8 18.4 %collective-permute-start.8 = (bf16[1,512,256]{2,1,0:T(8,128)(2,1)S(1)}, bf16[1,512,256]{2,1,0:T(8,128)(2,1)S(1)}, u32[]{:S(2)}, u32[]{:S(2)}) collective-permute-start(bf16[1,512,256]{2,1,0:T(8,128)(2,1)S(1)} %get-tuple-element.206), channel_id=1, source_target_pairs={{0,24},{8,0},{16,8},{24,16},{1,25},{9,1},{17,9},{25,17},{2,26},{10... | collective-permute-start | bytes 786440 | tf_op jit(solution)/shard_map/ppermute | solution.py:1927
  210.2 4.6 collective-permute-start.11
  214.8 4.4 collective-permute-start.12
  258.1 36.2 %copy-start.4 = (f32[8,1024]{1,0:T(8,128)S(1)}, f32[8,1024]{1,0:T(8,128)}, u32[]{:S(2)}) copy-start(f32[8,1024]{1,0:T(8,128)} %get-tuple-element.138) | copy-start | bytes 98308
  295.7 38.7 %copy-start.7 = (bf16[1024,768]{1,0:T(8,128)(2,1)S(1)}, bf16[1024,768]{1,0:T(8,128)(2,1)}, u32[]{:S(2)}) copy-start(bf16[1024,768]{1,0:T(8,128)(2,1)} %get-tuple-element.136.weight_ref) | copy-start | bytes 4718596
  331.4 72.1 %collective-permute-start.13 = (bf16[2,1024,640]{2,1,0:T(8,128)(2,1)}, bf16[2,1024,640]{2,1,0:T(8,128)(2,1)}, u32[]{:S(2)}, u32[]{:S(2)}) collective-permute-start(bf16[2,1024,640]{2,1,0:T(8,128)(2,1)} %get-tuple-element.133), channel_id=1, source_target_pairs={{0,4},{2,6},{4,0},{6,2},{1,5},{3,7},{5,1},{7,3},{8,12},{10,14},{12... | collective-permute-start | bytes 7864328 | tf_op jit(solution)/shard_map/ppermute | solution.py:1906
  333.0 70.5 %collective-permute-start.14 = (bf16[1024,1024]{1,0:T(8,128)(2,1)}, bf16[1024,1024]{1,0:T(8,128)(2,1)}, u32[]{:S(2)}, u32[]{:S(2)}) collective-permute-start(bf16[1024,1024]{1,0:T(8,128)(2,1)} %get-tuple-element.134), channel_id=1, source_target_pairs={{0,1},{1,0},{2,3},{3,2},{4,5},{5,4},{6,7},{7,6},{8,9},{9,8},{10,11... | collective-permute-start | bytes 6291464 | tf_op jit(solution)/shard_map/ppermute | solution.py:1906
  334.5 69.1 %collective-permute-start.15 = (bf16[1024,768]{1,0:T(8,128)(2,1)S(1)}, bf16[1024,768]{1,0:T(8,128)(2,1)}, u32[]{:S(2)}, u32[]{:S(2)}) collective-permute-start(bf16[1024,768]{1,0:T(8,128)(2,1)S(1)} %copy-done.7), channel_id=1, source_target_pairs={{0,8},{24,16},{1,9},{25,17},{2,10},{26,18},{3,11},{27,19},{4,12},{... | collective-permute-start | bytes 4718600 | tf_op jit(solution)/shard_map/ppermute | solution.py:2155
  603.0 1.6 copy-start.5
  603.0 2.8 copy-start.2
  607.0 6.5 %copy-start.1 = (bf16[1024,3,512]{2,0,1:T(8,128)(2,1)S(1)}, bf16[1024,3,512]{2,0,1:T(8,128)(2,1)}, u32[]{:S(2)}) copy-start(bf16[1024,3,512]{2,0,1:T(8,128)(2,1)} %param.19) | copy-start | bytes 9437188
  (1 other events, 1.3 us)

commit v6 on v5

--- a/solution.py
+++ b/solution.py
@@ -826,19 +826,25 @@
 def gather_kernel(
     count,
     chunks,
-    half_cols,
     x_ref,
     gain_ref,
     bias_ref,
     weight_ref,
+    out_ref,
+    up_ref,
+    up_bias_ref,
     all_ref,
     qkv_ref,
     own_ref,
+    out_other,
+    up_near,
+    up_bias_near,
     rows_in,
     shards,
     results,
     weight,
     weight_sems,
+    fetch_sems,
     load_sems,
     send_sems,
     recv_sems,
@@ -890,21 +896,52 @@
     over_chunks(lambda chunk: load(chunk).start())
     greet(me, count, 1 - place)
 
+    half_cols = weight_ref.shape[2]
     here = (me * cols) // half_cols == place
-    fetch = pltpu.make_async_remote_copy(
-        src_ref=weight_ref,
-        dst_ref=weight,
-        send_sem=weight_sems.at[0],
-        recv_sem=weight_sems.at[1],
-        device_id={"mp": 1 - place},
-        device_id_type=MESH,
-    )
-    copy = pltpu.make_async_copy(weight_ref, weight, weight_sems.at[2])
+    heads = pl.ds(pl.multiple_of((me * cols) % half_cols, 128), cols)
+    fetches, copies = [], []
+    for matrix in range(3):
+        source = weight_ref.at[matrix, :, heads]
+        target = weight.at[:, pl.ds(matrix * cols, cols)]
+        fetches.append(
+            pltpu.make_async_remote_copy(
+                src_ref=source,
+                dst_ref=target,
+                send_sem=weight_sems.at[0, matrix],
+                recv_sem=weight_sems.at[1, matrix],
+                device_id={"mp": 1 - place},
+                device_id_type=MESH,
+            )
+        )
+        copies.append(pltpu.make_async_copy(source, target, weight_sems.at[2, matrix]))
 
     @pl.when(here)
     def _():
-        fetch.start()
-        copy.start()
+        for each in fetches + copies:
+            each.start()
+
+    parity = lax.axis_index("batch") % 2
+    share = up_near.shape[1]
+    columns = pl.ds(pl.multiple_of(parity * share, share), share)
+    shares = [
+        pltpu.make_async_remote_copy(
+            src_ref=source,
+            dst_ref=target,
+            send_sem=fetch_sems.at[0, which],
+            recv_sem=fetch_sems.at[1, which],
+            device_id={"mp": 1 - place},
+            device_id_type=MESH,
+        )
+        for which, (source, target) in enumerate(
+            (
+                (out_ref, out_other),
+                (up_ref.at[:, columns], up_near),
+                (up_bias_ref.at[:, columns], up_bias_near),
+            )
+        )
+    ]
+    for each in shares:
+        each.start()
 
     def norm(chunk):
         load(chunk).wait()
@@ -955,13 +992,15 @@
 
     @pl.when(here)
     def _():
-        copy.wait()
+        for each in copies:
+            each.wait()
 
     @pl.when(jnp.logical_not(here))
     def _():
-        fetch.wait_recv()
-
-    keep_weight = pltpu.make_async_copy(weight, own_ref, weight_sems.at[3])
+        for each in fetches:
+            each.wait_recv()
+
+    keep_weight = pltpu.make_async_copy(weight, own_ref, weight_sems.at[3, 0])
     keep_weight.start()
 
     def last(chunk):
@@ -997,35 +1036,42 @@
 
     over_chunks(finish)
     keep_weight.wait()
+    for each in shares:
+        each.wait()
 
     @pl.when(here)
     def _():
-        fetch.wait_send()
-
-
-def gather_project(layer_input, gain, bias, weight, half_cols):
+        for each in fetches:
+            each.wait_send()
+
+
+def gather_project(layer_input, gain, bias, weight, out_weight, up_weight, up_bias):
     count = lax.axis_size("seq")
     _, rows, width = layer_input.shape
-    cols = weight.shape[1]
+    cols = 3 * width // count
     chunks = max(1, rows // 128)
     any_spec = pl.BlockSpec(memory_space=pl.ANY)
     vmem = pl.BlockSpec(memory_space=pltpu.VMEM)
     dma = pltpu.SemaphoreType.DMA
     return pl.pallas_call(
-        functools.partial(gather_kernel, count, chunks, half_cols),
-        in_specs=[any_spec, vmem, vmem, vmem],
-        out_specs=[any_spec, any_spec, any_spec],
+        functools.partial(gather_kernel, count, chunks),
+        in_specs=[any_spec, vmem, vmem] + [any_spec] * 4,
+        out_specs=[any_spec] * 6,
         out_shape=[
             jax.ShapeDtypeStruct((count, rows, width), BF16),
             jax.ShapeDtypeStruct((count, rows, cols), BF16),
             jax.ShapeDtypeStruct((width, cols), BF16),
+            jax.ShapeDtypeStruct(out_weight.shape, BF16),
+            jax.ShapeDtypeStruct((width, up_weight.shape[1] // 2), BF16),
+            jax.ShapeDtypeStruct((1, up_weight.shape[1] // 2), F32),
         ],
         scratch_shapes=[
             pltpu.VMEM((rows, width), F32),
             pltpu.VMEM((count, rows, width), BF16),
             pltpu.VMEM((count, rows, cols), BF16),
             pltpu.VMEM((width, cols), BF16),
-            dma((4,)),
+            dma((4, 3)),
+            dma((2, 3)),
             dma((chunks,)),
             dma((2, count - 1, chunks)),
             dma((2, count - 1, chunks)),
@@ -1038,7 +1084,7 @@
         cost_estimate=pl.CostEstimate(
             flops=150_000_000_000, bytes_accessed=1, transcendentals=0
         ),
-    )(layer_input, gain, bias, weight)
+    )(layer_input, gain, bias, weight, out_weight, up_weight, up_bias)
 
 
 class VectorSum:
@@ -1152,6 +1198,62 @@
         for start in range(0, vectors.shape[1], width):
             pieces.append(vectors[row : row + 1, start : start + width])
     return jnp.concatenate(pieces, axis=0)
+
+
+class ProjectionGrad:
+    def __init__(self, first_all, parts, grouped, slots, total, low, slot_sems, out_sems):
+        self.first_all, self.parts, self.grouped = first_all, parts, grouped
+        self.slots, self.total, self.low = slots, total, low
+        self.slot_sems, self.out_sems = slot_sems, out_sems
+        self.rows = slots.shape[1]
+        self.steps = first_all.shape[0] // self.rows
+
+    def fetch(self, step):
+        return pltpu.make_async_copy(
+            self.first_all.at[pl.ds(pl.multiple_of(step * self.rows, self.rows), self.rows)],
+            self.slots.at[step % 2],
+            self.slot_sems.at[step % 2],
+        )
+
+    def start(self):
+        self.fetch(0).start()
+        self.total[...] = jnp.zeros_like(self.total)
+
+    def multiply(self, step):
+        self.fetch(step).wait()
+
+        @pl.when(step + 1 < self.steps)
+        def _():
+            self.fetch(step + 1).start()
+
+        here = pl.ds(pl.multiple_of((step % 2) * self.rows, self.rows), self.rows)
+        grads = self.parts[step // 2, here, :]
+        width = self.total.shape[0]
+        size = width // 4
+        for start in range(0, width, size):
+            rows = self.slots[step % 2, :, start : start + size]
+            self.total[start : start + size, :] += dot_tn(rows, grads)
+
+        @pl.when(step == self.steps - 1)
+        def _():
+            self.low[...] = self.total[...].astype(BF16)
+            for copy in self.copies():
+                copy.start()
+
+    def copies(self):
+        members, count, rows, _ = self.grouped.shape
+        for member in range(members):
+            for part in range(count):
+                first = (part * members + member) * rows
+                yield pltpu.make_async_copy(
+                    self.low.at[pl.ds(first, rows)],
+                    self.grouped.at[member, part],
+                    self.out_sems.at[member, part],
+                )
+
+    def finish(self):
+        for copy in self.copies():
+            copy.wait()
 
 
 class WeightBegin:
@@ -1385,38 +1487,44 @@
     index_of,
     kinds,
     parts_ref,
-    weight_ref,
-    edge_weight_ref,
+    weight_from,
+    edge_weight_from,
     x_ref,
-    hidden_grad_ref,
+    hidden_grad_from,
     gain_ref,
     vectors_ref,
     *rest,
 ):
     extras = len(kinds)
     sources, rest = rest[:extras], rest[extras:]
-    weight_terms, rest = rest[:4], rest[4:]
-    if index_of:
-        qkv_terms, *rest = rest
+    terms_from, qkv_from, rest = rest[:4], rest[4], rest[5:]
     input_ref, sums_ref, total_ref, other_ref, *rest = rest
     targets, rest = rest[:extras], rest[extras:]
-    late_out, rest = (rest[:2], rest[2:]) if index_of else (rest[:4], rest[4:])
-    rows_in, sending, received, edge_in, summed, group, line, load_sem, *rest = rest
+    late_out, rest = (rest[:2], rest[2:]) if index_of else (rest[:5], rest[5:])
+    weight_ref, edge_weight_ref, hidden_grad_ref, *rest = rest
+    weight_terms, rest = rest[:4], rest[4:]
+    rows_in, sending, received, edge_in, summed, group, line, load_sems, *rest = rest
     send_sems, recv_sems, pair_send_sems, pair_recv_sems, vector_sems, *extra_sems = rest
     late = extra_sems[extras:]
     extras = [Extra(*each) for each in zip(kinds, sources, targets, extra_sems)]
     me = lax.axis_index("seq")
     place = lax.axis_index("mp")
-    rows = hidden_grad_ref.shape[0]
+    rows, width = rows_in.shape
     step = rows // chunks
-    width = gain_ref.shape[1]
     steps = (count - 1) * chunks
 
     def at(chunk):
         return pl.ds(pl.multiple_of(chunk * step, step), step)
 
-    load = pltpu.make_async_copy(x_ref.at[place, pl.ds(index_of * rows, rows)], rows_in, load_sem.at[0])
-    load.start()
+    pairs = [(weight_from, weight_ref), (edge_weight_from, edge_weight_ref)]
+    pairs += list(zip(terms_from, weight_terms))
+    pairs += [(hidden_grad_from, hidden_grad_ref), (x_ref.at[place, pl.ds(index_of * rows, rows)], rows_in)]
+    loads = [
+        pltpu.make_async_copy(source, target, load_sems.at[which])
+        for which, (source, target) in enumerate(pairs)
+    ]
+    for load in loads:
+        load.start()
     vector_sum = VectorSum(group, line, vector_sems)
     vector_sum.greet()
     if index_of == 0:
@@ -1475,12 +1583,16 @@
                 send(side, message, chunk).start()
 
     if index_of:
+        qkv_terms, qkv_sems, *late = late
+        trade = Extra("group", qkv_from, qkv_terms, qkv_sems)
+        trade.start()
         chain = WeightChain(weight_terms, qkv_terms, *late_out, *late)
-        chain.start()
         begin = None
     else:
         chain = None
-        begin = WeightBegin(weight_terms, late_out, *late)
+        begin = WeightBegin(weight_terms, late_out[:4], *late[:4])
+        projection = ProjectionGrad(qkv_from, parts_ref, late_out[4], *late[4:])
+        projection.start()
     ahead = chain.steps if chain else 0
     near = me // (count // 2)
 
@@ -1526,7 +1638,8 @@
         sums_ref[1:2, :] += jnp.sum(total, axis=0, keepdims=True)
 
     sums_ref[...] = jnp.zeros_like(sums_ref)
-    load.wait()
+    for load in loads[:2] + (loads[2:6] if index_of else []):
+        load.wait()
     wait_for = ahead + ((count - 2) * chunks + lag + 1 if index_of else steps + lag)
     steps_all = ahead + steps
 
@@ -1553,9 +1666,20 @@
         if begin is not None:
             @pl.when(index == 2)
             def _():
+                for load in loads[2:6]:
+                    load.wait()
                 begin.start()
 
+            @pl.when((index >= 3) & (index < 3 + projection.steps))
+            def _():
+                projection.multiply(index - 3)
+
         if chain is not None:
+
+            @pl.when(index == 6)
+            def _():
+                trade.finish()
+                chain.start()
 
             @pl.when(index == ahead + lag + 2)
             def _():
@@ -1564,6 +1688,11 @@
             @pl.when(index == ahead + lag + 6)
             def _():
                 chain.spread()
+
+        @pl.when(index == wait_for)
+        def _():
+            for load in loads[-2:]:
+                load.wait()
 
         @pl.when(index >= wait_for)
         def _():
@@ -1611,12 +1740,13 @@
         chain.finish()
     else:
         begin.finish()
+        projection.finish()
     for extra in extras:
         extra.finish()
 
 
 def return_part(
-    index, parts, weight, edge_weight, layer_input, hidden_grad, gain, vectors, extras, weight_terms, qkv_terms=None
+    index, parts, weight, edge_weight, layer_input, hidden_grad, gain, vectors, extras, weight_terms, qkv_from
 ):
     count, rows, cols = parts.shape
     rows = rows // 2
@@ -1625,25 +1755,33 @@
     members = lax.axis_size("batch") * lax.axis_size("mp")
     small = (8, 2 * width // 8) if index else vectors.shape
     kinds, sources = [kind for kind, _ in extras], [source for _, source in extras]
+    dma = pltpu.SemaphoreType.DMA
     late_in = [*weight_terms]
     if not index:
         keep, _, down, _ = weight_terms
         half = (width, down.shape[1] // 2)
-        late_out = [keep.shape[1:], keep.shape[1:], half, half]
+        grouped = (members, count, width // count // members, cols)
+        late_out = [keep.shape[1:], keep.shape[1:], half, half, grouped]
         late_scratch = [
             pltpu.VMEM(keep.shape[1:], BF16),
             pltpu.VMEM(keep.shape[1:], BF16),
             pltpu.VMEM(down.shape, BF16),
-            pltpu.SemaphoreType.DMA((6,)),
+            dma((6,)),
+            pltpu.VMEM((2, rows, width), BF16),
+            pltpu.VMEM((width, cols), F32),
+            pltpu.VMEM((width, cols), BF16),
+            dma((2,)),
+            dma((members, count)),
         ]
     else:
-        late_in = late_in + [qkv_terms]
         part = (width // count, weight_terms[0].shape[1] + weight_terms[2].shape[1])
         batches = lax.axis_size("batch")
-        head = qkv_terms.shape[2:]
+        head = qkv_from.shape[2:]
         late_out = [(batches,) + part, (members, count // 2) + head]
         messages = (2, count - 1) + part
         late_scratch = [
+            pltpu.VMEM(qkv_from.shape, BF16),
+            dma((2, members)),
             pltpu.VMEM(messages, BF16),
             pltpu.VMEM(messages, BF16),
             pltpu.VMEM((batches,) + part, BF16),
@@ -1652,22 +1790,21 @@
             pltpu.SemaphoreType.DMA((2, 4 * (count - 1) + count + members + 3)),
         ]
     any_spec = pl.BlockSpec(memory_space=pl.ANY)
-    dma = pltpu.SemaphoreType.DMA
     fixed = lambda step: (0, 0)
+    parts_rows = rows if index else 2 * rows
     return pl.pallas_call(
         functools.partial(return_kernel, count, chunks, 2, index, kinds),
         grid=(1,),
         in_specs=[
-            pl.BlockSpec((count, rows, cols), lambda step: (0, index, 0)),
-            pl.BlockSpec((width, cols), fixed),
-            pl.BlockSpec((width, cols), fixed),
+            pl.BlockSpec((count, parts_rows, cols), lambda step: (0, index, 0)),
             any_spec,
-            pl.BlockSpec((rows, width), fixed),
+            any_spec,
+            any_spec,
+            any_spec,
             pl.BlockSpec((1, width), fixed),
             pl.BlockSpec(vectors.shape, fixed),
         ]
-        + [any_spec] * len(extras)
-        + [pl.BlockSpec(memory_space=pltpu.VMEM)] * len(late_in),
+        + [any_spec] * (len(extras) + len(late_in) + 1),
         out_specs=[
             pl.BlockSpec((rows, width), fixed),
             pl.BlockSpec((8, width), fixed),
@@ -1684,6 +1821,12 @@
         + [jax.ShapeDtypeStruct(source.shape, BF16) for source in sources]
         + [jax.ShapeDtypeStruct(shape, BF16) for shape in late_out],
         scratch_shapes=[
+            pltpu.VMEM((width, cols), BF16),
+            pltpu.VMEM((width, cols), BF16),
+            pltpu.VMEM((rows, width), F32),
+        ]
+        + [pltpu.VMEM(each.shape, BF16) for each in late_in]
+        + [
             pltpu.VMEM((rows, width), F32),
             pltpu.VMEM((2, count - 1, rows, width), BF16),
             pltpu.VMEM((2, count - 1, rows, width), BF16),
@@ -1691,7 +1834,7 @@
             pltpu.VMEM((rows // chunks, width), F32),
             pltpu.VMEM((members,) + small, F32),
             pltpu.VMEM((count,) + small, F32),
-            dma((1,)),
+            dma((4 + len(late_in),)),
             dma((2, count - 1, chunks)),
             dma((2, count - 1, chunks)),
             dma((chunks,)),
@@ -1704,7 +1847,7 @@
             collective_id=1 + index, has_side_effects=True, vmem_limit_bytes=VMEM_LIMIT
         ),
         cost_estimate=pl.CostEstimate(flops=80_000_000_000, bytes_accessed=1, transcendentals=0),
-    )(parts, weight, edge_weight, layer_input, hidden_grad, gain, vectors, *sources, *late_in)
+    )(parts, weight, edge_weight, layer_input, hidden_grad, gain, vectors, *sources, *late_in, qkv_from)
 
 
 def weight_grad_kernel(
@@ -1986,10 +2129,10 @@
     members, parts, rows, cols = heads.shape
     cols = cols // 3
     for member in range(members):
+        here = slice(member * rows, (member + 1) * rows)
         for matrix in range(3):
             for part in range(parts):
-                start = (matrix * parts + part) * cols
-                qkv_ref[member * rows : (member + 1) * rows, start : start + cols] = heads[
+                qkv_ref[matrix, here, part * cols : (part + 1) * cols] = heads[
                     member, part, :, matrix * cols : (matrix + 1) * cols
                 ].astype(F32)
 
@@ -2001,7 +2144,7 @@
         (rows, batches * unit_cols),
         (batches * unit_cols, rows),
         (batches * out_cols, rows),
-        (heads.shape[0] * heads.shape[2], heads.shape[1] * heads.shape[3]),
+        (3, heads.shape[0] * heads.shape[2], heads.shape[1] * heads.shape[3] // 3),
     ]
     vmem = pl.BlockSpec(memory_space=pltpu.VMEM)
     return pl.pallas_call(
@@ -2013,40 +2156,53 @@
     )(pieces, heads)
 
 
-def place_kernel(place_ref, own_first, own_second, other_first, other_second, out_ref):
-    place = place_ref[0]
-
-    @pl.when(pl.program_id(0) == 0)
-    def _():
-        out_ref[place] = own_first[...].astype(F32)
-        out_ref[1 - place] = other_first[...].astype(F32)
-
-    @pl.when(pl.program_id(0) == 1)
-    def _():
-        out_ref[place] = own_second[...].astype(F32)
-        out_ref[1 - place] = other_second[...].astype(F32)
+def place_kernel(own_first, own_second, other_first, other_second, out_ref, low, high, in_sems, out_sems):
+    place = lax.axis_index("mp")
+    pieces, step = low.shape[0], low.shape[1]
+    per = pieces // 4
+
+    def fetch(index):
+        source = (own_first, own_second, other_first, other_second)[index // per]
+        return pltpu.make_async_copy(
+            source.at[pl.ds(index % per * step, step)], low.at[index], in_sems.at[index]
+        )
+
+    def put(index):
+        which = index // per
+        sequence = place if which < 2 else 1 - place
+        row = ((which % 2) * per + index % per) * step
+        return pltpu.make_async_copy(
+            high.at[index], out_ref.at[sequence, pl.ds(row, step)], out_sems.at[index]
+        )
+
+    for index in range(pieces):
+        fetch(index).start()
+    for index in range(pieces):
+        fetch(index).wait()
+        high[index] = low[index].astype(F32)
+        put(index).start()
+    for index in range(pieces):
+        put(index).wait()
 
 
 def both_sequences(own, other):
     rows, width = own[0].shape
-    step = min(256, rows)
-    steps = rows // step
-    first = pl.BlockSpec(
-        (step, width), lambda half, index, place_ref: (index * (1 - half) + (steps - 1) * half, 0)
-    )
-    second = pl.BlockSpec((step, width), lambda half, index, place_ref: (index * half, 0))
+    step = min(128, rows)
+    pieces = 4 * rows // step
+    any_spec = pl.BlockSpec(memory_space=pl.ANY)
     return pl.pallas_call(
         place_kernel,
-        grid_spec=pltpu.PrefetchScalarGridSpec(
-            num_scalar_prefetch=1,
-            grid=(2, steps),
-            in_specs=[first, second, first, second],
-            out_specs=pl.BlockSpec(
-                (2, step, width), lambda half, index, place_ref: (0, half * steps + index, 0)
-            ),
-        ),
+        in_specs=[any_spec] * 4,
+        out_specs=any_spec,
         out_shape=jax.ShapeDtypeStruct((2, 2 * rows, width), F32),
-    )(lax.axis_index("mp").astype(jnp.int32)[None], *own, *other)
+        scratch_shapes=[
+            pltpu.VMEM((pieces, step, width), BF16),
+            pltpu.VMEM((pieces, step, width), F32),
+            pltpu.SemaphoreType.DMA((pieces,)),
+            pltpu.SemaphoreType.DMA((pieces,)),
+        ],
+        compiler_params=pltpu.CompilerParams(vmem_limit_bytes=VMEM_LIMIT),
+    )(*own, *other)
 
 
 def local(
@@ -2082,18 +2238,19 @@
     lists, admits = block_lists(jnp.arange(blocks, dtype=jnp.int32), randoms, blocks)
     lists, admits = lists.reshape(-1), admits.reshape(-1)
 
-    qkv_near = lax.dynamic_slice_in_dim(qkv_weight, (seq_index * cols) % half_cols, cols, 2)
-    qkv_near = qkv_near.reshape(width, 3 * cols)
-    up_near = fetch_near(up_weight, 1)
-    bias_near = fetch_near(up_bias, 0)
-    out_other = swap(out_weight, "mp")
-
-    first_all, qkv, qkv_own = gather_project(
-        layer_input, first_gain[None], first_bias[None], qkv_near, half_cols
+    first_all, qkv, qkv_own, out_other, up_near, bias_near = gather_project(
+        layer_input,
+        first_gain[None],
+        first_bias[None],
+        qkv_weight.transpose(1, 0, 2),
+        out_weight,
+        up_weight,
+        up_bias[None],
     )
+    bias_near = bias_near[0]
     first_all = first_all.reshape(rows_total, width)
-    qkv, up_near, out_other, bias_near, lists, down_cut = lax.optimization_barrier(
-        (qkv.reshape(rows_total, 3 * cols), up_near, out_other, bias_near, lists, down_weight)
+    qkv, lists, down_cut = lax.optimization_barrier(
+        (qkv.reshape(rows_total, 3 * cols), lists, down_weight)
     )
     up_far, bias_far = swap(up_near, "batch"), swap(bias_near, "batch")
     down_near = fetch_near(down_cut, 0)
@@ -2164,16 +2321,10 @@
         lists,
         admits,
     )
-    qkv_sum = dot_tn(first_all, qkv_low_grad).astype(BF16)
-    members = lax.axis_size("batch") * 2
-    mine = lax.axis_index("batch") * 2 + mp_index
-    qkv_sum = qkv_sum.reshape(seq_count, members, -1, 3 * cols).transpose(1, 0, 2, 3)
-    qkv_low_grad, qkv_sum, come, down_come = lax.optimization_barrier(
-        (qkv_low_grad, qkv_sum, come, down_come)
-    )
+    qkv_low_grad, come, down_come = lax.optimization_barrier((qkv_low_grad, come, down_come))
     parts = qkv_low_grad.reshape(seq_count, local_rows, 3 * cols)
     early = jnp.concatenate([sums, bias_all.reshape(-1, width)], axis=0)
-    input_first, first_sums, early, _, qkv_terms, *weight_terms = return_part(
+    input_first, first_sums, early, _, *weight_terms, qkv_grouped = return_part(
         0,
         parts,
         qkv_own,
@@ -2182,8 +2333,9 @@
         results[0][1],
         first_gain[None],
         early.reshape(8, -1),
-        [("group", qkv_sum)],
+        [],
         (keep, come, down_own, down_come),
+        first_all,
     )
     input_second, _, late, other_second, other_first, weights_back, qkv_back = return_part(
         1,
@@ -2196,7 +2348,7 @@
         first_sums,
         [("mp", input_first)],
         weight_terms,
-        qkv_terms,
+        qkv_grouped,
     )
     layer_output = both_sequences(outputs, other_outputs)
     input_grad = both_sequences([input_first, input_second], [other_first, other_second])
@@ -2208,7 +2360,7 @@
         input_grad,
         late[:width],
         late[width:],
-        qkv_grad.reshape(-1, 3, half_cols),
+        qkv_grad.transpose(1, 0, 2),
         out_grad,
         early[width : 2 * width],
         early[2 * width : 3 * width],

time: 621 us -> 590 us (0.950)
  matrix products: 11 us -> 0 us
  local copies, waits for them, and re-layouts: 25 us -> 14.8 us
    dot_general x1 -> x0, matrix products: 11 us -> none  [dot_tn(): lax.dot_general(left, right, (((0,), (0,)), ((), ())), preferred_element_...]
    pallas_call x2, Pallas kernels: 193 us -> 186 us  [return_part(): pl.pallas_call(functools.partial(return_kernel, count, chunks, 2, index,...]
    ppermute x12 -> x9, starting transfers between devices: 12.8 us -> 9.34 us  [swap(): return lax.ppermute(value, axis, [(j, j ^ distance) for j in range(size)])]
  transfers between devices with their start and end apart: 16 -> 13, of which waited for: 2 -> 2; matrix products, arithmetic and copies ran while one was open for 4% -> 2% of each run, Pallas kernels for 38% -> 40%
where the time goes in v6:
time: 590 us; the launch traced here: 584 us
  Pallas kernels  538 us (91%)
  starting transfers between devices  17.9 us (3%)
  local copies, waits for them, and re-layouts  14.8 us (3%)
  waiting for transfers between devices  6.35 us (1%)
    pallas_call x2, Pallas kernels, return_part(): pl.pallas_call(functools.partial(return_kernel, count, chunks, 2, index,...  186 us
    pallas_call x1, Pallas kernels, gather_project(): pl.pallas_call(functools.partial(gather_kernel, count, chunks), in_specs=...  141 us
    pallas_call x2, Pallas kernels, token_part(): pl.pallas_call(functools.partial(token_kernel, min(256, rows), index), gr...  75.6 us
    pallas_call x1, Pallas kernels, attention_backward(): pl.pallas_call(functools.partial(backward_kernel, heads), grid=(1,), in_s...  48.3 us
    pallas_call x2, Pallas kernels, attention_forward(): pl.pallas_call(functools.partial(forward_kernel, heads, half), grid=(1,),...  37.4 us
    pallas_call x1, Pallas kernels, weight_grads(): pl.pallas_call(functools.partial(weight_grad_kernel, tile), in_specs=[vme...  35.7 us
  transfers between devices with their start and end apart: 13, of which 2 were waited for; matrix products, arithmetic and copies ran while one was open for 2% of the time, Pallas kernels for 40%

profile of v6, /device:TPU:0, one launch (start us, length us, event | category | flops | bytes accessed | tf_op | source)
XLA Modules:
  0.0 584.2 jit_solution(15691108596316409418)
XLA Ops:
  1.9 5.0 collective-permute-start.2
  7.5 141.4 %shard_map.229 = (bf16[4,1024,1024]{2,1,0:T(8,128)(2,1)}, bf16[4,1024,768]{2,1,0:T(8,128)(2,1)}, bf16[1024,768]{1,0:T(8,128)(2,1)}, bf16[512,1024]{1,0:T(8,128)(...) custom-call(f32[2,1024,1024]{2,1,0:T(8,128)} %x_ref.9, f32[1,1024]{1,0:T(1,128)} %bitcast.55, f32[1,1024]{1,0:T(1,128)} %bitcast.48, ...), custom_call_target="tpu_custom_call" | custom-call | flops 149999992832 | bytes 1 | tf_op jit(solution)/shard_map/pallas_call | solution.py:1056
  153.0 3.1 constant_dynamic-slice_fusion
  156.1 1.5 collective-permute-start.7
  157.6 22.5 %shard_map.230 = (bf16[4,512,256]{2,1,0:T(8,128)(2,1)}, f32[32,8,256]{2,1,0:T(8,128)}) custom-call(s32[4]{0:T(128)} %bitcast.72, s32[512]{0:T(512)} %min.12.lists_ref, s32[512]{0:T(512)} %reshape.163.admit_ref, bf16[4096,768]{1,0:T(8,128)(2,1)} %bitcast.59, bf16[4096,768]{1,0:T(8,128)(2,1)} %bitcast.60, bf16[4096,768]{1,0:T(8,128)(2,1)} %bitcast.61), custom_call_target="tpu_custom_call" | custom-call | flops 10737418240 | bytes 8388608 | tf_op jit(solution)/shard_map/pallas_call | solution.py:457
  180.1 1.3 constant_dynamic-slice_fusion.1
  181.4 3.2 collective-permute-start.4
  185.4 14.9 %shard_map.231 = (bf16[4,512,256]{2,1,0:T(8,128)(2,1)}, f32[32,8,256]{2,1,0:T(8,128)}) custom-call(s32[4]{0:T(128)} %bitcast.73, s32[512]{0:T(512)} %min.12.lists_ref, s32[512]{0:T(512)} %reshape.163.admit_ref, bf16[4096,768]{1,0:T(8,128)(2,1)} %bitcast.62, bf16[4096,768]{1,0:T(8,128)(2,1)} %bitcast.63, bf16[4096,768]{1,0:T(8,128)(2,1)} %bitcast.64), custom_call_target="tpu_custom_call" | custom-call | flops 10737418240 | bytes 8388608 | tf_op jit(solution)/shard_map/pallas_call | solution.py:457
  200.3 2.6 collective-permute-done.4
  203.2 1.4 fusion.att_ref
  205.2 3.7 collective-permute-done.9.down_far_ref
  210.3 39.0 %shard_map.232 = (bf16[512,1024]{1,0:T(8,128)(2,1)}, f32[512,1024]{1,0:T(8,128)}, bf16[4,512,256]{2,1,0:T(8,128)(2,1)}, bf16[1024,4096]{1,0:T(8,128)(2,1)}, bf16...) custom-call(s32[4]{0:T(128)} %bitcast.74, ...), custom_call_target="tpu_custom_call" | custom-call | flops 19327352832 | bytes 33554432 | tf_op jit(solution)/shard_map/pallas_call | solution.py:726
  249.3 36.7 %shard_map.233 = (bf16[512,1024]{1,0:T(8,128)(2,1)}, f32[512,1024]{1,0:T(8,128)}, bf16[4,512,256]{2,1,0:T(8,128)(2,1)}, bf16[1024,4096]{1,0:T(8,128)(2,1)}, bf16...) custom-call(s32[4]{0:T(128)} %bitcast.75, ...), custom_call_target="tpu_custom_call", output_to_operand_aliasing={{3}: (18, {}), {4}: (19, {}), {5}: (20, {}), {6}: (21, {}),... | custom-call | flops 19327352832 | bytes 33554432 | tf_op jit(solution)/shard_map/pallas_call | solution.py:726
  285.9 1.0 slice_add_fusion
  288.5 35.7 %shard_map.234 = (bf16[2,1024,640]{2,1,0:T(8,128)(2,1)}, bf16[2,1024,640]{2,1,0:T(8,128)(2,1)}, bf16[1024,1024]{1,0:T(8,128)(2,1)}, bf16[1024,1024]{1,0:T(8,128)...) custom-call(bf16[1024,1024]{1,0:T(8,128)(2,1)} %get-tuple-element.117.second_ref, ...), custom_call_target="tpu_custom_call" | custom-call | flops 19327352832 | bytes 16777216 | tf_op jit(solution)/shard_map/pallas_call | solution.py:2017
  324.2 1.6 collective-permute-start.10
  326.3 4.6 collective-permute-start.12
  330.8 4.5 shard_map.235
  335.4 48.3 %shard_map.236 = bf16[4096,768]{1,0:T(8,128)(2,1)} custom-call(s32[4]{0:T(128)} %bitcast.76, s32[512]{0:T(512)} %min.12.lists_ref, s32[512]{0:T(512)} %reshape.163.admit_ref, bf16[4096,768]{1,0:T(8,128)(2,1)} %bitcast.65, bf16[4096,768]{1,0:T(8,128)(2,1)} %bitcast.66, bf16[4096,768]{1,0:T(8,128)(2,1)} %bitcast.67, ...), custom_call_target="tpu_custom_call" | custom-call | flops 32212254720 | bytes 20971520 | tf_op jit(solution)/shard_map/pallas_call | solution.py:479
  383.8 1.6 copy-done.6
  385.3 64.8 %shard_map.237 = (bf16[512,1024]{1,0:T(8,128)(2,1)}, f32[8,1024]{1,0:T(8,128)}, f32[8,896]{1,0:T(8,128)}, bf16[512,1024]{1,0:T(8,128)(2,1)}, bf16[1024,640]{1,0:...) custom-call(bf16[4,1024,768]{2,1,0:T(8,128)(2,1)} %bitcast.68, ...), custom_call_target="tpu_custom_call" | custom-call | flops 80000000000 | bytes 1 | tf_op jit(solution)/shard_map/pallas_call | solution.py:1795
  450.1 121.2 %shard_map.238 = (bf16[512,1024]{1,0:T(8,128)(2,1)}, f32[8,1024]{1,0:T(8,128)}, f32[8,256]{1,0:T(8,128)}, bf16[512,1024]{1,0:T(8,128)(2,1)}, bf16[512,1024]{1,0:...) custom-call(bf16[4,1024,768]{2,1,0:T(8,128)(2,1)} %bitcast.69, ...), custom_call_target="tpu_custom_call" | custom-call | flops 80000000000 | bytes 1 | tf_op jit(solution)/shard_map/pallas_call | solution.py:1795
  574.4 5.0 shard_map.240
  579.4 4.6 shard_map.239
  (80 shorter events, 14.1 us)
Async XLA Ops:
  0.6 0.7 copy-start
  1.9 148.1 %collective-permute-start.2 = (s32[16,3]{0,1:T(4,128)}, s32[16,3]{0,1:T(4,128)}, u32[]{:S(2)}, u32[]{:S(2)}) collective-permute-start(s32[16,3]{0,1:T(4,128)} %bitcast.33.clone.2), channel_id=1, source_target_pairs={{0,24},{8,16},{16,8},{24,0},{1,25},{9,17},{17,9},{25,1},{2,26},{10... | collective-permute-start | bytes 584 | tf_op jit(solution)/shard_map/ppermute | solution.py:2049
  7.0 143.0 %collective-permute-start = (s32[16,3]{0,1:T(4,128)}, s32[16,3]{0,1:T(4,128)}, u32[]{:S(2)}, u32[]{:S(2)}) collective-permute-start(s32[16,3]{0,1:T(4,128)} %bitcast.33.clone.2), channel_id=1, source_target_pairs={{0,8},{8,0},{16,24},{24,16},{1,9},{9,1},{17,25},{25,17},{2,10},{10... | collective-permute-start | bytes 584 | tf_op jit(solution)/shard_map/ppermute | solution.py:2049
  7.0 143.0 %collective-permute-start.1 = (s32[16,3]{0,1:T(4,128)}, s32[16,3]{0,1:T(4,128)}, u32[]{:S(2)}, u32[]{:S(2)}) collective-permute-start(s32[16,3]{0,1:T(4,128)} %bitcast.33.clone.2), channel_id=1, source_target_pairs={{0,16},{8,24},{16,0},{24,8},{1,17},{9,25},{17,1},{25,9},{2,18},{10... | collective-permute-start | bytes 584 | tf_op jit(solution)/shard_map/ppermute | solution.py:2049
  7.5 141.8 %copy-start.8 = (s32[2,4]{1,0:T(2,128)S(1)}, s32[2,4]{1,0:T(2,128)}, u32[]{:S(2)}) copy-start(s32[2,4]{1,0:T(2,128)} %param.15) | copy-start | bytes 100
  148.9 55.6 %collective-permute-start.6 = (bf16[1024,1024]{1,0:T(8,128)(2,1)}, bf16[1024,1024]{1,0:T(8,128)(2,1)}, u32[]{:S(2)}, u32[]{:S(2)}) collective-permute-start(bf16[1024,1024]{1,0:T(8,128)(2,1)} %get-tuple-element.97.up_near_ref), channel_id=1, source_target_pairs={{0,2},{2,0},{4,6},{6,4},{1,3},{3,1},{5,7},{7,5},{8,10},{10,8},{12,... | collective-permute-start | bytes 6291464 | tf_op jit(solution)/shard_map/ppermute | solution.py:2049
  156.1 48.4 %collective-permute-start.7 = (bf16[1024,1024]{1,0:T(8,128)(2,1)}, bf16[1024,1024]{1,0:T(8,128)(2,1)}, u32[]{:S(2)}, u32[]{:S(2)}) collective-permute-start(bf16[1024,1024]{1,0:T(8,128)(2,1)} %constant_dynamic-slice_fusion), channel_id=1, source_target_pairs={{0,1},{1,0},{2,3},{3,2},{4,5},{5,4},{6,7},{7,6},{8,9},{9,8},{10,11... | collective-permute-start | bytes 6291464 | tf_op jit(solution)/shard_map/ppermute | solution.py:2049
  181.3 18.9 %collective-permute-start.3 = (bf16[1,512,256]{2,1,0:T(8,128)(2,1)S(1)}, bf16[1,512,256]{2,1,0:T(8,128)(2,1)S(1)}, u32[]{:S(2)}, u32[]{:S(2)}) collective-permute-start(bf16[1,512,256]{2,1,0:T(8,128)(2,1)S(1)} %get-tuple-element.170), channel_id=1, source_target_pairs={{0,8},{8,16},{16,24},{24,0},{1,9},{9,17},{17,25},{25,1},{2,10},{10... | collective-permute-start | bytes 786440 | tf_op jit(solution)/shard_map/ppermute | solution.py:2070
  181.4 21.5 %collective-permute-start.4 = (bf16[1,512,256]{2,1,0:T(8,128)(2,1)S(1)}, bf16[1,512,256]{2,1,0:T(8,128)(2,1)S(1)}, u32[]{:S(2)}, u32[]{:S(2)}) collective-permute-start(bf16[1,512,256]{2,1,0:T(8,128)(2,1)S(1)} %get-tuple-element.169), channel_id=1, source_target_pairs={{0,16},{8,24},{16,0},{24,8},{1,17},{9,25},{17,1},{25,9},{2,18},{10... | collective-permute-start | bytes 786440 | tf_op jit(solution)/shard_map/ppermute | solution.py:2070
  184.6 15.7 %copy-start.5 = (f32[1,1024]{1,0:T(1,128)S(1)}, f32[1,1024]{1,0:T(1,128)}, u32[]{:S(2)}) copy-start(f32[1,1024]{1,0:T(1,128)} %get-tuple-element.99) | copy-start | bytes 12292
  184.6 18.4 %collective-permute-start.5 = (bf16[1,512,256]{2,1,0:T(8,128)(2,1)S(1)}, bf16[1,512,256]{2,1,0:T(8,128)(2,1)S(1)}, u32[]{:S(2)}, u32[]{:S(2)}) collective-permute-start(bf16[1,512,256]{2,1,0:T(8,128)(2,1)S(1)} %get-tuple-element.168), channel_id=1, source_target_pairs={{0,24},{8,0},{16,8},{24,16},{1,25},{9,1},{17,9},{25,17},{2,26},{10... | collective-permute-start | bytes 786440 | tf_op jit(solution)/shard_map/ppermute | solution.py:2070
  200.3 4.3 collective-permute-start.8
  203.1 1.6 copy-start.4
  204.5 4.4 collective-permute-start.9
  209.0 1.3 copy-start.7
  249.3 37.8 %copy-start.3 = (f32[8,1024]{1,0:T(8,128)S(1)}, f32[8,1024]{1,0:T(8,128)}, u32[]{:S(2)}) copy-start(f32[8,1024]{1,0:T(8,128)} %get-tuple-element.136) | copy-start | bytes 98308
  324.2 59.5 %collective-permute-start.10 = (bf16[2,1024,640]{2,1,0:T(8,128)(2,1)}, bf16[2,1024,640]{2,1,0:T(8,128)(2,1)S(1)}, u32[]{:S(2)}, u32[]{:S(2)}) collective-permute-start(bf16[2,1024,640]{2,1,0:T(8,128)(2,1)} %get-tuple-element.131), channel_id=1, source_target_pairs={{0,4},{2,6},{4,0},{6,2},{1,5},{3,7},{5,1},{7,3},{8,12},{10,14},{12... | collective-permute-start | bytes 7864328 | tf_op jit(solution)/shard_map/ppermute | solution.py:2049
  325.8 58.0 %collective-permute-start.11 = (bf16[1024,1024]{1,0:T(8,128)(2,1)}, bf16[1024,1024]{1,0:T(8,128)(2,1)}, u32[]{:S(2)}, u32[]{:S(2)}) collective-permute-start(bf16[1024,1024]{1,0:T(8,128)(2,1)} %get-tuple-element.132), channel_id=1, source_target_pairs={{0,1},{1,0},{2,3},{3,2},{4,5},{5,4},{6,7},{7,6},{8,9},{9,8},{10,11... | collective-permute-start | bytes 6291464 | tf_op jit(solution)/shard_map/ppermute | solution.py:2049
  326.3 57.5 %collective-permute-start.12 = (bf16[1024,768]{1,0:T(8,128)(2,1)}, bf16[1024,768]{1,0:T(8,128)(2,1)}, u32[]{:S(2)}, u32[]{:S(2)}) collective-permute-start(bf16[1024,768]{1,0:T(8,128)(2,1)} %get-tuple-element.134.weight_from), channel_id=1, source_target_pairs={{0,8},{24,16},{1,9},{25,17},{2,10},{26,18},{3,11},{27,19},{4,12},{... | collective-permute-start | bytes 4718600 | tf_op jit(solution)/shard_map/ppermute | solution.py:2312
  383.7 1.6 copy-start.6
  450.1 123.1 %copy-start.2 = (f32[8,896]{1,0:T(8,128)S(1)}, f32[8,896]{1,0:T(8,128)}, u32[]{:S(2)}) copy-start(f32[8,896]{1,0:T(8,128)} %get-tuple-element.161) | copy-start | bytes 86020
  579.4 4.6 copy-start.1

commit v7 on v6

--- a/solution.py
+++ b/solution.py
@@ -62,7 +62,7 @@
         self.count = source.shape[0]
         self.me = lax.axis_index("seq")
 
-    def greet(self, others):
+    def greet(self):
         barrier = pltpu.get_barrier_semaphore()
         for distance in range(1, self.count):
             other = lax.rem(self.me + distance, self.count)
@@ -70,8 +70,6 @@
         if self.pair is not None:
             partner = 1 - lax.axis_index("mp")
             pl.semaphore_signal(barrier, inc=1, device_id={"mp": partner}, device_id_type=MESH)
-            others = others + 1
-        pl.semaphore_wait(barrier, self.count - 1 + others)
 
     def copy(self, distance):
         other = lax.rem(self.me + distance, self.count)
@@ -101,7 +99,8 @@
         )
 
     def start(self, others=0):
-        self.greet(others)
+        others = others + (self.pair is not None)
+        pl.semaphore_wait(pltpu.get_barrier_semaphore(), self.count - 1 + others)
         for distance in range(1, self.count):
             self.copy(distance).start()
         if self.pair is not None:
@@ -623,6 +622,7 @@
         for copy in row_copies:
             copy.start()
         fetch(step)
+        trade.greet()
         trade.start()
 
     @pl.when(step + 1 < steps)
@@ -805,7 +805,12 @@
     )
 
 
-def greet(me, count, partner=None):
+def batch_mate(distance):
+    batch = lax.axis_index("batch")
+    return batch + distance - 2 * distance * ((batch // distance) % 2)
+
+
+def greet(me, count, partner, mate):
     barrier = pltpu.get_barrier_semaphore()
 
     @pl.when(me > 0)
@@ -816,11 +821,9 @@
     def _():
         pl.semaphore_signal(barrier, inc=1, device_id={"seq": me + 1}, device_id_type=MESH)
 
-    peers = jnp.minimum(me, 1) + jnp.minimum(count - 1 - me, 1)
-    if partner is not None:
-        pl.semaphore_signal(barrier, inc=1, device_id={"mp": partner}, device_id_type=MESH)
-        peers = peers + 1
-    pl.semaphore_wait(barrier, peers)
+    pl.semaphore_signal(barrier, inc=1, device_id={"mp": partner}, device_id_type=MESH)
+    pl.semaphore_signal(barrier, inc=1, device_id={"batch": mate}, device_id_type=MESH)
+    pl.semaphore_wait(barrier, jnp.minimum(me, 1) + jnp.minimum(count - 1 - me, 1) + 2)
 
 
 def gather_kernel(
@@ -832,12 +835,15 @@
     weight_ref,
     out_ref,
     up_ref,
+    down_ref,
     up_bias_ref,
     all_ref,
     qkv_ref,
     own_ref,
+    edge_ref,
     out_other,
     up_near,
+    down_near,
     up_bias_near,
     rows_in,
     shards,
@@ -894,7 +900,7 @@
         lax.fori_loop(0, chunks, run, 0)
 
     over_chunks(lambda chunk: load(chunk).start())
-    greet(me, count, 1 - place)
+    greet(me, count, 1 - place, batch_mate(2))
 
     half_cols = weight_ref.shape[2]
     here = (me * cols) // half_cols == place
@@ -920,28 +926,41 @@
         for each in fetches + copies:
             each.start()
 
-    parity = lax.axis_index("batch") % 2
-    share = up_near.shape[1]
-    columns = pl.ds(pl.multiple_of(parity * share, share), share)
-    shares = [
-        pltpu.make_async_remote_copy(
+    batch = lax.axis_index("batch")
+    parity, side = batch % 2, batch // 2
+    share = up_near.shape[1] // 2
+    quarter = pl.ds(pl.multiple_of((2 * parity + side) * share, share), share)
+    there = pl.ds(pl.multiple_of(side * share, share), share)
+    half = up_bias_near.shape[1]
+    bias_half = pl.ds(pl.multiple_of(parity * half, half), half)
+
+    def give(which, source, target, device):
+        return pltpu.make_async_remote_copy(
             src_ref=source,
             dst_ref=target,
             send_sem=fetch_sems.at[0, which],
             recv_sem=fetch_sems.at[1, which],
-            device_id={"mp": 1 - place},
+            device_id=device,
             device_id_type=MESH,
         )
-        for which, (source, target) in enumerate(
-            (
-                (out_ref, out_other),
-                (up_ref.at[:, columns], up_near),
-                (up_bias_ref.at[:, columns], up_bias_near),
-            )
-        )
+
+    partner, chip = {"mp": 1 - place}, {"batch": batch + 2 - 4 * side}
+    shares = [
+        give(0, out_ref, out_other, partner),
+        give(1, up_ref.at[:, quarter], up_near.at[:, there], partner),
+        give(2, down_ref.at[quarter], down_near.at[there], partner),
+        give(3, up_bias_ref.at[:, bias_half], up_bias_near, partner),
     ]
-    for each in shares:
+    passed = [
+        give(4, up_near.at[:, there], up_near.at[:, there], chip),
+        give(5, down_near.at[there], down_near.at[there], chip),
+    ]
+    for each in (shares[1], shares[2], shares[3], shares[0]):
         each.start()
+
+    def pass_on(which):
+        shares[1 + which].wait()
+        passed[which].start()
 
     def norm(chunk):
         load(chunk).wait()
@@ -989,6 +1008,8 @@
 
     for hop in range(count - 2):
         over_chunks(functools.partial(receive, hop))
+        if hop == (count - 2) // 2 - 1:
+            pass_on(0)
 
     @pl.when(here)
     def _():
@@ -1002,6 +1023,22 @@
 
     keep_weight = pltpu.make_async_copy(weight, own_ref, weight_sems.at[3, 0])
     keep_weight.start()
+
+    last_place = count - 1
+    at_end, by_end = (me == 0) | (me == last_place), (me == 1) | (me == last_place - 1)
+    low_half = me // (count // 2)
+    edge = pltpu.make_async_remote_copy(
+        src_ref=weight,
+        dst_ref=edge_ref,
+        send_sem=weight_sems.at[3, 1],
+        recv_sem=weight_sems.at[3, 2],
+        device_id={"seq": me + 1 - 2 * low_half},
+        device_id_type=MESH,
+    )
+
+    @pl.when(at_end)
+    def _():
+        edge.start()
 
     def last(chunk):
         project(me, chunk)
@@ -1017,6 +1054,10 @@
             def _():
                 project(me + hop + 1, chunk)
 
+        @pl.when(chunk == 1)
+        def _():
+            pass_on(1)
+
     over_chunks(last)
 
     def finish(chunk):
@@ -1036,7 +1077,16 @@
 
     over_chunks(finish)
     keep_weight.wait()
-    for each in shares:
+
+    @pl.when(at_end)
+    def _():
+        edge.wait_send()
+
+    @pl.when(by_end)
+    def _():
+        edge.wait_recv()
+
+    for each in (shares[0], shares[3], *passed):
         each.wait()
 
     @pl.when(here)
@@ -1045,7 +1095,7 @@
             each.wait_send()
 
 
-def gather_project(layer_input, gain, bias, weight, out_weight, up_weight, up_bias):
+def gather_project(layer_input, gain, bias, weight, out_weight, up_weight, down_weight, up_bias):
     count = lax.axis_size("seq")
     _, rows, width = layer_input.shape
     cols = 3 * width // count
@@ -1055,14 +1105,16 @@
     dma = pltpu.SemaphoreType.DMA
     return pl.pallas_call(
         functools.partial(gather_kernel, count, chunks),
-        in_specs=[any_spec, vmem, vmem] + [any_spec] * 4,
-        out_specs=[any_spec] * 6,
+        in_specs=[any_spec, vmem, vmem] + [any_spec] * 5,
+        out_specs=[any_spec] * 8,
         out_shape=[
             jax.ShapeDtypeStruct((count, rows, width), BF16),
             jax.ShapeDtypeStruct((count, rows, cols), BF16),
             jax.ShapeDtypeStruct((width, cols), BF16),
+            jax.ShapeDtypeStruct((width, cols), BF16),
             jax.ShapeDtypeStruct(out_weight.shape, BF16),
             jax.ShapeDtypeStruct((width, up_weight.shape[1] // 2), BF16),
+            jax.ShapeDtypeStruct((down_weight.shape[0] // 2, width), BF16),
             jax.ShapeDtypeStruct((1, up_weight.shape[1] // 2), F32),
         ],
         scratch_shapes=[
@@ -1071,7 +1123,7 @@
             pltpu.VMEM((count, rows, cols), BF16),
             pltpu.VMEM((width, cols), BF16),
             dma((4, 3)),
-            dma((2, 3)),
+            dma((2, 6)),
             dma((chunks,)),
             dma((2, count - 1, chunks)),
             dma((2, count - 1, chunks)),
@@ -1084,7 +1136,7 @@
         cost_estimate=pl.CostEstimate(
             flops=150_000_000_000, bytes_accessed=1, transcendentals=0
         ),
-    )(layer_input, gain, bias, weight, out_weight, up_weight, up_bias)
+    )(layer_input, gain, bias, weight, out_weight, up_weight, down_weight, up_bias)
 
 
 class VectorSum:
@@ -1529,8 +1581,6 @@
     vector_sum.greet()
     if index_of == 0:
         vector_sum.start(vectors_ref[...])
-    for extra in extras:
-        extra.start()
 
     def send(side, message, chunk):
         return pltpu.make_async_remote_copy(
@@ -1586,6 +1636,8 @@
         qkv_terms, qkv_sems, *late = late
         trade = Extra("group", qkv_from, qkv_terms, qkv_sems)
         trade.start()
+        for extra in extras:
+            extra.start()
         chain = WeightChain(weight_terms, qkv_terms, *late_out, *late)
         begin = None
     else:
@@ -1681,11 +1733,11 @@
                 trade.finish()
                 chain.start()
 
-            @pl.when(index == ahead + lag + 2)
+            @pl.when(index == ahead + lag)
             def _():
                 chain.own()
 
-            @pl.when(index == ahead + lag + 6)
+            @pl.when(index == ahead + lag + 3)
             def _():
                 chain.spread()
 
@@ -1886,7 +1938,7 @@
     barrier = pltpu.get_barrier_semaphore()
     pl.semaphore_signal(barrier, inc=1, device_id={"batch": mate}, device_id_type=MESH)
     trade = Trade(trade_source, trade_target, *trade_sems, (pair_source, pair_target, pair_sems))
-    trade.start(1)
+    trade.greet()
 
     depth = slots.shape[0]
     piece = units // 4
@@ -1972,6 +2024,7 @@
             return 0
 
         lax.fori_loop(0, rows // 128, turn, 0)
+    trade.start(1)
 
     for index, (job, which) in enumerate(order):
         matrix, _, size, *_ = jobs[job]
@@ -2096,14 +2149,6 @@
     return lax.dynamic_slice_in_dim(value, index * size, size, axis)
 
 
-def fetch_near(weight, axis):
-    return swap(pick(weight, lax.axis_index("batch") % 2, 2, axis), "mp")
-
-
-def narrow_add(mine, received):
-    return (mine.astype(F32) + received.astype(F32)).astype(BF16)
-
-
 def assemble_kernel(unit_cols, pieces, heads, up_ref, down_ref, out_ref, qkv_ref):
     batch = lax.axis_index("batch")
     batches = pieces.shape[0]
@@ -2238,31 +2283,28 @@
     lists, admits = block_lists(jnp.arange(blocks, dtype=jnp.int32), randoms, blocks)
     lists, admits = lists.reshape(-1), admits.reshape(-1)
 
-    first_all, qkv, qkv_own, out_other, up_near, bias_near = gather_project(
+    first_all, qkv, qkv_own, qkv_edge, out_other, up_near, down_near, bias_near = gather_project(
         layer_input,
         first_gain[None],
         first_bias[None],
         qkv_weight.transpose(1, 0, 2),
         out_weight,
         up_weight,
+        down_weight,
         up_bias[None],
     )
     bias_near = bias_near[0]
     first_all = first_all.reshape(rows_total, width)
-    qkv, lists, down_cut = lax.optimization_barrier(
-        (qkv.reshape(rows_total, 3 * cols), lists, down_weight)
-    )
-    up_far, bias_far = swap(up_near, "batch"), swap(bias_near, "batch")
-    down_near = fetch_near(down_cut, 0)
+    qkv = qkv.reshape(rows_total, 3 * cols)
+    up_far, down_far, bias_far = (swap(near, "batch") for near in (up_near, down_near, bias_near))
     attended_first, lse_first = attention_forward(0, qkv, doc_ends, lists, admits, seq_count)
     att_pieces = trade_pieces(attended_first)
     attended_second, lse_second = attention_forward(1, qkv, doc_ends, lists, admits, seq_count)
     *att_pieces, attended_second = lax.optimization_barrier((*att_pieces, attended_second))
     att_first = place_pieces(att_pieces)
-    att_first, up_far, down_near, bias_far = lax.optimization_barrier(
-        (att_first, up_far, down_near, bias_far)
+    att_first, up_far, down_far, bias_far = lax.optimization_barrier(
+        (att_first, up_far, down_far, bias_far)
     )
-    down_far = swap(down_near, "batch")
     bias_full = jnp.concatenate([up_bias, bias_near, bias_far])[None]
     outs = [part.reshape(seq_count // 2, cols, width) for part in (out_weight, out_other)]
     kept, results = None, []
@@ -2308,9 +2350,6 @@
         jnp.concatenate([bias_sums[0], bias_other]),
         jnp.concatenate([bias_other, bias_sums[0]]),
     )
-    qkv_cut, grad_second = lax.optimization_barrier((qkv_own, grad_second))
-    qkv_edge = lax.ppermute(qkv_cut, "seq", [(0, 1), (seq_count - 1, seq_count - 2)])
-
     come, down_come = swap(away, "batch", 2), swap(down_near, "mp")
     qkv_low_grad = attention_backward(
         qkv,

time: 590 us -> 577 us (0.978)
  transfers between devices with their start and end apart: 13 -> 11, of which waited for: 2 -> 2; matrix products, arithmetic and copies ran while one was open for 2% -> 1% of each run, Pallas kernels for 40% -> 40%
where the time goes in v7:
time: 577 us; the launch traced here: 572 us
  Pallas kernels  535 us (93%)
  starting transfers between devices  13.5 us (2%)
  local copies, waits for them, and re-layouts  11 us (2%)
    pallas_call x2, Pallas kernels, return_part(): pl.pallas_call(functools.partial(return_kernel, count, chunks, 2, index,...  185 us
    pallas_call x1, Pallas kernels, gather_project(): pl.pallas_call(functools.partial(gather_kernel, count, chunks), in_specs=...  141 us
    pallas_call x2, Pallas kernels, token_part(): pl.pallas_call(functools.partial(token_kernel, min(256, rows), index), gr...  76.6 us
    pallas_call x1, Pallas kernels, attention_backward(): pl.pallas_call(functools.partial(backward_kernel, heads), grid=(1,), in_s...  48.3 us
    pallas_call x2, Pallas kernels, attention_forward(): pl.pallas_call(functools.partial(forward_kernel, heads, half), grid=(1,),...  37.4 us
    pallas_call x1, Pallas kernels, weight_grads(): pl.pallas_call(functools.partial(weight_grad_kernel, tile), in_specs=[vme...  32.8 us
  transfers between devices with their start and end apart: 11, of which 2 were waited for; matrix products, arithmetic and copies ran while one was open for 1% of the time, Pallas kernels for 40%

profile of v7, /device:TPU:0, one launch (start us, length us, event | category | flops | bytes accessed | tf_op | source)
XLA Modules:
  0.0 571.6 jit_solution(4568511551036872540)
XLA Ops:
  1.9 3.0 collective-permute-start
  4.9 2.6 collective-permute-start.1
  7.5 140.7 %shard_map.229 = (bf16[4,1024,1024]{2,1,0:T(8,128)(2,1)}, bf16[4,1024,768]{2,1,0:T(8,128)(2,1)}, bf16[1024,768]{1,0:T(8,128)(2,1)}, bf16[1024,768]{1,0:T(8,128)(...) custom-call(f32[2,1024,1024]{2,1,0:T(8,128)} %x_ref.9, ...), custom_call_target="tpu_custom_call" | custom-call | flops 149999992832 | bytes 1 | tf_op jit(solution)/shard_map/pallas_call | solution.py:1106
  152.8 22.5 %shard_map.230 = (bf16[4,512,256]{2,1,0:T(8,128)(2,1)}, f32[32,8,256]{2,1,0:T(8,128)}) custom-call(s32[4]{0:T(128)} %bitcast.72, s32[512]{0:T(512)} %min.12.lists_ref, s32[512]{0:T(512)} %reshape.163.admit_ref, bf16[4096,768]{1,0:T(8,128)(2,1)} %bitcast.59, bf16[4096,768]{1,0:T(8,128)(2,1)} %bitcast.60, bf16[4096,768]{1,0:T(8,128)(2,1)} %bitcast.61), custom_call_target="tpu_custom_call" | custom-call | flops 10737418240 | bytes 8388608 | tf_op jit(solution)/shard_map/pallas_call | solution.py:456
  175.3 1.3 constant_dynamic-slice_fusion
  176.6 3.9 collective-permute-start.4
  180.8 14.9 %shard_map.231 = (bf16[4,512,256]{2,1,0:T(8,128)(2,1)}, f32[32,8,256]{2,1,0:T(8,128)}) custom-call(s32[4]{0:T(128)} %bitcast.73, s32[512]{0:T(512)} %min.12.lists_ref, s32[512]{0:T(512)} %reshape.163.admit_ref, bf16[4096,768]{1,0:T(8,128)(2,1)} %bitcast.62, bf16[4096,768]{1,0:T(8,128)(2,1)} %bitcast.63, bf16[4096,768]{1,0:T(8,128)(2,1)} %bitcast.64), custom_call_target="tpu_custom_call" | custom-call | flops 10737418240 | bytes 8388608 | tf_op jit(solution)/shard_map/pallas_call | solution.py:456
  195.8 2.3 collective-permute-done.4
  198.3 1.4 fusion.att_ref
  200.9 39.7 %shard_map.232 = (bf16[512,1024]{1,0:T(8,128)(2,1)}, f32[512,1024]{1,0:T(8,128)}, bf16[4,512,256]{2,1,0:T(8,128)(2,1)}, bf16[1024,4096]{1,0:T(8,128)(2,1)}, bf16...) custom-call(s32[4]{0:T(128)} %bitcast.74, ...), custom_call_target="tpu_custom_call" | custom-call | flops 19327352832 | bytes 33554432 | tf_op jit(solution)/shard_map/pallas_call | solution.py:726
  240.6 36.9 %shard_map.233 = (bf16[512,1024]{1,0:T(8,128)(2,1)}, f32[512,1024]{1,0:T(8,128)}, bf16[4,512,256]{2,1,0:T(8,128)(2,1)}, bf16[1024,4096]{1,0:T(8,128)(2,1)}, bf16...) custom-call(s32[4]{0:T(128)} %bitcast.75, ...), custom_call_target="tpu_custom_call", output_to_operand_aliasing={{3}: (18, {}), {4}: (19, {}), {5}: (20, {}), {6}: (21, {}),... | custom-call | flops 19327352832 | bytes 33554432 | tf_op jit(solution)/shard_map/pallas_call | solution.py:726
  277.5 1.0 slice_add_fusion
  280.1 32.8 %shard_map.234 = (bf16[2,1024,640]{2,1,0:T(8,128)(2,1)}, bf16[2,1024,640]{2,1,0:T(8,128)(2,1)}, bf16[1024,1024]{1,0:T(8,128)(2,1)}, bf16[1024,1024]{1,0:T(8,128)...) custom-call(bf16[1024,1024]{1,0:T(8,128)(2,1)} %get-tuple-element.112.second_ref, ...), custom_call_target="tpu_custom_call" | custom-call | flops 19327352832 | bytes 16777216 | tf_op jit(solution)/shard_map/pallas_call | solution.py:2070
  312.9 1.5 collective-permute-start.9
  314.5 1.5 collective-permute-start.10
  316.0 4.5 shard_map.235
  320.5 48.3 %shard_map.236 = bf16[4096,768]{1,0:T(8,128)(2,1)} custom-call(s32[4]{0:T(128)} %bitcast.76, s32[512]{0:T(512)} %min.12.lists_ref, s32[512]{0:T(512)} %reshape.163.admit_ref, bf16[4096,768]{1,0:T(8,128)(2,1)} %bitcast.65, bf16[4096,768]{1,0:T(8,128)(2,1)} %bitcast.66, bf16[4096,768]{1,0:T(8,128)(2,1)} %bitcast.67, ...), custom_call_target="tpu_custom_call" | custom-call | flops 32212254720 | bytes 20971520 | tf_op jit(solution)/shard_map/pallas_call | solution.py:478
  368.8 2.8 collective-permute-done.9.rest_1_
  371.7 1.6 copy-done.6
  373.2 66.5 %shard_map.237 = (bf16[512,1024]{1,0:T(8,128)(2,1)}, f32[8,1024]{1,0:T(8,128)}, f32[8,896]{1,0:T(8,128)}, bf16[512,1024]{1,0:T(8,128)(2,1)}, bf16[1024,640]{1,0:...) custom-call(bf16[4,1024,768]{2,1,0:T(8,128)(2,1)} %bitcast.68, ...), custom_call_target="tpu_custom_call" | custom-call | flops 80000000000 | bytes 1 | tf_op jit(solution)/shard_map/pallas_call | solution.py:1847
  439.7 118.7 %shard_map.238 = (bf16[512,1024]{1,0:T(8,128)(2,1)}, f32[8,1024]{1,0:T(8,128)}, f32[8,256]{1,0:T(8,128)}, bf16[512,1024]{1,0:T(8,128)(2,1)}, bf16[512,1024]{1,0:...) custom-call(bf16[4,1024,768]{2,1,0:T(8,128)(2,1)} %bitcast.69, ...), custom_call_target="tpu_custom_call" | custom-call | flops 80000000000 | bytes 1 | tf_op jit(solution)/shard_map/pallas_call | solution.py:1847
  558.4 0.8 slice_bitcast_fusion
  561.6 5.0 shard_map.240
  566.6 4.6 shard_map.239
  (73 shorter events, 11.5 us)
Async XLA Ops:
  0.6 0.7 copy-start
  1.9 147.8 %collective-permute-start = (s32[16,3]{0,1:T(4,128)}, s32[16,3]{0,1:T(4,128)}, u32[]{:S(2)}, u32[]{:S(2)}) collective-permute-start(s32[16,3]{0,1:T(4,128)} %bitcast.33.clone.2), channel_id=1, source_target_pairs={{0,8},{8,0},{16,24},{24,16},{1,9},{9,1},{17,25},{25,17},{2,10},{10... | collective-permute-start | bytes 584 | tf_op jit(solution)/shard_map/ppermute | solution.py:2102
  4.9 144.8 %collective-permute-start.1 = (s32[16,3]{0,1:T(4,128)}, s32[16,3]{0,1:T(4,128)}, u32[]{:S(2)}, u32[]{:S(2)}) collective-permute-start(s32[16,3]{0,1:T(4,128)} %bitcast.33.clone.2), channel_id=1, source_target_pairs={{0,16},{8,24},{16,0},{24,8},{1,17},{9,25},{17,1},{25,9},{2,18},{10... | collective-permute-start | bytes 584 | tf_op jit(solution)/shard_map/ppermute | solution.py:2102
  7.5 142.2 %collective-permute-start.2 = (s32[16,3]{0,1:T(4,128)}, s32[16,3]{0,1:T(4,128)}, u32[]{:S(2)}, u32[]{:S(2)}) collective-permute-start(s32[16,3]{0,1:T(4,128)} %bitcast.33.clone.2), channel_id=1, source_target_pairs={{0,24},{8,16},{16,8},{24,0},{1,25},{9,17},{17,9},{25,1},{2,26},{10... | collective-permute-start | bytes 584 | tf_op jit(solution)/shard_map/ppermute | solution.py:2102
  7.5 141.5 %copy-start.7 = (s32[2,4]{1,0:T(2,128)S(1)}, s32[2,4]{1,0:T(2,128)}, u32[]{:S(2)}) copy-start(s32[2,4]{1,0:T(2,128)} %param.15) | copy-start | bytes 100
  148.2 51.4 %collective-permute-start.6 = (bf16[1024,1024]{1,0:T(8,128)(2,1)}, bf16[1024,1024]{1,0:T(8,128)(2,1)}, u32[]{:S(2)}, u32[]{:S(2)}) collective-permute-start(bf16[1024,1024]{1,0:T(8,128)(2,1)} %get-tuple-element.92.up_near_ref), channel_id=1, source_target_pairs={{0,2},{2,0},{4,6},{6,4},{1,3},{3,1},{5,7},{7,5},{8,10},{10,8},{12,... | collective-permute-start | bytes 6291464 | tf_op jit(solution)/shard_map/ppermute | solution.py:2102
  148.3 51.4 %collective-permute-start.7 = (bf16[1024,1024]{1,0:T(8,128)(2,1)}, bf16[1024,1024]{1,0:T(8,128)(2,1)}, u32[]{:S(2)}, u32[]{:S(2)}) collective-permute-start(bf16[1024,1024]{1,0:T(8,128)(2,1)} %get-tuple-element.93.down_near_ref), channel_id=1, source_target_pairs={{0,2},{2,0},{4,6},{6,4},{1,3},{3,1},{5,7},{7,5},{8,10},{10,8},{12,... | collective-permute-start | bytes 6291464 | tf_op jit(solution)/shard_map/ppermute | solution.py:2102
  176.6 19.1 %collective-permute-start.3 = (bf16[1,512,256]{2,1,0:T(8,128)(2,1)S(1)}, bf16[1,512,256]{2,1,0:T(8,128)(2,1)S(1)}, u32[]{:S(2)}, u32[]{:S(2)}) collective-permute-start(bf16[1,512,256]{2,1,0:T(8,128)(2,1)S(1)} %get-tuple-element.164), channel_id=1, source_target_pairs={{0,8},{8,16},{16,24},{24,0},{1,9},{9,17},{17,25},{25,1},{2,10},{10... | collective-permute-start | bytes 786440 | tf_op jit(solution)/shard_map/ppermute | solution.py:2123
  176.6 21.4 %collective-permute-start.4 = (bf16[1,512,256]{2,1,0:T(8,128)(2,1)S(1)}, bf16[1,512,256]{2,1,0:T(8,128)(2,1)S(1)}, u32[]{:S(2)}, u32[]{:S(2)}) collective-permute-start(bf16[1,512,256]{2,1,0:T(8,128)(2,1)S(1)} %get-tuple-element.163), channel_id=1, source_target_pairs={{0,16},{8,24},{16,0},{24,8},{1,17},{9,25},{17,1},{25,9},{2,18},{10... | collective-permute-start | bytes 786440 | tf_op jit(solution)/shard_map/ppermute | solution.py:2123
  180.5 15.2 %copy-start.5 = (f32[1,1024]{1,0:T(1,128)S(1)}, f32[1,1024]{1,0:T(1,128)}, u32[]{:S(2)}) copy-start(f32[1,1024]{1,0:T(1,128)} %get-tuple-element.94) | copy-start | bytes 12292
  180.5 17.6 %collective-permute-start.5 = (bf16[1,512,256]{2,1,0:T(8,128)(2,1)S(1)}, bf16[1,512,256]{2,1,0:T(8,128)(2,1)S(1)}, u32[]{:S(2)}, u32[]{:S(2)}) collective-permute-start(bf16[1,512,256]{2,1,0:T(8,128)(2,1)S(1)} %get-tuple-element.162), channel_id=1, source_target_pairs={{0,24},{8,0},{16,8},{24,16},{1,25},{9,1},{17,9},{25,17},{2,26},{10... | collective-permute-start | bytes 786440 | tf_op jit(solution)/shard_map/ppermute | solution.py:2123
  195.7 4.0 collective-permute-start.8
  198.2 1.5 copy-start.4
  240.6 38.1 %copy-start.3 = (f32[8,1024]{1,0:T(8,128)S(1)}, f32[8,1024]{1,0:T(8,128)}, u32[]{:S(2)}) copy-start(f32[8,1024]{1,0:T(8,128)} %get-tuple-element.130) | copy-start | bytes 98308
  312.9 58.7 %collective-permute-start.9 = (bf16[2,1024,640]{2,1,0:T(8,128)(2,1)}, bf16[2,1024,640]{2,1,0:T(8,128)(2,1)S(1)}, u32[]{:S(2)}, u32[]{:S(2)}) collective-permute-start(bf16[2,1024,640]{2,1,0:T(8,128)(2,1)} %get-tuple-element.124), channel_id=1, source_target_pairs={{0,4},{2,6},{4,0},{6,2},{1,5},{3,7},{5,1},{7,3},{8,12},{10,14},{12... | collective-permute-start | bytes 7864328 | tf_op jit(solution)/shard_map/ppermute | solution.py:2102
  314.5 54.4 %collective-permute-start.10 = (bf16[1024,1024]{1,0:T(8,128)(2,1)}, bf16[1024,1024]{1,0:T(8,128)(2,1)}, u32[]{:S(2)}, u32[]{:S(2)}) collective-permute-start(bf16[1024,1024]{1,0:T(8,128)(2,1)} %get-tuple-element.125), channel_id=1, source_target_pairs={{0,1},{1,0},{2,3},{3,2},{4,5},{5,4},{6,7},{7,6},{8,9},{9,8},{10,11... | collective-permute-start | bytes 6291464 | tf_op jit(solution)/shard_map/ppermute | solution.py:2102
  371.6 1.6 copy-start.6
  439.7 120.7 %copy-start.2 = (f32[8,896]{1,0:T(8,128)S(1)}, f32[8,896]{1,0:T(8,128)}, u32[]{:S(2)}) copy-start(f32[8,896]{1,0:T(8,128)} %get-tuple-element.155) | copy-start | bytes 86020
  566.6 4.6 copy-start.1

commit v8 on v7

--- a/solution.py
+++ b/solution.py
@@ -307,11 +307,11 @@
         store(unit, wide, jnp.concatenate(tops, axis=0), jnp.concatenate(totals, axis=0))
 
     def listed_group(group, _):
-        together([listed_block(first_unit + 4 * group + place) for place in range(4)])
+        together([listed_block(first_unit + 6 * group + place) for place in range(6)])
         return 0
 
-    lax.fori_loop(0, (units - first_unit) // 4, listed_group, 0)
-    together([listed_block(units - 1 - place) for place in range((units - first_unit) % 4)])
+    lax.fori_loop(0, (units - first_unit) // 6, listed_group, 0)
+    together([listed_block(units - 1 - place) for place in range((units - first_unit) % 6)])
 
 
 def backward_kernel(
@@ -422,11 +422,11 @@
         units = blocks // 2
 
         def listed_group(group, _):
-            together([listed_block(first_unit + 4 * group + place, half) for place in range(4)])
+            together([listed_block(first_unit + 6 * group + place, half) for place in range(6)])
             return 0
 
-        lax.fori_loop(0, (units - first_unit) // 4, listed_group, 0)
-        together([listed_block(units - 1 - place, half) for place in range((units - first_unit) % 4)])
+        lax.fori_loop(0, (units - first_unit) // 6, listed_group, 0)
+        together([listed_block(units - 1 - place, half) for place in range((units - first_unit) % 6)])
 
     def finish(block, _):
         here = block_at(block)
@@ -1685,7 +1685,10 @@
         )
         input_ref[here, :] = (hidden_grad_ref[here, :] + inverse * through).astype(BF16)
         if index_of:
-            pair(chunk).start()
+            @pl.when(chunk < chunks - 1)
+            def _():
+                pair(chunk).start()
+
         sums_ref[0:1, :] += jnp.sum(total * unit, axis=0, keepdims=True)
         sums_ref[1:2, :] += jnp.sum(total, axis=0, keepdims=True)
 
@@ -1755,6 +1758,7 @@
     lax.fori_loop(0, wait_for + chunks, advance, 0)
     if index_of:
         vector_sum.start(in_rows(sums_ref[0:2, :] + vectors_ref[0:2, :], group.shape[2]))
+        pair(chunks - 1).start()
     vector_sum.middle()
 
     def finish(index, _):

time: 577 us -> 574 us (level)
  transfers between devices with their start and end apart: 11 -> 11, of which waited for: 2 -> 2; matrix products, arithmetic and copies ran while one was open for 1% -> 1% of each run, Pallas kernels for 40% -> 41%
where the time goes in v8:
time: 574 us; the launch traced here: 569 us
  Pallas kernels  532 us (93%)
  starting transfers between devices  13.5 us (2%)
  local copies, waits for them, and re-layouts  11 us (2%)
    pallas_call x2, Pallas kernels, return_part(): pl.pallas_call(functools.partial(return_kernel, count, chunks, 2, index,...  182 us
    pallas_call x1, Pallas kernels, gather_project(): pl.pallas_call(functools.partial(gather_kernel, count, chunks), in_specs=...  141 us
    pallas_call x2, Pallas kernels, token_part(): pl.pallas_call(functools.partial(token_kernel, min(256, rows), index), gr...  76.5 us
    pallas_call x1, Pallas kernels, attention_backward(): pl.pallas_call(functools.partial(backward_kernel, heads), grid=(1,), in_s...  48.3 us
    pallas_call x2, Pallas kernels, attention_forward(): pl.pallas_call(functools.partial(forward_kernel, heads, half), grid=(1,),...  37.3 us
    pallas_call x1, Pallas kernels, weight_grads(): pl.pallas_call(functools.partial(weight_grad_kernel, tile), in_specs=[vme...  32.8 us
  transfers between devices with their start and end apart: 11, of which 2 were waited for; matrix products, arithmetic and copies ran while one was open for 1% of the time, Pallas kernels for 41%

profile of v8, /device:TPU:0, one launch (start us, length us, event | category | flops | bytes accessed | tf_op | source)
XLA Modules:
  0.0 568.6 jit_solution(13705946004213273039)
XLA Ops:
  1.9 3.0 collective-permute-start
  4.9 2.6 collective-permute-start.1
  7.5 140.7 %shard_map.229 = (bf16[4,1024,1024]{2,1,0:T(8,128)(2,1)}, bf16[4,1024,768]{2,1,0:T(8,128)(2,1)}, bf16[1024,768]{1,0:T(8,128)(2,1)}, bf16[1024,768]{1,0:T(8,128)(...) custom-call(f32[2,1024,1024]{2,1,0:T(8,128)} %x_ref.9, ...), custom_call_target="tpu_custom_call" | custom-call | flops 149999992832 | bytes 1 | tf_op jit(solution)/shard_map/pallas_call | solution.py:1106
  152.8 22.4 %shard_map.230 = (bf16[4,512,256]{2,1,0:T(8,128)(2,1)}, f32[32,8,256]{2,1,0:T(8,128)}) custom-call(s32[4]{0:T(128)} %bitcast.72, s32[512]{0:T(512)} %min.12.lists_ref, s32[512]{0:T(512)} %reshape.163.admit_ref, bf16[4096,768]{1,0:T(8,128)(2,1)} %bitcast.59, bf16[4096,768]{1,0:T(8,128)(2,1)} %bitcast.60, bf16[4096,768]{1,0:T(8,128)(2,1)} %bitcast.61), custom_call_target="tpu_custom_call" | custom-call | flops 10737418240 | bytes 8388608 | tf_op jit(solution)/shard_map/pallas_call | solution.py:456
  175.2 1.3 constant_dynamic-slice_fusion
  176.5 3.9 collective-permute-start.4
  180.6 14.9 %shard_map.231 = (bf16[4,512,256]{2,1,0:T(8,128)(2,1)}, f32[32,8,256]{2,1,0:T(8,128)}) custom-call(s32[4]{0:T(128)} %bitcast.73, s32[512]{0:T(512)} %min.12.lists_ref, s32[512]{0:T(512)} %reshape.163.admit_ref, bf16[4096,768]{1,0:T(8,128)(2,1)} %bitcast.62, bf16[4096,768]{1,0:T(8,128)(2,1)} %bitcast.63, bf16[4096,768]{1,0:T(8,128)(2,1)} %bitcast.64), custom_call_target="tpu_custom_call" | custom-call | flops 10737418240 | bytes 8388608 | tf_op jit(solution)/shard_map/pallas_call | solution.py:456
  195.5 2.4 collective-permute-done.4
  198.2 1.4 fusion.att_ref
  200.7 39.7 %shard_map.232 = (bf16[512,1024]{1,0:T(8,128)(2,1)}, f32[512,1024]{1,0:T(8,128)}, bf16[4,512,256]{2,1,0:T(8,128)(2,1)}, bf16[1024,4096]{1,0:T(8,128)(2,1)}, bf16...) custom-call(s32[4]{0:T(128)} %bitcast.74, ...), custom_call_target="tpu_custom_call" | custom-call | flops 19327352832 | bytes 33554432 | tf_op jit(solution)/shard_map/pallas_call | solution.py:726
  240.4 36.8 %shard_map.233 = (bf16[512,1024]{1,0:T(8,128)(2,1)}, f32[512,1024]{1,0:T(8,128)}, bf16[4,512,256]{2,1,0:T(8,128)(2,1)}, bf16[1024,4096]{1,0:T(8,128)(2,1)}, bf16...) custom-call(s32[4]{0:T(128)} %bitcast.75, ...), custom_call_target="tpu_custom_call", output_to_operand_aliasing={{3}: (18, {}), {4}: (19, {}), {5}: (20, {}), {6}: (21, {}),... | custom-call | flops 19327352832 | bytes 33554432 | tf_op jit(solution)/shard_map/pallas_call | solution.py:726
  277.2 1.0 slice_add_fusion
  279.8 32.8 %shard_map.234 = (bf16[2,1024,640]{2,1,0:T(8,128)(2,1)}, bf16[2,1024,640]{2,1,0:T(8,128)(2,1)}, bf16[1024,1024]{1,0:T(8,128)(2,1)}, bf16[1024,1024]{1,0:T(8,128)...) custom-call(bf16[1024,1024]{1,0:T(8,128)(2,1)} %get-tuple-element.112.second_ref, ...), custom_call_target="tpu_custom_call" | custom-call | flops 19327352832 | bytes 16777216 | tf_op jit(solution)/shard_map/pallas_call | solution.py:2074
  312.6 1.6 collective-permute-start.9
  314.1 1.5 collective-permute-start.10
  315.7 4.5 shard_map.235
  320.2 48.3 %shard_map.236 = bf16[4096,768]{1,0:T(8,128)(2,1)} custom-call(s32[4]{0:T(128)} %bitcast.76, s32[512]{0:T(512)} %min.12.lists_ref, s32[512]{0:T(512)} %reshape.163.admit_ref, bf16[4096,768]{1,0:T(8,128)(2,1)} %bitcast.65, bf16[4096,768]{1,0:T(8,128)(2,1)} %bitcast.66, bf16[4096,768]{1,0:T(8,128)(2,1)} %bitcast.67, ...), custom_call_target="tpu_custom_call" | custom-call | flops 32212254720 | bytes 20971520 | tf_op jit(solution)/shard_map/pallas_call | solution.py:478
  368.5 2.9 collective-permute-done.9.rest_1_
  371.4 1.6 copy-done.6
  372.9 66.5 %shard_map.237 = (bf16[512,1024]{1,0:T(8,128)(2,1)}, f32[8,1024]{1,0:T(8,128)}, f32[8,896]{1,0:T(8,128)}, bf16[512,1024]{1,0:T(8,128)(2,1)}, bf16[1024,640]{1,0:...) custom-call(bf16[4,1024,768]{2,1,0:T(8,128)(2,1)} %bitcast.68, ...), custom_call_target="tpu_custom_call" | custom-call | flops 80000000000 | bytes 1 | tf_op jit(solution)/shard_map/pallas_call | solution.py:1851
  439.5 115.9 %shard_map.238 = (bf16[512,1024]{1,0:T(8,128)(2,1)}, f32[8,1024]{1,0:T(8,128)}, f32[8,256]{1,0:T(8,128)}, bf16[512,1024]{1,0:T(8,128)(2,1)}, bf16[512,1024]{1,0:...) custom-call(bf16[4,1024,768]{2,1,0:T(8,128)(2,1)} %bitcast.69, ...), custom_call_target="tpu_custom_call" | custom-call | flops 80000000000 | bytes 1 | tf_op jit(solution)/shard_map/pallas_call | solution.py:1851
  555.4 0.8 slice_bitcast_fusion
  558.6 5.0 shard_map.240
  563.5 4.6 shard_map.239
  (73 shorter events, 11.4 us)
Async XLA Ops:
  0.6 0.7 copy-start
  1.9 147.8 %collective-permute-start = (s32[16,3]{0,1:T(4,128)}, s32[16,3]{0,1:T(4,128)}, u32[]{:S(2)}, u32[]{:S(2)}) collective-permute-start(s32[16,3]{0,1:T(4,128)} %bitcast.33.clone.2), channel_id=1, source_target_pairs={{0,8},{8,0},{16,24},{24,16},{1,9},{9,1},{17,25},{25,17},{2,10},{10... | collective-permute-start | bytes 584 | tf_op jit(solution)/shard_map/ppermute | solution.py:2106
  4.9 144.8 %collective-permute-start.1 = (s32[16,3]{0,1:T(4,128)}, s32[16,3]{0,1:T(4,128)}, u32[]{:S(2)}, u32[]{:S(2)}) collective-permute-start(s32[16,3]{0,1:T(4,128)} %bitcast.33.clone.2), channel_id=1, source_target_pairs={{0,16},{8,24},{16,0},{24,8},{1,17},{9,25},{17,1},{25,9},{2,18},{10... | collective-permute-start | bytes 584 | tf_op jit(solution)/shard_map/ppermute | solution.py:2106
  7.5 142.2 %collective-permute-start.2 = (s32[16,3]{0,1:T(4,128)}, s32[16,3]{0,1:T(4,128)}, u32[]{:S(2)}, u32[]{:S(2)}) collective-permute-start(s32[16,3]{0,1:T(4,128)} %bitcast.33.clone.2), channel_id=1, source_target_pairs={{0,24},{8,16},{16,8},{24,0},{1,25},{9,17},{17,9},{25,1},{2,26},{10... | collective-permute-start | bytes 584 | tf_op jit(solution)/shard_map/ppermute | solution.py:2106
  7.5 141.5 %copy-start.7 = (s32[2,4]{1,0:T(2,128)S(1)}, s32[2,4]{1,0:T(2,128)}, u32[]{:S(2)}) copy-start(s32[2,4]{1,0:T(2,128)} %param.15) | copy-start | bytes 100
  148.2 51.3 %collective-permute-start.6 = (bf16[1024,1024]{1,0:T(8,128)(2,1)}, bf16[1024,1024]{1,0:T(8,128)(2,1)}, u32[]{:S(2)}, u32[]{:S(2)}) collective-permute-start(bf16[1024,1024]{1,0:T(8,128)(2,1)} %get-tuple-element.92.up_near_ref), channel_id=1, source_target_pairs={{0,2},{2,0},{4,6},{6,4},{1,3},{3,1},{5,7},{7,5},{8,10},{10,8},{12,... | collective-permute-start | bytes 6291464 | tf_op jit(solution)/shard_map/ppermute | solution.py:2106
  148.3 51.2 %collective-permute-start.7 = (bf16[1024,1024]{1,0:T(8,128)(2,1)}, bf16[1024,1024]{1,0:T(8,128)(2,1)}, u32[]{:S(2)}, u32[]{:S(2)}) collective-permute-start(bf16[1024,1024]{1,0:T(8,128)(2,1)} %get-tuple-element.93.down_near_ref), channel_id=1, source_target_pairs={{0,2},{2,0},{4,6},{6,4},{1,3},{3,1},{5,7},{7,5},{8,10},{10,8},{12,... | collective-permute-start | bytes 6291464 | tf_op jit(solution)/shard_map/ppermute | solution.py:2106
  176.4 19.0 %collective-permute-start.3 = (bf16[1,512,256]{2,1,0:T(8,128)(2,1)S(1)}, bf16[1,512,256]{2,1,0:T(8,128)(2,1)S(1)}, u32[]{:S(2)}, u32[]{:S(2)}) collective-permute-start(bf16[1,512,256]{2,1,0:T(8,128)(2,1)S(1)} %get-tuple-element.164), channel_id=1, source_target_pairs={{0,8},{8,16},{16,24},{24,0},{1,9},{9,17},{17,25},{25,1},{2,10},{10... | collective-permute-start | bytes 786440 | tf_op jit(solution)/shard_map/ppermute | solution.py:2127
  176.5 21.4 %collective-permute-start.4 = (bf16[1,512,256]{2,1,0:T(8,128)(2,1)S(1)}, bf16[1,512,256]{2,1,0:T(8,128)(2,1)S(1)}, u32[]{:S(2)}, u32[]{:S(2)}) collective-permute-start(bf16[1,512,256]{2,1,0:T(8,128)(2,1)S(1)} %get-tuple-element.163), channel_id=1, source_target_pairs={{0,16},{8,24},{16,0},{24,8},{1,17},{9,25},{17,1},{25,9},{2,18},{10... | collective-permute-start | bytes 786440 | tf_op jit(solution)/shard_map/ppermute | solution.py:2127
  180.4 15.1 %copy-start.5 = (f32[1,1024]{1,0:T(1,128)S(1)}, f32[1,1024]{1,0:T(1,128)}, u32[]{:S(2)}) copy-start(f32[1,1024]{1,0:T(1,128)} %get-tuple-element.94) | copy-start | bytes 12292
  180.4 17.6 %collective-permute-start.5 = (bf16[1,512,256]{2,1,0:T(8,128)(2,1)S(1)}, bf16[1,512,256]{2,1,0:T(8,128)(2,1)S(1)}, u32[]{:S(2)}, u32[]{:S(2)}) collective-permute-start(bf16[1,512,256]{2,1,0:T(8,128)(2,1)S(1)} %get-tuple-element.162), channel_id=1, source_target_pairs={{0,24},{8,0},{16,8},{24,16},{1,25},{9,1},{17,9},{25,17},{2,26},{10... | collective-permute-start | bytes 786440 | tf_op jit(solution)/shard_map/ppermute | solution.py:2127
  195.5 4.0 collective-permute-start.8
  198.1 1.5 copy-start.4
  240.4 37.9 %copy-start.3 = (f32[8,1024]{1,0:T(8,128)S(1)}, f32[8,1024]{1,0:T(8,128)}, u32[]{:S(2)}) copy-start(f32[8,1024]{1,0:T(8,128)} %get-tuple-element.130) | copy-start | bytes 98308
  312.6 58.8 %collective-permute-start.9 = (bf16[2,1024,640]{2,1,0:T(8,128)(2,1)}, bf16[2,1024,640]{2,1,0:T(8,128)(2,1)S(1)}, u32[]{:S(2)}, u32[]{:S(2)}) collective-permute-start(bf16[2,1024,640]{2,1,0:T(8,128)(2,1)} %get-tuple-element.124), channel_id=1, source_target_pairs={{0,4},{2,6},{4,0},{6,2},{1,5},{3,7},{5,1},{7,3},{8,12},{10,14},{12... | collective-permute-start | bytes 7864328 | tf_op jit(solution)/shard_map/ppermute | solution.py:2106
  314.1 54.3 %collective-permute-start.10 = (bf16[1024,1024]{1,0:T(8,128)(2,1)}, bf16[1024,1024]{1,0:T(8,128)(2,1)}, u32[]{:S(2)}, u32[]{:S(2)}) collective-permute-start(bf16[1024,1024]{1,0:T(8,128)(2,1)} %get-tuple-element.125), channel_id=1, source_target_pairs={{0,1},{1,0},{2,3},{3,2},{4,5},{5,4},{6,7},{7,6},{8,9},{9,8},{10,11... | collective-permute-start | bytes 6291464 | tf_op jit(solution)/shard_map/ppermute | solution.py:2106
  371.4 1.6 copy-start.6
  439.4 117.9 %copy-start.2 = (f32[8,896]{1,0:T(8,128)S(1)}, f32[8,896]{1,0:T(8,128)}, u32[]{:S(2)}) copy-start(f32[8,896]{1,0:T(8,128)} %get-tuple-element.155) | copy-start | bytes 86020
  563.5 4.6 copy-start.1
